TPU v7x, 32 devices: a whole 2x2x4 slice. The times are simulated.
32 devices in a mesh: groups: 2 (over y), tm: 4 (over z), space: 2 (over x), clip: 2 (over core).
Axes of the slice: x: 2, y: 2, z: 4, core: 2. Of those that a mesh axis runs over, the one named last changes fastest.
Arguments:
- latents: bfloat16 [4, 16, 8, 6144], P(('groups', 'clip'), 'tm', 'space'), parts along dimension 0, may hold values from -6 to 6
- frame_counts: int32 [4], P(('groups', 'clip')), parts along dimension 0, may hold values from 2 to 16, as said below
- gain_first: float32 [192], replicated, may hold values from 0.5 to 1.5
- bias_first: float32 [192], replicated, may hold values from -3 to 3
- weight_first: bfloat16 [3, 3, 3, 192, 192], replicated, may hold values from -0.078125 to 0.078125
- gain_second: float32 [192], replicated, may hold values from 0.5 to 1.5
- bias_second: float32 [192], replicated, may hold values from -3 to 3
- weight_second: bfloat16 [3, 3, 3, 192, 192], replicated, may hold values from -0.078125 to 0.078125
Outputs:
- encoded: bfloat16 [4, 16, 8, 6144], P(('groups', 'clip'), 'tm', 'space'), parts along dimension 0
There are 2 independent parts, one for each index of `groups`. A program takes and returns all parts, laid end to end along the dimension named above; an argument that names none is the same for every part. Nothing has to cross between parts.
Inputs may be any that keep to these rules, and one draw needn't show every extreme that they name: `frame_counts`: in every part exactly one clip has all 16 frames valid; every other clip has fewer.
All inputs are finite; a program needn't handle non-finite values.
Results may differ from a plain program's by a relative error of at most 0.007.
Values may be sent and summed in bfloat16 or wider, within the bound.
No kernel may reach another device: no remote copies, remote signals or barrier semaphores. Data moves between devices by JAX's collectives and lax.ppermute only.
A program may use at most 64 MiB of HBM per device.

v0:
```python
import jax
import jax.numpy as jnp
from jax import lax
from jax.sharding import PartitionSpec as P


def from_behind(x, axis, by):
    size = lax.axis_size(axis)
    pairs = [(i, i + by) for i in range(size) if 0 <= i + by < size]
    return lax.ppermute(x, axis, pairs)


def padded_2(x, sides, width):
    for axis, dim in sides:
        size, length = (lax.axis_size(axis), x.shape[dim])
        up = [(i, (i + 1) % size) for i in range(size - 1)]
        down = [(j, i) for i, j in up]
        last = lax.slice_in_dim(x, length - width, length, axis=dim)
        first = lax.slice_in_dim(x, 0, width, axis=dim)
        before = lax.ppermute(last, axis, up)
        after = lax.ppermute(first, axis, down)
        x = jnp.concatenate([before, x, after], axis=dim)
    return x


def norm_silu(values, gain):
    values = values.astype(jnp.float32)
    mean_square = jnp.mean(values * values, axis=-1, keepdims=True)
    scaled = values * lax.rsqrt(mean_square + 1e-06) * gain
    return jax.nn.silu(scaled).astype(jnp.bfloat16)


def conv_local(widened, kernel, out_frames, out_rows):
    channels = widened.shape[3]
    band_cols = widened.shape[2]
    padded = jnp.pad(widened, ((0, 0), (0, 0), (1, 1), (0, 0)))
    stacked = jnp.concatenate(
        [
            padded[:, :, 0:band_cols],
            padded[:, :, 1 : band_cols + 1],
            padded[:, :, 2 : band_cols + 2],
        ],
        axis=3,
    )
    merged = kernel.reshape(3, 3, 3 * channels, channels)
    total = jnp.zeros((out_frames * out_rows * band_cols, channels), jnp.float32)
    for shift_time in range(3):
        for shift_row in range(3):
            patch_rows = stacked[
                shift_time : shift_time + out_frames, shift_row : shift_row + out_rows
            ]
            total = total + jnp.dot(
                patch_rows.reshape(-1, 3 * channels),
                merged[shift_time, shift_row],
                preferred_element_type=jnp.float32,
            )
    return total.reshape(out_frames, out_rows, band_cols, channels)


def shards(
    latents,
    frame_counts,
    gain_first,
    bias_first,
    weight_first,
    gain_second,
    bias_second,
    weight_second,
):
    channels = gain_first.shape[0]
    span_frames, band_rows, flat_width = (latents.shape[1], latents.shape[2], latents.shape[3])
    band_cols = flat_width // channels
    limit_frames = frame_counts[0]
    first_frame = lax.axis_index("tm") * span_frames
    first_row = lax.axis_index("space") * band_rows
    total_rows = band_rows * lax.axis_size("space")
    frame_index = first_frame + jnp.arange(span_frames, dtype=jnp.int32)
    frame_mask = (frame_index < limit_frames)[:, None, None, None]
    shaped = latents[0].reshape(span_frames, band_rows, band_cols, channels)
    masked_input = jnp.where(frame_mask, shaped, jnp.zeros_like(shaped))
    flat_input = masked_input.reshape(span_frames, band_rows, flat_width)
    earlier = from_behind(flat_input, "tm", 1)
    joined = jnp.concatenate([earlier, flat_input], axis=0)
    rimmed = padded_2(joined, (("space", 1),), 2)
    window = rimmed.reshape(span_frames + 4, band_rows + 4, band_cols, channels)
    normed_first = norm_silu(window, gain_first)
    convolved = conv_local(normed_first, weight_first, span_frames + 2, band_rows + 2)
    wide_frames = first_frame - 2 + jnp.arange(span_frames + 2, dtype=jnp.int32)
    wide_rows = first_row - 1 + jnp.arange(band_rows + 2, dtype=jnp.int32)
    keep_frames = (wide_frames >= 0) & (wide_frames < limit_frames)
    keep_rows = (wide_rows >= 0) & (wide_rows < total_rows)
    keep_both = keep_frames[:, None, None, None] & keep_rows[None, :, None, None]
    hidden_first = jnp.where(keep_both, convolved + bias_first, 0.0).astype(jnp.bfloat16)
    widened_second = norm_silu(hidden_first, gain_second)
    second = conv_local(widened_second, weight_second, span_frames, band_rows)
    summed = masked_input.astype(jnp.float32) + second + bias_second
    encoded = jnp.where(frame_mask, summed, 0.0).astype(jnp.bfloat16)
    return encoded.reshape(1, span_frames, band_rows, flat_width)


def solution(mesh):
    return jax.shard_map(
        shards,
        mesh=mesh,
        in_specs=(
            P(("groups", "clip"), "tm", "space", None),
            P(("groups", "clip")),
            P(),
            P(),
            P(),
            P(),
            P(),
            P(),
        ),
        out_specs=P(("groups", "clip"), "tm", "space", None),
        check_vma=False,
    )
```

profile of v0, /device:TPU:16, one launch (start us, length us, event | category | flops | bytes accessed | tf_op | source)
XLA Modules:
  0.0 45.9 jit_solution(9589094844563484832)
XLA Ops:
  0.7 1.1 %bitcast_select_fusion = bf16[4,4,6144]{2,1,0:T(4,128)(2,1)S(1)} fusion(bf16[1,4,4,6144]{3,2,1,0:T(4,128)(2,1)} %param.8, pred[4]{0:T(512)(128)(4,1)S(1)} %add_compare_fusion), kind=kLoop, calls=%fused_computation.54 | loop fusion | flops 98304 | bytes 393220 | tf_op jit(solution)/shard_map/jit(_where)/select_n | solution.py:80
  1.8 3.5 %collective-permute-start = (bf16[4,4,6144]{2,1,0:T(4,128)(2,1)S(1)}, bf16[4,4,6144]{2,1,0:T(4,128)(2,1)S(1)}, u32[]{:S(2)}, u32[]{:S(2)}) collective-permute-start(bf16[4,4,6144]{2,1,0:T(4,128)(2,1)S(1)} %bitcast_select_fusion), channel_id=1, source_target_pairs={{0,4},{4,8},{8,12},{1,5},{5,9},{9,13},{2,6},{6,10},{10,14},{3,7},{... | collective-permute-start | bytes 589832 | tf_op jit(solution)/shard_map/ppermute | solution.py:10
  5.3 5.0 %collective-permute-done = bf16[4,4,6144]{2,1,0:T(4,128)(2,1)S(1)} collective-permute-done((bf16[4,4,6144]{2,1,0:T(4,128)(2,1)S(1)}, bf16[4,4,6144]{2,1,0:T(4,128)(2,1)S(1)}, u32[]{:S(2)}, u32[]{:S(2)}) %collective-permute-start) | collective-permute-done | bytes 196640 | tf_op jit(solution)/shard_map/ppermute | solution.py:10
  10.6 3.4 %collective-permute-start.1 = (bf16[8,2,6144]{2,1,0:T(2,128)(2,1)S(1)}, bf16[8,2,6144]{2,1,0:T(2,128)(2,1)S(1)}, u32[]{:S(2)}, u32[]{:S(2)}) collective-permute-start(bf16[8,2,6144]{2,1,0:T(2,128)(2,1)S(1)} %get-tuple-element.27), channel_id=1, source_target_pairs={{0,2},{1,3},{4,6},{5,7},{8,10},{9,11},{12,14},{13,15},{16,18},{17,... | collective-permute-start | bytes 589832 | tf_op jit(solution)/shard_map/ppermute | solution.py:20
  14.0 1.3 %collective-permute-start.2 = (bf16[8,2,6144]{2,1,0:T(2,128)(2,1)S(1)}, bf16[8,2,6144]{2,1,0:T(2,128)(2,1)S(1)}, u32[]{:S(2)}, u32[]{:S(2)}) collective-permute-start(bf16[8,2,6144]{2,1,0:T(2,128)(2,1)S(1)} %get-tuple-element.28), channel_id=1, source_target_pairs={{2,0},{3,1},{6,4},{7,5},{10,8},{11,9},{14,12},{15,13},{18,16},{19,... | collective-permute-start | bytes 589832 | tf_op jit(solution)/shard_map/ppermute | solution.py:21
  15.6 0.7 %add.178 = f32[32,192]{1,0:T(8,128)S(1)} broadcast(f32[192]{0:T(256)} %param.14), dimensions={1} | broadcast | bytes 25344 | tf_op jit(solution)/shard_map/add | solution.py:96
  16.3 0.9 %collective-permute-done.1 = bf16[8,2,6144]{2,1,0:T(2,128)(2,1)S(1)} collective-permute-done((bf16[8,2,6144]{2,1,0:T(2,128)(2,1)S(1)}, bf16[8,2,6144]{2,1,0:T(2,128)(2,1)S(1)}, u32[]{:S(2)}, u32[]{:S(2)}) %collective-permute-start.1) | collective-permute-done | bytes 196640 | tf_op jit(solution)/shard_map/ppermute | solution.py:20
  17.3 4.3 %collective-permute-done.2 = bf16[8,2,6144]{2,1,0:T(2,128)(2,1)S(1)} collective-permute-done((bf16[8,2,6144]{2,1,0:T(2,128)(2,1)S(1)}, bf16[8,2,6144]{2,1,0:T(2,128)(2,1)S(1)}, u32[]{:S(2)}, u32[]{:S(2)}) %collective-permute-start.2) | collective-permute-done | bytes 196640 | tf_op jit(solution)/shard_map/ppermute | solution.py:21
  21.6 1.8 %maximum_convert_fusion = f32[8,8,6144]{2,1,0:T(8,128)} fusion(bf16[8,2,6144]{2,1,0:T(2,128)(2,1)S(1)} %collective-permute-done.2, bf16[4,4,6144]{2,1,0:T(4,128)(2,1)S(1)} %bitcast_select_fusion, bf16[4,4,6144]{2,1,0:T(4,128)(2,1)S(1)} %collective-permute-done, bf16[8,2,6144]{2,1,0:T(2,128)(2,1)S(1)} %collective-permute-done.1), kind=kLoop, calls=%fused_computation.26 | loop fusion | flops 3145728 | bytes 2359296 | tf_op jit(solution)/shard_map/convert_element_type | solution.py:27
  23.3 2.2 %reshape.177 = f32[8,8,32,192]{3,2,1,0:T(8,128)S(1)} reshape(f32[8,8,6144]{2,1,0:T(8,128)} %maximum_convert_fusion) | data formatting | bytes 3145728 | tf_op jit(solution)/shard_map/convert_element_type | solution.py:27
  26.2 0.7 %multiply_convert_fusion = bf16[8,8,32,192]{3,2,1,0:T(8,128)(2,1)S(1)} fusion(f32[8,8,32,192]{3,2,1,0:T(8,128)S(1)} %reshape.177, f32[192]{0:T(256)S(1)} %copy-done.4, f32[8,8,32]{2,1,0:T(8,128)S(1)} %add_rsqrt_fusion), kind=kLoop, calls=%fused_computation.9 | loop fusion | flops 2752512 | bytes 2368256 | tf_op jit(solution)/shard_map/convert_element_type | solution.py:30
  26.9 0.9 %pad_slice_fusion.1 = (bf16[8,8,32,192]{3,2,1,0:T(8,128)(2,1)S(1)}, bf16[8,8,32,192]{3,2,1,0:T(8,128)(2,1)S(1)}) fusion(bf16[8,8,32,192]{3,2,1,0:T(8,128)(2,1)S(1)} %multiply_convert_fusion), kind=kLoop, calls=%fused_computation.13 | loop fusion | bytes 2359296 | tf_op jit(solution)/shard_map/slice | solution.py:39
  27.8 1.1 %pad_maximum_fusion = bf16[8,8,32,576]{3,2,1,0:T(8,128)(2,1)S(1)} fusion(bf16[8,8,32,192]{3,2,1,0:T(8,128)(2,1)S(1)} %get-tuple-element.24, bf16[8,8,32,192]{3,2,1,0:T(8,128)(2,1)S(1)} %multiply_convert_fusion, bf16[8,8,32,192]{3,2,1,0:T(8,128)(2,1)S(1)} %get-tuple-element.23), kind=kLoop, calls=%fused_computation.8 | loop fusion | flops 7077888 | bytes 4718592 | tf_op jit(solution)/shard_map/concatenate | solution.py:37
  28.9 2.0 %fusion.3 = (bf16[6,6,32,576]{3,2,1,0:T(8,128)(2,1)S(1)}, bf16[6,6,32,576]{3,2,1,0:T(8,128)(2,1)S(1)}, bf16[6,6,32,576]{3,2,1,0:T(8,128)(2,1)S(1)}, bf16[6,6,32,...) fusion(bf16[8,8,32,576]{3,2,1,0:T(8,128)(2,1)S(1)} %pad_maximum, ...), kind=kLoop, calls=%fused_computation.61 | loop fusion | bytes 23887872 | tf_op jit(solution)/shard_map/slice | solution.py:49
  31.0 0.6 %fusion.1 = f32[1152,192]{0,1:T(8,128)S(1)} fusion(bf16[1152,576]{1,0:T(8,128)(2,1)S(1)} %bitcast.108, bf16[3,3,576,192]{3,2,1,0:T(8,128)(2,1)S(1)} %bitcast.110), kind=kOutput, calls=%fused_computation.51 | convolution fusion | flops 254803968 | bytes 2654208 | tf_op jit(solution)/shard_map/dot_general | solution.py:52
  31.6 0.7 %convolution_add_fusion.7 = f32[1152,192]{0,1:T(8,128)S(1)} fusion(f32[1152,192]{0,1:T(8,128)S(1)} %fusion.1, bf16[1152,576]{1,0:T(8,128)(2,1)S(1)} %bitcast.107, bf16[3,3,576,192]{3,2,1,0:T(8,128)(2,1)S(1)} %bitcast.111), kind=kOutput, calls=%fused_computation.7 | convolution fusion | flops 255025152 | bytes 3538944 | tf_op jit(solution)/shard_map/dot_general | solution.py:52
  32.3 0.7 %convolution_add_fusion.6 = f32[1152,192]{0,1:T(8,128)S(1)} fusion(f32[1152,192]{0,1:T(8,128)S(1)} %convolution_add_fusion.7, bf16[1152,576]{1,0:T(8,128)(2,1)S(1)} %bitcast.106, bf16[3,3,576,192]{3,2,1,0:T(8,128)(2,1)S(1)} %bitcast.112), kind=kOutput, calls=%fused_computation.6 | convolution fusion | flops 255025152 | bytes 3538944 | tf_op jit(solution)/shard_map/dot_general | solution.py:52
  33.6 0.7 %convolution_add_fusion.4 = f32[1152,192]{0,1:T(8,128)S(1)} fusion(f32[1152,192]{0,1:T(8,128)S(1)} %convolution_add_fusion.5, bf16[1152,576]{1,0:T(8,128)(2,1)S(1)} %bitcast.104, bf16[3,3,576,192]{3,2,1,0:T(8,128)(2,1)S(1)} %bitcast.114), kind=kOutput, calls=%fused_computation.4 | convolution fusion | flops 255025152 | bytes 3538944 | tf_op jit(solution)/shard_map/dot_general | solution.py:52
  34.9 0.7 %convolution_add_fusion.2 = f32[1152,192]{0,1:T(8,128)S(1)} fusion(f32[1152,192]{0,1:T(8,128)S(1)} %convolution_add_fusion.3, bf16[1152,576]{1,0:T(8,128)(2,1)S(1)} %bitcast.102, bf16[3,3,576,192]{3,2,1,0:T(8,128)(2,1)S(1)} %bitcast.116), kind=kOutput, calls=%fused_computation.2 | convolution fusion | flops 255025152 | bytes 3538944 | tf_op jit(solution)/shard_map/dot_general | solution.py:52
  35.6 0.6 %convolution_add_fusion.1 = f32[1152,192]{0,1:T(8,128)S(1)} fusion(f32[1152,192]{0,1:T(8,128)S(1)} %convolution_add_fusion.2, bf16[1152,576]{1,0:T(8,128)(2,1)S(1)} %bitcast.101, bf16[3,3,576,192]{3,2,1,0:T(8,128)(2,1)S(1)} %bitcast.117), kind=kOutput, calls=%fused_computation.1 | convolution fusion | flops 255025152 | bytes 3538944 | tf_op jit(solution)/shard_map/dot_general | solution.py:52
  36.3 0.7 %multiply_reduce_fusion.1 = (f32[1152]{0:T(1024)S(1)}, f32[1152,192]{0,1:T(8,128)S(1)}) fusion(f32[192]{0:T(256)S(1)} %copy-done.3, pred[1152]{0:T(1024)(128)(4,1)S(1)} %broadcast_in_dim.61, f32[1152,192]{0,1:T(8,128)S(1)} %convolution_add_fusion.1, bf16[1152,576]{1,0:T(8,128)(2,1)S(1)} %bitcast.100, bf16[3,3,576,192]{3,2,1,0:T(8,128)(2,1)S(1)} %bitcast.118), kind=kOutput, calls=%fused_computation.24 | convolution fusion | flops 256351104 | bytes 3546624 | tf_op jit(solution)/shard_map/dot_general | solution.py:52
  39.1 0.7 %fusion.4 = (bf16[4,4,32,576]{3,2,1,0:T(8,128)(2,1)S(1)}, bf16[4,4,32,576]{3,2,1,0:T(8,128)(2,1)S(1)}, bf16[4,4,32,576]{3,2,1,0:T(8,128)(2,1)S(1)}, bf16[4,4,32,...) fusion(bf16[6,6,32,576]{3,2,1,0:T(8,128)(2,1)S(1)} %pad_maximum, ...), kind=kLoop, calls=%fused_computation.62 | loop fusion | bytes 10616832 | tf_op jit(solution)/shard_map/slice | solution.py:49
  39.8 1.1 %copy-done.1 = bf16[3,3,3,192,192]{4,3,2,1,0:T(8,128)(2,1)S(1)} copy-done((bf16[3,3,3,192,192]{4,3,2,1,0:T(8,128)(2,1)S(1)}, bf16[3,3,3,192,192]{4,3,2,1,0:T(8,128)(2,1)}, u32[]{:S(2)}) %copy-start.1) | copy-done | bytes 1990680
  45.0 0.9 %select_convert_fusion.2 = bf16[1,4,4,6144]{3,2,1,0:T(4,128)(2,1)} fusion(f32[1,4,4,6144]{3,2,1,0:T(4,128)S(1)} %reshape.176, f32[6144]{0:T(1024)S(1)} %add.179, bf16[1,4,4,6144]{3,2,1,0:T(4,128)(2,1)S(1)} %copy-done.2, pred[4]{0:T(512)(128)(4,1)S(1)} %add_compare_fusion), kind=kLoop, calls=%fused_computation.31 | loop fusion | flops 589824 | bytes 811012 | tf_op jit(solution)/shard_map/convert_element_type | solution.py:97
  (40 shorter events, 8.8 us)
Async XLA Ops:
  1.8 8.5 %collective-permute-start = (bf16[4,4,6144]{2,1,0:T(4,128)(2,1)S(1)}, bf16[4,4,6144]{2,1,0:T(4,128)(2,1)S(1)}, u32[]{:S(2)}, u32[]{:S(2)}) collective-permute-start(bf16[4,4,6144]{2,1,0:T(4,128)(2,1)S(1)} %bitcast_select_fusion), channel_id=1, source_target_pairs={{0,4},{4,8},{8,12},{1,5},{5,9},{9,13},{2,6},{6,10},{10,14},{3,7},{... | collective-permute-start | bytes 589832 | tf_op jit(solution)/shard_map/ppermute | solution.py:10
  10.6 6.7 %collective-permute-start.1 = (bf16[8,2,6144]{2,1,0:T(2,128)(2,1)S(1)}, bf16[8,2,6144]{2,1,0:T(2,128)(2,1)S(1)}, u32[]{:S(2)}, u32[]{:S(2)}) collective-permute-start(bf16[8,2,6144]{2,1,0:T(2,128)(2,1)S(1)} %get-tuple-element.27), channel_id=1, source_target_pairs={{0,2},{1,3},{4,6},{5,7},{8,10},{9,11},{12,14},{13,15},{16,18},{17,... | collective-permute-start | bytes 589832 | tf_op jit(solution)/shard_map/ppermute | solution.py:20
  14.0 7.6 %collective-permute-start.2 = (bf16[8,2,6144]{2,1,0:T(2,128)(2,1)S(1)}, bf16[8,2,6144]{2,1,0:T(2,128)(2,1)S(1)}, u32[]{:S(2)}, u32[]{:S(2)}) collective-permute-start(bf16[8,2,6144]{2,1,0:T(2,128)(2,1)S(1)} %get-tuple-element.28), channel_id=1, source_target_pairs={{2,0},{3,1},{6,4},{7,5},{10,8},{11,9},{14,12},{15,13},{18,16},{19,... | collective-permute-start | bytes 589832 | tf_op jit(solution)/shard_map/ppermute | solution.py:21
  25.5 0.7 %copy-start.4 = (f32[192]{0:T(256)S(1)}, f32[192]{0:T(256)}, u32[]{:S(2)}) copy-start(f32[192]{0:T(256)} %param.10) | copy-start | bytes 2308
  28.9 2.1 %copy-start = (bf16[3,3,3,192,192]{4,3,2,1,0:T(8,128)(2,1)S(1)}, bf16[3,3,3,192,192]{4,3,2,1,0:T(8,128)(2,1)}, u32[]{:S(2)}) copy-start(bf16[3,3,3,192,192]{4,3,2,1,0:T(8,128)(2,1)} %param.12) | copy-start | bytes 5971972
  35.6 0.7 %copy-start.3 = (f32[192]{0:T(256)S(1)}, f32[192]{0:T(256)}, u32[]{:S(2)}) copy-start(f32[192]{0:T(256)} %param.11) | copy-start | bytes 2308
  37.0 0.7 %copy-start.5 = (f32[192]{0:T(256)S(1)}, f32[192]{0:T(256)}, u32[]{:S(2)}) copy-start(f32[192]{0:T(256)} %param.13) | copy-start | bytes 2308
  39.1 1.8 %copy-start.1 = (bf16[3,3,3,192,192]{4,3,2,1,0:T(8,128)(2,1)S(1)}, bf16[3,3,3,192,192]{4,3,2,1,0:T(8,128)(2,1)}, u32[]{:S(2)}) copy-start(bf16[3,3,3,192,192]{4,3,2,1,0:T(8,128)(2,1)} %param.15) | copy-start | bytes 5971972
  44.0 0.9 %copy-start.2 = (bf16[1,4,4,6144]{3,2,1,0:T(4,128)(2,1)S(1)}, bf16[1,4,4,6144]{3,2,1,0:T(4,128)(2,1)}, u32[]{:S(2)}) copy-start(bf16[1,4,4,6144]{3,2,1,0:T(4,128)(2,1)} %param.8) | copy-start | bytes 589828
where the time goes:
time: 46.8 us; the launch traced here: 45.9 us
  waiting for transfers between devices  10.3 us (22%)
  local copies, waits for them, and re-layouts  9.67 us (21%)
  matrix products  9.39 us (20%)
  starting transfers between devices  8.18 us (17%)
  other arithmetic  7.37 us (16%)
  between operations  1.03 us (2%)
    dot_general x18, matrix products, conv_local(): jnp.dot(patch_rows.reshape(-1, 3 * channels), merged[shift_time, shift_ro...  9.39 us
    ppermute x1, waiting for transfers between devices, from_behind(): return lax.ppermute(x, axis, pairs)  5 us
    ppermute x1, waiting for transfers between devices, padded_2(): after = lax.ppermute(first, axis, down)  4.3 us
    ppermute x1, starting transfers between devices, from_behind(): return lax.ppermute(x, axis, pairs)  3.48 us
    ppermute x1, starting transfers between devices, padded_2(): before = lax.ppermute(last, axis, up)  3.41 us
    slice x2, local copies, waits for them, and re-layouts, conv_local(): stacked[shift_time:shift_time + out_frames, shift_row:shift_row + out_rows]  2.72 us
    convert_element_type x1, local copies, waits for them, and re-layouts, norm_silu(): values = values.astype(jnp.float32)  2.18 us
    convert_element_type x1, other arithmetic, norm_silu(): values = values.astype(jnp.float32)  1.76 us
  transfers between devices with their start and end apart: 3, of which 3 were waited for; matrix products, arithmetic and copies ran while one was open for 2% of the time, Pallas kernels for 0%

commit v1 on v0

v1 whole, which is shorter than its diff:
```python
import functools

import jax
import jax.numpy as jnp
from jax import lax
from jax.experimental import pallas as pl
from jax.experimental.pallas import tpu as pltpu
from jax.sharding import PartitionSpec as P

F32 = jnp.float32
BF16 = jnp.bfloat16
LANES = 128
PAD = 8


def norm_silu_pair(t, gain, channels):
    square = t * t
    first = lax.broadcasted_iota(jnp.int32, t.shape, 1) < channels
    left = jnp.sum(jnp.where(first, square, 0.0), axis=1, keepdims=True)
    right = jnp.sum(jnp.where(first, 0.0, square), axis=1, keepdims=True)
    left = lax.rsqrt(left * (1.0 / channels) + 1e-06)
    right = lax.rsqrt(right * (1.0 / channels) + 1e-06)
    y = t * jnp.where(first, left, right) * gain
    return y * (0.5 + 0.5 * jnp.tanh(0.5 * y))


def clear_pads(stage, steps, pairs):
    stride = pairs + PAD
    zeros = jnp.zeros((PAD, LANES), F32)
    for f in range(stage.shape[0]):
        for k in range(3):
            for r in range(steps + 1):
                stage[f, k, pl.ds(r * stride, PAD), :] = zeros


def widen(dst, at, stage, f, r, pairs):
    base = r * (pairs + PAD) + PAD
    pieces = ((1, -1), (2, -1), (0, 0), (1, 0), (2, 0), (0, 1), (1, 1))
    for n, (k, shift) in enumerate(pieces):
        part = stage[f, k, pl.ds(base + shift, pairs), :]
        dst[at[0], at[1], :, n * LANES : (n + 1) * LANES] = part.astype(BF16)


def fill_window(window, stage, own, before, after, gain, keep_frame, keep_row, pairs, channels):
    frames, rows = own.shape[0], own.shape[1]
    halo = before.shape[1]
    tall = rows + 2 * halo
    wide = 2 * channels
    stride = pairs + PAD
    for f in range(frames):
        keep = keep_row & keep_frame(f)
        for p in range(pairs):
            lanes = pl.ds(p * wide, wide)
            t = jnp.concatenate(
                [ref[f, :, lanes].astype(F32) for ref in (before, own, after)], axis=0
            )
            y = norm_silu_pair(jnp.where(keep, t, 0.0), gain, channels)
            for k in range(3):
                stage[f, k, pl.ds(PAD + p, tall, stride=stride), :] = y[
                    :, k * LANES : (k + 1) * LANES
                ]
        for r in range(tall):
            widen(window, (f, r), stage, f, r, pairs)


def taps(window, weight, parity, source, frames, start, rows, a, channels):
    pairs = window.shape[2]
    low = 2 * LANES * parity
    span = 5 * LANES
    lead = span - 3 * channels
    zeros = jnp.zeros((lead, channels), BF16)
    left, right = [], []
    for b in range(3):
        part = window[source : source + frames, pl.ds(start + b, rows), :, low : low + span]
        left.append(part.reshape(frames * rows * pairs, span))
        right += [zeros, weight[a, b]] if parity == 0 else [weight[a, b], zeros]
    return jnp.dot(
        jnp.concatenate(left, axis=1), jnp.concatenate(right, axis=0), preferred_element_type=F32
    )


def place():
    return lax.axis_index("tm"), lax.axis_index("space")


def twice(ref):
    return jnp.concatenate([ref[...], ref[...]], axis=1)


def row_mask(halo, rows, total_rows):
    row = lax.axis_index("space") * rows - halo
    row = row + lax.broadcasted_iota(jnp.int32, (rows + 2 * halo, 1), 0)
    return (row >= 0) & (row < total_rows)


def first_kernel(dims, count, own, before, after, gain, weight, partial, window, stage):
    frames, rows, pairs, channels, total_rows, deep = dims
    tm, space = place()
    start = (1 - space) if deep == rows + 1 else 0
    clear_pads(stage, rows + 4, pairs)
    fill_window(
        window, stage, own, before, after, twice(gain),
        lambda f: tm * frames + f < count[0], row_mask(2, rows, total_rows), pairs, channels,
    )
    for parity in range(2):
        for a in (2, 1, 0):
            skip = 2 - a
            part = taps(window, weight, parity, 0, frames - skip, start, deep, a, channels)
            if skip == 0:
                partial[parity] = part
            else:
                at = pl.ds(skip * deep * pairs, (frames - skip) * deep * pairs)
                partial[parity, at, :] += part


def second_kernel(
    dims, count, own, earlier, before, after, partial, gain, bias, weight, gain_two, bias_two,
    weight_two, out, window, stage, total, hidden, hidden_stage, final,
):
    frames, rows, pairs, channels, total_rows, deep = dims
    tm, space = place()
    first_frame = tm * frames
    start = (1 - space) if deep == rows + 1 else 0
    fill = deep * pairs
    clear_pads(stage, rows + 4, pairs)
    clear_pads(hidden_stage, deep, pairs)
    fill_window(
        window, stage, earlier, before, after, twice(gain),
        lambda f: (tm > 0) & (first_frame - frames + f < count[0]),
        row_mask(2, rows, total_rows), pairs, channels,
    )
    late = (frames - 2) * fill
    for parity in range(2):
        total[parity, 0 : 2 * fill] = jnp.zeros((2 * fill, channels), F32)
        total[parity, 2 * fill :] = partial[parity]
        for a in (0, 1, 2):
            part = taps(window, weight, parity, a, frames - a, start, deep, a, channels)
            total[parity, 0 : (frames - a) * fill] += part

    bias_wide, gain_wide = twice(bias), twice(gain_two)
    row = lax.broadcasted_iota(jnp.int32, (fill, 1), 0) // pairs + (space * rows - 1 + start)
    row_ok = (row >= 0) & (row < total_rows)
    for h in range(frames + 2):
        at = first_frame + h - 2
        keep = row_ok & (at >= 0) & (at < count[0])
        t = jnp.concatenate([total[q, h * fill : (h + 1) * fill, :] for q in range(2)], axis=1)
        t = jnp.where(keep, t + bias_wide, 0.0).astype(BF16).astype(F32)
        y = norm_silu_pair(t, gain_wide, channels)
        hidden[h, 0] = jnp.zeros(hidden.shape[2:], BF16)
        hidden[h, rows + 1] = jnp.zeros(hidden.shape[2:], BF16)
        for r in range(deep):
            for k in range(3):
                hidden_stage[h, k, pl.ds(r * (pairs + PAD) + PAD, pairs), :] = y[
                    r * pairs : (r + 1) * pairs, k * LANES : (k + 1) * LANES
                ]
            widen(hidden, (h, start + r), hidden_stage, h, r, pairs)

    sums = []
    for parity in range(2):
        acc = taps(hidden, weight_two, parity, 0, frames, 0, rows, 0, channels)
        acc = acc + taps(hidden, weight_two, parity, 1, frames, 0, rows, 1, channels)
        sums.append(acc + taps(hidden, weight_two, parity, 2, frames, 0, rows, 2, channels))
    both = jnp.concatenate(sums, axis=1) + twice(bias_two)
    for k in range(3):
        final[k] = both[:, k * LANES : (k + 1) * LANES]
    for f in range(0, frames, 2):
        for p in range(pairs):
            for k in range(3):
                block = final[k, pl.ds(f * rows * pairs + p, 2 * rows, stride=pairs), :]
                lanes = pl.ds(p * 2 * channels + k * LANES, LANES)
                for n in range(2):
                    value = own[f + n, :, lanes].astype(F32) + block[n * rows : (n + 1) * rows]
                    keep = first_frame + f + n < count[0]
                    out[f + n, :, lanes] = jnp.where(keep, value, 0.0).astype(BF16)


def shards(latents, counts, gain_first, bias_first, weight_first, gain_second, bias_second, weight_second):
    channels = gain_first.shape[0]
    frames, rows, flat = latents.shape[1:]
    pairs = flat // (2 * channels)
    blocks, bands = lax.axis_size("tm"), lax.axis_size("space")
    total_rows = bands * rows
    own = latents.reshape(frames, rows, flat)
    space = lax.axis_index("space")
    axes = ("tm", "space")

    def halo(sent, step, along):
        pairs_of = [
            (t * bands + s, (t + along) * bands + s + step)
            for t in range(blocks - along)
            for s in range(bands)
            if 0 <= s + step < bands
        ]
        return lax.ppermute(sent, axes, pairs_of)

    earlier = halo(own, 0, 1)
    if bands == 2:
        sent = lax.dynamic_slice_in_dim(own, (rows - 2) * (1 - space), 2, axis=1)
        swaps = [(t * 2 + s, t * 2 + 1 - s) for t in range(blocks) for s in range(2)]
        near = (lax.ppermute(sent, axes, swaps),) * 2
        swaps = [(t * 2 + s, t * 2 + 3 - s) for t in range(blocks - 1) for s in range(2)]
        far = (lax.ppermute(sent, axes, swaps),) * 2
        deep = rows + 1
    else:
        low, high = own[:, rows - 2 :], own[:, :2]
        near = (halo(low, 1, 0), halo(high, -1, 0))
        far = (halo(low, 1, 1), halo(high, -1, 1))
        deep = rows + 2

    dims = (frames, rows, pairs, channels, total_rows, deep)
    fill = deep * pairs
    tall = rows + 4
    stride = pairs + PAD
    vmem = pl.BlockSpec(memory_space=pltpu.VMEM)
    smem = pl.BlockSpec(memory_space=pltpu.SMEM)
    window = pltpu.VMEM((frames, tall, pairs, 7 * LANES), BF16)
    stage = pltpu.VMEM((frames, 3, (tall + 1) * stride, LANES), F32)
    first_weight = weight_first.reshape(3, 3, 3 * channels, channels)
    second_weight = weight_second.reshape(3, 3, 3 * channels, channels)
    flops = 2 * 9 * fill * 9 * channels * channels * 3
    params = pltpu.CompilerParams(vmem_limit_bytes=24 << 20)
    partial = pl.pallas_call(
        functools.partial(first_kernel, dims),
        out_shape=jax.ShapeDtypeStruct((2, frames * fill, channels), F32),
        in_specs=[smem] + [vmem] * 5,
        out_specs=vmem,
        scratch_shapes=[window, stage],
        compiler_params=params,
        cost_estimate=pl.CostEstimate(flops=flops, bytes_accessed=4 << 20, transcendentals=0),
        name="first_half",
    )(counts, own, *near, gain_first.reshape(1, channels), first_weight)
    out = pl.pallas_call(
        functools.partial(second_kernel, dims),
        out_shape=jax.ShapeDtypeStruct((frames, rows, flat), BF16),
        in_specs=[smem] + [vmem] * 11,
        out_specs=vmem,
        scratch_shapes=[
            window,
            stage,
            pltpu.VMEM((2, (frames + 2) * fill, channels), F32),
            pltpu.VMEM((frames + 2, rows + 2, pairs, 7 * LANES), BF16),
            pltpu.VMEM((frames + 2, 3, (deep + 1) * stride, LANES), F32),
            pltpu.VMEM((3, frames * rows * pairs, LANES), F32),
        ],
        compiler_params=params,
        cost_estimate=pl.CostEstimate(flops=2 * flops, bytes_accessed=6 << 20, transcendentals=0),
        name="second_half",
    )(
        counts, own, earlier, *far, partial,
        gain_first.reshape(1, channels), bias_first.reshape(1, channels), first_weight,
        gain_second.reshape(1, channels), bias_second.reshape(1, channels), second_weight,
    )
    return out.reshape(1, frames, rows, flat)


def solution(mesh):
    spread = P(("groups", "clip"), "tm", "space", None)
    return jax.shard_map(
        shards,
        mesh=mesh,
        in_specs=(spread, P(("groups", "clip")), P(), P(), P(), P(), P(), P()),
        out_specs=spread,
        check_vma=False,
    )
```

time: 46.8 us -> 23.6 us (0.50)
  the two profiles are of different devices: /device:TPU:16 before, /device:TPU:0 now
where the time goes in v1:
time: 23.6 us; the launch traced here: 23.4 us
  starting transfers between devices  9.94 us (42%)
  Pallas kernels  8.24 us (35%)
  local copies, waits for them, and re-layouts  4.42 us (19%)
  between operations  0.77 us (3%)
    pallas_call x1, Pallas kernels, shards(): pl.pallas_call(functools.partial(second_kernel, dims), out_shape=jax.Shap...  5.75 us
    ppermute x1, starting transfers between devices, halo(): return lax.ppermute(sent, axes, pairs_of)  3.48 us
    ppermute x1, starting transfers between devices, shards(): far = (lax.ppermute(sent, axes, swaps),) * 2  3.45 us
    unnamed x18, local copies, waits for them, and re-layouts  3.37 us
    ppermute x1, starting transfers between devices, shards(): near = (lax.ppermute(sent, axes, swaps),) * 2  3 us
    pallas_call x1, Pallas kernels, shards(): pl.pallas_call(functools.partial(first_kernel, dims), out_shape=jax.Shape...  2.49 us
    dynamic_slice x1, local copies, waits for them, and re-layouts, shards(): sent = lax.dynamic_slice_in_dim(own, (rows - 2) * (1 - space), 2, axis=1)  1.04 us
  transfers between devices with their start and end apart: 3, of which 0 were waited for; matrix products, arithmetic and copies ran while one was open for 0% of the time, Pallas kernels for 11%

profile of v1, /device:TPU:0, one launch (start us, length us, event | category | flops | bytes accessed | tf_op | source)
XLA Modules:
  0.0 23.4 jit_solution(13670978815082653489)
XLA Ops:
  0.0 0.0 copy-start.8
  0.0 1.0 %dynamic-slice_bitcast_fusion = bf16[4,2,6144]{2,1,0:T(2,128)(2,1)S(1)} fusion(bf16[1,4,4,6144]{3,2,1,0:T(4,128)(2,1)} %param.8, s32[]{:T(128)S(6)} %select_n.3), kind=kLoop, calls=%fused_computation | loop fusion | bytes 196612 | tf_op jit(solution)/shard_map/dynamic_slice | solution.py:198
  1.1 3.0 %collective-permute-start.2 = (bf16[4,2,6144]{2,1,0:T(2,128)(2,1)S(1)}, bf16[4,2,6144]{2,1,0:T(2,128)(2,1)S(1)}, u32[]{:S(2)}, u32[]{:S(2)}) collective-permute-start(bf16[4,2,6144]{2,1,0:T(2,128)(2,1)S(1)} %dynamic-slice_bitcast_fusion), channel_id=1, source_target_pairs={{0,2},{2,0},{4,6},{6,4},{8,10},{10,8},{12,14},{14,12},{1,3},{3,1},... | collective-permute-start | bytes 294920 | tf_op jit(solution)/shard_map/ppermute | solution.py:200
  4.1 3.5 %collective-permute-start = (bf16[4,4,6144]{2,1,0:T(4,128)(2,1)}, bf16[4,4,6144]{2,1,0:T(4,128)(2,1)S(1)}, u32[]{:S(2)}, u32[]{:S(2)}) collective-permute-start(bf16[4,4,6144]{2,1,0:T(4,128)(2,1)} %bitcast.10), channel_id=1, source_target_pairs={{0,4},{2,6},{4,8},{6,10},{8,12},{10,14},{1,5},{3,7},{5,9},{7,11},{... | collective-permute-start | bytes 589832 | tf_op jit(solution)/shard_map/ppermute | solution.py:194
  7.5 3.4 %collective-permute-start.1 = (bf16[4,2,6144]{2,1,0:T(2,128)(2,1)S(1)}, bf16[4,2,6144]{2,1,0:T(2,128)(2,1)S(1)}, u32[]{:S(2)}, u32[]{:S(2)}) collective-permute-start(bf16[4,2,6144]{2,1,0:T(2,128)(2,1)S(1)} %dynamic-slice_bitcast_fusion), channel_id=1, source_target_pairs={{0,6},{2,4},{4,10},{6,8},{8,14},{10,12},{1,7},{3,5},{5,11},{7,9},{... | collective-permute-start | bytes 294920 | tf_op jit(solution)/shard_map/ppermute | solution.py:202
  11.6 0.0 collective-permute-done.2.before.after
  11.7 0.0 copy-start
  11.7 0.9 %copy-done = bf16[1,4,4,6144]{3,2,1,0:T(4,128)(2,1)S(1)} copy-done((bf16[1,4,4,6144]{3,2,1,0:T(4,128)(2,1)S(1)}, bf16[1,4,4,6144]{3,2,1,0:T(4,128)(2,1)}, u32[]{:S(2)}) %copy-start) | copy-done | bytes 196632
  12.6 0.0 copy-start.1
  12.6 1.7 %copy-done.1 = bf16[3,3,3,192,192]{4,3,2,1,0:T(8,128)(2,1)S(1)} copy-done((bf16[3,3,3,192,192]{4,3,2,1,0:T(8,128)(2,1)S(1)}, bf16[3,3,3,192,192]{4,3,2,1,0:T(8,128)(2,1)}, u32[]{:S(2)}) %copy-start.1) | copy-done | bytes 1990680
  14.3 0.0 copy-start.4
  14.3 0.7 %copy-done.4 = f32[192]{0:T(256)S(1)} copy-done((f32[192]{0:T(256)S(1)}, f32[192]{0:T(256)}, u32[]{:S(2)}) %copy-start.4) | copy-done | bytes 792
  15.0 0.0 copy-start.2
  15.0 0.0 copy-start.7
  15.0 2.5 %first_half.1.partial = f32[2,320,192]{2,1,0:T(8,128)S(1)} custom-call(s32[1]{0:T(128)S(6)} %copy.9.count, bf16[4,4,6144]{2,1,0:T(4,128)(2,1)S(1)} %bitcast.11, bf16[4,2,6144]{2,1,0:T(2,128)(2,1)S(1)} %collective-permute-done.2.before.after, bf16[4,2,6144]{2,1,0:T(2,128)(2,1)S(1)} %collective-permute-done.2.before.after, f32[1,192]{1,0:T(1,128)S(1)} %bitcast.16, ...), custom_call_target="tpu_custom_call" | custom-call | flops 1433272320 | bytes 4194304 | tf_op jit(solution)/shard_map/first_half/pallas_call | solution.py:222
  17.5 0.0 collective-permute-done.1.before.after
  17.5 0.0 collective-permute-done.earlier
  17.6 0.0 copy-done.8
  17.6 0.0 copy-done.2
  17.6 0.0 copy-done.3
  17.6 0.0 copy-done.5
  17.6 0.0 copy-done.6
  17.6 0.0 copy-done.7
  17.6 5.8 %second_half.1 = bf16[4,4,6144]{2,1,0:T(4,128)(2,1)} custom-call(s32[1]{0:T(128)S(6)} %copy.9.count, bf16[4,4,6144]{2,1,0:T(4,128)(2,1)S(1)} %bitcast.12, bf16[4,4,6144]{2,1,0:T(4,128)(2,1)S(1)} %collective-permute-done.earlier, bf16[4,2,6144]{2,1,0:T(2,128)(2,1)S(1)} %collective-permute-done.1.before.after, ...), custom_call_target="tpu_custom_call" | custom-call | flops 2866544640 | bytes 6291456 | tf_op jit(solution)/shard_map/second_half/pallas_call | solution.py:232
  (3 shorter events, 0.0 us)
Async XLA Ops:
  0.0 17.6 %copy-start.8 = (f32[192]{0:T(256)S(1)}, f32[192]{0:T(256)}, u32[]{:S(2)}) copy-start(f32[192]{0:T(256)} %param.14) | copy-start | bytes 2308
  1.1 10.6 %collective-permute-start.2 = (bf16[4,2,6144]{2,1,0:T(2,128)(2,1)S(1)}, bf16[4,2,6144]{2,1,0:T(2,128)(2,1)S(1)}, u32[]{:S(2)}, u32[]{:S(2)}) collective-permute-start(bf16[4,2,6144]{2,1,0:T(2,128)(2,1)S(1)} %dynamic-slice_bitcast_fusion), channel_id=1, source_target_pairs={{0,2},{2,0},{4,6},{6,4},{8,10},{10,8},{12,14},{14,12},{1,3},{3,1},... | collective-permute-start | bytes 294920 | tf_op jit(solution)/shard_map/ppermute | solution.py:200
  4.1 13.5 %collective-permute-start = (bf16[4,4,6144]{2,1,0:T(4,128)(2,1)}, bf16[4,4,6144]{2,1,0:T(4,128)(2,1)S(1)}, u32[]{:S(2)}, u32[]{:S(2)}) collective-permute-start(bf16[4,4,6144]{2,1,0:T(4,128)(2,1)} %bitcast.10), channel_id=1, source_target_pairs={{0,4},{2,6},{4,8},{6,10},{8,12},{10,14},{1,5},{3,7},{5,9},{7,11},{... | collective-permute-start | bytes 589832 | tf_op jit(solution)/shard_map/ppermute | solution.py:194
  7.5 10.0 %collective-permute-start.1 = (bf16[4,2,6144]{2,1,0:T(2,128)(2,1)S(1)}, bf16[4,2,6144]{2,1,0:T(2,128)(2,1)S(1)}, u32[]{:S(2)}, u32[]{:S(2)}) collective-permute-start(bf16[4,2,6144]{2,1,0:T(2,128)(2,1)S(1)} %dynamic-slice_bitcast_fusion), channel_id=1, source_target_pairs={{0,6},{2,4},{4,10},{6,8},{8,14},{10,12},{1,7},{3,5},{5,11},{7,9},{... | collective-permute-start | bytes 294920 | tf_op jit(solution)/shard_map/ppermute | solution.py:202
  11.7 0.9 %copy-start = (bf16[1,4,4,6144]{3,2,1,0:T(4,128)(2,1)S(1)}, bf16[1,4,4,6144]{3,2,1,0:T(4,128)(2,1)}, u32[]{:S(2)}) copy-start(bf16[1,4,4,6144]{3,2,1,0:T(4,128)(2,1)} %param.8) | copy-start | bytes 589828
  12.6 1.7 %copy-start.1 = (bf16[3,3,3,192,192]{4,3,2,1,0:T(8,128)(2,1)S(1)}, bf16[3,3,3,192,192]{4,3,2,1,0:T(8,128)(2,1)}, u32[]{:S(2)}) copy-start(bf16[3,3,3,192,192]{4,3,2,1,0:T(8,128)(2,1)} %param.12) | copy-start | bytes 5971972
  14.3 0.7 %copy-start.4 = (f32[192]{0:T(256)S(1)}, f32[192]{0:T(256)}, u32[]{:S(2)}) copy-start(f32[192]{0:T(256)} %param.10) | copy-start | bytes 2308
  15.0 2.6 %copy-start.2 = (bf16[3,3,3,192,192]{4,3,2,1,0:T(8,128)(2,1)S(1)}, bf16[3,3,3,192,192]{4,3,2,1,0:T(8,128)(2,1)}, u32[]{:S(2)}) copy-start(bf16[3,3,3,192,192]{4,3,2,1,0:T(8,128)(2,1)} %param.12) | copy-start | bytes 5971972
  15.0 2.6 %copy-start.3 = (bf16[3,3,3,192,192]{4,3,2,1,0:T(8,128)(2,1)S(1)}, bf16[3,3,3,192,192]{4,3,2,1,0:T(8,128)(2,1)}, u32[]{:S(2)}) copy-start(bf16[3,3,3,192,192]{4,3,2,1,0:T(8,128)(2,1)} %param.15) | copy-start | bytes 5971972
  15.0 2.6 %copy-start.5 = (f32[192]{0:T(256)S(1)}, f32[192]{0:T(256)}, u32[]{:S(2)}) copy-start(f32[192]{0:T(256)} %param.10) | copy-start | bytes 2308
  15.0 2.6 %copy-start.6 = (f32[192]{0:T(256)S(1)}, f32[192]{0:T(256)}, u32[]{:S(2)}) copy-start(f32[192]{0:T(256)} %param.11) | copy-start | bytes 2308
  15.0 2.6 %copy-start.7 = (f32[192]{0:T(256)S(1)}, f32[192]{0:T(256)}, u32[]{:S(2)}) copy-start(f32[192]{0:T(256)} %param.13) | copy-start | bytes 2308

commit v2 on v1

--- a/solution.py
+++ b/solution.py
@@ -93,14 +93,25 @@
     return (row >= 0) & (row < total_rows)
 
 
+def cut_kernel(swap, own, *sent):
+    frames, rows = own.shape[0], own.shape[1]
+    for f in range(frames):
+        if swap:
+            below = lax.axis_index("space") == 0
+            sent[0][f] = jnp.where(below, own[f, rows - 2 :, :], own[f, :2, :])
+        else:
+            sent[0][f] = own[f, rows - 2 :, :]
+            sent[1][f] = own[f, :2, :]
+
+
 def first_kernel(dims, count, own, before, after, gain, weight, partial, window, stage):
     frames, rows, pairs, channels, total_rows, deep = dims
     tm, space = place()
     start = (1 - space) if deep == rows + 1 else 0
     clear_pads(stage, rows + 4, pairs)
     fill_window(
-        window, stage, own, before, after, twice(gain),
-        lambda f: tm * frames + f < count[0], row_mask(2, rows, total_rows), pairs, channels,
+        window, stage, own, before, after, twice(gain), lambda f: tm * frames + f < count[...],
+        row_mask(2, rows, total_rows), pairs, channels,
     )
     for parity in range(2):
         for a in (2, 1, 0):
@@ -119,17 +130,19 @@
 ):
     frames, rows, pairs, channels, total_rows, deep = dims
     tm, space = place()
-    first_frame = tm * frames
     start = (1 - space) if deep == rows + 1 else 0
     fill = deep * pairs
+
+    def valid(f):
+        at = (tm - 1) * frames + f
+        return (at >= 0) & (at < count[...])
+
     clear_pads(stage, rows + 4, pairs)
     clear_pads(hidden_stage, deep, pairs)
     fill_window(
-        window, stage, earlier, before, after, twice(gain),
-        lambda f: (tm > 0) & (first_frame - frames + f < count[0]),
+        window, stage, earlier, before, after, twice(gain), valid,
         row_mask(2, rows, total_rows), pairs, channels,
     )
-    late = (frames - 2) * fill
     for parity in range(2):
         total[parity, 0 : 2 * fill] = jnp.zeros((2 * fill, channels), F32)
         total[parity, 2 * fill :] = partial[parity]
@@ -137,14 +150,13 @@
             part = taps(window, weight, parity, a, frames - a, start, deep, a, channels)
             total[parity, 0 : (frames - a) * fill] += part
 
-    bias_wide, gain_wide = twice(bias), twice(gain_two)
     row = lax.broadcasted_iota(jnp.int32, (fill, 1), 0) // pairs + (space * rows - 1 + start)
     row_ok = (row >= 0) & (row < total_rows)
+    bias_wide, gain_wide = twice(bias), twice(gain_two)
     for h in range(frames + 2):
-        at = first_frame + h - 2
-        keep = row_ok & (at >= 0) & (at < count[0])
+        good = row_ok & valid(frames + h - 2)
         t = jnp.concatenate([total[q, h * fill : (h + 1) * fill, :] for q in range(2)], axis=1)
-        t = jnp.where(keep, t + bias_wide, 0.0).astype(BF16).astype(F32)
+        t = jnp.where(good, t + bias_wide, 0.0).astype(BF16).astype(F32)
         y = norm_silu_pair(t, gain_wide, channels)
         hidden[h, 0] = jnp.zeros(hidden.shape[2:], BF16)
         hidden[h, rows + 1] = jnp.zeros(hidden.shape[2:], BF16)
@@ -164,14 +176,14 @@
     for k in range(3):
         final[k] = both[:, k * LANES : (k + 1) * LANES]
     for f in range(0, frames, 2):
+        good = [valid(frames + f + n) for n in range(2)]
         for p in range(pairs):
             for k in range(3):
                 block = final[k, pl.ds(f * rows * pairs + p, 2 * rows, stride=pairs), :]
                 lanes = pl.ds(p * 2 * channels + k * LANES, LANES)
                 for n in range(2):
                     value = own[f + n, :, lanes].astype(F32) + block[n * rows : (n + 1) * rows]
-                    keep = first_frame + f + n < count[0]
-                    out[f + n, :, lanes] = jnp.where(keep, value, 0.0).astype(BF16)
+                    out[f + n, :, lanes] = jnp.where(good[n], value, 0.0).astype(BF16)
 
 
 def shards(latents, counts, gain_first, bias_first, weight_first, gain_second, bias_second, weight_second):
@@ -180,39 +192,42 @@
     pairs = flat // (2 * channels)
     blocks, bands = lax.axis_size("tm"), lax.axis_size("space")
     total_rows = bands * rows
-    own = latents.reshape(frames, rows, flat)
-    space = lax.axis_index("space")
-    axes = ("tm", "space")
-
-    def halo(sent, step, along):
+    block = latents.reshape(frames, rows, flat)
+    count = counts.reshape(1, 1)
+
+    def shift(sent, step, along):
         pairs_of = [
-            (t * bands + s, (t + along) * bands + s + step)
-            for t in range(blocks - along)
+            (t * bands + s, (t + along) % blocks * bands + (s + step) % bands)
+            for t in range(blocks)
             for s in range(bands)
-            if 0 <= s + step < bands
         ]
-        return lax.ppermute(sent, axes, pairs_of)
-
-    earlier = halo(own, 0, 1)
-    if bands == 2:
-        sent = lax.dynamic_slice_in_dim(own, (rows - 2) * (1 - space), 2, axis=1)
-        swaps = [(t * 2 + s, t * 2 + 1 - s) for t in range(blocks) for s in range(2)]
-        near = (lax.ppermute(sent, axes, swaps),) * 2
-        swaps = [(t * 2 + s, t * 2 + 3 - s) for t in range(blocks - 1) for s in range(2)]
-        far = (lax.ppermute(sent, axes, swaps),) * 2
+        return lax.ppermute(sent, ("tm", "space"), pairs_of)
+
+    earlier = shift(block, 0, 1)
+    vmem = pl.BlockSpec(memory_space=pltpu.VMEM)
+    swap = bands == 2
+    rim = jax.ShapeDtypeStruct((frames, 2, flat), BF16)
+    sent = pl.pallas_call(
+        functools.partial(cut_kernel, swap),
+        out_shape=[rim] * (1 if swap else 2),
+        in_specs=[vmem],
+        out_specs=[vmem] * (1 if swap else 2),
+        cost_estimate=pl.CostEstimate(flops=4 << 30, bytes_accessed=1 << 20, transcendentals=0),
+        name="cut_rows",
+    )(block)
+    if swap:
+        near = (shift(sent[0], 1, 0),) * 2
+        far = (shift(sent[0], 1, 1),) * 2
         deep = rows + 1
     else:
-        low, high = own[:, rows - 2 :], own[:, :2]
-        near = (halo(low, 1, 0), halo(high, -1, 0))
-        far = (halo(low, 1, 1), halo(high, -1, 1))
+        near = (shift(sent[0], 1, 0), shift(sent[1], -1, 0))
+        far = (shift(sent[0], 1, 1), shift(sent[1], -1, 1))
         deep = rows + 2
 
     dims = (frames, rows, pairs, channels, total_rows, deep)
     fill = deep * pairs
     tall = rows + 4
     stride = pairs + PAD
-    vmem = pl.BlockSpec(memory_space=pltpu.VMEM)
-    smem = pl.BlockSpec(memory_space=pltpu.SMEM)
     window = pltpu.VMEM((frames, tall, pairs, 7 * LANES), BF16)
     stage = pltpu.VMEM((frames, 3, (tall + 1) * stride, LANES), F32)
     first_weight = weight_first.reshape(3, 3, 3 * channels, channels)
@@ -222,17 +237,17 @@
     partial = pl.pallas_call(
         functools.partial(first_kernel, dims),
         out_shape=jax.ShapeDtypeStruct((2, frames * fill, channels), F32),
-        in_specs=[smem] + [vmem] * 5,
+        in_specs=[vmem] * 6,
         out_specs=vmem,
         scratch_shapes=[window, stage],
         compiler_params=params,
         cost_estimate=pl.CostEstimate(flops=flops, bytes_accessed=4 << 20, transcendentals=0),
         name="first_half",
-    )(counts, own, *near, gain_first.reshape(1, channels), first_weight)
+    )(count, block, *near, gain_first.reshape(1, channels), first_weight)
     out = pl.pallas_call(
         functools.partial(second_kernel, dims),
         out_shape=jax.ShapeDtypeStruct((frames, rows, flat), BF16),
-        in_specs=[smem] + [vmem] * 11,
+        in_specs=[vmem] * 12,
         out_specs=vmem,
         scratch_shapes=[
             window,
@@ -246,7 +261,7 @@
         cost_estimate=pl.CostEstimate(flops=2 * flops, bytes_accessed=6 << 20, transcendentals=0),
         name="second_half",
     )(
-        counts, own, earlier, *far, partial,
+        count, block, earlier, *far, partial,
         gain_first.reshape(1, channels), bias_first.reshape(1, channels), first_weight,
         gain_second.reshape(1, channels), bias_second.reshape(1, channels), second_weight,
     )

time: 23.6 us -> 21 us (0.89)
  local copies, waits for them, and re-layouts: 4.42 us -> 0.04 us
  waiting for transfers between devices: 0.01 us -> 3.91 us
  starting transfers between devices: 9.94 us -> 6.07 us
  Pallas kernels: 8.24 us -> 10.1 us
    ppermute x3, waiting for transfers between devices: 0.01 us -> 3.91 us  [shift(): return lax.ppermute(sent, ('tm', 'space'), pairs_of)]
    ppermute x3, starting transfers between devices: 9.94 us -> 6.07 us  [shift(): return lax.ppermute(sent, ('tm', 'space'), pairs_of)]
    unnamed x18 -> x14, local copies, waits for them, and re-layouts: 3.37 us -> 0.04 us
    pallas_call x0 -> x1, Pallas kernels: none -> 1.75 us  [shards(): pl.pallas_call(functools.partial(cut_kernel, swap), out_shape=[rim] * (1...]
    dynamic_slice x1 -> x0, local copies, waits for them, and re-layouts: 1.04 us -> none  [shards(): sent = lax.dynamic_slice_in_dim(own, (rows - 2) * (1 - space), 2, axis=1)]
  transfers between devices with their start and end apart: 3 -> 3, of which waited for: 0 -> 1; matrix products, arithmetic and copies ran while one was open for 0% -> 0% of each run, Pallas kernels for 11% -> 12%
where the time goes in v2:
time: 21 us; the launch traced here: 20.9 us
  Pallas kernels  10.1 us (48%)
  starting transfers between devices  6.07 us (29%)
  waiting for transfers between devices  3.91 us (19%)
  between operations  0.74 us (4%)
    ppermute x3, starting transfers between devices, shift(): return lax.ppermute(sent, ('tm', 'space'), pairs_of)  6.07 us
    pallas_call x1, Pallas kernels, shards(): pl.pallas_call(functools.partial(second_kernel, dims), out_shape=jax.Shap...  5.83 us
    ppermute x3, waiting for transfers between devices, shift(): return lax.ppermute(sent, ('tm', 'space'), pairs_of)  3.91 us
    pallas_call x1, Pallas kernels, shards(): pl.pallas_call(functools.partial(first_kernel, dims), out_shape=jax.Shape...  2.54 us
    pallas_call x1, Pallas kernels, shards(): pl.pallas_call(functools.partial(cut_kernel, swap), out_shape=[rim] * (1...  1.75 us
  transfers between devices with their start and end apart: 3, of which 1 were waited for; matrix products, arithmetic and copies ran while one was open for 0% of the time, Pallas kernels for 12%

profile of v2, /device:TPU:0, one launch (start us, length us, event | category | flops | bytes accessed | tf_op | source)
XLA Modules:
  0.0 20.9 jit_solution(7731720616831686272)
XLA Ops:
  0.0 0.0 copy-start.2
  0.0 0.0 copy-start
  0.0 0.0 copy-start.3
  0.0 1.8 %cut_rows.1 = bf16[4,2,6144]{2,1,0:T(2,128)(2,1)} custom-call(bf16[4,4,6144]{2,1,0:T(4,128)(2,1)} %bitcast.14), custom_call_target="tpu_custom_call" | custom-call | flops 4294967296 | bytes 1048576 | tf_op jit(solution)/shard_map/cut_rows/pallas_call | solution.py:210
  1.8 2.9 %collective-permute-start.2 = (bf16[4,2,6144]{2,1,0:T(2,128)(2,1)}, bf16[4,2,6144]{2,1,0:T(2,128)(2,1)S(1)}, u32[]{:S(2)}, u32[]{:S(2)}) collective-permute-start(bf16[4,2,6144]{2,1,0:T(2,128)(2,1)} %cut_rows.1), channel_id=1, source_target_pairs={{0,2},{2,0},{4,6},{6,4},{8,10},{10,8},{12,14},{14,12},{1,3},{3,1},... | collective-permute-start | bytes 294920 | tf_op jit(solution)/shard_map/ppermute | solution.py:204
  4.7 0.0 copy-done.2
  4.7 1.6 %collective-permute-start = (bf16[4,4,6144]{2,1,0:T(4,128)(2,1)S(1)}, bf16[4,4,6144]{2,1,0:T(4,128)(2,1)S(1)}, u32[]{:S(2)}, u32[]{:S(2)}) collective-permute-start(bf16[4,4,6144]{2,1,0:T(4,128)(2,1)S(1)} %bitcast.15), channel_id=1, source_target_pairs={{0,4},{2,6},{4,8},{6,10},{8,12},{10,14},{12,0},{14,2},{1,5},{3,7},... | collective-permute-start | bytes 589832 | tf_op jit(solution)/shard_map/ppermute | solution.py:204
  6.3 1.5 %collective-permute-start.1 = (bf16[4,2,6144]{2,1,0:T(2,128)(2,1)}, bf16[4,2,6144]{2,1,0:T(2,128)(2,1)S(1)}, u32[]{:S(2)}, u32[]{:S(2)}) collective-permute-start(bf16[4,2,6144]{2,1,0:T(2,128)(2,1)} %cut_rows.1), channel_id=1, source_target_pairs={{0,6},{2,4},{4,10},{6,8},{8,14},{10,12},{12,2},{14,0},{1,7},{3,5},... | collective-permute-start | bytes 294920 | tf_op jit(solution)/shard_map/ppermute | solution.py:204
  8.5 0.0 collective-permute-done.2.before.after
  8.5 0.0 copy-done
  8.5 0.0 copy-done.3
  8.5 0.0 copy-start.1
  8.5 0.0 copy-start.4
  8.5 0.0 copy-start.5
  8.5 0.0 copy-start.6
  8.6 2.5 %first_half.1.partial = f32[2,320,192]{2,1,0:T(8,128)S(1)} custom-call(s32[1,1]{1,0:T(1,128)} %bitcast.9.count, bf16[4,4,6144]{2,1,0:T(4,128)(2,1)S(1)} %bitcast.16, bf16[4,2,6144]{2,1,0:T(2,128)(2,1)S(1)} %collective-permute-done.2.before.after, bf16[4,2,6144]{2,1,0:T(2,128)(2,1)S(1)} %collective-permute-done.2.before.after, f32[1,192]{1,0:T(1,128)S(1)} %bitcast.18, ...), custom_call_target="tpu_custom_call" | custom-call | flops 1433272320 | bytes 4194304 | tf_op jit(solution)/shard_map/first_half/pallas_call | solution.py:237
  11.1 3.9 %collective-permute-done.1.before.after = bf16[4,2,6144]{2,1,0:T(2,128)(2,1)S(1)} collective-permute-done((bf16[4,2,6144]{2,1,0:T(2,128)(2,1)}, bf16[4,2,6144]{2,1,0:T(2,128)(2,1)S(1)}, u32[]{:S(2)}, u32[]{:S(2)}) %collective-permute-start.1) | collective-permute-done | bytes 98336 | tf_op jit(solution)/shard_map/ppermute | solution.py:204
  15.0 0.0 collective-permute-done.earlier
  15.0 0.0 copy-done.1
  15.0 0.0 copy-done.4
  15.0 0.0 copy-done.5
  15.0 0.0 copy-done.6
  15.0 5.8 %second_half.1 = bf16[4,4,6144]{2,1,0:T(4,128)(2,1)} custom-call(s32[1,1]{1,0:T(1,128)} %bitcast.10.count, bf16[4,4,6144]{2,1,0:T(4,128)(2,1)S(1)} %bitcast.17, bf16[4,4,6144]{2,1,0:T(4,128)(2,1)S(1)} %collective-permute-done.earlier, bf16[4,2,6144]{2,1,0:T(2,128)(2,1)S(1)} %collective-permute-done.1.before.after, ...), custom_call_target="tpu_custom_call" | custom-call | flops 2866544640 | bytes 6291456 | tf_op jit(solution)/shard_map/second_half/pallas_call | solution.py:247
Async XLA Ops:
  0.0 4.7 %copy-start.2 = (bf16[1,4,4,6144]{3,2,1,0:T(4,128)(2,1)S(1)}, bf16[1,4,4,6144]{3,2,1,0:T(4,128)(2,1)}, u32[]{:S(2)}) copy-start(bf16[1,4,4,6144]{3,2,1,0:T(4,128)(2,1)} %param.8) | copy-start | bytes 589828
  0.0 8.5 %copy-start = (bf16[3,3,3,192,192]{4,3,2,1,0:T(8,128)(2,1)S(1)}, bf16[3,3,3,192,192]{4,3,2,1,0:T(8,128)(2,1)}, u32[]{:S(2)}) copy-start(bf16[3,3,3,192,192]{4,3,2,1,0:T(8,128)(2,1)} %param.12) | copy-start | bytes 5971972
  0.0 8.5 %copy-start.3 = (f32[192]{0:T(256)S(1)}, f32[192]{0:T(256)}, u32[]{:S(2)}) copy-start(f32[192]{0:T(256)} %param.10) | copy-start | bytes 2308
  1.8 6.7 %collective-permute-start.2 = (bf16[4,2,6144]{2,1,0:T(2,128)(2,1)}, bf16[4,2,6144]{2,1,0:T(2,128)(2,1)S(1)}, u32[]{:S(2)}, u32[]{:S(2)}) collective-permute-start(bf16[4,2,6144]{2,1,0:T(2,128)(2,1)} %cut_rows.1), channel_id=1, source_target_pairs={{0,2},{2,0},{4,6},{6,4},{8,10},{10,8},{12,14},{14,12},{1,3},{3,1},... | collective-permute-start | bytes 294920 | tf_op jit(solution)/shard_map/ppermute | solution.py:204
  4.7 10.3 %collective-permute-start = (bf16[4,4,6144]{2,1,0:T(4,128)(2,1)S(1)}, bf16[4,4,6144]{2,1,0:T(4,128)(2,1)S(1)}, u32[]{:S(2)}, u32[]{:S(2)}) collective-permute-start(bf16[4,4,6144]{2,1,0:T(4,128)(2,1)S(1)} %bitcast.15), channel_id=1, source_target_pairs={{0,4},{2,6},{4,8},{6,10},{8,12},{10,14},{12,0},{14,2},{1,5},{3,7},... | collective-permute-start | bytes 589832 | tf_op jit(solution)/shard_map/ppermute | solution.py:204
  6.3 8.7 %collective-permute-start.1 = (bf16[4,2,6144]{2,1,0:T(2,128)(2,1)}, bf16[4,2,6144]{2,1,0:T(2,128)(2,1)S(1)}, u32[]{:S(2)}, u32[]{:S(2)}) collective-permute-start(bf16[4,2,6144]{2,1,0:T(2,128)(2,1)} %cut_rows.1), channel_id=1, source_target_pairs={{0,6},{2,4},{4,10},{6,8},{8,14},{10,12},{12,2},{14,0},{1,7},{3,5},... | collective-permute-start | bytes 294920 | tf_op jit(solution)/shard_map/ppermute | solution.py:204
  8.5 6.5 %copy-start.1 = (bf16[3,3,3,192,192]{4,3,2,1,0:T(8,128)(2,1)S(1)}, bf16[3,3,3,192,192]{4,3,2,1,0:T(8,128)(2,1)}, u32[]{:S(2)}) copy-start(bf16[3,3,3,192,192]{4,3,2,1,0:T(8,128)(2,1)} %param.15) | copy-start | bytes 5971972
  8.5 6.5 %copy-start.4 = (f32[192]{0:T(256)S(1)}, f32[192]{0:T(256)}, u32[]{:S(2)}) copy-start(f32[192]{0:T(256)} %param.11) | copy-start | bytes 2308
  8.5 6.5 %copy-start.5 = (f32[192]{0:T(256)S(1)}, f32[192]{0:T(256)}, u32[]{:S(2)}) copy-start(f32[192]{0:T(256)} %param.13) | copy-start | bytes 2308
  8.5 6.5 %copy-start.6 = (f32[192]{0:T(256)S(1)}, f32[192]{0:T(256)}, u32[]{:S(2)}) copy-start(f32[192]{0:T(256)} %param.14) | copy-start | bytes 2308

commit v3 on v2

--- a/solution.py
+++ b/solution.py
@@ -110,7 +110,7 @@
     start = (1 - space) if deep == rows + 1 else 0
     clear_pads(stage, rows + 4, pairs)
     fill_window(
-        window, stage, own, before, after, twice(gain), lambda f: tm * frames + f < count[...],
+        window, stage, own, before, after, twice(gain), lambda f: tm * frames + f < count[0],
         row_mask(2, rows, total_rows), pairs, channels,
     )
     for parity in range(2):
@@ -135,7 +135,7 @@
 
     def valid(f):
         at = (tm - 1) * frames + f
-        return (at >= 0) & (at < count[...])
+        return (at >= 0) & (at < count[0])
 
     clear_pads(stage, rows + 4, pairs)
     clear_pads(hidden_stage, deep, pairs)
@@ -193,7 +193,6 @@
     blocks, bands = lax.axis_size("tm"), lax.axis_size("space")
     total_rows = bands * rows
     block = latents.reshape(frames, rows, flat)
-    count = counts.reshape(1, 1)
 
     def shift(sent, step, along):
         pairs_of = [
@@ -205,6 +204,7 @@
 
     earlier = shift(block, 0, 1)
     vmem = pl.BlockSpec(memory_space=pltpu.VMEM)
+    smem = pl.BlockSpec(memory_space=pltpu.SMEM)
     swap = bands == 2
     rim = jax.ShapeDtypeStruct((frames, 2, flat), BF16)
     sent = pl.pallas_call(
@@ -237,17 +237,17 @@
     partial = pl.pallas_call(
         functools.partial(first_kernel, dims),
         out_shape=jax.ShapeDtypeStruct((2, frames * fill, channels), F32),
-        in_specs=[vmem] * 6,
+        in_specs=[smem] + [vmem] * 5,
         out_specs=vmem,
         scratch_shapes=[window, stage],
         compiler_params=params,
-        cost_estimate=pl.CostEstimate(flops=flops, bytes_accessed=4 << 20, transcendentals=0),
+        cost_estimate=pl.CostEstimate(flops=1 << 20, bytes_accessed=1 << 16, transcendentals=0),
         name="first_half",
-    )(count, block, *near, gain_first.reshape(1, channels), first_weight)
+    )(counts, block, *near, gain_first.reshape(1, channels), first_weight)
     out = pl.pallas_call(
         functools.partial(second_kernel, dims),
         out_shape=jax.ShapeDtypeStruct((frames, rows, flat), BF16),
-        in_specs=[vmem] * 12,
+        in_specs=[smem] + [vmem] * 11,
         out_specs=vmem,
         scratch_shapes=[
             window,
@@ -261,7 +261,7 @@
         cost_estimate=pl.CostEstimate(flops=2 * flops, bytes_accessed=6 << 20, transcendentals=0),
         name="second_half",
     )(
-        count, block, earlier, *far, partial,
+        counts, block, earlier, *far, partial,
         gain_first.reshape(1, channels), bias_first.reshape(1, channels), first_weight,
         gain_second.reshape(1, channels), bias_second.reshape(1, channels), second_weight,
     )

time: 21 us -> 19.7 us (0.938)
  waiting for transfers between devices: 3.91 us -> 2.8 us
    ppermute x3, waiting for transfers between devices: 3.91 us -> 2.8 us  [shift(): return lax.ppermute(sent, ('tm', 'space'), pairs_of)]
  transfers between devices with their start and end apart: 3 -> 3, of which waited for: 1 -> 2; matrix products, arithmetic and copies ran while one was open for 0% -> 0% of each run, Pallas kernels for 12% -> 21%
where the time goes in v3:
time: 19.7 us; the launch traced here: 19.6 us
  Pallas kernels  9.9 us (50%)
  starting transfers between devices  6.18 us (31%)
  waiting for transfers between devices  2.8 us (14%)
  between operations  0.69 us (4%)
    ppermute x3, starting transfers between devices, shift(): return lax.ppermute(sent, ('tm', 'space'), pairs_of)  6.18 us
    pallas_call x1, Pallas kernels, shards(): pl.pallas_call(functools.partial(second_kernel, dims), out_shape=jax.Shap...  5.75 us
    ppermute x3, waiting for transfers between devices, shift(): return lax.ppermute(sent, ('tm', 'space'), pairs_of)  2.8 us
    pallas_call x1, Pallas kernels, shards(): pl.pallas_call(functools.partial(first_kernel, dims), out_shape=jax.Shape...  2.51 us
    pallas_call x1, Pallas kernels, shards(): pl.pallas_call(functools.partial(cut_kernel, swap), out_shape=[rim] * (1...  1.63 us
  transfers between devices with their start and end apart: 3, of which 2 were waited for; matrix products, arithmetic and copies ran while one was open for 0% of the time, Pallas kernels for 21%

profile of v3, /device:TPU:0, one launch (start us, length us, event | category | flops | bytes accessed | tf_op | source)
XLA Modules:
  0.0 19.6 jit_solution(2731570164357839887)
XLA Ops:
  0.0 0.0 copy-start
  0.0 0.0 copy-start.1
  0.0 0.0 copy-start.2
  0.0 3.1 %collective-permute-start = (bf16[4,4,6144]{2,1,0:T(4,128)(2,1)}, bf16[4,4,6144]{2,1,0:T(4,128)(2,1)S(1)}, u32[]{:S(2)}, u32[]{:S(2)}) collective-permute-start(bf16[4,4,6144]{2,1,0:T(4,128)(2,1)} %bitcast.10), channel_id=1, source_target_pairs={{0,4},{2,6},{4,8},{6,10},{8,12},{10,14},{12,0},{14,2},{1,5},{3,7},... | collective-permute-start | bytes 589832 | tf_op jit(solution)/shard_map/ppermute | solution.py:203
  3.1 1.6 %cut_rows.1 = bf16[4,2,6144]{2,1,0:T(2,128)(2,1)} custom-call(bf16[4,4,6144]{2,1,0:T(4,128)(2,1)} %bitcast.11), custom_call_target="tpu_custom_call" | custom-call | flops 4294967296 | bytes 1048576 | tf_op jit(solution)/shard_map/cut_rows/pallas_call | solution.py:210
  4.7 0.0 copy-start.3
  4.7 0.0 copy-start.4
  4.7 0.0 copy-start.5
  4.7 0.0 copy-start.6
  4.7 1.6 %collective-permute-start.2 = (bf16[4,2,6144]{2,1,0:T(2,128)(2,1)}, bf16[4,2,6144]{2,1,0:T(2,128)(2,1)S(1)}, u32[]{:S(2)}, u32[]{:S(2)}) collective-permute-start(bf16[4,2,6144]{2,1,0:T(2,128)(2,1)} %cut_rows.1), channel_id=1, source_target_pairs={{0,2},{2,0},{4,6},{6,4},{8,10},{10,8},{12,14},{14,12},{1,3},{3,1},... | collective-permute-start | bytes 294920 | tf_op jit(solution)/shard_map/ppermute | solution.py:203
  6.3 1.5 %collective-permute-start.1 = (bf16[4,2,6144]{2,1,0:T(2,128)(2,1)}, bf16[4,2,6144]{2,1,0:T(2,128)(2,1)S(1)}, u32[]{:S(2)}, u32[]{:S(2)}) collective-permute-start(bf16[4,2,6144]{2,1,0:T(2,128)(2,1)} %cut_rows.1), channel_id=1, source_target_pairs={{0,6},{2,4},{4,10},{6,8},{8,14},{10,12},{12,2},{14,0},{1,7},{3,5},... | collective-permute-start | bytes 294920 | tf_op jit(solution)/shard_map/ppermute | solution.py:203
  8.5 1.1 %collective-permute-done.2.before.after = bf16[4,2,6144]{2,1,0:T(2,128)(2,1)S(1)} collective-permute-done((bf16[4,2,6144]{2,1,0:T(2,128)(2,1)}, bf16[4,2,6144]{2,1,0:T(2,128)(2,1)S(1)}, u32[]{:S(2)}, u32[]{:S(2)}) %collective-permute-start.2) | collective-permute-done | bytes 98336 | tf_op jit(solution)/shard_map/ppermute | solution.py:203
  9.6 0.0 copy-done
  9.6 0.0 copy-done.1
  9.6 0.0 copy-done.2
  9.6 2.5 %first_half.1.partial = f32[2,320,192]{2,1,0:T(8,128)S(1)} custom-call(s32[1]{0:T(128)S(6)} %copy.9.count, bf16[4,4,6144]{2,1,0:T(4,128)(2,1)S(1)} %bitcast.12, bf16[4,2,6144]{2,1,0:T(2,128)(2,1)S(1)} %collective-permute-done.2.before.after, bf16[4,2,6144]{2,1,0:T(2,128)(2,1)S(1)} %collective-permute-done.2.before.after, f32[1,192]{1,0:T(1,128)S(1)} %bitcast.14, ...), custom_call_target="tpu_custom_call" | custom-call | flops 1048576 | bytes 65536 | tf_op jit(solution)/shard_map/first_half/pallas_call | solution.py:237
  12.1 1.7 %collective-permute-done.1.before.after = bf16[4,2,6144]{2,1,0:T(2,128)(2,1)S(1)} collective-permute-done((bf16[4,2,6144]{2,1,0:T(2,128)(2,1)}, bf16[4,2,6144]{2,1,0:T(2,128)(2,1)S(1)}, u32[]{:S(2)}, u32[]{:S(2)}) %collective-permute-start.1) | collective-permute-done | bytes 98336 | tf_op jit(solution)/shard_map/ppermute | solution.py:203
  13.8 0.0 collective-permute-done.earlier
  13.8 0.0 copy-done.3
  13.8 0.0 copy-done.4
  13.8 0.0 copy-done.5
  13.8 0.0 copy-done.6
  13.8 5.8 %second_half.1 = bf16[4,4,6144]{2,1,0:T(4,128)(2,1)} custom-call(s32[1]{0:T(128)S(6)} %copy.9.count, bf16[4,4,6144]{2,1,0:T(4,128)(2,1)S(1)} %bitcast.13, bf16[4,4,6144]{2,1,0:T(4,128)(2,1)S(1)} %collective-permute-done.earlier, bf16[4,2,6144]{2,1,0:T(2,128)(2,1)S(1)} %collective-permute-done.1.before.after, ...), custom_call_target="tpu_custom_call" | custom-call | flops 2866544640 | bytes 6291456 | tf_op jit(solution)/shard_map/second_half/pallas_call | solution.py:247
Async XLA Ops:
  0.0 9.6 %copy-start = (bf16[3,3,3,192,192]{4,3,2,1,0:T(8,128)(2,1)S(1)}, bf16[3,3,3,192,192]{4,3,2,1,0:T(8,128)(2,1)}, u32[]{:S(2)}) copy-start(bf16[3,3,3,192,192]{4,3,2,1,0:T(8,128)(2,1)} %param.12) | copy-start | bytes 5971972
  0.0 9.6 %copy-start.1 = (bf16[1,4,4,6144]{3,2,1,0:T(4,128)(2,1)S(1)}, bf16[1,4,4,6144]{3,2,1,0:T(4,128)(2,1)}, u32[]{:S(2)}) copy-start(bf16[1,4,4,6144]{3,2,1,0:T(4,128)(2,1)} %param.8) | copy-start | bytes 589828
  0.0 9.6 %copy-start.2 = (f32[192]{0:T(256)S(1)}, f32[192]{0:T(256)}, u32[]{:S(2)}) copy-start(f32[192]{0:T(256)} %param.10) | copy-start | bytes 2308
  0.0 13.8 %collective-permute-start = (bf16[4,4,6144]{2,1,0:T(4,128)(2,1)}, bf16[4,4,6144]{2,1,0:T(4,128)(2,1)S(1)}, u32[]{:S(2)}, u32[]{:S(2)}) collective-permute-start(bf16[4,4,6144]{2,1,0:T(4,128)(2,1)} %bitcast.10), channel_id=1, source_target_pairs={{0,4},{2,6},{4,8},{6,10},{8,12},{10,14},{12,0},{14,2},{1,5},{3,7},... | collective-permute-start | bytes 589832 | tf_op jit(solution)/shard_map/ppermute | solution.py:203
  4.7 9.1 %copy-start.3 = (bf16[3,3,3,192,192]{4,3,2,1,0:T(8,128)(2,1)S(1)}, bf16[3,3,3,192,192]{4,3,2,1,0:T(8,128)(2,1)}, u32[]{:S(2)}) copy-start(bf16[3,3,3,192,192]{4,3,2,1,0:T(8,128)(2,1)} %param.15) | copy-start | bytes 5971972
  4.7 9.1 %copy-start.4 = (f32[192]{0:T(256)S(1)}, f32[192]{0:T(256)}, u32[]{:S(2)}) copy-start(f32[192]{0:T(256)} %param.11) | copy-start | bytes 2308
  4.7 9.1 %copy-start.5 = (f32[192]{0:T(256)S(1)}, f32[192]{0:T(256)}, u32[]{:S(2)}) copy-start(f32[192]{0:T(256)} %param.13) | copy-start | bytes 2308
  4.7 9.1 %copy-start.6 = (f32[192]{0:T(256)S(1)}, f32[192]{0:T(256)}, u32[]{:S(2)}) copy-start(f32[192]{0:T(256)} %param.14) | copy-start | bytes 2308
  4.7 4.9 %collective-permute-start.2 = (bf16[4,2,6144]{2,1,0:T(2,128)(2,1)}, bf16[4,2,6144]{2,1,0:T(2,128)(2,1)S(1)}, u32[]{:S(2)}, u32[]{:S(2)}) collective-permute-start(bf16[4,2,6144]{2,1,0:T(2,128)(2,1)} %cut_rows.1), channel_id=1, source_target_pairs={{0,2},{2,0},{4,6},{6,4},{8,10},{10,8},{12,14},{14,12},{1,3},{3,1},... | collective-permute-start | bytes 294920 | tf_op jit(solution)/shard_map/ppermute | solution.py:203
  6.3 7.5 %collective-permute-start.1 = (bf16[4,2,6144]{2,1,0:T(2,128)(2,1)}, bf16[4,2,6144]{2,1,0:T(2,128)(2,1)S(1)}, u32[]{:S(2)}, u32[]{:S(2)}) collective-permute-start(bf16[4,2,6144]{2,1,0:T(2,128)(2,1)} %cut_rows.1), channel_id=1, source_target_pairs={{0,6},{2,4},{4,10},{6,8},{8,14},{10,12},{12,2},{14,0},{1,7},{3,5},... | collective-permute-start | bytes 294920 | tf_op jit(solution)/shard_map/ppermute | solution.py:203

commit v4 on v3

v4 whole, which is shorter than its diff:
```python
import functools

import jax
import jax.numpy as jnp
from jax import lax
from jax.experimental import pallas as pl
from jax.experimental.pallas import tpu as pltpu
from jax.sharding import PartitionSpec as P

F32 = jnp.float32
BF16 = jnp.bfloat16
LANES = 128


def mask_kernel(channels, mask):
    lane = lax.broadcasted_iota(jnp.int32, mask.shape, 1)
    mask[...] = jnp.where(lane < channels, 1.0, 0.0)


def norm_silu_pair(t, gain, first, channels):
    square = t * t
    left = jnp.sum(jnp.where(first, square, 0.0), axis=1, keepdims=True)
    right = jnp.sum(jnp.where(first, 0.0, square), axis=1, keepdims=True)
    left = lax.rsqrt(left * (1.0 / channels) + 1e-06)
    right = lax.rsqrt(right * (1.0 / channels) + 1e-06)
    y = t * jnp.where(first, left, right) * gain
    return y * (0.5 + 0.5 * jnp.tanh(0.5 * y))


def twice(ref):
    return jnp.concatenate([ref[...], ref[...]], axis=1)


def norm_kernel(swap, mask, own, gain, normed, *rest):
    sent, stage = rest[:-1], rest[-1]
    frames, rows, pairs, wide = normed.shape
    gain_wide = twice(gain)
    first = mask[...] > 0.5
    for f in range(0, frames, 2):
        for p in range(pairs):
            lanes = pl.ds(p * wide, wide)
            t = jnp.concatenate([own[f + n, :, lanes].astype(F32) for n in range(2)], axis=0)
            y = norm_silu_pair(t, gain_wide, first, wide // 2)
            for k in range(3):
                at = pl.ds(f * rows * pairs + p, 2 * rows, stride=pairs)
                stage[k, at, :] = y[:, k * LANES : (k + 1) * LANES]
        for n in range(2):
            for r in range(rows):
                for k in range(3):
                    part = stage[k, pl.ds(((f + n) * rows + r) * pairs, pairs), :]
                    normed[f + n, r, :, k * LANES : (k + 1) * LANES] = part.astype(BF16)
    if swap:
        first = (rows - 2) * (1 - lax.axis_index("space"))
        sent[0][...] = normed[:, pl.ds(first, 2)]
    else:
        sent[0][...] = normed[:, rows - 2 :]
        sent[1][...] = normed[:, :2]


def gather_rows(window, own, before, after, keep, bands):
    frames, rows, pairs, wide = own.shape
    space = lax.axis_index("space")
    nothing = jnp.zeros((pairs, wide), BF16)
    for f in range(frames):
        good = keep(f)
        if bands == 2:
            window[f, (rows + 2) * space] = nothing
            for r in range(2):
                window[f, (rows + 1) * (1 - space) + r] = jnp.where(good, before[f, r], nothing)
            for r in range(rows):
                window[f, 1 + space + r] = jnp.where(good, own[f, r], nothing)
        else:
            for r in range(2):
                window[f, r] = jnp.where(good & (space > 0), before[f, r], nothing)
                window[f, rows + 2 + r] = jnp.where(good & (space < bands - 1), after[f, r], nothing)
            for r in range(rows):
                window[f, 2 + r] = jnp.where(good, own[f, r], nothing)


def taps(window, weight, source, frames, rows, a, channels):
    pairs, wide = window.shape[2], window.shape[3]
    lead = jnp.zeros((2 * LANES - channels, channels), BF16)
    parts = [
        window[source : source + frames, b : b + rows].reshape(frames * rows * pairs, wide)
        for b in range(3)
    ]
    rims = [weight[a, b] for b in range(3)]
    whole = jnp.concatenate(parts, axis=1)
    high = jnp.concatenate([x[:, LANES:] for x in parts], axis=1)
    low = jnp.concatenate([x[:, : 2 * LANES] for x in parts], axis=1)

    def product(left, right):
        return jnp.dot(left, jnp.concatenate(right, axis=0), preferred_element_type=F32)

    mine = (
        product(whole, [w[channels:] for w in rims]),
        product(whole, [w[: 2 * channels] for w in rims]),
    )
    moved = (
        product(high, [x for w in rims for x in (lead, w[:channels])]),
        product(low, [x for w in rims for x in (w[2 * channels :], lead)]),
    )
    return mine, moved


def add_moved(mine, moved, pairs):
    place = lax.broadcasted_iota(jnp.int32, mine[0].shape, 0) % pairs
    count = mine[0].shape[0]
    left = jnp.where(place == 0, 0.0, pltpu.roll(moved[0], 1, 0))
    right = jnp.where(place == pairs - 1, 0.0, pltpu.roll(moved[1], count - 1, 0))
    return mine[0] + left, mine[1] + right


def first_kernel(bands, deep, count, own, before, after, weight, partial, window, moved):
    frames, rows, pairs, wide = own.shape
    channels = wide // 2
    tm = lax.axis_index("tm")
    gather_rows(window, own, before, after, lambda f: tm * frames + f < count[0], bands)
    fill = deep * pairs
    for a in (2, 1, 0):
        skip = 2 - a
        new = taps(window, weight, 0, frames - skip, deep, a, channels)
        at = pl.ds(skip * fill, (frames - skip) * fill)
        for q in range(2):
            if skip == 0:
                partial[q] = new[0][q]
                moved[q] = new[1][q]
            else:
                partial[q, at, :] += new[0][q]
                moved[q, at, :] += new[1][q]
    both = add_moved([partial[q] for q in range(2)], [moved[q] for q in range(2)], pairs)
    for q in range(2):
        partial[q] = both[q]


def second_kernel(
    bands, deep, count, own, earlier, before, after, partial, bias, weight, gain_two, bias_two,
    weight_two, out, window, total, moved, hidden, final,
):
    frames, rows, pairs, wide = earlier.shape
    channels = wide // 2
    tm, space = lax.axis_index("tm"), lax.axis_index("space")
    first_frame = tm * frames
    fill = deep * pairs

    def valid(f):
        at = first_frame - frames + f
        return (at >= 0) & (at < count[0])

    gather_rows(window, earlier, before, after, valid, bands)
    for a in (0, 1, 2):
        new = taps(window, weight, a, frames - a, deep, a, channels)
        size = (frames - a) * fill
        for q in range(2):
            if a == 0:
                total[q, 0:size] = new[0][q]
                moved[q] = new[1][q]
            else:
                total[q, 0:size] += new[0][q]
                moved[q, 0:size] += new[1][q]
    both = add_moved(
        [total[q, 0 : frames * fill] for q in range(2)], [moved[q] for q in range(2)], pairs
    )
    for q in range(2):
        total[q, 0 : 2 * fill] = both[q][: 2 * fill]
        total[q, 2 * fill : 4 * fill] = both[q][2 * fill :] + partial[q, 0 : 2 * fill]
        total[q, 4 * fill :] = partial[q, 2 * fill :]

    start = (1 - space) if bands == 2 else 0
    row = lax.broadcasted_iota(jnp.int32, (fill, 1), 0) // pairs + (space * rows - 1 + start)
    row_ok = (row >= 0) & (row < bands * rows)
    bias_wide, gain_wide = twice(bias), twice(gain_two)
    first_lanes = lax.broadcasted_iota(jnp.int32, (fill, wide), 1) < channels
    for h in range(frames + 2):
        good = row_ok & valid(frames + h - 2)
        t = jnp.concatenate([total[q, h * fill : (h + 1) * fill, :] for q in range(2)], axis=1)
        t = jnp.where(good, t + bias_wide, 0.0).astype(BF16).astype(F32)
        y = norm_silu_pair(t, gain_wide, first_lanes, channels).astype(BF16)
        hidden[h, 0] = jnp.zeros((pairs, wide), BF16)
        hidden[h, rows + 1] = jnp.zeros((pairs, wide), BF16)
        for r in range(deep):
            hidden[h, start + r] = y[r * pairs : (r + 1) * pairs]

    mine, shifted = taps(hidden, weight_two, 0, frames, rows, 0, channels)
    for a in (1, 2):
        new = taps(hidden, weight_two, a, frames, rows, a, channels)
        mine = [mine[q] + new[0][q] for q in range(2)]
        shifted = [shifted[q] + new[1][q] for q in range(2)]
    both = jnp.concatenate(add_moved(mine, shifted, pairs), axis=1) + twice(bias_two)
    for k in range(3):
        final[k] = both[:, k * LANES : (k + 1) * LANES]
    for f in range(0, frames, 2):
        good = [valid(frames + f + n) for n in range(2)]
        for p in range(pairs):
            for k in range(3):
                block = final[k, pl.ds(f * rows * pairs + p, 2 * rows, stride=pairs), :]
                lanes = pl.ds(p * wide + k * LANES, LANES)
                for n in range(2):
                    value = own[f + n, :, lanes].astype(F32) + block[n * rows : (n + 1) * rows]
                    out[f + n, :, lanes] = jnp.where(good[n], value, 0.0).astype(BF16)


def shards(latents, counts, gain_first, bias_first, weight_first, gain_second, bias_second, weight_second):
    channels = gain_first.shape[0]
    frames, rows, flat = latents.shape[1:]
    wide = 2 * channels
    pairs = flat // wide
    blocks, bands = lax.axis_size("tm"), lax.axis_size("space")
    block = latents.reshape(frames, rows, flat)

    def shift(sent, step, along):
        pairs_of = [
            (t * bands + s, (t + along) % blocks * bands + (s + step) % bands)
            for t in range(blocks)
            for s in range(bands)
        ]
        return lax.ppermute(sent, ("tm", "space"), pairs_of)

    vmem = pl.BlockSpec(memory_space=pltpu.VMEM)
    smem = pl.BlockSpec(memory_space=pltpu.SMEM)
    swap = bands == 2
    rims = 1 if swap else 2
    rim = jax.ShapeDtypeStruct((frames, 2, pairs, wide), BF16)
    mask = pl.pallas_call(
        functools.partial(mask_kernel, channels),
        out_shape=jax.ShapeDtypeStruct((2 * rows, wide), F32),
        out_specs=vmem,
        cost_estimate=pl.CostEstimate(flops=4 << 30, bytes_accessed=1 << 16, transcendentals=0),
        name="lane_mask",
    )()
    normed, *sent = pl.pallas_call(
        functools.partial(norm_kernel, swap),
        out_shape=[jax.ShapeDtypeStruct((frames, rows, pairs, wide), BF16)] + [rim] * rims,
        in_specs=[vmem] * 3,
        out_specs=[vmem] * (1 + rims),
        scratch_shapes=[pltpu.VMEM((3, frames * rows * pairs, LANES), F32)],
        cost_estimate=pl.CostEstimate(flops=4 << 30, bytes_accessed=1 << 20, transcendentals=0),
        name="norm_and_cut",
    )(mask, block, gain_first.reshape(1, channels))
    earlier = shift(normed, 0, 1)
    if swap:
        near = (shift(sent[0], 1, 0),) * 2
        far = (shift(sent[0], 1, 1),) * 2
        deep = rows + 1
    else:
        near = (shift(sent[0], 1, 0), shift(sent[1], -1, 0))
        far = (shift(sent[0], 1, 1), shift(sent[1], -1, 1))
        deep = rows + 2

    fill = deep * pairs
    window = pltpu.VMEM((frames, deep + 2, pairs, wide), BF16)
    moved = pltpu.VMEM((2, frames * fill, channels), F32)
    first_weight = weight_first.reshape(3, 3, 3 * channels, channels)
    second_weight = weight_second.reshape(3, 3, 3 * channels, channels)
    params = pltpu.CompilerParams(vmem_limit_bytes=24 << 20)
    partial = pl.pallas_call(
        functools.partial(first_kernel, bands, deep),
        out_shape=jax.ShapeDtypeStruct((2, frames * fill, channels), F32),
        in_specs=[smem] + [vmem] * 4,
        out_specs=vmem,
        scratch_shapes=[window, moved],
        compiler_params=params,
        cost_estimate=pl.CostEstimate(flops=1 << 20, bytes_accessed=1 << 16, transcendentals=0),
        name="first_half",
    )(counts, normed, *near, first_weight)
    out = pl.pallas_call(
        functools.partial(second_kernel, bands, deep),
        out_shape=jax.ShapeDtypeStruct((frames, rows, flat), BF16),
        in_specs=[smem] + [vmem] * 10,
        out_specs=vmem,
        scratch_shapes=[
            window,
            pltpu.VMEM((2, (frames + 2) * fill, channels), F32),
            moved,
            pltpu.VMEM((frames + 2, rows + 2, pairs, wide), BF16),
            pltpu.VMEM((3, frames * rows * pairs, LANES), F32),
        ],
        compiler_params=params,
        cost_estimate=pl.CostEstimate(flops=4 << 30, bytes_accessed=6 << 20, transcendentals=0),
        name="second_half",
    )(
        counts, block, earlier, *far, partial,
        bias_first.reshape(1, channels), first_weight,
        gain_second.reshape(1, channels), bias_second.reshape(1, channels), second_weight,
    )
    return out.reshape(1, frames, rows, flat)


def solution(mesh):
    spread = P(("groups", "clip"), "tm", "space", None)
    return jax.shard_map(
        shards,
        mesh=mesh,
        in_specs=(spread, P(("groups", "clip")), P(), P(), P(), P(), P(), P()),
        out_specs=spread,
        check_vma=False,
    )
```

time: 19.7 us -> 21.1 us (1.071)
  waiting for transfers between devices: 2.8 us -> 3.77 us
  local copies, waits for them, and re-layouts: 0.03 us -> 0.95 us
  Pallas kernels: 9.9 us -> 9.44 us
    ppermute x3, waiting for transfers between devices: 2.8 us -> 3.77 us  [shift(): return lax.ppermute(sent, ('tm', 'space'), pairs_of)]
    unnamed x14, local copies, waits for them, and re-layouts: 0.03 us -> 0.95 us
    pallas_call x3 -> x4, Pallas kernels: 9.9 us -> 9.44 us  [the longest x1 4.92 us: shards(): pl.pallas_call(functools.partial(second_kernel, bands, deep), out_shape=j...]
  transfers between devices with their start and end apart: 3 -> 3, of which waited for: 2 -> 2; matrix products, arithmetic and copies ran while one was open for 0% -> 0% of each run, Pallas kernels for 21% -> 8%
where the time goes in v4:
time: 21.1 us; the launch traced here: 21 us
  Pallas kernels  9.44 us (45%)
  starting transfers between devices  6.11 us (29%)
  waiting for transfers between devices  3.77 us (18%)
  local copies, waits for them, and re-layouts  0.95 us (5%)
  between operations  0.7 us (3%)
    ppermute x3, starting transfers between devices, shift(): return lax.ppermute(sent, ('tm', 'space'), pairs_of)  6.11 us
    pallas_call x1, Pallas kernels, shards(): pl.pallas_call(functools.partial(second_kernel, bands, deep), out_shape=j...  4.92 us
    ppermute x3, waiting for transfers between devices, shift(): return lax.ppermute(sent, ('tm', 'space'), pairs_of)  3.77 us
    pallas_call x1, Pallas kernels, shards(): pl.pallas_call(functools.partial(norm_kernel, swap), out_shape=[jax.Shape...  2.16 us
    pallas_call x1, Pallas kernels, shards(): pl.pallas_call(functools.partial(first_kernel, bands, deep), out_shape=ja...  1.77 us
    unnamed x14, local copies, waits for them, and re-layouts  0.95 us
    pallas_call x1, Pallas kernels, shards(): pl.pallas_call(functools.partial(mask_kernel, channels), out_shape=jax.Sh...  0.6 us
  transfers between devices with their start and end apart: 3, of which 2 were waited for; matrix products, arithmetic and copies ran while one was open for 0% of the time, Pallas kernels for 8%

profile of v4, /device:TPU:0, one launch (start us, length us, event | category | flops | bytes accessed | tf_op | source)
XLA Modules:
  0.0 21.0 jit_solution(10327049263812295845)
XLA Ops:
  0.0 0.6 %lane_mask.1.mask = f32[8,384]{1,0:T(8,128)} custom-call(), custom_call_target="tpu_custom_call" | custom-call | flops 4294967296 | bytes 65536 | tf_op jit(solution)/shard_map/lane_mask/pallas_call | solution.py:224
  0.6 0.0 copy-start
  0.6 0.0 copy-start.3
  0.6 2.2 %norm_and_cut.1 = (bf16[4,4,16,384]{3,2,1,0:T(8,128)(2,1)}, bf16[4,2,16,384]{3,2,1,0:T(8,128)(2,1)}) custom-call(f32[8,384]{1,0:T(8,128)} %lane_mask.1.mask, bf16[4,4,6144]{2,1,0:T(4,128)(2,1)} %bitcast.11, f32[1,192]{1,0:T(1,128)} %bitcast.16), custom_call_target="tpu_custom_call" | custom-call | flops 4294967296 | bytes 1048576 | tf_op jit(solution)/shard_map/norm_and_cut/pallas_call | solution.py:231
  2.8 0.0 copy-start.4
  2.8 0.0 copy-start.5
  2.8 0.0 copy-start.6
  2.8 3.1 %collective-permute-start = (bf16[4,4,16,384]{3,2,1,0:T(8,128)(2,1)}, bf16[4,4,16,384]{3,2,1,0:T(8,128)(2,1)S(1)}, u32[]{:S(2)}, u32[]{:S(2)}) collective-permute-start(bf16[4,4,16,384]{3,2,1,0:T(8,128)(2,1)} %get-tuple-element.7.own), channel_id=1, source_target_pairs={{0,4},{2,6},{4,8},{6,10},{8,12},{10,14},{12,0},{14,2},{1,5},{3,7},... | collective-permute-start | bytes 589832 | tf_op jit(solution)/shard_map/ppermute | solution.py:217
  5.8 1.5 %collective-permute-start.2 = (bf16[4,2,16,384]{3,2,1,0:T(8,128)(2,1)}, bf16[4,2,16,384]{3,2,1,0:T(8,128)(2,1)S(1)}, u32[]{:S(2)}, u32[]{:S(2)}) collective-permute-start(bf16[4,2,16,384]{3,2,1,0:T(8,128)(2,1)} %get-tuple-element.8), channel_id=1, source_target_pairs={{0,2},{2,0},{4,6},{6,4},{8,10},{10,8},{12,14},{14,12},{1,3},{3,1},... | collective-permute-start | bytes 294920 | tf_op jit(solution)/shard_map/ppermute | solution.py:217
  7.3 1.5 %collective-permute-start.1 = (bf16[4,2,16,384]{3,2,1,0:T(8,128)(2,1)}, bf16[4,2,16,384]{3,2,1,0:T(8,128)(2,1)S(1)}, u32[]{:S(2)}, u32[]{:S(2)}) collective-permute-start(bf16[4,2,16,384]{3,2,1,0:T(8,128)(2,1)} %get-tuple-element.8), channel_id=1, source_target_pairs={{0,6},{2,4},{4,10},{6,8},{8,14},{10,12},{12,2},{14,0},{1,7},{3,5},... | collective-permute-start | bytes 294920 | tf_op jit(solution)/shard_map/ppermute | solution.py:217
  9.5 1.1 %collective-permute-done.2.before.after = bf16[4,2,16,384]{3,2,1,0:T(8,128)(2,1)S(1)} collective-permute-done((bf16[4,2,16,384]{3,2,1,0:T(8,128)(2,1)}, bf16[4,2,16,384]{3,2,1,0:T(8,128)(2,1)S(1)}, u32[]{:S(2)}, u32[]{:S(2)}) %collective-permute-start.2) | collective-permute-done | bytes 98336 | tf_op jit(solution)/shard_map/ppermute | solution.py:217
  10.7 0.0 copy-done
  10.7 0.0 copy-start.1
  10.7 0.9 %copy-done.1 = bf16[4,4,16,384]{3,2,1,0:T(8,128)(2,1)S(1)} copy-done((bf16[4,4,16,384]{3,2,1,0:T(8,128)(2,1)S(1)}, bf16[4,4,16,384]{3,2,1,0:T(8,128)(2,1)}, u32[]{:S(2)}) %copy-start.1) | copy-done | bytes 196632
  11.6 0.0 copy-start.2
  11.6 1.8 %first_half.1.partial = f32[2,320,192]{2,1,0:T(8,128)S(1)} custom-call(s32[1]{0:T(128)S(6)} %copy.9.count, bf16[4,4,16,384]{3,2,1,0:T(8,128)(2,1)S(1)} %copy-done.1, bf16[4,2,16,384]{3,2,1,0:T(8,128)(2,1)S(1)} %collective-permute-done.2.before.after, bf16[4,2,16,384]{3,2,1,0:T(8,128)(2,1)S(1)} %collective-permute-done.2.before.after, ...), custom_call_target="tpu_custom_call" | custom-call | flops 1048576 | bytes 65536 | tf_op jit(solution)/shard_map/first_half/pallas_call | solution.py:256
  13.4 2.6 %collective-permute-done.1.before.after = bf16[4,2,16,384]{3,2,1,0:T(8,128)(2,1)S(1)} collective-permute-done((bf16[4,2,16,384]{3,2,1,0:T(8,128)(2,1)}, bf16[4,2,16,384]{3,2,1,0:T(8,128)(2,1)S(1)}, u32[]{:S(2)}, u32[]{:S(2)}) %collective-permute-start.1) | collective-permute-done | bytes 98336 | tf_op jit(solution)/shard_map/ppermute | solution.py:217
  16.0 0.0 collective-permute-done.earlier
  16.0 0.0 copy-done.3
  16.0 0.0 copy-done.4
  16.0 0.0 copy-done.5
  16.0 0.0 copy-done.6
  16.0 0.0 copy-done.2
  16.1 4.9 %second_half.1 = bf16[4,4,6144]{2,1,0:T(4,128)(2,1)} custom-call(s32[1]{0:T(128)S(6)} %copy.9.count, bf16[4,4,6144]{2,1,0:T(4,128)(2,1)S(1)} %bitcast.12, bf16[4,4,16,384]{3,2,1,0:T(8,128)(2,1)S(1)} %collective-permute-done.earlier, bf16[4,2,16,384]{3,2,1,0:T(8,128)(2,1)S(1)} %collective-permute-done.1.before.after, ...), custom_call_target="tpu_custom_call" | custom-call | flops 4294967296 | bytes 6291456 | tf_op jit(solution)/shard_map/second_half/pallas_call | solution.py:266
Async XLA Ops:
  0.6 10.1 %copy-start = (bf16[3,3,3,192,192]{4,3,2,1,0:T(8,128)(2,1)S(1)}, bf16[3,3,3,192,192]{4,3,2,1,0:T(8,128)(2,1)}, u32[]{:S(2)}) copy-start(bf16[3,3,3,192,192]{4,3,2,1,0:T(8,128)(2,1)} %param.12) | copy-start | bytes 5971972
  0.6 15.4 %copy-start.3 = (bf16[1,4,4,6144]{3,2,1,0:T(4,128)(2,1)S(1)}, bf16[1,4,4,6144]{3,2,1,0:T(4,128)(2,1)}, u32[]{:S(2)}) copy-start(bf16[1,4,4,6144]{3,2,1,0:T(4,128)(2,1)} %param.8) | copy-start | bytes 589828
  2.8 13.3 %copy-start.4 = (f32[192]{0:T(256)S(1)}, f32[192]{0:T(256)}, u32[]{:S(2)}) copy-start(f32[192]{0:T(256)} %param.11) | copy-start | bytes 2308
  2.8 13.3 %copy-start.5 = (f32[192]{0:T(256)S(1)}, f32[192]{0:T(256)}, u32[]{:S(2)}) copy-start(f32[192]{0:T(256)} %param.13) | copy-start | bytes 2308
  2.8 13.3 %copy-start.6 = (f32[192]{0:T(256)S(1)}, f32[192]{0:T(256)}, u32[]{:S(2)}) copy-start(f32[192]{0:T(256)} %param.14) | copy-start | bytes 2308
  2.8 13.2 %collective-permute-start = (bf16[4,4,16,384]{3,2,1,0:T(8,128)(2,1)}, bf16[4,4,16,384]{3,2,1,0:T(8,128)(2,1)S(1)}, u32[]{:S(2)}, u32[]{:S(2)}) collective-permute-start(bf16[4,4,16,384]{3,2,1,0:T(8,128)(2,1)} %get-tuple-element.7.own), channel_id=1, source_target_pairs={{0,4},{2,6},{4,8},{6,10},{8,12},{10,14},{12,0},{14,2},{1,5},{3,7},... | collective-permute-start | bytes 589832 | tf_op jit(solution)/shard_map/ppermute | solution.py:217
  5.8 4.8 %collective-permute-start.2 = (bf16[4,2,16,384]{3,2,1,0:T(8,128)(2,1)}, bf16[4,2,16,384]{3,2,1,0:T(8,128)(2,1)S(1)}, u32[]{:S(2)}, u32[]{:S(2)}) collective-permute-start(bf16[4,2,16,384]{3,2,1,0:T(8,128)(2,1)} %get-tuple-element.8), channel_id=1, source_target_pairs={{0,2},{2,0},{4,6},{6,4},{8,10},{10,8},{12,14},{14,12},{1,3},{3,1},... | collective-permute-start | bytes 294920 | tf_op jit(solution)/shard_map/ppermute | solution.py:217
  7.3 8.7 %collective-permute-start.1 = (bf16[4,2,16,384]{3,2,1,0:T(8,128)(2,1)}, bf16[4,2,16,384]{3,2,1,0:T(8,128)(2,1)S(1)}, u32[]{:S(2)}, u32[]{:S(2)}) collective-permute-start(bf16[4,2,16,384]{3,2,1,0:T(8,128)(2,1)} %get-tuple-element.8), channel_id=1, source_target_pairs={{0,6},{2,4},{4,10},{6,8},{8,14},{10,12},{12,2},{14,0},{1,7},{3,5},... | collective-permute-start | bytes 294920 | tf_op jit(solution)/shard_map/ppermute | solution.py:217
  10.7 0.9 %copy-start.1 = (bf16[4,4,16,384]{3,2,1,0:T(8,128)(2,1)S(1)}, bf16[4,4,16,384]{3,2,1,0:T(8,128)(2,1)}, u32[]{:S(2)}) copy-start(bf16[4,4,16,384]{3,2,1,0:T(8,128)(2,1)} %get-tuple-element.7.own) | copy-start | bytes 589828
  11.6 4.4 %copy-start.2 = (bf16[3,3,3,192,192]{4,3,2,1,0:T(8,128)(2,1)S(1)}, bf16[3,3,3,192,192]{4,3,2,1,0:T(8,128)(2,1)}, u32[]{:S(2)}) copy-start(bf16[3,3,3,192,192]{4,3,2,1,0:T(8,128)(2,1)} %param.15) | copy-start | bytes 5971972

commit v5 on v4

--- a/solution.py
+++ b/solution.py
@@ -218,6 +218,7 @@
 
     vmem = pl.BlockSpec(memory_space=pltpu.VMEM)
     smem = pl.BlockSpec(memory_space=pltpu.SMEM)
+    params = pltpu.CompilerParams(vmem_limit_bytes=24 << 20)
     swap = bands == 2
     rims = 1 if swap else 2
     rim = jax.ShapeDtypeStruct((frames, 2, pairs, wide), BF16)
@@ -225,6 +226,7 @@
         functools.partial(mask_kernel, channels),
         out_shape=jax.ShapeDtypeStruct((2 * rows, wide), F32),
         out_specs=vmem,
+        compiler_params=params,
         cost_estimate=pl.CostEstimate(flops=4 << 30, bytes_accessed=1 << 16, transcendentals=0),
         name="lane_mask",
     )()
@@ -234,6 +236,7 @@
         in_specs=[vmem] * 3,
         out_specs=[vmem] * (1 + rims),
         scratch_shapes=[pltpu.VMEM((3, frames * rows * pairs, LANES), F32)],
+        compiler_params=params,
         cost_estimate=pl.CostEstimate(flops=4 << 30, bytes_accessed=1 << 20, transcendentals=0),
         name="norm_and_cut",
     )(mask, block, gain_first.reshape(1, channels))
@@ -252,7 +255,6 @@
     moved = pltpu.VMEM((2, frames * fill, channels), F32)
     first_weight = weight_first.reshape(3, 3, 3 * channels, channels)
     second_weight = weight_second.reshape(3, 3, 3 * channels, channels)
-    params = pltpu.CompilerParams(vmem_limit_bytes=24 << 20)
     partial = pl.pallas_call(
         functools.partial(first_kernel, bands, deep),
         out_shape=jax.ShapeDtypeStruct((2, frames * fill, channels), F32),

time: 21.1 us -> 19.6 us (0.929)
  Pallas kernels: 9.44 us -> 7.17 us
  waiting for transfers between devices: 3.77 us -> 4.45 us
    pallas_call x1, Pallas kernels: 2.16 us -> 0.38 us  [shards(): pl.pallas_call(functools.partial(norm_kernel, swap), out_shape=[jax.Shape...]
    ppermute x3, waiting for transfers between devices: 3.77 us -> 4.45 us  [shift(): return lax.ppermute(sent, ('tm', 'space'), pairs_of)]
    pallas_call x1, Pallas kernels: 0.6 us -> 0.01 us  [shards(): pl.pallas_call(functools.partial(mask_kernel, channels), out_shape=jax.Sh...]
  transfers between devices with their start and end apart: 3 -> 3, of which waited for: 2 -> 2; matrix products, arithmetic and copies ran while one was open for 0% -> 0% of each run, Pallas kernels for 8% -> 9%
where the time goes in v5:
time: 19.6 us; the launch traced here: 19.4 us
  Pallas kernels  7.17 us (37%)
  starting transfers between devices  6.11 us (31%)
  waiting for transfers between devices  4.45 us (23%)
  local copies, waits for them, and re-layouts  0.95 us (5%)
  between operations  0.73 us (4%)
    ppermute x3, starting transfers between devices, shift(): return lax.ppermute(sent, ('tm', 'space'), pairs_of)  6.11 us
    pallas_call x1, Pallas kernels, shards(): pl.pallas_call(functools.partial(second_kernel, bands, deep), out_shape=j...  4.97 us
    ppermute x3, waiting for transfers between devices, shift(): return lax.ppermute(sent, ('tm', 'space'), pairs_of)  4.45 us
    pallas_call x1, Pallas kernels, shards(): pl.pallas_call(functools.partial(first_kernel, bands, deep), out_shape=ja...  1.81 us
    unnamed x14, local copies, waits for them, and re-layouts  0.95 us
  transfers between devices with their start and end apart: 3, of which 2 were waited for; matrix products, arithmetic and copies ran while one was open for 0% of the time, Pallas kernels for 9%

profile of v5, /device:TPU:0, one launch (start us, length us, event | category | flops | bytes accessed | tf_op | source)
XLA Modules:
  0.0 19.4 jit_solution(11922087129658886615)
XLA Ops:
  0.0 0.0 copy-start.2
  0.0 0.0 copy-start.3
  0.0 0.9 %copy-done.2 = bf16[1,4,4,6144]{3,2,1,0:T(4,128)(2,1)S(1)} copy-done((bf16[1,4,4,6144]{3,2,1,0:T(4,128)(2,1)S(1)}, bf16[1,4,4,6144]{3,2,1,0:T(4,128)(2,1)}, u32[]{:S(2)}) %copy-start.2) | copy-done | bytes 196632
  0.9 0.0 copy-done.3
  0.9 0.0 copy-start
  0.9 0.4 %norm_and_cut.1 = (bf16[4,4,16,384]{3,2,1,0:T(8,128)(2,1)S(1)}, bf16[4,2,16,384]{3,2,1,0:T(8,128)(2,1)S(1)}) custom-call(f32[8,384]{1,0:T(8,128)S(1)} %lane_mask.1.mask, bf16[4,4,6144]{2,1,0:T(4,128)(2,1)S(1)} %bitcast.11, f32[1,192]{1,0:T(1,128)S(1)} %bitcast.13), custom_call_target="tpu_custom_call" | custom-call | flops 4294967296 | bytes 1048576 | tf_op jit(solution)/shard_map/norm_and_cut/pallas_call | solution.py:233
  1.3 0.0 copy-start.1
  1.3 0.0 copy-start.4
  1.3 0.0 copy-start.5
  1.4 0.0 copy-start.6
  1.4 3.1 %collective-permute-start = (bf16[4,4,16,384]{3,2,1,0:T(8,128)(2,1)S(1)}, bf16[4,4,16,384]{3,2,1,0:T(8,128)(2,1)S(1)}, u32[]{:S(2)}, u32[]{:S(2)}) collective-permute-start(bf16[4,4,16,384]{3,2,1,0:T(8,128)(2,1)S(1)} %get-tuple-element.7.own), channel_id=1, source_target_pairs={{0,4},{2,6},{4,8},{6,10},{8,12},{10,14},{12,0},{14,2},{1,5},{3,7},... | collective-permute-start | bytes 589832 | tf_op jit(solution)/shard_map/ppermute | solution.py:217
  4.4 1.5 %collective-permute-start.2 = (bf16[4,2,16,384]{3,2,1,0:T(8,128)(2,1)S(1)}, bf16[4,2,16,384]{3,2,1,0:T(8,128)(2,1)S(1)}, u32[]{:S(2)}, u32[]{:S(2)}) collective-permute-start(bf16[4,2,16,384]{3,2,1,0:T(8,128)(2,1)S(1)} %get-tuple-element.8), channel_id=1, source_target_pairs={{0,2},{2,0},{4,6},{6,4},{8,10},{10,8},{12,14},{14,12},{1,3},{3,1},... | collective-permute-start | bytes 294920 | tf_op jit(solution)/shard_map/ppermute | solution.py:217
  5.9 1.5 %collective-permute-start.1 = (bf16[4,2,16,384]{3,2,1,0:T(8,128)(2,1)S(1)}, bf16[4,2,16,384]{3,2,1,0:T(8,128)(2,1)S(1)}, u32[]{:S(2)}, u32[]{:S(2)}) collective-permute-start(bf16[4,2,16,384]{3,2,1,0:T(8,128)(2,1)S(1)} %get-tuple-element.8), channel_id=1, source_target_pairs={{0,6},{2,4},{4,10},{6,8},{8,14},{10,12},{12,2},{14,0},{1,7},{3,5},... | collective-permute-start | bytes 294920 | tf_op jit(solution)/shard_map/ppermute | solution.py:217
  8.1 0.9 %collective-permute-done.2.before.after = bf16[4,2,16,384]{3,2,1,0:T(8,128)(2,1)S(1)} collective-permute-done((bf16[4,2,16,384]{3,2,1,0:T(8,128)(2,1)S(1)}, bf16[4,2,16,384]{3,2,1,0:T(8,128)(2,1)S(1)}, u32[]{:S(2)}, u32[]{:S(2)}) %collective-permute-start.2) | collective-permute-done | bytes 98336 | tf_op jit(solution)/shard_map/ppermute | solution.py:217
  9.1 0.0 copy-done
  9.1 1.8 %first_half.1.partial = f32[2,320,192]{2,1,0:T(8,128)S(1)} custom-call(s32[1]{0:T(128)S(6)} %copy.9.count, bf16[4,4,16,384]{3,2,1,0:T(8,128)(2,1)S(1)} %get-tuple-element.7.own, bf16[4,2,16,384]{3,2,1,0:T(8,128)(2,1)S(1)} %collective-permute-done.2.before.after, bf16[4,2,16,384]{3,2,1,0:T(8,128)(2,1)S(1)} %collective-permute-done.2.before.after, ...), custom_call_target="tpu_custom_call" | custom-call | flops 1048576 | bytes 65536 | tf_op jit(solution)/shard_map/first_half/pallas_call | solution.py:258
  10.9 3.5 %collective-permute-done.1.before.after = bf16[4,2,16,384]{3,2,1,0:T(8,128)(2,1)S(1)} collective-permute-done((bf16[4,2,16,384]{3,2,1,0:T(8,128)(2,1)S(1)}, bf16[4,2,16,384]{3,2,1,0:T(8,128)(2,1)S(1)}, u32[]{:S(2)}, u32[]{:S(2)}) %collective-permute-start.1) | collective-permute-done | bytes 98336 | tf_op jit(solution)/shard_map/ppermute | solution.py:217
  14.4 0.0 collective-permute-done.earlier
  14.4 0.0 copy-done.1
  14.4 0.0 copy-done.4
  14.4 0.0 copy-done.5
  14.4 0.0 copy-done.6
  14.4 5.0 %second_half.1 = bf16[4,4,6144]{2,1,0:T(4,128)(2,1)} custom-call(s32[1]{0:T(128)S(6)} %copy.9.count, bf16[4,4,6144]{2,1,0:T(4,128)(2,1)S(1)} %bitcast.12, bf16[4,4,16,384]{3,2,1,0:T(8,128)(2,1)S(1)} %collective-permute-done.earlier, bf16[4,2,16,384]{3,2,1,0:T(8,128)(2,1)S(1)} %collective-permute-done.1.before.after, ...), custom_call_target="tpu_custom_call" | custom-call | flops 4294967296 | bytes 6291456 | tf_op jit(solution)/shard_map/second_half/pallas_call | solution.py:268
  (1 shorter events, 0.0 us)
Async XLA Ops:
  0.0 0.9 %copy-start.2 = (bf16[1,4,4,6144]{3,2,1,0:T(4,128)(2,1)S(1)}, bf16[1,4,4,6144]{3,2,1,0:T(4,128)(2,1)}, u32[]{:S(2)}) copy-start(bf16[1,4,4,6144]{3,2,1,0:T(4,128)(2,1)} %param.8) | copy-start | bytes 589828
  0.0 0.9 %copy-start.3 = (f32[192]{0:T(256)S(1)}, f32[192]{0:T(256)}, u32[]{:S(2)}) copy-start(f32[192]{0:T(256)} %param.10) | copy-start | bytes 2308
  0.9 8.1 %copy-start = (bf16[3,3,3,192,192]{4,3,2,1,0:T(8,128)(2,1)S(1)}, bf16[3,3,3,192,192]{4,3,2,1,0:T(8,128)(2,1)}, u32[]{:S(2)}) copy-start(bf16[3,3,3,192,192]{4,3,2,1,0:T(8,128)(2,1)} %param.12) | copy-start | bytes 5971972
  1.3 13.1 %copy-start.1 = (bf16[3,3,3,192,192]{4,3,2,1,0:T(8,128)(2,1)S(1)}, bf16[3,3,3,192,192]{4,3,2,1,0:T(8,128)(2,1)}, u32[]{:S(2)}) copy-start(bf16[3,3,3,192,192]{4,3,2,1,0:T(8,128)(2,1)} %param.15) | copy-start | bytes 5971972
  1.3 13.1 %copy-start.4 = (f32[192]{0:T(256)S(1)}, f32[192]{0:T(256)}, u32[]{:S(2)}) copy-start(f32[192]{0:T(256)} %param.11) | copy-start | bytes 2308
  1.3 13.1 %copy-start.5 = (f32[192]{0:T(256)S(1)}, f32[192]{0:T(256)}, u32[]{:S(2)}) copy-start(f32[192]{0:T(256)} %param.13) | copy-start | bytes 2308
  1.4 13.1 %copy-start.6 = (f32[192]{0:T(256)S(1)}, f32[192]{0:T(256)}, u32[]{:S(2)}) copy-start(f32[192]{0:T(256)} %param.14) | copy-start | bytes 2308
  1.4 13.0 %collective-permute-start = (bf16[4,4,16,384]{3,2,1,0:T(8,128)(2,1)S(1)}, bf16[4,4,16,384]{3,2,1,0:T(8,128)(2,1)S(1)}, u32[]{:S(2)}, u32[]{:S(2)}) collective-permute-start(bf16[4,4,16,384]{3,2,1,0:T(8,128)(2,1)S(1)} %get-tuple-element.7.own), channel_id=1, source_target_pairs={{0,4},{2,6},{4,8},{6,10},{8,12},{10,14},{12,0},{14,2},{1,5},{3,7},... | collective-permute-start | bytes 589832 | tf_op jit(solution)/shard_map/ppermute | solution.py:217
  4.4 4.6 %collective-permute-start.2 = (bf16[4,2,16,384]{3,2,1,0:T(8,128)(2,1)S(1)}, bf16[4,2,16,384]{3,2,1,0:T(8,128)(2,1)S(1)}, u32[]{:S(2)}, u32[]{:S(2)}) collective-permute-start(bf16[4,2,16,384]{3,2,1,0:T(8,128)(2,1)S(1)} %get-tuple-element.8), channel_id=1, source_target_pairs={{0,2},{2,0},{4,6},{6,4},{8,10},{10,8},{12,14},{14,12},{1,3},{3,1},... | collective-permute-start | bytes 294920 | tf_op jit(solution)/shard_map/ppermute | solution.py:217
  5.9 8.5 %collective-permute-start.1 = (bf16[4,2,16,384]{3,2,1,0:T(8,128)(2,1)S(1)}, bf16[4,2,16,384]{3,2,1,0:T(8,128)(2,1)S(1)}, u32[]{:S(2)}, u32[]{:S(2)}) collective-permute-start(bf16[4,2,16,384]{3,2,1,0:T(8,128)(2,1)S(1)} %get-tuple-element.8), channel_id=1, source_target_pairs={{0,6},{2,4},{4,10},{6,8},{8,14},{10,12},{12,2},{14,0},{1,7},{3,5},... | collective-permute-start | bytes 294920 | tf_op jit(solution)/shard_map/ppermute | solution.py:217

commit v6 on v5

v6 whole, which is shorter than its diff:
```python
import functools

import jax
import jax.numpy as jnp
from jax import lax
from jax.experimental import pallas as pl
from jax.experimental.pallas import tpu as pltpu
from jax.sharding import PartitionSpec as P

F32 = jnp.float32
BF16 = jnp.bfloat16
LANES = 128


def mask_kernel(channels, mask):
    lane = lax.broadcasted_iota(jnp.int32, mask.shape, 1)
    mask[...] = jnp.where(lane < channels, 1.0, 0.0)


def norm_silu_pair(t, gain, first, channels):
    square = t * t
    left = jnp.sum(jnp.where(first, square, 0.0), axis=1, keepdims=True)
    right = jnp.sum(jnp.where(first, 0.0, square), axis=1, keepdims=True)
    left = lax.rsqrt(left * (1.0 / channels) + 1e-06)
    right = lax.rsqrt(right * (1.0 / channels) + 1e-06)
    y = t * jnp.where(first, left, right) * gain
    return y * (0.5 + 0.5 * jnp.tanh(0.5 * y))


def twice(ref):
    return jnp.concatenate([ref[...], ref[...]], axis=1)


def norm_block(block, gain_wide, first, stage, store, pairs):
    frames, rows = block.shape[0], block.shape[1]
    wide = gain_wide.shape[1]
    for f in range(0, frames, 2):
        for p in range(pairs):
            lanes = pl.ds(p * wide, wide)
            t = jnp.concatenate([block[f + n, :, lanes].astype(F32) for n in range(2)], axis=0)
            y = norm_silu_pair(t, gain_wide, first, wide // 2)
            for k in range(3):
                at = pl.ds(f * rows * pairs + p, 2 * rows, stride=pairs)
                stage[k, at, :] = y[:, k * LANES : (k + 1) * LANES]
        for n in range(2):
            for r in range(rows):
                at = pl.ds(((f + n) * rows + r) * pairs, pairs)
                store(f + n, r, [stage[k, at, :].astype(BF16) for k in range(3)])


def norm_kernel(swap, mask, block, gain, normed, *rest):
    sent, stage = rest[:-1], rest[-1]
    rows, pairs = normed.shape[1], normed.shape[2]

    def store(f, r, parts):
        for k in range(3):
            normed[f, r, :, k * LANES : (k + 1) * LANES] = parts[k]

    norm_block(block, twice(gain), mask[...] > 0.5, stage, store, pairs)
    if swap:
        first = (rows - 2) * (1 - lax.axis_index("space"))
        sent[0][...] = normed[:, pl.ds(first, 2)]
    else:
        sent[0][...] = normed[:, rows - 2 :]
        sent[1][...] = normed[:, :2]


def dot(left, right):
    return jnp.dot(
        jnp.concatenate(left, axis=1), jnp.concatenate(right, axis=0), preferred_element_type=F32
    )


def products(parts, rims, channels):
    lead = jnp.zeros((2 * LANES - channels, channels), BF16)
    mine = (
        dot(parts, [w[channels:] for w in rims]),
        dot(parts, [w[: 2 * channels] for w in rims]),
    )
    high = [x[:, LANES:] for x in parts]
    low = [x[:, : 2 * LANES] for x in parts]
    moved = (
        dot(high, [x for w in rims for x in (lead, w[:channels])]),
        dot(low, [x for w in rims for x in (w[2 * channels :], lead)]),
    )
    return mine, moved


def conv(window, weight, frames, rows, channels):
    pairs, wide = window.shape[2], window.shape[3]
    taps = [(a, b) for a in range(3) for b in range(3)]
    parts = [
        window[a : a + frames, b : b + rows].reshape(frames * rows * pairs, wide) for a, b in taps
    ]
    return add_moved(*products(parts, [weight[a, b] for a, b in taps], channels), pairs)


def add_moved(mine, moved, pairs):
    place = lax.broadcasted_iota(jnp.int32, mine[0].shape, 0) % pairs
    count = mine[0].shape[0]
    left = jnp.where(place == 0, 0.0, pltpu.roll(moved[0], 1, 0))
    right = jnp.where(place == pairs - 1, 0.0, pltpu.roll(moved[1], count - 1, 0))
    return mine[0] + left, mine[1] + right


def first_kernel(
    bands, deep, count, mask, normed, earlier, before, after, gain, weight, total, window, stage
):
    frames, rows, pairs, wide = normed.shape
    tm, space = lax.axis_index("tm"), lax.axis_index("space")
    nothing = jnp.zeros((pairs, wide), BF16)
    top = 1 + space if bands == 2 else 2

    def valid(f):
        at = (tm - 1) * frames + f
        return (at >= 0) & (at < count[0])

    def store(f, r, parts):
        good = valid(f)
        for k in range(3):
            part = jnp.where(good, parts[k], jnp.zeros_like(parts[k]))
            window[f, top + r, :, k * LANES : (k + 1) * LANES] = part

    for f in range(2 * frames):
        good = valid(f)
        near = f >= frames
        if bands == 2:
            window[f, (rows + 2) * space] = nothing
            for r in range(2):
                rim = jnp.where(good, before[f - frames, r], nothing) if near else nothing
                window[f, (rows + 1) * (1 - space) + r] = rim
        else:
            for r in range(2):
                above = jnp.where(good & (space > 0), before[f - frames, r], nothing) if near else nothing
                below = (
                    jnp.where(good & (space < bands - 1), after[f - frames, r], nothing)
                    if near else nothing
                )
                window[f, r] = above
                window[f, rows + 2 + r] = below
        if near:
            for r in range(rows):
                window[f, top + r] = jnp.where(good, normed[f - frames, r], nothing)
    norm_block(earlier, twice(gain), mask[...] > 0.5, stage, store, pairs)
    both = conv(window, weight, frames + 2, deep, wide // 2)
    for q in range(2):
        total[q] = both[q].reshape(total.shape[1:])


def add_corner(total, corner, weight, side, keep, channels):
    frames, pairs, wide = corner.shape[0], corner.shape[2], corner.shape[3]
    deep = total.shape[2]
    low = (deep - 2) * side
    halo = (deep - 1) * side
    nothing = jnp.zeros((pairs, wide), BF16)
    rows = [
        [jnp.where(keep(f), corner[f, r], nothing) if f < frames else nothing for r in range(2)]
        for f in range(frames + 2)
    ]
    inner = [
        jnp.where(keep(f), corner[f, 1 - side], nothing) if f < frames else nothing
        for f in range(frames + 2)
    ]
    parts = [
        jnp.concatenate([x for f in range(frames) for x in rows[f + a]], axis=0) for a in range(3)
    ]
    added = add_moved(*products(parts, [weight[a, 2 * side] for a in range(3)], channels), pairs)
    for q in range(2):
        total[q, 0:frames, pl.ds(low, 2)] += added[q].reshape(frames, 2, pairs, channels)
    parts = [jnp.concatenate([inner[f + a] for f in range(frames)], axis=0) for a in range(3)]
    added = add_moved(*products(parts, [weight[a, 1] for a in range(3)], channels), pairs)
    for q in range(2):
        total[q, 0:frames, halo] += added[q].reshape(frames, pairs, channels)


def second_kernel(
    bands, deep, count, own, before, after, first_total, bias, weight, gain_two, bias_two,
    weight_two, out, total, hidden, final,
):
    frames, rows, pairs, wide = before.shape[0], own.shape[1], before.shape[2], before.shape[3]
    channels = wide // 2
    tm, space = lax.axis_index("tm"), lax.axis_index("space")
    fill = deep * pairs

    def valid(f):
        at = (tm - 1) * frames + f
        return (at >= 0) & (at < count[0])

    total[...] = first_total[...]
    if bands == 2:
        add_corner(total, before, weight, 1 - space, valid, channels)
    else:
        add_corner(total, before, weight, 0, lambda f: valid(f) & (space > 0), channels)
        add_corner(total, after, weight, 1, lambda f: valid(f) & (space < bands - 1), channels)

    start = (1 - space) if bands == 2 else 0
    row = lax.broadcasted_iota(jnp.int32, (fill, 1), 0) // pairs + (space * rows - 1 + start)
    row_ok = (row >= 0) & (row < bands * rows)
    bias_wide, gain_wide = twice(bias), twice(gain_two)
    first_lanes = lax.broadcasted_iota(jnp.int32, (fill, wide), 1) < channels
    for h in range(frames + 2):
        good = row_ok & valid(frames + h - 2)
        t = jnp.concatenate([total[q, h].reshape(fill, channels) for q in range(2)], axis=1)
        t = jnp.where(good, t + bias_wide, 0.0).astype(BF16).astype(F32)
        y = norm_silu_pair(t, gain_wide, first_lanes, channels).astype(BF16)
        hidden[h, 0] = jnp.zeros((pairs, wide), BF16)
        hidden[h, rows + 1] = jnp.zeros((pairs, wide), BF16)
        for r in range(deep):
            hidden[h, start + r] = y[r * pairs : (r + 1) * pairs]

    both = jnp.concatenate(conv(hidden, weight_two, frames, rows, channels), axis=1)
    both = both + twice(bias_two)
    for k in range(3):
        final[k] = both[:, k * LANES : (k + 1) * LANES]
    for f in range(0, frames, 2):
        good = [valid(frames + f + n) for n in range(2)]
        for p in range(pairs):
            for k in range(3):
                block = final[k, pl.ds(f * rows * pairs + p, 2 * rows, stride=pairs), :]
                lanes = pl.ds(p * wide + k * LANES, LANES)
                for n in range(2):
                    value = own[f + n, :, lanes].astype(F32) + block[n * rows : (n + 1) * rows]
                    out[f + n, :, lanes] = jnp.where(good[n], value, 0.0).astype(BF16)


def shards(latents, counts, gain_first, bias_first, weight_first, gain_second, bias_second, weight_second):
    channels = gain_first.shape[0]
    frames, rows, flat = latents.shape[1:]
    wide = 2 * channels
    pairs = flat // wide
    blocks, bands = lax.axis_size("tm"), lax.axis_size("space")
    block = latents.reshape(frames, rows, flat)

    def shift(sent, step, along):
        pairs_of = [
            (t * bands + s, (t + along) % blocks * bands + (s + step) % bands)
            for t in range(blocks)
            for s in range(bands)
        ]
        return lax.ppermute(sent, ("tm", "space"), pairs_of)

    vmem = pl.BlockSpec(memory_space=pltpu.VMEM)
    smem = pl.BlockSpec(memory_space=pltpu.SMEM)
    params = pltpu.CompilerParams(vmem_limit_bytes=24 << 20)
    swap = bands == 2
    rims = 1 if swap else 2
    rim = jax.ShapeDtypeStruct((frames, 2, pairs, wide), BF16)
    mask = pl.pallas_call(
        functools.partial(mask_kernel, channels),
        out_shape=jax.ShapeDtypeStruct((2 * rows, wide), F32),
        out_specs=vmem,
        compiler_params=params,
        cost_estimate=pl.CostEstimate(flops=4 << 30, bytes_accessed=1 << 16, transcendentals=0),
        name="lane_mask",
    )()
    normed, *sent = pl.pallas_call(
        functools.partial(norm_kernel, swap),
        out_shape=[jax.ShapeDtypeStruct((frames, rows, pairs, wide), BF16)] + [rim] * rims,
        in_specs=[vmem] * 3,
        out_specs=[vmem] * (1 + rims),
        scratch_shapes=[pltpu.VMEM((3, frames * rows * pairs, LANES), F32)],
        compiler_params=params,
        cost_estimate=pl.CostEstimate(flops=4 << 30, bytes_accessed=1 << 20, transcendentals=0),
        name="norm_and_cut",
    )(mask, block, gain_first.reshape(1, channels))
    earlier = shift(block, 0, 1)
    if swap:
        near = (shift(sent[0], 1, 0),) * 2
        far = (shift(sent[0], 1, 1),) * 2
        deep = rows + 1
    else:
        near = (shift(sent[0], 1, 0), shift(sent[1], -1, 0))
        far = (shift(sent[0], 1, 1), shift(sent[1], -1, 1))
        deep = rows + 2

    first_weight = weight_first.reshape(3, 3, 3 * channels, channels)
    second_weight = weight_second.reshape(3, 3, 3 * channels, channels)
    total = (2, frames + 2, deep, pairs, channels)
    first_total = pl.pallas_call(
        functools.partial(first_kernel, bands, deep),
        out_shape=jax.ShapeDtypeStruct(total, F32),
        in_specs=[smem] + [vmem] * 7,
        out_specs=vmem,
        scratch_shapes=[
            pltpu.VMEM((2 * frames, deep + 2, pairs, wide), BF16),
            pltpu.VMEM((3, frames * rows * pairs, LANES), F32),
        ],
        compiler_params=params,
        cost_estimate=pl.CostEstimate(flops=1 << 20, bytes_accessed=1 << 16, transcendentals=0),
        name="first_conv",
    )(counts, mask, normed, earlier, *near, gain_first.reshape(1, channels), first_weight)
    out = pl.pallas_call(
        functools.partial(second_kernel, bands, deep),
        out_shape=jax.ShapeDtypeStruct((frames, rows, flat), BF16),
        in_specs=[smem] + [vmem] * 9,
        out_specs=vmem,
        scratch_shapes=[
            pltpu.VMEM(total, F32),
            pltpu.VMEM((frames + 2, rows + 2, pairs, wide), BF16),
            pltpu.VMEM((3, frames * rows * pairs, LANES), F32),
        ],
        compiler_params=params,
        cost_estimate=pl.CostEstimate(flops=4 << 30, bytes_accessed=6 << 20, transcendentals=0),
        name="second_conv",
    )(
        counts, block, *far, first_total,
        bias_first.reshape(1, channels), first_weight,
        gain_second.reshape(1, channels), bias_second.reshape(1, channels), second_weight,
    )
    return out.reshape(1, frames, rows, flat)


def solution(mesh):
    spread = P(("groups", "clip"), "tm", "space", None)
    return jax.shard_map(
        shards,
        mesh=mesh,
        in_specs=(spread, P(("groups", "clip")), P(), P(), P(), P(), P(), P()),
        out_specs=spread,
        check_vma=False,
    )
```

time: 19.6 us -> 18.4 us (0.939)
  local copies, waits for them, and re-layouts: 0.95 us -> 0.04 us
  waiting for transfers between devices: 4.45 us -> 3.79 us
  Pallas kernels: 7.17 us -> 7.54 us
    pallas_call x1, Pallas kernels: 1.81 us -> 3.41 us  [shards(): pl.pallas_call(functools.partial(first_kernel, bands, deep), out_shape=ja...]
    pallas_call x1, Pallas kernels: 4.97 us -> 3.76 us  [shards(): pl.pallas_call(functools.partial(second_kernel, bands, deep), out_shape=j...]
    unnamed x14, local copies, waits for them, and re-layouts: 0.95 us -> 0.04 us
    ppermute x3, waiting for transfers between devices: 4.45 us -> 3.79 us  [shift(): return lax.ppermute(sent, ('tm', 'space'), pairs_of)]
  transfers between devices with their start and end apart: 3 -> 3, of which waited for: 2 -> 2; matrix products, arithmetic and copies ran while one was open for 0% -> 0% of each run, Pallas kernels for 9% -> 21%
where the time goes in v6:
time: 18.4 us; the launch traced here: 18.3 us
  Pallas kernels  7.54 us (41%)
  starting transfers between devices  6.13 us (33%)
  waiting for transfers between devices  3.79 us (21%)
  between operations  0.75 us (4%)
    ppermute x3, starting transfers between devices, shift(): return lax.ppermute(sent, ('tm', 'space'), pairs_of)  6.13 us
    ppermute x3, waiting for transfers between devices, shift(): return lax.ppermute(sent, ('tm', 'space'), pairs_of)  3.79 us
    pallas_call x1, Pallas kernels, shards(): pl.pallas_call(functools.partial(second_kernel, bands, deep), out_shape=j...  3.76 us
    pallas_call x1, Pallas kernels, shards(): pl.pallas_call(functools.partial(first_kernel, bands, deep), out_shape=ja...  3.41 us
    pallas_call x1, Pallas kernels, shards(): pl.pallas_call(functools.partial(norm_kernel, swap), out_shape=[jax.Shape...  0.37 us
  transfers between devices with their start and end apart: 3, of which 2 were waited for; matrix products, arithmetic and copies ran while one was open for 0% of the time, Pallas kernels for 21%

profile of v6, /device:TPU:0, one launch (start us, length us, event | category | flops | bytes accessed | tf_op | source)
XLA Modules:
  0.0 18.3 jit_solution(10472600870785694907)
XLA Ops:
  0.0 0.0 copy-start.1
  0.0 0.0 copy-start.3
  0.0 3.0 %collective-permute-start.1 = (bf16[4,4,6144]{2,1,0:T(4,128)(2,1)}, bf16[4,4,6144]{2,1,0:T(4,128)(2,1)S(1)}, u32[]{:S(2)}, u32[]{:S(2)}) collective-permute-start(bf16[4,4,6144]{2,1,0:T(4,128)(2,1)} %bitcast.13), channel_id=1, source_target_pairs={{0,4},{2,6},{4,8},{6,10},{8,12},{10,14},{12,0},{14,2},{1,5},{3,7},... | collective-permute-start | bytes 589832 | tf_op jit(solution)/shard_map/ppermute | solution.py:240
  3.0 0.0 copy-done.1
  3.0 0.0 copy-done.3
  3.0 0.0 copy-start
  3.1 0.4 %norm_and_cut.1 = (bf16[4,4,16,384]{3,2,1,0:T(8,128)(2,1)S(1)}, bf16[4,2,16,384]{3,2,1,0:T(8,128)(2,1)S(1)}) custom-call(f32[8,384]{1,0:T(8,128)S(1)} %lane_mask.1.mask, bf16[4,4,6144]{2,1,0:T(4,128)(2,1)S(1)} %bitcast.14, f32[1,192]{1,0:T(1,128)S(1)} %bitcast.10), custom_call_target="tpu_custom_call" | custom-call | flops 4294967296 | bytes 1048576 | tf_op jit(solution)/shard_map/norm_and_cut/pallas_call | solution.py:256
  3.4 0.0 copy-start.2
  3.4 0.0 copy-start.4
  3.5 0.0 copy-start.5
  3.5 0.0 copy-start.6
  3.5 1.6 %collective-permute-start.2 = (bf16[4,2,16,384]{3,2,1,0:T(8,128)(2,1)S(1)}, bf16[4,2,16,384]{3,2,1,0:T(8,128)(2,1)S(1)}, u32[]{:S(2)}, u32[]{:S(2)}) collective-permute-start(bf16[4,2,16,384]{3,2,1,0:T(8,128)(2,1)S(1)} %get-tuple-element.7), channel_id=1, source_target_pairs={{0,2},{2,0},{4,6},{6,4},{8,10},{10,8},{12,14},{14,12},{1,3},{3,1},... | collective-permute-start | bytes 294920 | tf_op jit(solution)/shard_map/ppermute | solution.py:240
  5.0 1.5 %collective-permute-start = (bf16[4,2,16,384]{3,2,1,0:T(8,128)(2,1)S(1)}, bf16[4,2,16,384]{3,2,1,0:T(8,128)(2,1)S(1)}, u32[]{:S(2)}, u32[]{:S(2)}) collective-permute-start(bf16[4,2,16,384]{3,2,1,0:T(8,128)(2,1)S(1)} %get-tuple-element.7), channel_id=1, source_target_pairs={{0,6},{2,4},{4,10},{6,8},{8,14},{10,12},{12,2},{14,0},{1,7},{3,5},... | collective-permute-start | bytes 294920 | tf_op jit(solution)/shard_map/ppermute | solution.py:240
  7.2 0.9 %collective-permute-done.2.before.after = bf16[4,2,16,384]{3,2,1,0:T(8,128)(2,1)S(1)} collective-permute-done((bf16[4,2,16,384]{3,2,1,0:T(8,128)(2,1)S(1)}, bf16[4,2,16,384]{3,2,1,0:T(8,128)(2,1)S(1)}, u32[]{:S(2)}, u32[]{:S(2)}) %collective-permute-start.2) | collective-permute-done | bytes 98336 | tf_op jit(solution)/shard_map/ppermute | solution.py:240
  8.2 2.9 %collective-permute-done.1.earlier = bf16[4,4,6144]{2,1,0:T(4,128)(2,1)S(1)} collective-permute-done((bf16[4,4,6144]{2,1,0:T(4,128)(2,1)}, bf16[4,4,6144]{2,1,0:T(4,128)(2,1)S(1)}, u32[]{:S(2)}, u32[]{:S(2)}) %collective-permute-start.1) | collective-permute-done | bytes 196640 | tf_op jit(solution)/shard_map/ppermute | solution.py:240
  11.0 0.0 copy-done
  11.0 3.4 %first_conv.1.first_total = f32[2,6,5,16,192]{4,3,2,1,0:T(8,128)S(1)} custom-call(s32[1]{0:T(128)S(6)} %copy.9.count, f32[8,384]{1,0:T(8,128)S(1)} %lane_mask.1.mask, bf16[4,4,16,384]{3,2,1,0:T(8,128)(2,1)S(1)} %get-tuple-element.8.normed, bf16[4,4,6144]{2,1,0:T(4,128)(2,1)S(1)} %collective-permute-done.1.earlier, ...), custom_call_target="tpu_custom_call" | custom-call | flops 1048576 | bytes 65536 | tf_op jit(solution)/shard_map/first_conv/pallas_call | solution.py:279
  14.4 0.0 collective-permute-done.before.after
  14.4 0.0 copy-done.2
  14.5 0.0 copy-done.4
  14.5 0.0 copy-done.5
  14.5 0.0 copy-done.6
  14.5 3.8 %second_conv.1 = bf16[4,4,6144]{2,1,0:T(4,128)(2,1)} custom-call(s32[1]{0:T(128)S(6)} %copy.9.count, bf16[4,4,6144]{2,1,0:T(4,128)(2,1)S(1)} %bitcast.15, bf16[4,2,16,384]{3,2,1,0:T(8,128)(2,1)S(1)} %collective-permute-done.before.after, bf16[4,2,16,384]{3,2,1,0:T(8,128)(2,1)S(1)} %collective-permute-done.before.after, ...), custom_call_target="tpu_custom_call" | custom-call | flops 4294967296 | bytes 6291456 | tf_op jit(solution)/shard_map/second_conv/pallas_call | solution.py:292
  (1 shorter events, 0.0 us)
Async XLA Ops:
  0.0 3.0 %copy-start.1 = (f32[192]{0:T(256)S(1)}, f32[192]{0:T(256)}, u32[]{:S(2)}) copy-start(f32[192]{0:T(256)} %param.10) | copy-start | bytes 2308
  0.0 3.0 %copy-start.3 = (bf16[1,4,4,6144]{3,2,1,0:T(4,128)(2,1)S(1)}, bf16[1,4,4,6144]{3,2,1,0:T(4,128)(2,1)}, u32[]{:S(2)}) copy-start(bf16[1,4,4,6144]{3,2,1,0:T(4,128)(2,1)} %param.8) | copy-start | bytes 589828
  0.0 11.0 %collective-permute-start.1 = (bf16[4,4,6144]{2,1,0:T(4,128)(2,1)}, bf16[4,4,6144]{2,1,0:T(4,128)(2,1)S(1)}, u32[]{:S(2)}, u32[]{:S(2)}) collective-permute-start(bf16[4,4,6144]{2,1,0:T(4,128)(2,1)} %bitcast.13), channel_id=1, source_target_pairs={{0,4},{2,6},{4,8},{6,10},{8,12},{10,14},{12,0},{14,2},{1,5},{3,7},... | collective-permute-start | bytes 589832 | tf_op jit(solution)/shard_map/ppermute | solution.py:240
  3.0 8.0 %copy-start = (bf16[3,3,3,192,192]{4,3,2,1,0:T(8,128)(2,1)S(1)}, bf16[3,3,3,192,192]{4,3,2,1,0:T(8,128)(2,1)}, u32[]{:S(2)}) copy-start(bf16[3,3,3,192,192]{4,3,2,1,0:T(8,128)(2,1)} %param.12) | copy-start | bytes 5971972
  3.4 11.0 %copy-start.2 = (bf16[3,3,3,192,192]{4,3,2,1,0:T(8,128)(2,1)S(1)}, bf16[3,3,3,192,192]{4,3,2,1,0:T(8,128)(2,1)}, u32[]{:S(2)}) copy-start(bf16[3,3,3,192,192]{4,3,2,1,0:T(8,128)(2,1)} %param.15) | copy-start | bytes 5971972
  3.4 11.0 %copy-start.4 = (f32[192]{0:T(256)S(1)}, f32[192]{0:T(256)}, u32[]{:S(2)}) copy-start(f32[192]{0:T(256)} %param.11) | copy-start | bytes 2308
  3.5 11.0 %copy-start.5 = (f32[192]{0:T(256)S(1)}, f32[192]{0:T(256)}, u32[]{:S(2)}) copy-start(f32[192]{0:T(256)} %param.13) | copy-start | bytes 2308
  3.5 11.0 %copy-start.6 = (f32[192]{0:T(256)S(1)}, f32[192]{0:T(256)}, u32[]{:S(2)}) copy-start(f32[192]{0:T(256)} %param.14) | copy-start | bytes 2308
  3.5 4.7 %collective-permute-start.2 = (bf16[4,2,16,384]{3,2,1,0:T(8,128)(2,1)S(1)}, bf16[4,2,16,384]{3,2,1,0:T(8,128)(2,1)S(1)}, u32[]{:S(2)}, u32[]{:S(2)}) collective-permute-start(bf16[4,2,16,384]{3,2,1,0:T(8,128)(2,1)S(1)} %get-tuple-element.7), channel_id=1, source_target_pairs={{0,2},{2,0},{4,6},{6,4},{8,10},{10,8},{12,14},{14,12},{1,3},{3,1},... | collective-permute-start | bytes 294920 | tf_op jit(solution)/shard_map/ppermute | solution.py:240
  5.0 9.4 %collective-permute-start = (bf16[4,2,16,384]{3,2,1,0:T(8,128)(2,1)S(1)}, bf16[4,2,16,384]{3,2,1,0:T(8,128)(2,1)S(1)}, u32[]{:S(2)}, u32[]{:S(2)}) collective-permute-start(bf16[4,2,16,384]{3,2,1,0:T(8,128)(2,1)S(1)} %get-tuple-element.7), channel_id=1, source_target_pairs={{0,6},{2,4},{4,10},{6,8},{8,14},{10,12},{12,2},{14,0},{1,7},{3,5},... | collective-permute-start | bytes 294920 | tf_op jit(solution)/shard_map/ppermute | solution.py:240

commit v7 on v6

--- a/solution.py
+++ b/solution.py
@@ -86,11 +86,14 @@
     return mine, moved
 
 
-def conv(window, weight, frames, rows, channels):
+def conv(window, weight, source, frames, rows, times, channels):
     pairs, wide = window.shape[2], window.shape[3]
-    taps = [(a, b) for a in range(3) for b in range(3)]
+    taps = [(a, b) for a in times for b in range(3)]
     parts = [
-        window[a : a + frames, b : b + rows].reshape(frames * rows * pairs, wide) for a, b in taps
+        window[
+            source + a - times[0] : source + a - times[0] + frames, b : b + rows
+        ].reshape(frames * rows * pairs, wide)
+        for a, b in taps
     ]
     return add_moved(*products(parts, [weight[a, b] for a, b in taps], channels), pairs)
 
@@ -103,48 +106,62 @@
     return mine[0] + left, mine[1] + right
 
 
-def first_kernel(
-    bands, deep, count, mask, normed, earlier, before, after, gain, weight, total, window, stage
-):
+def own_kernel(bands, deep, count, normed, before, after, weight, total, window):
     frames, rows, pairs, wide = normed.shape
     tm, space = lax.axis_index("tm"), lax.axis_index("space")
     nothing = jnp.zeros((pairs, wide), BF16)
     top = 1 + space if bands == 2 else 2
-
-    def valid(f):
-        at = (tm - 1) * frames + f
-        return (at >= 0) & (at < count[0])
+    window[0] = jnp.zeros(window.shape[1:], BF16)
+    for f in range(frames):
+        good = tm * frames + f < count[0]
+        if bands == 2:
+            window[f + 1, (rows + 2) * space] = nothing
+        for r in range(2):
+            if bands == 2:
+                at = (rows + 1) * (1 - space) + r
+                window[f + 1, at] = jnp.where(good, before[f, r], nothing)
+            else:
+                window[f + 1, r] = jnp.where(good & (space > 0), before[f, r], nothing)
+                below = jnp.where(good & (space < bands - 1), after[f, r], nothing)
+                window[f + 1, rows + 2 + r] = below
+        for r in range(rows):
+            window[f + 1, top + r] = jnp.where(good, normed[f, r], nothing)
+    late = conv(window, weight, 1, frames - 2, deep, (0, 1, 2), wide // 2)
+    soon = conv(window, weight, 0, 2, deep, (1, 2), wide // 2)
+    for q in range(2):
+        total[q, 0:2] = soon[q].reshape(2, *total.shape[2:])
+        total[q, 2:] = late[q].reshape(frames - 2, *total.shape[2:])
+
+
+def earlier_kernel(bands, deep, count, mask, earlier, gain, weight, total, window, stage):
+    frames, rows = earlier.shape[0], earlier.shape[1]
+    pairs, wide = window.shape[2], window.shape[3]
+    tm, space = lax.axis_index("tm"), lax.axis_index("space")
+    top = 1 + space if bands == 2 else 2
 
     def store(f, r, parts):
-        good = valid(f)
+        good = (tm - 1) * frames + f < count[0]
         for k in range(3):
             part = jnp.where(good, parts[k], jnp.zeros_like(parts[k]))
             window[f, top + r, :, k * LANES : (k + 1) * LANES] = part
 
-    for f in range(2 * frames):
-        good = valid(f)
-        near = f >= frames
-        if bands == 2:
-            window[f, (rows + 2) * space] = nothing
+    @pl.when(tm > 0)
+    def _():
+        nothing = jnp.zeros((pairs, wide), BF16)
+        window[frames] = jnp.zeros(window.shape[1:], BF16)
+        for f in range(frames):
+            if bands == 2:
+                window[f, (rows + 2) * space] = nothing
             for r in range(2):
-                rim = jnp.where(good, before[f - frames, r], nothing) if near else nothing
-                window[f, (rows + 1) * (1 - space) + r] = rim
-        else:
-            for r in range(2):
-                above = jnp.where(good & (space > 0), before[f - frames, r], nothing) if near else nothing
-                below = (
-                    jnp.where(good & (space < bands - 1), after[f - frames, r], nothing)
-                    if near else nothing
-                )
-                window[f, r] = above
-                window[f, rows + 2 + r] = below
-        if near:
-            for r in range(rows):
-                window[f, top + r] = jnp.where(good, normed[f - frames, r], nothing)
-    norm_block(earlier, twice(gain), mask[...] > 0.5, stage, store, pairs)
-    both = conv(window, weight, frames + 2, deep, wide // 2)
-    for q in range(2):
-        total[q] = both[q].reshape(total.shape[1:])
+                window[f, ((rows + 1) * (1 - space) if bands == 2 else 0) + r] = nothing
+                if bands != 2:
+                    window[f, rows + 2 + r] = nothing
+        norm_block(earlier, twice(gain), mask[...] > 0.5, stage, store, pairs)
+        soon = conv(window, weight, 0, frames - 2, deep, (0, 1, 2), wide // 2)
+        late = conv(window, weight, frames - 2, 2, deep, (0, 1), wide // 2)
+        for q in range(2):
+            total[q, 0 : frames - 2] = soon[q].reshape(frames - 2, *total.shape[2:])
+            total[q, frames - 2 :] = late[q].reshape(2, *total.shape[2:])
 
 
 def add_corner(total, corner, weight, side, keep, channels):
@@ -174,8 +191,8 @@
 
 
 def second_kernel(
-    bands, deep, count, own, before, after, first_total, bias, weight, gain_two, bias_two,
-    weight_two, out, total, hidden, final,
+    bands, deep, count, own, before, after, from_own, from_earlier, bias, weight, gain_two,
+    bias_two, weight_two, out, total, hidden, final,
 ):
     frames, rows, pairs, wide = before.shape[0], own.shape[1], before.shape[2], before.shape[3]
     channels = wide // 2
@@ -186,19 +203,29 @@
         at = (tm - 1) * frames + f
         return (at >= 0) & (at < count[0])
 
-    total[...] = first_total[...]
-    if bands == 2:
-        add_corner(total, before, weight, 1 - space, valid, channels)
-    else:
-        add_corner(total, before, weight, 0, lambda f: valid(f) & (space > 0), channels)
-        add_corner(total, after, weight, 1, lambda f: valid(f) & (space < bands - 1), channels)
+    total[:, frames:] = from_own[:, frames - 2 :]
+
+    @pl.when(tm == 0)
+    def _():
+        total[:, 2:frames] = from_own[:, : frames - 2]
+
+    @pl.when(tm > 0)
+    def _():
+        total[:, :2] = from_earlier[:, :2]
+        total[:, 2:frames] = from_own[:, : frames - 2] + from_earlier[:, 2:]
+        if bands == 2:
+            add_corner(total, before, weight, 1 - space, valid, channels)
+        else:
+            add_corner(total, before, weight, 0, lambda f: valid(f) & (space > 0), channels)
+            add_corner(total, after, weight, 1, lambda f: valid(f) & (space < bands - 1), channels)
 
     start = (1 - space) if bands == 2 else 0
     row = lax.broadcasted_iota(jnp.int32, (fill, 1), 0) // pairs + (space * rows - 1 + start)
     row_ok = (row >= 0) & (row < bands * rows)
     bias_wide, gain_wide = twice(bias), twice(gain_two)
     first_lanes = lax.broadcasted_iota(jnp.int32, (fill, wide), 1) < channels
-    for h in range(frames + 2):
+
+    def norm_hidden(h):
         good = row_ok & valid(frames + h - 2)
         t = jnp.concatenate([total[q, h].reshape(fill, channels) for q in range(2)], axis=1)
         t = jnp.where(good, t + bias_wide, 0.0).astype(BF16).astype(F32)
@@ -208,7 +235,19 @@
         for r in range(deep):
             hidden[h, start + r] = y[r * pairs : (r + 1) * pairs]
 
-    both = jnp.concatenate(conv(hidden, weight_two, frames, rows, channels), axis=1)
+    @pl.when(tm == 0)
+    def _():
+        hidden[0:2] = jnp.zeros((2, *hidden.shape[1:]), BF16)
+
+    @pl.when(tm > 0)
+    def _():
+        for h in range(2):
+            norm_hidden(h)
+
+    for h in range(2, frames + 2):
+        norm_hidden(h)
+
+    both = jnp.concatenate(conv(hidden, weight_two, 0, frames, rows, (0, 1, 2), channels), axis=1)
     both = both + twice(bias_two)
     for k in range(3):
         final[k] = both[:, k * LANES : (k + 1) * LANES]
@@ -275,35 +314,45 @@
 
     first_weight = weight_first.reshape(3, 3, 3 * channels, channels)
     second_weight = weight_second.reshape(3, 3, 3 * channels, channels)
-    total = (2, frames + 2, deep, pairs, channels)
-    first_total = pl.pallas_call(
-        functools.partial(first_kernel, bands, deep),
-        out_shape=jax.ShapeDtypeStruct(total, F32),
-        in_specs=[smem] + [vmem] * 7,
+    share = (2, frames, deep, pairs, channels)
+    window = pltpu.VMEM((frames + 1, deep + 2, pairs, wide), BF16)
+    stage = pltpu.VMEM((3, frames * rows * pairs, LANES), F32)
+    cost = pl.CostEstimate(flops=1 << 20, bytes_accessed=1 << 16, transcendentals=0)
+    from_own = pl.pallas_call(
+        functools.partial(own_kernel, bands, deep),
+        out_shape=jax.ShapeDtypeStruct(share, F32),
+        in_specs=[smem] + [vmem] * 4,
         out_specs=vmem,
-        scratch_shapes=[
-            pltpu.VMEM((2 * frames, deep + 2, pairs, wide), BF16),
-            pltpu.VMEM((3, frames * rows * pairs, LANES), F32),
-        ],
-        compiler_params=params,
-        cost_estimate=pl.CostEstimate(flops=1 << 20, bytes_accessed=1 << 16, transcendentals=0),
-        name="first_conv",
-    )(counts, mask, normed, earlier, *near, gain_first.reshape(1, channels), first_weight)
+        scratch_shapes=[window],
+        compiler_params=params,
+        cost_estimate=cost,
+        name="conv_one_own",
+    )(counts, normed, *near, first_weight)
+    from_earlier = pl.pallas_call(
+        functools.partial(earlier_kernel, bands, deep),
+        out_shape=jax.ShapeDtypeStruct(share, F32),
+        in_specs=[smem] + [vmem] * 4,
+        out_specs=vmem,
+        scratch_shapes=[window, stage],
+        compiler_params=params,
+        cost_estimate=cost,
+        name="conv_one_earlier",
+    )(counts, mask, earlier, gain_first.reshape(1, channels), first_weight)
     out = pl.pallas_call(
         functools.partial(second_kernel, bands, deep),
         out_shape=jax.ShapeDtypeStruct((frames, rows, flat), BF16),
-        in_specs=[smem] + [vmem] * 9,
+        in_specs=[smem] + [vmem] * 10,
         out_specs=vmem,
         scratch_shapes=[
-            pltpu.VMEM(total, F32),
+            pltpu.VMEM((2, frames + 2, deep, pairs, channels), F32),
             pltpu.VMEM((frames + 2, rows + 2, pairs, wide), BF16),
-            pltpu.VMEM((3, frames * rows * pairs, LANES), F32),
+            stage,
         ],
         compiler_params=params,
         cost_estimate=pl.CostEstimate(flops=4 << 30, bytes_accessed=6 << 20, transcendentals=0),
-        name="second_conv",
+        name="corner_and_conv_two",
     )(
-        counts, block, *far, first_total,
+        counts, block, *far, from_own, from_earlier,
         bias_first.reshape(1, channels), first_weight,
         gain_second.reshape(1, channels), bias_second.reshape(1, channels), second_weight,
     )

time: 18.4 us -> 16.4 us (0.89)
  Pallas kernels: 7.54 us -> 5.27 us
  waiting for transfers between devices: 3.79 us -> 4.13 us
    pallas_call x1 -> x2, Pallas kernels: 3.41 us -> 1.85 us  [the longest x1 1.85 us: shards(): pl.pallas_call(functools.partial(own_kernel, bands, deep), out_shape=jax....]
    pallas_call x1, Pallas kernels: 3.76 us -> 3.04 us  [shards(): pl.pallas_call(functools.partial(second_kernel, bands, deep), out_shape=j...]
    ppermute x3, waiting for transfers between devices: 3.79 us -> 4.13 us  [shift(): return lax.ppermute(sent, ('tm', 'space'), pairs_of)]
  transfers between devices with their start and end apart: 3 -> 3, of which waited for: 2 -> 3; matrix products, arithmetic and copies ran while one was open for 0% -> 0% of each run, Pallas kernels for 21% -> 14%
where the time goes in v7:
time: 16.4 us; the launch traced here: 16.3 us
  starting transfers between devices  6.13 us (37%)
  Pallas kernels  5.27 us (32%)
  waiting for transfers between devices  4.13 us (25%)
  between operations  0.73 us (4%)
    ppermute x3, starting transfers between devices, shift(): return lax.ppermute(sent, ('tm', 'space'), pairs_of)  6.13 us
    ppermute x3, waiting for transfers between devices, shift(): return lax.ppermute(sent, ('tm', 'space'), pairs_of)  4.13 us
    pallas_call x1, Pallas kernels, shards(): pl.pallas_call(functools.partial(second_kernel, bands, deep), out_shape=j...  3.04 us
    pallas_call x1, Pallas kernels, shards(): pl.pallas_call(functools.partial(own_kernel, bands, deep), out_shape=jax....  1.85 us
    pallas_call x1, Pallas kernels, shards(): pl.pallas_call(functools.partial(norm_kernel, swap), out_shape=[jax.Shape...  0.37 us
  transfers between devices with their start and end apart: 3, of which 3 were waited for; matrix products, arithmetic and copies ran while one was open for 0% of the time, Pallas kernels for 14%

profile of v7, /device:TPU:0, one launch (start us, length us, event | category | flops | bytes accessed | tf_op | source)
XLA Modules:
  0.0 16.3 jit_solution(1998406932526271459)
XLA Ops:
  0.0 0.0 copy-start.1
  0.0 0.0 copy-start.3
  0.0 3.0 %collective-permute-start.2 = (bf16[4,4,6144]{2,1,0:T(4,128)(2,1)}, bf16[4,4,6144]{2,1,0:T(4,128)(2,1)S(1)}, u32[]{:S(2)}, u32[]{:S(2)}) collective-permute-start(bf16[4,4,6144]{2,1,0:T(4,128)(2,1)} %bitcast.14), channel_id=1, source_target_pairs={{0,4},{2,6},{4,8},{6,10},{8,12},{10,14},{12,0},{14,2},{1,5},{3,7},... | collective-permute-start | bytes 589832 | tf_op jit(solution)/shard_map/ppermute | solution.py:279
  3.0 0.0 copy-done.1
  3.0 0.0 copy-done.3
  3.0 0.0 copy-start
  3.1 0.4 %norm_and_cut.1 = (bf16[4,4,16,384]{3,2,1,0:T(8,128)(2,1)S(1)}, bf16[4,2,16,384]{3,2,1,0:T(8,128)(2,1)S(1)}) custom-call(f32[8,384]{1,0:T(8,128)S(1)} %lane_mask.1.mask, bf16[4,4,6144]{2,1,0:T(4,128)(2,1)S(1)} %bitcast.15, f32[1,192]{1,0:T(1,128)S(1)} %bitcast.11), custom_call_target="tpu_custom_call" | custom-call | flops 4294967296 | bytes 1048576 | tf_op jit(solution)/shard_map/norm_and_cut/pallas_call | solution.py:295
  3.4 1.6 %collective-permute-start.1 = (bf16[4,2,16,384]{3,2,1,0:T(8,128)(2,1)S(1)}, bf16[4,2,16,384]{3,2,1,0:T(8,128)(2,1)S(1)}, u32[]{:S(2)}, u32[]{:S(2)}) collective-permute-start(bf16[4,2,16,384]{3,2,1,0:T(8,128)(2,1)S(1)} %get-tuple-element.7), channel_id=1, source_target_pairs={{0,2},{2,0},{4,6},{6,4},{8,10},{10,8},{12,14},{14,12},{1,3},{3,1},... | collective-permute-start | bytes 294920 | tf_op jit(solution)/shard_map/ppermute | solution.py:279
  5.0 1.5 %collective-permute-start = (bf16[4,2,16,384]{3,2,1,0:T(8,128)(2,1)S(1)}, bf16[4,2,16,384]{3,2,1,0:T(8,128)(2,1)S(1)}, u32[]{:S(2)}, u32[]{:S(2)}) collective-permute-start(bf16[4,2,16,384]{3,2,1,0:T(8,128)(2,1)S(1)} %get-tuple-element.7), channel_id=1, source_target_pairs={{0,6},{2,4},{4,10},{6,8},{8,14},{10,12},{12,2},{14,0},{1,7},{3,5},... | collective-permute-start | bytes 294920 | tf_op jit(solution)/shard_map/ppermute | solution.py:279
  7.2 0.9 %collective-permute-done.1.before.after = bf16[4,2,16,384]{3,2,1,0:T(8,128)(2,1)S(1)} collective-permute-done((bf16[4,2,16,384]{3,2,1,0:T(8,128)(2,1)S(1)}, bf16[4,2,16,384]{3,2,1,0:T(8,128)(2,1)S(1)}, u32[]{:S(2)}, u32[]{:S(2)}) %collective-permute-start.1) | collective-permute-done | bytes 98336 | tf_op jit(solution)/shard_map/ppermute | solution.py:279
  8.1 0.0 copy-done
  8.1 1.9 %conv_one_own.1.from_own = f32[2,4,5,16,192]{4,3,2,1,0:T(8,128)S(1)} custom-call(s32[1]{0:T(128)S(6)} %copy.9.count, bf16[4,4,16,384]{3,2,1,0:T(8,128)(2,1)S(1)} %get-tuple-element.8.normed, bf16[4,2,16,384]{3,2,1,0:T(8,128)(2,1)S(1)} %collective-permute-done.1.before.after, bf16[4,2,16,384]{3,2,1,0:T(8,128)(2,1)S(1)} %collective-permute-done.1.before.after, ...), custom_call_target="tpu_custom_call" | custom-call | flops 1048576 | bytes 65536 | tf_op jit(solution)/shard_map/conv_one_own/pallas_call | solution.py:321
  10.0 0.0 copy-start.2
  10.0 0.0 copy-start.4
  10.0 0.0 copy-start.5
  10.0 0.0 copy-start.6
  10.0 1.0 %collective-permute-done.2.earlier = bf16[4,4,6144]{2,1,0:T(4,128)(2,1)S(1)} collective-permute-done((bf16[4,4,6144]{2,1,0:T(4,128)(2,1)}, bf16[4,4,6144]{2,1,0:T(4,128)(2,1)S(1)}, u32[]{:S(2)}, u32[]{:S(2)}) %collective-permute-start.2) | collective-permute-done | bytes 196640 | tf_op jit(solution)/shard_map/ppermute | solution.py:279
  11.0 2.2 %collective-permute-done.before.after = bf16[4,2,16,384]{3,2,1,0:T(8,128)(2,1)S(1)} collective-permute-done((bf16[4,2,16,384]{3,2,1,0:T(8,128)(2,1)S(1)}, bf16[4,2,16,384]{3,2,1,0:T(8,128)(2,1)S(1)}, u32[]{:S(2)}, u32[]{:S(2)}) %collective-permute-start) | collective-permute-done | bytes 98336 | tf_op jit(solution)/shard_map/ppermute | solution.py:279
  13.2 0.0 copy-done.2
  13.2 0.0 copy-done.4
  13.2 0.0 copy-done.5
  13.2 0.0 copy-done.6
  13.2 3.0 %corner_and_conv_two.1 = bf16[4,4,6144]{2,1,0:T(4,128)(2,1)} custom-call(s32[1]{0:T(128)S(6)} %copy.9.count, bf16[4,4,6144]{2,1,0:T(4,128)(2,1)S(1)} %bitcast.16, bf16[4,2,16,384]{3,2,1,0:T(8,128)(2,1)S(1)} %collective-permute-done.before.after, bf16[4,2,16,384]{3,2,1,0:T(8,128)(2,1)S(1)} %collective-permute-done.before.after, ...), custom_call_target="tpu_custom_call" | custom-call | flops 4294967296 | bytes 6291456 | tf_op jit(solution)/shard_map/corner_and_conv_two/pallas_call | solution.py:341
  (2 shorter events, 0.0 us)
Async XLA Ops:
  0.0 3.0 %copy-start.1 = (f32[192]{0:T(256)S(1)}, f32[192]{0:T(256)}, u32[]{:S(2)}) copy-start(f32[192]{0:T(256)} %param.10) | copy-start | bytes 2308
  0.0 3.0 %copy-start.3 = (bf16[1,4,4,6144]{3,2,1,0:T(4,128)(2,1)S(1)}, bf16[1,4,4,6144]{3,2,1,0:T(4,128)(2,1)}, u32[]{:S(2)}) copy-start(bf16[1,4,4,6144]{3,2,1,0:T(4,128)(2,1)} %param.8) | copy-start | bytes 589828
  0.0 11.0 %collective-permute-start.2 = (bf16[4,4,6144]{2,1,0:T(4,128)(2,1)}, bf16[4,4,6144]{2,1,0:T(4,128)(2,1)S(1)}, u32[]{:S(2)}, u32[]{:S(2)}) collective-permute-start(bf16[4,4,6144]{2,1,0:T(4,128)(2,1)} %bitcast.14), channel_id=1, source_target_pairs={{0,4},{2,6},{4,8},{6,10},{8,12},{10,14},{12,0},{14,2},{1,5},{3,7},... | collective-permute-start | bytes 589832 | tf_op jit(solution)/shard_map/ppermute | solution.py:279
  3.0 5.1 %copy-start = (bf16[3,3,3,192,192]{4,3,2,1,0:T(8,128)(2,1)S(1)}, bf16[3,3,3,192,192]{4,3,2,1,0:T(8,128)(2,1)}, u32[]{:S(2)}) copy-start(bf16[3,3,3,192,192]{4,3,2,1,0:T(8,128)(2,1)} %param.12) | copy-start | bytes 5971972
  3.4 4.7 %collective-permute-start.1 = (bf16[4,2,16,384]{3,2,1,0:T(8,128)(2,1)S(1)}, bf16[4,2,16,384]{3,2,1,0:T(8,128)(2,1)S(1)}, u32[]{:S(2)}, u32[]{:S(2)}) collective-permute-start(bf16[4,2,16,384]{3,2,1,0:T(8,128)(2,1)S(1)} %get-tuple-element.7), channel_id=1, source_target_pairs={{0,2},{2,0},{4,6},{6,4},{8,10},{10,8},{12,14},{14,12},{1,3},{3,1},... | collective-permute-start | bytes 294920 | tf_op jit(solution)/shard_map/ppermute | solution.py:279
  5.0 8.2 %collective-permute-start = (bf16[4,2,16,384]{3,2,1,0:T(8,128)(2,1)S(1)}, bf16[4,2,16,384]{3,2,1,0:T(8,128)(2,1)S(1)}, u32[]{:S(2)}, u32[]{:S(2)}) collective-permute-start(bf16[4,2,16,384]{3,2,1,0:T(8,128)(2,1)S(1)} %get-tuple-element.7), channel_id=1, source_target_pairs={{0,6},{2,4},{4,10},{6,8},{8,14},{10,12},{12,2},{14,0},{1,7},{3,5},... | collective-permute-start | bytes 294920 | tf_op jit(solution)/shard_map/ppermute | solution.py:279
  10.0 3.3 %copy-start.2 = (bf16[3,3,3,192,192]{4,3,2,1,0:T(8,128)(2,1)S(1)}, bf16[3,3,3,192,192]{4,3,2,1,0:T(8,128)(2,1)}, u32[]{:S(2)}) copy-start(bf16[3,3,3,192,192]{4,3,2,1,0:T(8,128)(2,1)} %param.15) | copy-start | bytes 5971972
  10.0 3.2 %copy-start.4 = (f32[192]{0:T(256)S(1)}, f32[192]{0:T(256)}, u32[]{:S(2)}) copy-start(f32[192]{0:T(256)} %param.11) | copy-start | bytes 2308
  10.0 3.2 %copy-start.5 = (f32[192]{0:T(256)S(1)}, f32[192]{0:T(256)}, u32[]{:S(2)}) copy-start(f32[192]{0:T(256)} %param.13) | copy-start | bytes 2308
  10.0 3.2 %copy-start.6 = (f32[192]{0:T(256)S(1)}, f32[192]{0:T(256)}, u32[]{:S(2)}) copy-start(f32[192]{0:T(256)} %param.14) | copy-start | bytes 2308

commit v8 on v7

--- a/solution.py
+++ b/solution.py
@@ -106,24 +106,14 @@
     return mine[0] + left, mine[1] + right
 
 
-def own_kernel(bands, deep, count, normed, before, after, weight, total, window):
+def own_kernel(bands, deep, count, normed, weight, total, window):
     frames, rows, pairs, wide = normed.shape
     tm, space = lax.axis_index("tm"), lax.axis_index("space")
     nothing = jnp.zeros((pairs, wide), BF16)
-    top = 1 + space if bands == 2 else 2
+    top = clear_rims(window, bands, space, rows, range(1, frames + 1))
     window[0] = jnp.zeros(window.shape[1:], BF16)
     for f in range(frames):
         good = tm * frames + f < count[0]
-        if bands == 2:
-            window[f + 1, (rows + 2) * space] = nothing
-        for r in range(2):
-            if bands == 2:
-                at = (rows + 1) * (1 - space) + r
-                window[f + 1, at] = jnp.where(good, before[f, r], nothing)
-            else:
-                window[f + 1, r] = jnp.where(good & (space > 0), before[f, r], nothing)
-                below = jnp.where(good & (space < bands - 1), after[f, r], nothing)
-                window[f + 1, rows + 2 + r] = below
         for r in range(rows):
             window[f + 1, top + r] = jnp.where(good, normed[f, r], nothing)
     late = conv(window, weight, 1, frames - 2, deep, (0, 1, 2), wide // 2)
@@ -133,29 +123,38 @@
         total[q, 2:] = late[q].reshape(frames - 2, *total.shape[2:])
 
 
-def earlier_kernel(bands, deep, count, mask, earlier, gain, weight, total, window, stage):
+def clear_rims(window, bands, space, rows, at):
+    nothing = jnp.zeros(window.shape[2:], BF16)
+    for f in at:
+        if bands == 2:
+            window[f, (rows + 2) * space] = nothing
+            for r in range(2):
+                window[f, (rows + 1) * (1 - space) + r] = nothing
+        else:
+            for r in range(2):
+                window[f, r] = nothing
+                window[f, rows + 2 + r] = nothing
+    return 1 + space if bands == 2 else 2
+
+
+def earlier_kernel(
+    bands, deep, count, mask, earlier, gain, weight, after, total, window, stage
+):
     frames, rows = earlier.shape[0], earlier.shape[1]
     pairs, wide = window.shape[2], window.shape[3]
     tm, space = lax.axis_index("tm"), lax.axis_index("space")
-    top = 1 + space if bands == 2 else 2
-
-    def store(f, r, parts):
-        good = (tm - 1) * frames + f < count[0]
-        for k in range(3):
-            part = jnp.where(good, parts[k], jnp.zeros_like(parts[k]))
-            window[f, top + r, :, k * LANES : (k + 1) * LANES] = part
 
     @pl.when(tm > 0)
     def _():
-        nothing = jnp.zeros((pairs, wide), BF16)
+        top = clear_rims(window, bands, space, rows, range(frames))
         window[frames] = jnp.zeros(window.shape[1:], BF16)
-        for f in range(frames):
-            if bands == 2:
-                window[f, (rows + 2) * space] = nothing
-            for r in range(2):
-                window[f, ((rows + 1) * (1 - space) if bands == 2 else 0) + r] = nothing
-                if bands != 2:
-                    window[f, rows + 2 + r] = nothing
+
+        def store(f, r, parts):
+            good = (tm - 1) * frames + f < count[0]
+            for k in range(3):
+                part = jnp.where(good, parts[k], jnp.zeros_like(parts[k]))
+                window[f, top + r, :, k * LANES : (k + 1) * LANES] = part
+
         norm_block(earlier, twice(gain), mask[...] > 0.5, stage, store, pairs)
         soon = conv(window, weight, 0, frames - 2, deep, (0, 1, 2), wide // 2)
         late = conv(window, weight, frames - 2, 2, deep, (0, 1), wide // 2)
@@ -164,38 +163,36 @@
             total[q, frames - 2 :] = late[q].reshape(2, *total.shape[2:])
 
 
-def add_corner(total, corner, weight, side, keep, channels):
-    frames, pairs, wide = corner.shape[0], corner.shape[2], corner.shape[3]
+def add_rims(total, near, far, weight, side, keep, channels):
+    frames, pairs, wide = near.shape[0], near.shape[2], near.shape[3]
     deep = total.shape[2]
     low = (deep - 2) * side
     halo = (deep - 1) * side
     nothing = jnp.zeros((pairs, wide), BF16)
-    rows = [
-        [jnp.where(keep(f), corner[f, r], nothing) if f < frames else nothing for r in range(2)]
-        for f in range(frames + 2)
-    ]
-    inner = [
-        jnp.where(keep(f), corner[f, 1 - side], nothing) if f < frames else nothing
-        for f in range(frames + 2)
-    ]
+
+    def row(f, r):
+        ref, at = (far, f) if f < frames else (near, f - frames)
+        return jnp.where(keep(f), ref[at, r], nothing)
+
+    rows = [[row(f, r) for r in range(2)] for f in range(2 * frames)]
+    inner = [row(f, 1 - side) for f in range(2 * frames)]
+    span = frames + 2
     parts = [
-        jnp.concatenate([x for f in range(frames) for x in rows[f + a]], axis=0) for a in range(3)
+        jnp.concatenate([x for f in range(span) for x in rows[f + a]], axis=0) for a in range(3)
     ]
     added = add_moved(*products(parts, [weight[a, 2 * side] for a in range(3)], channels), pairs)
     for q in range(2):
-        total[q, 0:frames, pl.ds(low, 2)] += added[q].reshape(frames, 2, pairs, channels)
-    parts = [jnp.concatenate([inner[f + a] for f in range(frames)], axis=0) for a in range(3)]
+        total[q, :, pl.ds(low, 2)] += added[q].reshape(span, 2, pairs, channels)
+    parts = [jnp.concatenate([inner[f + a] for f in range(span)], axis=0) for a in range(3)]
     added = add_moved(*products(parts, [weight[a, 1] for a in range(3)], channels), pairs)
     for q in range(2):
-        total[q, 0:frames, halo] += added[q].reshape(frames, pairs, channels)
-
-
-def second_kernel(
-    bands, deep, count, own, before, after, from_own, from_earlier, bias, weight, gain_two,
-    bias_two, weight_two, out, total, hidden, final,
-):
-    frames, rows, pairs, wide = before.shape[0], own.shape[1], before.shape[2], before.shape[3]
+        total[q, :, halo] += added[q].reshape(span, pairs, channels)
+
+
+def finish(bands, count, own, near, far, bias, weight, gain_two, bias_two, weight_two, out, total, hidden, final):
+    frames, rows, pairs, wide = near[0].shape[0], own.shape[1], near[0].shape[2], near[0].shape[3]
     channels = wide // 2
+    deep = total.shape[2]
     tm, space = lax.axis_index("tm"), lax.axis_index("space")
     fill = deep * pairs
 
@@ -203,29 +200,20 @@
         at = (tm - 1) * frames + f
         return (at >= 0) & (at < count[0])
 
-    total[:, frames:] = from_own[:, frames - 2 :]
-
-    @pl.when(tm == 0)
-    def _():
-        total[:, 2:frames] = from_own[:, : frames - 2]
-
-    @pl.when(tm > 0)
-    def _():
-        total[:, :2] = from_earlier[:, :2]
-        total[:, 2:frames] = from_own[:, : frames - 2] + from_earlier[:, 2:]
-        if bands == 2:
-            add_corner(total, before, weight, 1 - space, valid, channels)
-        else:
-            add_corner(total, before, weight, 0, lambda f: valid(f) & (space > 0), channels)
-            add_corner(total, after, weight, 1, lambda f: valid(f) & (space < bands - 1), channels)
+    if bands == 2:
+        add_rims(total, near[0], far[0], weight, 1 - space, valid, channels)
+    else:
+        above = lambda f: valid(f) & (space > 0)
+        below = lambda f: valid(f) & (space < bands - 1)
+        add_rims(total, near[0], far[0], weight, 0, above, channels)
+        add_rims(total, near[1], far[1], weight, 1, below, channels)
 
     start = (1 - space) if bands == 2 else 0
     row = lax.broadcasted_iota(jnp.int32, (fill, 1), 0) // pairs + (space * rows - 1 + start)
     row_ok = (row >= 0) & (row < bands * rows)
     bias_wide, gain_wide = twice(bias), twice(gain_two)
     first_lanes = lax.broadcasted_iota(jnp.int32, (fill, wide), 1) < channels
-
-    def norm_hidden(h):
+    for h in range(frames + 2):
         good = row_ok & valid(frames + h - 2)
         t = jnp.concatenate([total[q, h].reshape(fill, channels) for q in range(2)], axis=1)
         t = jnp.where(good, t + bias_wide, 0.0).astype(BF16).astype(F32)
@@ -234,18 +222,6 @@
         hidden[h, rows + 1] = jnp.zeros((pairs, wide), BF16)
         for r in range(deep):
             hidden[h, start + r] = y[r * pairs : (r + 1) * pairs]
-
-    @pl.when(tm == 0)
-    def _():
-        hidden[0:2] = jnp.zeros((2, *hidden.shape[1:]), BF16)
-
-    @pl.when(tm > 0)
-    def _():
-        for h in range(2):
-            norm_hidden(h)
-
-    for h in range(2, frames + 2):
-        norm_hidden(h)
 
     both = jnp.concatenate(conv(hidden, weight_two, 0, frames, rows, (0, 1, 2), channels), axis=1)
     both = both + twice(bias_two)
@@ -262,6 +238,45 @@
                     out[f + n, :, lanes] = jnp.where(good[n], value, 0.0).astype(BF16)
 
 
+def first_block_kernel(
+    bands, count, own, above, below, from_own, bias, weight, gain_two, bias_two, weight_two,
+    out, total, hidden, final,
+):
+    frames = own.shape[0]
+
+    @pl.when(lax.axis_index("tm") == 0)
+    def _():
+        total[:, :2] = jnp.zeros((2, 2, *total.shape[2:]), F32)
+        total[:, 2:] = from_own[...]
+        near = (above, below)
+        finish(
+            bands, count, own, near, near, bias, weight, gain_two, bias_two, weight_two,
+            out, total, hidden, final,
+        )
+
+
+def last_kernel(
+    bands, count, own, above, below, far_above, far_below, from_own, from_earlier, first_out, bias,
+    weight, gain_two, bias_two, weight_two, out, total, hidden, final,
+):
+    frames = own.shape[0]
+    tm = lax.axis_index("tm")
+
+    @pl.when(tm == 0)
+    def _():
+        out[...] = first_out[...]
+
+    @pl.when(tm > 0)
+    def _():
+        total[:, :2] = from_earlier[:, :2]
+        total[:, 2:frames] = from_own[:, : frames - 2] + from_earlier[:, 2:]
+        total[:, frames:] = from_own[:, frames - 2 :]
+        finish(
+            bands, count, own, (above, below), (far_above, far_below), bias, weight, gain_two,
+            bias_two, weight_two, out, total, hidden, final,
+        )
+
+
 def shards(latents, counts, gain_first, bias_first, weight_first, gain_second, bias_second, weight_second):
     channels = gain_first.shape[0]
     frames, rows, flat = latents.shape[1:]
@@ -321,41 +336,53 @@
     from_own = pl.pallas_call(
         functools.partial(own_kernel, bands, deep),
         out_shape=jax.ShapeDtypeStruct(share, F32),
-        in_specs=[smem] + [vmem] * 4,
+        in_specs=[smem] + [vmem] * 2,
         out_specs=vmem,
         scratch_shapes=[window],
         compiler_params=params,
         cost_estimate=cost,
         name="conv_one_own",
-    )(counts, normed, *near, first_weight)
+    )(counts, normed, first_weight)
+    constants = (
+        bias_first.reshape(1, channels), first_weight,
+        gain_second.reshape(1, channels), bias_second.reshape(1, channels), second_weight,
+    )
+    result = jax.ShapeDtypeStruct((frames, rows, flat), BF16)
+    scratch = [
+        pltpu.VMEM((2, frames + 2, deep, pairs, channels), F32),
+        pltpu.VMEM((frames + 2, rows + 2, pairs, wide), BF16),
+        stage,
+    ]
+    first_out = pl.pallas_call(
+        functools.partial(first_block_kernel, bands),
+        out_shape=result,
+        in_specs=[smem] + [vmem] * 9,
+        out_specs=vmem,
+        scratch_shapes=scratch,
+        compiler_params=params,
+        cost_estimate=cost,
+        name="first_block",
+    )(counts, block, *near, from_own, *constants)
     from_earlier = pl.pallas_call(
         functools.partial(earlier_kernel, bands, deep),
         out_shape=jax.ShapeDtypeStruct(share, F32),
-        in_specs=[smem] + [vmem] * 4,
+        in_specs=[smem] + [vmem] * 5,
         out_specs=vmem,
         scratch_shapes=[window, stage],
         compiler_params=params,
         cost_estimate=cost,
         name="conv_one_earlier",
-    )(counts, mask, earlier, gain_first.reshape(1, channels), first_weight)
+    )(counts, mask, earlier, gain_first.reshape(1, channels), first_weight, first_out)
     out = pl.pallas_call(
-        functools.partial(second_kernel, bands, deep),
-        out_shape=jax.ShapeDtypeStruct((frames, rows, flat), BF16),
-        in_specs=[smem] + [vmem] * 10,
-        out_specs=vmem,
-        scratch_shapes=[
-            pltpu.VMEM((2, frames + 2, deep, pairs, channels), F32),
-            pltpu.VMEM((frames + 2, rows + 2, pairs, wide), BF16),
-            stage,
-        ],
+        functools.partial(last_kernel, bands),
+        out_shape=result,
+        in_specs=[smem] + [vmem] * 13,
+        out_specs=vmem,
+        scratch_shapes=scratch,
         compiler_params=params,
         cost_estimate=pl.CostEstimate(flops=4 << 30, bytes_accessed=6 << 20, transcendentals=0),
-        name="corner_and_conv_two",
-    )(
-        counts, block, *far, from_own, from_earlier,
-        bias_first.reshape(1, channels), first_weight,
-        gain_second.reshape(1, channels), bias_second.reshape(1, channels), second_weight,
-    )
+        name="last",
+    )(counts, block, *near, *far, from_own, from_earlier, first_out, *constants)
     return out.reshape(1, frames, rows, flat)
 
 

time: 16.4 us -> 14.2 us (0.87)
  the two profiles are of different devices: /device:TPU:0 before, /device:TPU:16 now
where the time goes in v8:
time: 14.2 us; the launch traced here: 14 us
  Pallas kernels  8.29 us (58%)
  starting transfers between devices  4 us (28%)
  waiting for transfers between devices  0.88 us (6%)
  between operations  0.79 us (6%)
    ppermute x3, starting transfers between devices, shift(): return lax.ppermute(sent, ('tm', 'space'), pairs_of)  4 us
    pallas_call x1, Pallas kernels, shards(): pl.pallas_call(functools.partial(last_kernel, bands), out_shape=result, i...  3.97 us
    pallas_call x1, Pallas kernels, shards(): pl.pallas_call(functools.partial(earlier_kernel, bands, deep), out_shape=...  2.11 us
    pallas_call x1, Pallas kernels, shards(): pl.pallas_call(functools.partial(own_kernel, bands, deep), out_shape=jax....  1.82 us
    ppermute x3, waiting for transfers between devices, shift(): return lax.ppermute(sent, ('tm', 'space'), pairs_of)  0.88 us
    pallas_call x1, Pallas kernels, shards(): pl.pallas_call(functools.partial(norm_kernel, swap), out_shape=[jax.Shape...  0.37 us
  transfers between devices with their start and end apart: 3, of which 1 were waited for; matrix products, arithmetic and copies ran while one was open for 0% of the time, Pallas kernels for 31%

profile of v8, /device:TPU:16, one launch (start us, length us, event | category | flops | bytes accessed | tf_op | source)
XLA Modules:
  0.0 14.0 jit_solution(10078818695898296074)
XLA Ops:
  0.0 0.0 copy-start.2
  0.0 0.0 copy-start.3
  0.0 1.6 %collective-permute-start.2 = (bf16[4,4,6144]{2,1,0:T(4,128)(2,1)}, bf16[4,4,6144]{2,1,0:T(4,128)(2,1)S(1)}, u32[]{:S(2)}, u32[]{:S(2)}) collective-permute-start(bf16[4,4,6144]{2,1,0:T(4,128)(2,1)} %bitcast.14), channel_id=1, source_target_pairs={{0,4},{2,6},{4,8},{6,10},{8,12},{10,14},{12,0},{14,2},{1,5},{3,7},... | collective-permute-start | bytes 589832 | tf_op jit(solution)/shard_map/ppermute | solution.py:294
  1.6 0.0 copy-done.2
  1.6 0.0 copy-done.3
  1.6 0.0 copy-start
  1.6 0.4 %norm_and_cut.1 = (bf16[4,4,16,384]{3,2,1,0:T(8,128)(2,1)S(1)}, bf16[4,2,16,384]{3,2,1,0:T(8,128)(2,1)S(1)}) custom-call(f32[8,384]{1,0:T(8,128)S(1)} %lane_mask.1.mask, bf16[4,4,6144]{2,1,0:T(4,128)(2,1)S(1)} %bitcast.15, f32[1,192]{1,0:T(1,128)S(1)} %bitcast.18), custom_call_target="tpu_custom_call" | custom-call | flops 4294967296 | bytes 1048576 | tf_op jit(solution)/shard_map/norm_and_cut/pallas_call | solution.py:310
  2.0 0.0 copy-start.1
  2.0 0.0 copy-start.4
  2.0 0.0 copy-start.5
  2.0 0.0 copy-start.6
  2.0 1.6 %collective-permute-start = (bf16[4,2,16,384]{3,2,1,0:T(8,128)(2,1)S(1)}, bf16[4,2,16,384]{3,2,1,0:T(8,128)(2,1)S(1)}, u32[]{:S(2)}, u32[]{:S(2)}) collective-permute-start(bf16[4,2,16,384]{3,2,1,0:T(8,128)(2,1)S(1)} %get-tuple-element.7), channel_id=1, source_target_pairs={{0,2},{2,0},{4,6},{6,4},{8,10},{10,8},{12,14},{14,12},{1,3},{3,1},... | collective-permute-start | bytes 294920 | tf_op jit(solution)/shard_map/ppermute | solution.py:294
  3.6 0.9 %collective-permute-start.1 = (bf16[4,2,16,384]{3,2,1,0:T(8,128)(2,1)S(1)}, bf16[4,2,16,384]{3,2,1,0:T(8,128)(2,1)S(1)}, u32[]{:S(2)}, u32[]{:S(2)}) collective-permute-start(bf16[4,2,16,384]{3,2,1,0:T(8,128)(2,1)S(1)} %get-tuple-element.7), channel_id=1, source_target_pairs={{0,6},{2,4},{4,10},{6,8},{8,14},{10,12},{12,2},{14,0},{1,7},{3,5},... | collective-permute-start | bytes 294920 | tf_op jit(solution)/shard_map/ppermute | solution.py:294
  5.1 0.0 copy-done
  5.1 1.8 %conv_one_own.1.from_own = f32[2,4,5,16,192]{4,3,2,1,0:T(8,128)S(1)} custom-call(s32[1]{0:T(128)S(6)} %copy.9.count, bf16[4,4,16,384]{3,2,1,0:T(8,128)(2,1)S(1)} %get-tuple-element.8.normed, bf16[3,3,576,192]{3,2,1,0:T(8,128)(2,1)S(1)} %bitcast.8), custom_call_target="tpu_custom_call" | custom-call | flops 1048576 | bytes 65536 | tf_op jit(solution)/shard_map/conv_one_own/pallas_call | solution.py:336
  7.0 0.0 collective-permute-done.above.below
  7.0 0.0 copy-done.1
  7.0 0.0 copy-done.4
  7.0 0.0 copy-done.5
  7.0 0.0 copy-done.6
  7.0 0.9 %collective-permute-done.2.earlier = bf16[4,4,6144]{2,1,0:T(4,128)(2,1)S(1)} collective-permute-done((bf16[4,4,6144]{2,1,0:T(4,128)(2,1)}, bf16[4,4,6144]{2,1,0:T(4,128)(2,1)S(1)}, u32[]{:S(2)}, u32[]{:S(2)}) %collective-permute-start.2) | collective-permute-done | bytes 196640 | tf_op jit(solution)/shard_map/ppermute | solution.py:294
  7.9 2.1 %conv_one_earlier.1.from_earlier = f32[2,4,5,16,192]{4,3,2,1,0:T(8,128)S(1)} custom-call(s32[1]{0:T(128)S(6)} %copy.9.count, f32[8,384]{1,0:T(8,128)S(1)} %lane_mask.1.mask, bf16[4,4,6144]{2,1,0:T(4,128)(2,1)S(1)} %collective-permute-done.2.earlier, f32[1,192]{1,0:T(1,128)S(1)} %bitcast.19, bf16[3,3,576,192]{3,2,1,0:T(8,128)(2,1)S(1)} %bitcast.10, ...), custom_call_target="tpu_custom_call" | custom-call | flops 1048576 | bytes 65536 | tf_op jit(solution)/shard_map/conv_one_earlier/pallas_call | solution.py:366
  10.0 0.0 collective-permute-done.1.far_above.far_below
  10.0 4.0 %last.1 = bf16[4,4,6144]{2,1,0:T(4,128)(2,1)} custom-call(s32[1]{0:T(128)S(6)} %copy.9.count, bf16[4,4,6144]{2,1,0:T(4,128)(2,1)S(1)} %bitcast.17, bf16[4,2,16,384]{3,2,1,0:T(8,128)(2,1)S(1)} %collective-permute-done.above.below, bf16[4,2,16,384]{3,2,1,0:T(8,128)(2,1)S(1)} %collective-permute-done.above.below, ...), custom_call_target="tpu_custom_call" | custom-call | flops 4294967296 | bytes 6291456 | tf_op jit(solution)/shard_map/last/pallas_call | solution.py:376
  (2 shorter events, 0.0 us)
Async XLA Ops:
  0.0 1.6 %copy-start.2 = (bf16[1,4,4,6144]{3,2,1,0:T(4,128)(2,1)S(1)}, bf16[1,4,4,6144]{3,2,1,0:T(4,128)(2,1)}, u32[]{:S(2)}) copy-start(bf16[1,4,4,6144]{3,2,1,0:T(4,128)(2,1)} %param.8) | copy-start | bytes 589828
  0.0 1.6 %copy-start.3 = (f32[192]{0:T(256)S(1)}, f32[192]{0:T(256)}, u32[]{:S(2)}) copy-start(f32[192]{0:T(256)} %param.10) | copy-start | bytes 2308
  0.0 7.9 %collective-permute-start.2 = (bf16[4,4,6144]{2,1,0:T(4,128)(2,1)}, bf16[4,4,6144]{2,1,0:T(4,128)(2,1)S(1)}, u32[]{:S(2)}, u32[]{:S(2)}) collective-permute-start(bf16[4,4,6144]{2,1,0:T(4,128)(2,1)} %bitcast.14), channel_id=1, source_target_pairs={{0,4},{2,6},{4,8},{6,10},{8,12},{10,14},{12,0},{14,2},{1,5},{3,7},... | collective-permute-start | bytes 589832 | tf_op jit(solution)/shard_map/ppermute | solution.py:294
  1.6 3.5 %copy-start = (bf16[3,3,3,192,192]{4,3,2,1,0:T(8,128)(2,1)S(1)}, bf16[3,3,3,192,192]{4,3,2,1,0:T(8,128)(2,1)}, u32[]{:S(2)}) copy-start(bf16[3,3,3,192,192]{4,3,2,1,0:T(8,128)(2,1)} %param.12) | copy-start | bytes 5971972
  2.0 5.0 %copy-start.1 = (bf16[3,3,3,192,192]{4,3,2,1,0:T(8,128)(2,1)S(1)}, bf16[3,3,3,192,192]{4,3,2,1,0:T(8,128)(2,1)}, u32[]{:S(2)}) copy-start(bf16[3,3,3,192,192]{4,3,2,1,0:T(8,128)(2,1)} %param.15) | copy-start | bytes 5971972
  2.0 5.0 %copy-start.4 = (f32[192]{0:T(256)S(1)}, f32[192]{0:T(256)}, u32[]{:S(2)}) copy-start(f32[192]{0:T(256)} %param.11) | copy-start | bytes 2308
  2.0 5.0 %copy-start.5 = (f32[192]{0:T(256)S(1)}, f32[192]{0:T(256)}, u32[]{:S(2)}) copy-start(f32[192]{0:T(256)} %param.13) | copy-start | bytes 2308
  2.0 5.0 %copy-start.6 = (f32[192]{0:T(256)S(1)}, f32[192]{0:T(256)}, u32[]{:S(2)}) copy-start(f32[192]{0:T(256)} %param.14) | copy-start | bytes 2308
  2.0 4.9 %collective-permute-start = (bf16[4,2,16,384]{3,2,1,0:T(8,128)(2,1)S(1)}, bf16[4,2,16,384]{3,2,1,0:T(8,128)(2,1)S(1)}, u32[]{:S(2)}, u32[]{:S(2)}) collective-permute-start(bf16[4,2,16,384]{3,2,1,0:T(8,128)(2,1)S(1)} %get-tuple-element.7), channel_id=1, source_target_pairs={{0,2},{2,0},{4,6},{6,4},{8,10},{10,8},{12,14},{14,12},{1,3},{3,1},... | collective-permute-start | bytes 294920 | tf_op jit(solution)/shard_map/ppermute | solution.py:294
  3.6 6.4 %collective-permute-start.1 = (bf16[4,2,16,384]{3,2,1,0:T(8,128)(2,1)S(1)}, bf16[4,2,16,384]{3,2,1,0:T(8,128)(2,1)S(1)}, u32[]{:S(2)}, u32[]{:S(2)}) collective-permute-start(bf16[4,2,16,384]{3,2,1,0:T(8,128)(2,1)S(1)} %get-tuple-element.7), channel_id=1, source_target_pairs={{0,6},{2,4},{4,10},{6,8},{8,14},{10,12},{12,2},{14,0},{1,7},{3,5},... | collective-permute-start | bytes 294920 | tf_op jit(solution)/shard_map/ppermute | solution.py:294

commit v9 on v8

--- a/solution.py
+++ b/solution.py
@@ -87,14 +87,15 @@
 
 
 def conv(window, weight, source, frames, rows, times, channels):
-    pairs, wide = window.shape[2], window.shape[3]
+    pairs, wide = window[0].shape[1:]
     taps = [(a, b) for a in times for b in range(3)]
-    parts = [
-        window[
-            source + a - times[0] : source + a - times[0] + frames, b : b + rows
-        ].reshape(frames * rows * pairs, wide)
-        for a, b in taps
-    ]
+
+    def patch(a, b):
+        at = source + a - times[0]
+        rows_of = [window[f][b : b + rows].reshape(rows * pairs, wide) for f in range(at, at + frames)]
+        return jnp.concatenate(rows_of, axis=0)
+
+    parts = [patch(a, b) for a, b in taps]
     return add_moved(*products(parts, [weight[a, b] for a, b in taps], channels), pairs)
 
 
@@ -116,8 +117,8 @@
         good = tm * frames + f < count[0]
         for r in range(rows):
             window[f + 1, top + r] = jnp.where(good, normed[f, r], nothing)
-    late = conv(window, weight, 1, frames - 2, deep, (0, 1, 2), wide // 2)
-    soon = conv(window, weight, 0, 2, deep, (1, 2), wide // 2)
+    late = conv([window.at[f] for f in range(frames + 1)], weight, 1, frames - 2, deep, (0, 1, 2), wide // 2)
+    soon = conv([window.at[f] for f in range(frames + 1)], weight, 0, 2, deep, (1, 2), wide // 2)
     for q in range(2):
         total[q, 0:2] = soon[q].reshape(2, *total.shape[2:])
         total[q, 2:] = late[q].reshape(frames - 2, *total.shape[2:])
@@ -156,8 +157,8 @@
                 window[f, top + r, :, k * LANES : (k + 1) * LANES] = part
 
         norm_block(earlier, twice(gain), mask[...] > 0.5, stage, store, pairs)
-        soon = conv(window, weight, 0, frames - 2, deep, (0, 1, 2), wide // 2)
-        late = conv(window, weight, frames - 2, 2, deep, (0, 1), wide // 2)
+        soon = conv([window.at[f] for f in range(frames + 1)], weight, 0, frames - 2, deep, (0, 1, 2), wide // 2)
+        late = conv([window.at[f] for f in range(frames + 1)], weight, frames - 2, 2, deep, (0, 1), wide // 2)
         for q in range(2):
             total[q, 0 : frames - 2] = soon[q].reshape(frames - 2, *total.shape[2:])
             total[q, frames - 2 :] = late[q].reshape(2, *total.shape[2:])
@@ -213,36 +214,51 @@
     row_ok = (row >= 0) & (row < bands * rows)
     bias_wide, gain_wide = twice(bias), twice(gain_two)
     first_lanes = lax.broadcasted_iota(jnp.int32, (fill, wide), 1) < channels
-    for h in range(frames + 2):
+
+    def norm_hidden(h):
         good = row_ok & valid(frames + h - 2)
         t = jnp.concatenate([total[q, h].reshape(fill, channels) for q in range(2)], axis=1)
         t = jnp.where(good, t + bias_wide, 0.0).astype(BF16).astype(F32)
         y = norm_silu_pair(t, gain_wide, first_lanes, channels).astype(BF16)
-        hidden[h, 0] = jnp.zeros((pairs, wide), BF16)
-        hidden[h, rows + 1] = jnp.zeros((pairs, wide), BF16)
+        hidden[h][0] = jnp.zeros((pairs, wide), BF16)
+        hidden[h][rows + 1] = jnp.zeros((pairs, wide), BF16)
         for r in range(deep):
-            hidden[h, start + r] = y[r * pairs : (r + 1) * pairs]
-
-    both = jnp.concatenate(conv(hidden, weight_two, 0, frames, rows, (0, 1, 2), channels), axis=1)
-    both = both + twice(bias_two)
-    for k in range(3):
-        final[k] = both[:, k * LANES : (k + 1) * LANES]
-    for f in range(0, frames, 2):
+            hidden[h][start + r] = y[r * pairs : (r + 1) * pairs]
+
+    def second_conv(f):
+        both = conv(hidden, weight_two, f, 2, rows, (0, 1, 2), channels)
+        both = jnp.concatenate(both, axis=1) + bias_two_wide
+        for k in range(3):
+            final[f // 2][k] = both[:, k * LANES : (k + 1) * LANES]
+
+    def emit(f):
         good = [valid(frames + f + n) for n in range(2)]
         for p in range(pairs):
             for k in range(3):
-                block = final[k, pl.ds(f * rows * pairs + p, 2 * rows, stride=pairs), :]
+                block = final[f // 2][k, pl.ds(p, 2 * rows, stride=pairs), :]
                 lanes = pl.ds(p * wide + k * LANES, LANES)
                 for n in range(2):
                     value = own[f + n, :, lanes].astype(F32) + block[n * rows : (n + 1) * rows]
                     out[f + n, :, lanes] = jnp.where(good[n], value, 0.0).astype(BF16)
 
+    bias_two_wide = twice(bias_two)
+    for h in range(4):
+        norm_hidden(h)
+    second_conv(0)
+    for f in range(2, frames, 2):
+        norm_hidden(f + 2)
+        norm_hidden(f + 3)
+        emit(f - 2)
+        second_conv(f)
+    emit(frames - 2)
+
 
 def first_block_kernel(
     bands, count, own, above, below, from_own, bias, weight, gain_two, bias_two, weight_two,
-    out, total, hidden, final,
+    out, total, *scratch,
 ):
     frames = own.shape[0]
+    hidden, final = scratch[: frames + 2], scratch[frames + 2 :]
 
     @pl.when(lax.axis_index("tm") == 0)
     def _():
@@ -257,9 +273,10 @@
 
 def last_kernel(
     bands, count, own, above, below, far_above, far_below, from_own, from_earlier, first_out, bias,
-    weight, gain_two, bias_two, weight_two, out, total, hidden, final,
+    weight, gain_two, bias_two, weight_two, out, total, *scratch,
 ):
     frames = own.shape[0]
+    hidden, final = scratch[: frames + 2], scratch[frames + 2 :]
     tm = lax.axis_index("tm")
 
     @pl.when(tm == 0)
@@ -287,7 +304,7 @@
 
     def shift(sent, step, along):
         pairs_of = [
-            (t * bands + s, (t + along) % blocks * bands + (s + step) % bands)
+            (t * bands + s, (t + along) % blocks * bands + (s + step * (t + along < blocks)) % bands)
             for t in range(blocks)
             for s in range(bands)
         ]
@@ -350,8 +367,8 @@
     result = jax.ShapeDtypeStruct((frames, rows, flat), BF16)
     scratch = [
         pltpu.VMEM((2, frames + 2, deep, pairs, channels), F32),
-        pltpu.VMEM((frames + 2, rows + 2, pairs, wide), BF16),
-        stage,
+        *[pltpu.VMEM((rows + 2, pairs, wide), BF16)] * (frames + 2),
+        *[pltpu.VMEM((3, 2 * rows * pairs, LANES), F32)] * (frames // 2),
     ]
     first_out = pl.pallas_call(
         functools.partial(first_block_kernel, bands),

time: 14.2 us -> 14.2 us (level)
  no operation moved by 1% of the time
where the time goes in v9:
time: 14.2 us; the launch traced here: 14.1 us
  Pallas kernels  8.36 us (59%)
  starting transfers between devices  4 us (28%)
  waiting for transfers between devices  0.89 us (6%)
  between operations  0.79 us (6%)
    pallas_call x1, Pallas kernels, shards(): pl.pallas_call(functools.partial(last_kernel, bands), out_shape=result, i...  4.03 us
    ppermute x3, starting transfers between devices, shift(): return lax.ppermute(sent, ('tm', 'space'), pairs_of)  4 us
    pallas_call x1, Pallas kernels, shards(): pl.pallas_call(functools.partial(earlier_kernel, bands, deep), out_shape=...  2.12 us
    pallas_call x1, Pallas kernels, shards(): pl.pallas_call(functools.partial(own_kernel, bands, deep), out_shape=jax....  1.82 us
    ppermute x3, waiting for transfers between devices, shift(): return lax.ppermute(sent, ('tm', 'space'), pairs_of)  0.89 us
    pallas_call x1, Pallas kernels, shards(): pl.pallas_call(functools.partial(norm_kernel, swap), out_shape=[jax.Shape...  0.37 us
  transfers between devices with their start and end apart: 3, of which 1 were waited for; matrix products, arithmetic and copies ran while one was open for 0% of the time, Pallas kernels for 31%

profile of v9, /device:TPU:16, one launch (start us, length us, event | category | flops | bytes accessed | tf_op | source)
XLA Modules:
  0.0 14.1 jit_solution(4968126700543377850)
XLA Ops:
  0.0 0.0 copy-start.2
  0.0 0.0 copy-start.3
  0.0 1.6 %collective-permute-start.2 = (bf16[4,4,6144]{2,1,0:T(4,128)(2,1)}, bf16[4,4,6144]{2,1,0:T(4,128)(2,1)S(1)}, u32[]{:S(2)}, u32[]{:S(2)}) collective-permute-start(bf16[4,4,6144]{2,1,0:T(4,128)(2,1)} %bitcast.14), channel_id=1, source_target_pairs={{0,4},{2,6},{4,8},{6,10},{8,12},{10,14},{12,0},{14,2},{1,5},{3,7},... | collective-permute-start | bytes 589832 | tf_op jit(solution)/shard_map/ppermute | solution.py:311
  1.6 0.0 copy-done.2
  1.6 0.0 copy-done.3
  1.6 0.0 copy-start
  1.6 0.4 %norm_and_cut.1 = (bf16[4,4,16,384]{3,2,1,0:T(8,128)(2,1)S(1)}, bf16[4,2,16,384]{3,2,1,0:T(8,128)(2,1)S(1)}) custom-call(f32[8,384]{1,0:T(8,128)S(1)} %lane_mask.1.mask, bf16[4,4,6144]{2,1,0:T(4,128)(2,1)S(1)} %bitcast.15, f32[1,192]{1,0:T(1,128)S(1)} %bitcast.18), custom_call_target="tpu_custom_call" | custom-call | flops 4294967296 | bytes 1048576 | tf_op jit(solution)/shard_map/norm_and_cut/pallas_call | solution.py:327
  2.0 0.0 copy-start.1
  2.0 0.0 copy-start.4
  2.0 0.0 copy-start.5
  2.0 0.0 copy-start.6
  2.0 1.6 %collective-permute-start = (bf16[4,2,16,384]{3,2,1,0:T(8,128)(2,1)S(1)}, bf16[4,2,16,384]{3,2,1,0:T(8,128)(2,1)S(1)}, u32[]{:S(2)}, u32[]{:S(2)}) collective-permute-start(bf16[4,2,16,384]{3,2,1,0:T(8,128)(2,1)S(1)} %get-tuple-element.7), channel_id=1, source_target_pairs={{0,2},{2,0},{4,6},{6,4},{8,10},{10,8},{12,14},{14,12},{1,3},{3,1},... | collective-permute-start | bytes 294920 | tf_op jit(solution)/shard_map/ppermute | solution.py:311
  3.6 0.9 %collective-permute-start.1 = (bf16[4,2,16,384]{3,2,1,0:T(8,128)(2,1)S(1)}, bf16[4,2,16,384]{3,2,1,0:T(8,128)(2,1)S(1)}, u32[]{:S(2)}, u32[]{:S(2)}) collective-permute-start(bf16[4,2,16,384]{3,2,1,0:T(8,128)(2,1)S(1)} %get-tuple-element.7), channel_id=1, source_target_pairs={{0,6},{2,4},{4,10},{6,8},{8,14},{10,12},{12,0},{14,2},{1,7},{3,5},... | collective-permute-start | bytes 294920 | tf_op jit(solution)/shard_map/ppermute | solution.py:311
  5.1 0.0 copy-done
  5.1 1.8 %conv_one_own.1.from_own = f32[2,4,5,16,192]{4,3,2,1,0:T(8,128)S(1)} custom-call(s32[1]{0:T(128)S(6)} %copy.9.count, bf16[4,4,16,384]{3,2,1,0:T(8,128)(2,1)S(1)} %get-tuple-element.8.normed, bf16[3,3,576,192]{3,2,1,0:T(8,128)(2,1)S(1)} %bitcast.8), custom_call_target="tpu_custom_call" | custom-call | flops 1048576 | bytes 65536 | tf_op jit(solution)/shard_map/conv_one_own/pallas_call | solution.py:353
  7.0 0.0 collective-permute-done.above.below
  7.0 0.0 copy-done.1
  7.0 0.0 copy-done.4
  7.0 0.0 copy-done.5
  7.0 0.0 copy-done.6
  7.0 0.9 %collective-permute-done.2.earlier = bf16[4,4,6144]{2,1,0:T(4,128)(2,1)S(1)} collective-permute-done((bf16[4,4,6144]{2,1,0:T(4,128)(2,1)}, bf16[4,4,6144]{2,1,0:T(4,128)(2,1)S(1)}, u32[]{:S(2)}, u32[]{:S(2)}) %collective-permute-start.2) | collective-permute-done | bytes 196640 | tf_op jit(solution)/shard_map/ppermute | solution.py:311
  7.9 2.1 %conv_one_earlier.1.from_earlier = f32[2,4,5,16,192]{4,3,2,1,0:T(8,128)S(1)} custom-call(s32[1]{0:T(128)S(6)} %copy.9.count, f32[8,384]{1,0:T(8,128)S(1)} %lane_mask.1.mask, bf16[4,4,6144]{2,1,0:T(4,128)(2,1)S(1)} %collective-permute-done.2.earlier, f32[1,192]{1,0:T(1,128)S(1)} %bitcast.19, bf16[3,3,576,192]{3,2,1,0:T(8,128)(2,1)S(1)} %bitcast.10, ...), custom_call_target="tpu_custom_call" | custom-call | flops 1048576 | bytes 65536 | tf_op jit(solution)/shard_map/conv_one_earlier/pallas_call | solution.py:383
  10.0 0.0 collective-permute-done.1.far_above.far_below
  10.0 4.0 %last.1 = bf16[4,4,6144]{2,1,0:T(4,128)(2,1)} custom-call(s32[1]{0:T(128)S(6)} %copy.9.count, bf16[4,4,6144]{2,1,0:T(4,128)(2,1)S(1)} %bitcast.17, bf16[4,2,16,384]{3,2,1,0:T(8,128)(2,1)S(1)} %collective-permute-done.above.below, bf16[4,2,16,384]{3,2,1,0:T(8,128)(2,1)S(1)} %collective-permute-done.above.below, ...), custom_call_target="tpu_custom_call" | custom-call | flops 4294967296 | bytes 6291456 | tf_op jit(solution)/shard_map/last/pallas_call | solution.py:393
  (2 shorter events, 0.0 us)
Async XLA Ops:
  0.0 1.6 %copy-start.2 = (bf16[1,4,4,6144]{3,2,1,0:T(4,128)(2,1)S(1)}, bf16[1,4,4,6144]{3,2,1,0:T(4,128)(2,1)}, u32[]{:S(2)}) copy-start(bf16[1,4,4,6144]{3,2,1,0:T(4,128)(2,1)} %param.8) | copy-start | bytes 589828
  0.0 1.6 %copy-start.3 = (f32[192]{0:T(256)S(1)}, f32[192]{0:T(256)}, u32[]{:S(2)}) copy-start(f32[192]{0:T(256)} %param.10) | copy-start | bytes 2308
  0.0 7.9 %collective-permute-start.2 = (bf16[4,4,6144]{2,1,0:T(4,128)(2,1)}, bf16[4,4,6144]{2,1,0:T(4,128)(2,1)S(1)}, u32[]{:S(2)}, u32[]{:S(2)}) collective-permute-start(bf16[4,4,6144]{2,1,0:T(4,128)(2,1)} %bitcast.14), channel_id=1, source_target_pairs={{0,4},{2,6},{4,8},{6,10},{8,12},{10,14},{12,0},{14,2},{1,5},{3,7},... | collective-permute-start | bytes 589832 | tf_op jit(solution)/shard_map/ppermute | solution.py:311
  1.6 3.5 %copy-start = (bf16[3,3,3,192,192]{4,3,2,1,0:T(8,128)(2,1)S(1)}, bf16[3,3,3,192,192]{4,3,2,1,0:T(8,128)(2,1)}, u32[]{:S(2)}) copy-start(bf16[3,3,3,192,192]{4,3,2,1,0:T(8,128)(2,1)} %param.12) | copy-start | bytes 5971972
  2.0 5.0 %copy-start.1 = (bf16[3,3,3,192,192]{4,3,2,1,0:T(8,128)(2,1)S(1)}, bf16[3,3,3,192,192]{4,3,2,1,0:T(8,128)(2,1)}, u32[]{:S(2)}) copy-start(bf16[3,3,3,192,192]{4,3,2,1,0:T(8,128)(2,1)} %param.15) | copy-start | bytes 5971972
  2.0 5.0 %copy-start.4 = (f32[192]{0:T(256)S(1)}, f32[192]{0:T(256)}, u32[]{:S(2)}) copy-start(f32[192]{0:T(256)} %param.11) | copy-start | bytes 2308
  2.0 5.0 %copy-start.5 = (f32[192]{0:T(256)S(1)}, f32[192]{0:T(256)}, u32[]{:S(2)}) copy-start(f32[192]{0:T(256)} %param.13) | copy-start | bytes 2308
  2.0 5.0 %copy-start.6 = (f32[192]{0:T(256)S(1)}, f32[192]{0:T(256)}, u32[]{:S(2)}) copy-start(f32[192]{0:T(256)} %param.14) | copy-start | bytes 2308
  2.0 4.9 %collective-permute-start = (bf16[4,2,16,384]{3,2,1,0:T(8,128)(2,1)S(1)}, bf16[4,2,16,384]{3,2,1,0:T(8,128)(2,1)S(1)}, u32[]{:S(2)}, u32[]{:S(2)}) collective-permute-start(bf16[4,2,16,384]{3,2,1,0:T(8,128)(2,1)S(1)} %get-tuple-element.7), channel_id=1, source_target_pairs={{0,2},{2,0},{4,6},{6,4},{8,10},{10,8},{12,14},{14,12},{1,3},{3,1},... | collective-permute-start | bytes 294920 | tf_op jit(solution)/shard_map/ppermute | solution.py:311
  3.6 6.4 %collective-permute-start.1 = (bf16[4,2,16,384]{3,2,1,0:T(8,128)(2,1)S(1)}, bf16[4,2,16,384]{3,2,1,0:T(8,128)(2,1)S(1)}, u32[]{:S(2)}, u32[]{:S(2)}) collective-permute-start(bf16[4,2,16,384]{3,2,1,0:T(8,128)(2,1)S(1)} %get-tuple-element.7), channel_id=1, source_target_pairs={{0,6},{2,4},{4,10},{6,8},{8,14},{10,12},{12,0},{14,2},{1,7},{3,5},... | collective-permute-start | bytes 294920 | tf_op jit(solution)/shard_map/ppermute | solution.py:311

commit v10 on v9

--- a/solution.py
+++ b/solution.py
@@ -107,7 +107,11 @@
     return mine[0] + left, mine[1] + right
 
 
-def own_kernel(bands, deep, count, normed, weight, total, window):
+def own_kernel(bands, deep, count, normed, weight, *rest):
+    number = (len(rest) - 2) // 2
+    sent, total, later, window = rest[:number], rest[number], rest[number + 1 : -1], rest[-1]
+    for old, new in zip(sent, later):
+        new[...] = old[...]
     frames, rows, pairs, wide = normed.shape
     tm, space = lax.axis_index("tm"), lax.axis_index("space")
     nothing = jnp.zeros((pairs, wide), BF16)
@@ -337,11 +341,9 @@
     earlier = shift(block, 0, 1)
     if swap:
         near = (shift(sent[0], 1, 0),) * 2
-        far = (shift(sent[0], 1, 1),) * 2
         deep = rows + 1
     else:
         near = (shift(sent[0], 1, 0), shift(sent[1], -1, 0))
-        far = (shift(sent[0], 1, 1), shift(sent[1], -1, 1))
         deep = rows + 2
 
     first_weight = weight_first.reshape(3, 3, 3 * channels, channels)
@@ -350,16 +352,20 @@
     window = pltpu.VMEM((frames + 1, deep + 2, pairs, wide), BF16)
     stage = pltpu.VMEM((3, frames * rows * pairs, LANES), F32)
     cost = pl.CostEstimate(flops=1 << 20, bytes_accessed=1 << 16, transcendentals=0)
-    from_own = pl.pallas_call(
+    from_own, *later = pl.pallas_call(
         functools.partial(own_kernel, bands, deep),
-        out_shape=jax.ShapeDtypeStruct(share, F32),
-        in_specs=[smem] + [vmem] * 2,
-        out_specs=vmem,
+        out_shape=[jax.ShapeDtypeStruct(share, F32)] + [rim] * rims,
+        in_specs=[smem] + [vmem] * (2 + rims),
+        out_specs=[vmem] * (1 + rims),
         scratch_shapes=[window],
         compiler_params=params,
         cost_estimate=cost,
         name="conv_one_own",
-    )(counts, normed, first_weight)
+    )(counts, normed, first_weight, *sent)
+    if swap:
+        far = (shift(later[0], 1, 1),) * 2
+    else:
+        far = (shift(later[0], 1, 1), shift(later[1], -1, 1))
     constants = (
         bias_first.reshape(1, channels), first_weight,
         gain_second.reshape(1, channels), bias_second.reshape(1, channels), second_weight,

time: 14.2 us -> 15.8 us (1.11)
  waiting for transfers between devices: 0.89 us -> 1.96 us
  starting transfers between devices: 4 us -> 4.54 us
    ppermute x3, waiting for transfers between devices: 0.89 us -> 1.96 us  [shift(): return lax.ppermute(sent, ('tm', 'space'), pairs_of)]
    ppermute x3, starting transfers between devices: 4 us -> 4.54 us  [shift(): return lax.ppermute(sent, ('tm', 'space'), pairs_of)]
  transfers between devices with their start and end apart: 3 -> 3, of which waited for: 1 -> 1; matrix products, arithmetic and copies ran while one was open for 0% -> 0% of each run, Pallas kernels for 31% -> 28%
where the time goes in v10:
time: 15.8 us; the launch traced here: 15.7 us
  Pallas kernels  8.38 us (53%)
  starting transfers between devices  4.54 us (29%)
  waiting for transfers between devices  1.96 us (12%)
  between operations  0.77 us (5%)
    ppermute x3, starting transfers between devices, shift(): return lax.ppermute(sent, ('tm', 'space'), pairs_of)  4.54 us
    pallas_call x1, Pallas kernels, shards(): pl.pallas_call(functools.partial(last_kernel, bands), out_shape=result, i...  4 us
    pallas_call x1, Pallas kernels, shards(): pl.pallas_call(functools.partial(earlier_kernel, bands, deep), out_shape=...  2.13 us
    ppermute x3, waiting for transfers between devices, shift(): return lax.ppermute(sent, ('tm', 'space'), pairs_of)  1.96 us
    pallas_call x1, Pallas kernels, shards(): pl.pallas_call(functools.partial(own_kernel, bands, deep), out_shape=[jax...  1.85 us
    pallas_call x1, Pallas kernels, shards(): pl.pallas_call(functools.partial(norm_kernel, swap), out_shape=[jax.Shape...  0.37 us
  transfers between devices with their start and end apart: 3, of which 1 were waited for; matrix products, arithmetic and copies ran while one was open for 0% of the time, Pallas kernels for 28%

profile of v10, /device:TPU:16, one launch (start us, length us, event | category | flops | bytes accessed | tf_op | source)
XLA Modules:
  0.0 15.7 jit_solution(10028747028410686200)
XLA Ops:
  0.0 0.0 copy-start.2
  0.0 0.0 copy-start.3
  0.0 1.6 %collective-permute-start.2 = (bf16[4,4,6144]{2,1,0:T(4,128)(2,1)}, bf16[4,4,6144]{2,1,0:T(4,128)(2,1)S(1)}, u32[]{:S(2)}, u32[]{:S(2)}) collective-permute-start(bf16[4,4,6144]{2,1,0:T(4,128)(2,1)} %bitcast.14), channel_id=1, source_target_pairs={{0,4},{2,6},{4,8},{6,10},{8,12},{10,14},{12,0},{14,2},{1,5},{3,7},... | collective-permute-start | bytes 589832 | tf_op jit(solution)/shard_map/ppermute | solution.py:315
  1.6 0.0 copy-done.2
  1.6 0.0 copy-done.3
  1.6 0.0 copy-start
  1.6 0.4 %norm_and_cut.1 = (bf16[4,4,16,384]{3,2,1,0:T(8,128)(2,1)S(1)}, bf16[4,2,16,384]{3,2,1,0:T(8,128)(2,1)S(1)}) custom-call(f32[8,384]{1,0:T(8,128)S(1)} %lane_mask.1.mask, bf16[4,4,6144]{2,1,0:T(4,128)(2,1)S(1)} %bitcast.15, f32[1,192]{1,0:T(1,128)S(1)} %bitcast.18), custom_call_target="tpu_custom_call" | custom-call | flops 4294967296 | bytes 1048576 | tf_op jit(solution)/shard_map/norm_and_cut/pallas_call | solution.py:331
  2.0 0.0 copy-start.1
  2.0 0.0 copy-start.4
  2.0 0.0 copy-start.5
  2.0 0.0 copy-start.6
  2.0 1.6 %collective-permute-start = (bf16[4,2,16,384]{3,2,1,0:T(8,128)(2,1)S(1)}, bf16[4,2,16,384]{3,2,1,0:T(8,128)(2,1)S(1)}, u32[]{:S(2)}, u32[]{:S(2)}) collective-permute-start(bf16[4,2,16,384]{3,2,1,0:T(8,128)(2,1)S(1)} %get-tuple-element.9.rest_0_), channel_id=1, source_target_pairs={{0,2},{2,0},{4,6},{6,4},{8,10},{10,8},{12,14},{14,12},{1,3},{3,1},... | collective-permute-start | bytes 294920 | tf_op jit(solution)/shard_map/ppermute | solution.py:315
  4.2 0.0 copy-done
  4.3 1.8 %conv_one_own.1 = (f32[2,4,5,16,192]{4,3,2,1,0:T(8,128)S(1)}, bf16[4,2,16,384]{3,2,1,0:T(8,128)(2,1)S(1)}) custom-call(s32[1]{0:T(128)S(6)} %copy.9.count, bf16[4,4,16,384]{3,2,1,0:T(8,128)(2,1)S(1)} %get-tuple-element.10.normed, bf16[3,3,576,192]{3,2,1,0:T(8,128)(2,1)S(1)} %bitcast.8, bf16[4,2,16,384]{3,2,1,0:T(8,128)(2,1)S(1)} %get-tuple-element.9.rest_0_), custom_call_target="tpu_custom_call" | custom-call | flops 1048576 | bytes 65536 | tf_op jit(solution)/shard_map/conv_one_own/pallas_call | solution.py:355
  6.1 1.4 %collective-permute-start.1 = (bf16[4,2,16,384]{3,2,1,0:T(8,128)(2,1)S(1)}, bf16[4,2,16,384]{3,2,1,0:T(8,128)(2,1)S(1)}, u32[]{:S(2)}, u32[]{:S(2)}) collective-permute-start(bf16[4,2,16,384]{3,2,1,0:T(8,128)(2,1)S(1)} %get-tuple-element.11), channel_id=1, source_target_pairs={{0,6},{2,4},{4,10},{6,8},{8,14},{10,12},{12,0},{14,2},{1,7},{3,5},... | collective-permute-start | bytes 294920 | tf_op jit(solution)/shard_map/ppermute | solution.py:315
  7.5 0.0 collective-permute-done.above.below
  7.5 0.0 copy-done.1
  7.5 0.0 copy-done.4
  7.5 0.0 copy-done.5
  7.5 0.0 copy-done.6
  7.6 0.0 collective-permute-done.2.earlier
  7.6 2.1 %conv_one_earlier.1.from_earlier = f32[2,4,5,16,192]{4,3,2,1,0:T(8,128)S(1)} custom-call(s32[1]{0:T(128)S(6)} %copy.9.count, f32[8,384]{1,0:T(8,128)S(1)} %lane_mask.1.mask, bf16[4,4,6144]{2,1,0:T(4,128)(2,1)S(1)} %collective-permute-done.2.earlier, f32[1,192]{1,0:T(1,128)S(1)} %bitcast.19, bf16[3,3,576,192]{3,2,1,0:T(8,128)(2,1)S(1)} %bitcast.10, ...), custom_call_target="tpu_custom_call" | custom-call | flops 1048576 | bytes 65536 | tf_op jit(solution)/shard_map/conv_one_earlier/pallas_call | solution.py:389
  9.7 2.0 %collective-permute-done.1.far_above.far_below = bf16[4,2,16,384]{3,2,1,0:T(8,128)(2,1)S(1)} collective-permute-done((bf16[4,2,16,384]{3,2,1,0:T(8,128)(2,1)S(1)}, bf16[4,2,16,384]{3,2,1,0:T(8,128)(2,1)S(1)}, u32[]{:S(2)}, u32[]{:S(2)}) %collective-permute-start.1) | collective-permute-done | bytes 98336 | tf_op jit(solution)/shard_map/ppermute | solution.py:315
  11.7 4.0 %last.1 = bf16[4,4,6144]{2,1,0:T(4,128)(2,1)} custom-call(s32[1]{0:T(128)S(6)} %copy.9.count, bf16[4,4,6144]{2,1,0:T(4,128)(2,1)S(1)} %bitcast.17, bf16[4,2,16,384]{3,2,1,0:T(8,128)(2,1)S(1)} %collective-permute-done.above.below, bf16[4,2,16,384]{3,2,1,0:T(8,128)(2,1)S(1)} %collective-permute-done.above.below, ...), custom_call_target="tpu_custom_call" | custom-call | flops 4294967296 | bytes 6291456 | tf_op jit(solution)/shard_map/last/pallas_call | solution.py:399
  (2 shorter events, 0.0 us)
Async XLA Ops:
  0.0 1.6 %copy-start.2 = (bf16[1,4,4,6144]{3,2,1,0:T(4,128)(2,1)S(1)}, bf16[1,4,4,6144]{3,2,1,0:T(4,128)(2,1)}, u32[]{:S(2)}) copy-start(bf16[1,4,4,6144]{3,2,1,0:T(4,128)(2,1)} %param.8) | copy-start | bytes 589828
  0.0 1.6 %copy-start.3 = (f32[192]{0:T(256)S(1)}, f32[192]{0:T(256)}, u32[]{:S(2)}) copy-start(f32[192]{0:T(256)} %param.10) | copy-start | bytes 2308
  0.0 7.6 %collective-permute-start.2 = (bf16[4,4,6144]{2,1,0:T(4,128)(2,1)}, bf16[4,4,6144]{2,1,0:T(4,128)(2,1)S(1)}, u32[]{:S(2)}, u32[]{:S(2)}) collective-permute-start(bf16[4,4,6144]{2,1,0:T(4,128)(2,1)} %bitcast.14), channel_id=1, source_target_pairs={{0,4},{2,6},{4,8},{6,10},{8,12},{10,14},{12,0},{14,2},{1,5},{3,7},... | collective-permute-start | bytes 589832 | tf_op jit(solution)/shard_map/ppermute | solution.py:315
  1.6 2.7 %copy-start = (bf16[3,3,3,192,192]{4,3,2,1,0:T(8,128)(2,1)S(1)}, bf16[3,3,3,192,192]{4,3,2,1,0:T(8,128)(2,1)}, u32[]{:S(2)}) copy-start(bf16[3,3,3,192,192]{4,3,2,1,0:T(8,128)(2,1)} %param.12) | copy-start | bytes 5971972
  2.0 5.5 %copy-start.1 = (bf16[3,3,3,192,192]{4,3,2,1,0:T(8,128)(2,1)S(1)}, bf16[3,3,3,192,192]{4,3,2,1,0:T(8,128)(2,1)}, u32[]{:S(2)}) copy-start(bf16[3,3,3,192,192]{4,3,2,1,0:T(8,128)(2,1)} %param.15) | copy-start | bytes 5971972
  2.0 5.5 %copy-start.4 = (f32[192]{0:T(256)S(1)}, f32[192]{0:T(256)}, u32[]{:S(2)}) copy-start(f32[192]{0:T(256)} %param.11) | copy-start | bytes 2308
  2.0 5.5 %copy-start.5 = (f32[192]{0:T(256)S(1)}, f32[192]{0:T(256)}, u32[]{:S(2)}) copy-start(f32[192]{0:T(256)} %param.13) | copy-start | bytes 2308
  2.0 5.5 %copy-start.6 = (f32[192]{0:T(256)S(1)}, f32[192]{0:T(256)}, u32[]{:S(2)}) copy-start(f32[192]{0:T(256)} %param.14) | copy-start | bytes 2308
  2.0 5.5 %collective-permute-start = (bf16[4,2,16,384]{3,2,1,0:T(8,128)(2,1)S(1)}, bf16[4,2,16,384]{3,2,1,0:T(8,128)(2,1)S(1)}, u32[]{:S(2)}, u32[]{:S(2)}) collective-permute-start(bf16[4,2,16,384]{3,2,1,0:T(8,128)(2,1)S(1)} %get-tuple-element.9.rest_0_), channel_id=1, source_target_pairs={{0,2},{2,0},{4,6},{6,4},{8,10},{10,8},{12,14},{14,12},{1,3},{3,1},... | collective-permute-start | bytes 294920 | tf_op jit(solution)/shard_map/ppermute | solution.py:315
  6.1 5.6 %collective-permute-start.1 = (bf16[4,2,16,384]{3,2,1,0:T(8,128)(2,1)S(1)}, bf16[4,2,16,384]{3,2,1,0:T(8,128)(2,1)S(1)}, u32[]{:S(2)}, u32[]{:S(2)}) collective-permute-start(bf16[4,2,16,384]{3,2,1,0:T(8,128)(2,1)S(1)} %get-tuple-element.11), channel_id=1, source_target_pairs={{0,6},{2,4},{4,10},{6,8},{8,14},{10,12},{12,0},{14,2},{1,7},{3,5},... | collective-permute-start | bytes 294920 | tf_op jit(solution)/shard_map/ppermute | solution.py:315

commit v11 on v9

--- a/solution.py
+++ b/solution.py
@@ -12,43 +12,47 @@
 LANES = 128
 
 
-def mask_kernel(channels, mask):
-    lane = lax.broadcasted_iota(jnp.int32, mask.shape, 1)
-    mask[...] = jnp.where(lane < channels, 1.0, 0.0)
-
-
-def norm_silu_pair(t, gain, first, channels):
-    square = t * t
-    left = jnp.sum(jnp.where(first, square, 0.0), axis=1, keepdims=True)
-    right = jnp.sum(jnp.where(first, 0.0, square), axis=1, keepdims=True)
-    left = lax.rsqrt(left * (1.0 / channels) + 1e-06)
-    right = lax.rsqrt(right * (1.0 / channels) + 1e-06)
-    y = t * jnp.where(first, left, right) * gain
-    return y * (0.5 + 0.5 * jnp.tanh(0.5 * y))
+def sums_kernel(channels, sums):
+    lane = lax.broadcasted_iota(jnp.int32, sums.shape, 0) < channels
+    half = lax.broadcasted_iota(jnp.int32, sums.shape, 1) < LANES
+    sums[...] = jnp.where(lane == half, 1.0, 0.0).astype(BF16)
+
+
+def norm_silu_pair(t, half_gain, sums, channels):
+    squares = jnp.dot((t * t).astype(BF16), sums, preferred_element_type=F32)
+    scale = lax.rsqrt(squares * (1.0 / channels) + 1e-06)
+    left, right = scale[:, :LANES], scale[:, LANES:]
+    first = lax.broadcasted_iota(jnp.int32, left.shape, 1) < channels - LANES
+    scale = jnp.concatenate([left, jnp.where(first, left, right), right], axis=1)
+    h = t * scale * half_gain
+    return h + h * jnp.tanh(h)
 
 
 def twice(ref):
     return jnp.concatenate([ref[...], ref[...]], axis=1)
 
 
-def norm_block(block, gain_wide, first, stage, store, pairs):
+def norm_block(block, half_gain, sums, stage, store, pairs):
     frames, rows = block.shape[0], block.shape[1]
-    wide = gain_wide.shape[1]
+    wide = half_gain.shape[1]
+    tall = 2 * rows
     for f in range(0, frames, 2):
+        parts = []
         for p in range(pairs):
             lanes = pl.ds(p * wide, wide)
-            t = jnp.concatenate([block[f + n, :, lanes].astype(F32) for n in range(2)], axis=0)
-            y = norm_silu_pair(t, gain_wide, first, wide // 2)
+            parts += [block[f + n, :, lanes].astype(F32) for n in range(2)]
+        y = norm_silu_pair(jnp.concatenate(parts, axis=0), half_gain, sums, wide // 2)
+        for p in range(pairs):
             for k in range(3):
-                at = pl.ds(f * rows * pairs + p, 2 * rows, stride=pairs)
-                stage[k, at, :] = y[:, k * LANES : (k + 1) * LANES]
+                at = pl.ds(f * rows * pairs + p, tall, stride=pairs)
+                stage[k, at, :] = y[p * tall : (p + 1) * tall, k * LANES : (k + 1) * LANES]
         for n in range(2):
             for r in range(rows):
                 at = pl.ds(((f + n) * rows + r) * pairs, pairs)
                 store(f + n, r, [stage[k, at, :].astype(BF16) for k in range(3)])
 
 
-def norm_kernel(swap, mask, block, gain, normed, *rest):
+def norm_kernel(swap, sums, block, gain, normed, *rest):
     sent, stage = rest[:-1], rest[-1]
     rows, pairs = normed.shape[1], normed.shape[2]
 
@@ -56,7 +60,7 @@
         for k in range(3):
             normed[f, r, :, k * LANES : (k + 1) * LANES] = parts[k]
 
-    norm_block(block, twice(gain), mask[...] > 0.5, stage, store, pairs)
+    norm_block(block, twice(gain) * 0.5, sums[...], stage, store, pairs)
     if swap:
         first = (rows - 2) * (1 - lax.axis_index("space"))
         sent[0][...] = normed[:, pl.ds(first, 2)]
@@ -139,7 +143,7 @@
 
 
 def earlier_kernel(
-    bands, deep, count, mask, earlier, gain, weight, after, total, window, stage
+    bands, deep, count, sums, earlier, gain, weight, after, total, window, stage
 ):
     frames, rows = earlier.shape[0], earlier.shape[1]
     pairs, wide = window.shape[2], window.shape[3]
@@ -156,7 +160,7 @@
                 part = jnp.where(good, parts[k], jnp.zeros_like(parts[k]))
                 window[f, top + r, :, k * LANES : (k + 1) * LANES] = part
 
-        norm_block(earlier, twice(gain), mask[...] > 0.5, stage, store, pairs)
+        norm_block(earlier, twice(gain) * 0.5, sums[...], stage, store, pairs)
         soon = conv([window.at[f] for f in range(frames + 1)], weight, 0, frames - 2, deep, (0, 1, 2), wide // 2)
         late = conv([window.at[f] for f in range(frames + 1)], weight, frames - 2, 2, deep, (0, 1), wide // 2)
         for q in range(2):
@@ -190,7 +194,7 @@
         total[q, :, halo] += added[q].reshape(span, pairs, channels)
 
 
-def finish(bands, count, own, near, far, bias, weight, gain_two, bias_two, weight_two, out, total, hidden, final):
+def finish(bands, count, sums, own, near, far, bias, weight, gain_two, bias_two, weight_two, out, total, hidden, final):
     frames, rows, pairs, wide = near[0].shape[0], own.shape[1], near[0].shape[2], near[0].shape[3]
     channels = wide // 2
     deep = total.shape[2]
@@ -212,14 +216,13 @@
     start = (1 - space) if bands == 2 else 0
     row = lax.broadcasted_iota(jnp.int32, (fill, 1), 0) // pairs + (space * rows - 1 + start)
     row_ok = (row >= 0) & (row < bands * rows)
-    bias_wide, gain_wide = twice(bias), twice(gain_two)
-    first_lanes = lax.broadcasted_iota(jnp.int32, (fill, wide), 1) < channels
+    bias_wide, gain_wide = twice(bias), twice(gain_two) * 0.5
 
     def norm_hidden(h):
         good = row_ok & valid(frames + h - 2)
         t = jnp.concatenate([total[q, h].reshape(fill, channels) for q in range(2)], axis=1)
         t = jnp.where(good, t + bias_wide, 0.0).astype(BF16).astype(F32)
-        y = norm_silu_pair(t, gain_wide, first_lanes, channels).astype(BF16)
+        y = norm_silu_pair(t, gain_wide, sums[...], channels).astype(BF16)
         hidden[h][0] = jnp.zeros((pairs, wide), BF16)
         hidden[h][rows + 1] = jnp.zeros((pairs, wide), BF16)
         for r in range(deep):
@@ -254,7 +257,7 @@
 
 
 def first_block_kernel(
-    bands, count, own, above, below, from_own, bias, weight, gain_two, bias_two, weight_two,
+    bands, count, sums, own, above, below, from_own, bias, weight, gain_two, bias_two, weight_two,
     out, total, *scratch,
 ):
     frames = own.shape[0]
@@ -266,13 +269,13 @@
         total[:, 2:] = from_own[...]
         near = (above, below)
         finish(
-            bands, count, own, near, near, bias, weight, gain_two, bias_two, weight_two,
+            bands, count, sums, own, near, near, bias, weight, gain_two, bias_two, weight_two,
             out, total, hidden, final,
         )
 
 
 def last_kernel(
-    bands, count, own, above, below, far_above, far_below, from_own, from_earlier, first_out, bias,
+    bands, count, sums, own, above, below, far_above, far_below, from_own, from_earlier, first_out, bias,
     weight, gain_two, bias_two, weight_two, out, total, *scratch,
 ):
     frames = own.shape[0]
@@ -289,7 +292,7 @@
         total[:, 2:frames] = from_own[:, : frames - 2] + from_earlier[:, 2:]
         total[:, frames:] = from_own[:, frames - 2 :]
         finish(
-            bands, count, own, (above, below), (far_above, far_below), bias, weight, gain_two,
+            bands, count, sums, own, (above, below), (far_above, far_below), bias, weight, gain_two,
             bias_two, weight_two, out, total, hidden, final,
         )
 
@@ -316,13 +319,13 @@
     swap = bands == 2
     rims = 1 if swap else 2
     rim = jax.ShapeDtypeStruct((frames, 2, pairs, wide), BF16)
-    mask = pl.pallas_call(
-        functools.partial(mask_kernel, channels),
-        out_shape=jax.ShapeDtypeStruct((2 * rows, wide), F32),
+    sums = pl.pallas_call(
+        functools.partial(sums_kernel, channels),
+        out_shape=jax.ShapeDtypeStruct((wide, 2 * LANES), BF16),
         out_specs=vmem,
         compiler_params=params,
         cost_estimate=pl.CostEstimate(flops=4 << 30, bytes_accessed=1 << 16, transcendentals=0),
-        name="lane_mask",
+        name="sum_matrix",
     )()
     normed, *sent = pl.pallas_call(
         functools.partial(norm_kernel, swap),
@@ -333,7 +336,7 @@
         compiler_params=params,
         cost_estimate=pl.CostEstimate(flops=4 << 30, bytes_accessed=1 << 20, transcendentals=0),
         name="norm_and_cut",
-    )(mask, block, gain_first.reshape(1, channels))
+    )(sums, block, gain_first.reshape(1, channels))
     earlier = shift(block, 0, 1)
     if swap:
         near = (shift(sent[0], 1, 0),) * 2
@@ -373,13 +376,13 @@
     first_out = pl.pallas_call(
         functools.partial(first_block_kernel, bands),
         out_shape=result,
-        in_specs=[smem] + [vmem] * 9,
+        in_specs=[smem] + [vmem] * 10,
         out_specs=vmem,
         scratch_shapes=scratch,
         compiler_params=params,
         cost_estimate=cost,
         name="first_block",
-    )(counts, block, *near, from_own, *constants)
+    )(counts, sums, block, *near, from_own, *constants)
     from_earlier = pl.pallas_call(
         functools.partial(earlier_kernel, bands, deep),
         out_shape=jax.ShapeDtypeStruct(share, F32),
@@ -389,17 +392,17 @@
         compiler_params=params,
         cost_estimate=cost,
         name="conv_one_earlier",
-    )(counts, mask, earlier, gain_first.reshape(1, channels), first_weight, first_out)
+    )(counts, sums, earlier, gain_first.reshape(1, channels), first_weight, first_out)
     out = pl.pallas_call(
         functools.partial(last_kernel, bands),
         out_shape=result,
-        in_specs=[smem] + [vmem] * 13,
+        in_specs=[smem] + [vmem] * 14,
         out_specs=vmem,
         scratch_shapes=scratch,
         compiler_params=params,
         cost_estimate=pl.CostEstimate(flops=4 << 30, bytes_accessed=6 << 20, transcendentals=0),
         name="last",
-    )(counts, block, *near, *far, from_own, from_earlier, first_out, *constants)
+    )(counts, sums, block, *near, *far, from_own, from_earlier, first_out, *constants)
     return out.reshape(1, frames, rows, flat)
 
 

time: 14.2 us -> 14.4 us (1.014)
  Pallas kernels: 8.36 us -> 8.61 us
  transfers between devices with their start and end apart: 3 -> 3, of which waited for: 1 -> 1; matrix products, arithmetic and copies ran while one was open for 0% -> 0% of each run, Pallas kernels for 31% -> 32%
where the time goes in v11:
time: 14.4 us; the launch traced here: 14.2 us
  Pallas kernels  8.61 us (60%)
  starting transfers between devices  3.98 us (28%)
  waiting for transfers between devices  0.81 us (6%)
  between operations  0.8 us (6%)
    pallas_call x1, Pallas kernels, shards(): pl.pallas_call(functools.partial(last_kernel, bands), out_shape=result, i...  4.06 us
    ppermute x3, starting transfers between devices, shift(): return lax.ppermute(sent, ('tm', 'space'), pairs_of)  3.98 us
    pallas_call x1, Pallas kernels, shards(): pl.pallas_call(functools.partial(earlier_kernel, bands, deep), out_shape=...  2.24 us
    pallas_call x1, Pallas kernels, shards(): pl.pallas_call(functools.partial(own_kernel, bands, deep), out_shape=jax....  1.82 us
    ppermute x3, waiting for transfers between devices, shift(): return lax.ppermute(sent, ('tm', 'space'), pairs_of)  0.81 us
    pallas_call x1, Pallas kernels, shards(): pl.pallas_call(functools.partial(norm_kernel, swap), out_shape=[jax.Shape...  0.46 us
  transfers between devices with their start and end apart: 3, of which 1 were waited for; matrix products, arithmetic and copies ran while one was open for 0% of the time, Pallas kernels for 32%

profile of v11, /device:TPU:16, one launch (start us, length us, event | category | flops | bytes accessed | tf_op | source)
XLA Modules:
  0.0 14.2 jit_solution(540831545072310857)
XLA Ops:
  0.0 0.0 copy-start.2
  0.0 0.0 copy-start.3
  0.0 1.6 %collective-permute-start.2 = (bf16[4,4,6144]{2,1,0:T(4,128)(2,1)}, bf16[4,4,6144]{2,1,0:T(4,128)(2,1)S(1)}, u32[]{:S(2)}, u32[]{:S(2)}) collective-permute-start(bf16[4,4,6144]{2,1,0:T(4,128)(2,1)} %bitcast.14), channel_id=1, source_target_pairs={{0,4},{2,6},{4,8},{6,10},{8,12},{10,14},{12,0},{14,2},{1,5},{3,7},... | collective-permute-start | bytes 589832 | tf_op jit(solution)/shard_map/ppermute | solution.py:314
  1.6 0.0 copy-done.2
  1.6 0.0 copy-done.3
  1.6 0.0 copy-start
  1.6 0.5 %norm_and_cut.1 = (bf16[4,4,16,384]{3,2,1,0:T(8,128)(2,1)S(1)}, bf16[4,2,16,384]{3,2,1,0:T(8,128)(2,1)S(1)}) custom-call(bf16[384,256]{1,0:T(8,128)(2,1)S(1)} %sum_matrix.1.sums, bf16[4,4,6144]{2,1,0:T(4,128)(2,1)S(1)} %bitcast.15, f32[1,192]{1,0:T(1,128)S(1)} %bitcast.18), custom_call_target="tpu_custom_call" | custom-call | flops 4294967296 | bytes 1048576 | tf_op jit(solution)/shard_map/norm_and_cut/pallas_call | solution.py:330
  2.1 0.0 copy-start.1
  2.1 0.0 copy-start.4
  2.1 0.0 copy-start.5
  2.1 0.0 copy-start.6
  2.1 1.6 %collective-permute-start = (bf16[4,2,16,384]{3,2,1,0:T(8,128)(2,1)S(1)}, bf16[4,2,16,384]{3,2,1,0:T(8,128)(2,1)S(1)}, u32[]{:S(2)}, u32[]{:S(2)}) collective-permute-start(bf16[4,2,16,384]{3,2,1,0:T(8,128)(2,1)S(1)} %get-tuple-element.7), channel_id=1, source_target_pairs={{0,2},{2,0},{4,6},{6,4},{8,10},{10,8},{12,14},{14,12},{1,3},{3,1},... | collective-permute-start | bytes 294920 | tf_op jit(solution)/shard_map/ppermute | solution.py:314
  3.7 0.8 %collective-permute-start.1 = (bf16[4,2,16,384]{3,2,1,0:T(8,128)(2,1)S(1)}, bf16[4,2,16,384]{3,2,1,0:T(8,128)(2,1)S(1)}, u32[]{:S(2)}, u32[]{:S(2)}) collective-permute-start(bf16[4,2,16,384]{3,2,1,0:T(8,128)(2,1)S(1)} %get-tuple-element.7), channel_id=1, source_target_pairs={{0,6},{2,4},{4,10},{6,8},{8,14},{10,12},{12,0},{14,2},{1,7},{3,5},... | collective-permute-start | bytes 294920 | tf_op jit(solution)/shard_map/ppermute | solution.py:314
  5.2 0.0 copy-done
  5.2 1.8 %conv_one_own.1.from_own = f32[2,4,5,16,192]{4,3,2,1,0:T(8,128)S(1)} custom-call(s32[1]{0:T(128)S(6)} %copy.9.count, bf16[4,4,16,384]{3,2,1,0:T(8,128)(2,1)S(1)} %get-tuple-element.8.normed, bf16[3,3,576,192]{3,2,1,0:T(8,128)(2,1)S(1)} %bitcast.8), custom_call_target="tpu_custom_call" | custom-call | flops 1048576 | bytes 65536 | tf_op jit(solution)/shard_map/conv_one_own/pallas_call | solution.py:356
  7.0 0.0 collective-permute-done.above.below
  7.0 0.0 copy-done.1
  7.1 0.0 copy-done.4
  7.1 0.0 copy-done.5
  7.1 0.0 copy-done.6
  7.1 0.8 %collective-permute-done.2.earlier = bf16[4,4,6144]{2,1,0:T(4,128)(2,1)S(1)} collective-permute-done((bf16[4,4,6144]{2,1,0:T(4,128)(2,1)}, bf16[4,4,6144]{2,1,0:T(4,128)(2,1)S(1)}, u32[]{:S(2)}, u32[]{:S(2)}) %collective-permute-start.2) | collective-permute-done | bytes 196640 | tf_op jit(solution)/shard_map/ppermute | solution.py:314
  7.9 2.2 %conv_one_earlier.1.from_earlier = f32[2,4,5,16,192]{4,3,2,1,0:T(8,128)S(1)} custom-call(s32[1]{0:T(128)S(6)} %copy.9.count, bf16[384,256]{1,0:T(8,128)(2,1)S(1)} %sum_matrix.1.sums, bf16[4,4,6144]{2,1,0:T(4,128)(2,1)S(1)} %collective-permute-done.2.earlier, f32[1,192]{1,0:T(1,128)S(1)} %bitcast.19, bf16[3,3,576,192]{3,2,1,0:T(8,128)(2,1)S(1)} %bitcast.10, ...), custom_call_target="tpu_custom_call" | custom-call | flops 1048576 | bytes 65536 | tf_op jit(solution)/shard_map/conv_one_earlier/pallas_call | solution.py:386
  10.2 0.0 collective-permute-done.1.far_above.far_below
  10.2 4.1 %last.1 = bf16[4,4,6144]{2,1,0:T(4,128)(2,1)} custom-call(s32[1]{0:T(128)S(6)} %copy.9.count, bf16[384,256]{1,0:T(8,128)(2,1)S(1)} %sum_matrix.1.sums, bf16[4,4,6144]{2,1,0:T(4,128)(2,1)S(1)} %bitcast.17, bf16[4,2,16,384]{3,2,1,0:T(8,128)(2,1)S(1)} %collective-permute-done.above.below, bf16[4,2,16,384]{3,2,1,0:T(8,128)(2,1)S(1)} %collective-permute-done.above.below, ...), custom_call_target="tpu_custom_call" | custom-call | flops 4294967296 | bytes 6291456 | tf_op jit(solution)/shard_map/last/pallas_call | solution.py:396
  (2 shorter events, 0.0 us)
Async XLA Ops:
  0.0 1.6 %copy-start.2 = (bf16[1,4,4,6144]{3,2,1,0:T(4,128)(2,1)S(1)}, bf16[1,4,4,6144]{3,2,1,0:T(4,128)(2,1)}, u32[]{:S(2)}) copy-start(bf16[1,4,4,6144]{3,2,1,0:T(4,128)(2,1)} %param.8) | copy-start | bytes 589828
  0.0 1.6 %copy-start.3 = (f32[192]{0:T(256)S(1)}, f32[192]{0:T(256)}, u32[]{:S(2)}) copy-start(f32[192]{0:T(256)} %param.10) | copy-start | bytes 2308
  0.0 7.9 %collective-permute-start.2 = (bf16[4,4,6144]{2,1,0:T(4,128)(2,1)}, bf16[4,4,6144]{2,1,0:T(4,128)(2,1)S(1)}, u32[]{:S(2)}, u32[]{:S(2)}) collective-permute-start(bf16[4,4,6144]{2,1,0:T(4,128)(2,1)} %bitcast.14), channel_id=1, source_target_pairs={{0,4},{2,6},{4,8},{6,10},{8,12},{10,14},{12,0},{14,2},{1,5},{3,7},... | collective-permute-start | bytes 589832 | tf_op jit(solution)/shard_map/ppermute | solution.py:314
  1.6 3.6 %copy-start = (bf16[3,3,3,192,192]{4,3,2,1,0:T(8,128)(2,1)S(1)}, bf16[3,3,3,192,192]{4,3,2,1,0:T(8,128)(2,1)}, u32[]{:S(2)}) copy-start(bf16[3,3,3,192,192]{4,3,2,1,0:T(8,128)(2,1)} %param.12) | copy-start | bytes 5971972
  2.1 4.9 %copy-start.1 = (bf16[3,3,3,192,192]{4,3,2,1,0:T(8,128)(2,1)S(1)}, bf16[3,3,3,192,192]{4,3,2,1,0:T(8,128)(2,1)}, u32[]{:S(2)}) copy-start(bf16[3,3,3,192,192]{4,3,2,1,0:T(8,128)(2,1)} %param.15) | copy-start | bytes 5971972
  2.1 4.9 %copy-start.4 = (f32[192]{0:T(256)S(1)}, f32[192]{0:T(256)}, u32[]{:S(2)}) copy-start(f32[192]{0:T(256)} %param.11) | copy-start | bytes 2308
  2.1 4.9 %copy-start.5 = (f32[192]{0:T(256)S(1)}, f32[192]{0:T(256)}, u32[]{:S(2)}) copy-start(f32[192]{0:T(256)} %param.13) | copy-start | bytes 2308
  2.1 4.9 %copy-start.6 = (f32[192]{0:T(256)S(1)}, f32[192]{0:T(256)}, u32[]{:S(2)}) copy-start(f32[192]{0:T(256)} %param.14) | copy-start | bytes 2308
  2.1 4.9 %collective-permute-start = (bf16[4,2,16,384]{3,2,1,0:T(8,128)(2,1)S(1)}, bf16[4,2,16,384]{3,2,1,0:T(8,128)(2,1)S(1)}, u32[]{:S(2)}, u32[]{:S(2)}) collective-permute-start(bf16[4,2,16,384]{3,2,1,0:T(8,128)(2,1)S(1)} %get-tuple-element.7), channel_id=1, source_target_pairs={{0,2},{2,0},{4,6},{6,4},{8,10},{10,8},{12,14},{14,12},{1,3},{3,1},... | collective-permute-start | bytes 294920 | tf_op jit(solution)/shard_map/ppermute | solution.py:314
  3.7 6.5 %collective-permute-start.1 = (bf16[4,2,16,384]{3,2,1,0:T(8,128)(2,1)S(1)}, bf16[4,2,16,384]{3,2,1,0:T(8,128)(2,1)S(1)}, u32[]{:S(2)}, u32[]{:S(2)}) collective-permute-start(bf16[4,2,16,384]{3,2,1,0:T(8,128)(2,1)S(1)} %get-tuple-element.7), channel_id=1, source_target_pairs={{0,6},{2,4},{4,10},{6,8},{8,14},{10,12},{12,0},{14,2},{1,7},{3,5},... | collective-permute-start | bytes 294920 | tf_op jit(solution)/shard_map/ppermute | solution.py:314

commit v12 on v8

--- a/solution.py
+++ b/solution.py
@@ -90,9 +90,9 @@
     pairs, wide = window.shape[2], window.shape[3]
     taps = [(a, b) for a in times for b in range(3)]
     parts = [
-        window[
-            source + a - times[0] : source + a - times[0] + frames, b : b + rows
-        ].reshape(frames * rows * pairs, wide)
+        window[pl.ds(source + a - times[0], frames), b : b + rows].reshape(
+            frames * rows * pairs, wide
+        )
         for a, b in taps
     ]
     return add_moved(*products(parts, [weight[a, b] for a, b in taps], channels), pairs)
@@ -213,7 +213,10 @@
     row_ok = (row >= 0) & (row < bands * rows)
     bias_wide, gain_wide = twice(bias), twice(gain_two)
     first_lanes = lax.broadcasted_iota(jnp.int32, (fill, wide), 1) < channels
-    for h in range(frames + 2):
+
+    bias_two_wide = twice(bias_two)
+
+    def norm_hidden(h, _):
         good = row_ok & valid(frames + h - 2)
         t = jnp.concatenate([total[q, h].reshape(fill, channels) for q in range(2)], axis=1)
         t = jnp.where(good, t + bias_wide, 0.0).astype(BF16).astype(F32)
@@ -222,20 +225,30 @@
         hidden[h, rows + 1] = jnp.zeros((pairs, wide), BF16)
         for r in range(deep):
             hidden[h, start + r] = y[r * pairs : (r + 1) * pairs]
-
-    both = jnp.concatenate(conv(hidden, weight_two, 0, frames, rows, (0, 1, 2), channels), axis=1)
-    both = both + twice(bias_two)
-    for k in range(3):
-        final[k] = both[:, k * LANES : (k + 1) * LANES]
-    for f in range(0, frames, 2):
-        good = [valid(frames + f + n) for n in range(2)]
+        return 0
+
+    def second_conv(i, _):
+        both = conv(hidden, weight_two, 2 * i, 2, rows, (0, 1, 2), channels)
+        both = jnp.concatenate(both, axis=1) + bias_two_wide
+        for k in range(3):
+            final[i, k] = both[:, k * LANES : (k + 1) * LANES]
+        return 0
+
+    def emit(i, _):
+        good = [valid(frames + 2 * i + n) for n in range(2)]
         for p in range(pairs):
             for k in range(3):
-                block = final[k, pl.ds(f * rows * pairs + p, 2 * rows, stride=pairs), :]
+                block = final[i, k, pl.ds(p, 2 * rows, stride=pairs), :]
                 lanes = pl.ds(p * wide + k * LANES, LANES)
                 for n in range(2):
-                    value = own[f + n, :, lanes].astype(F32) + block[n * rows : (n + 1) * rows]
-                    out[f + n, :, lanes] = jnp.where(good[n], value, 0.0).astype(BF16)
+                    f = 2 * i + n
+                    value = own[f, :, lanes].astype(F32) + block[n * rows : (n + 1) * rows]
+                    out[f, :, lanes] = jnp.where(good[n], value, 0.0).astype(BF16)
+        return 0
+
+    lax.fori_loop(0, frames + 2, norm_hidden, 0)
+    lax.fori_loop(0, frames // 2, second_conv, 0)
+    lax.fori_loop(0, frames // 2, emit, 0)
 
 
 def first_block_kernel(
@@ -287,7 +300,7 @@
 
     def shift(sent, step, along):
         pairs_of = [
-            (t * bands + s, (t + along) % blocks * bands + (s + step) % bands)
+            (t * bands + s, (t + along) % blocks * bands + (s + step * (t + along < blocks)) % bands)
             for t in range(blocks)
             for s in range(bands)
         ]
@@ -351,7 +364,7 @@
     scratch = [
         pltpu.VMEM((2, frames + 2, deep, pairs, channels), F32),
         pltpu.VMEM((frames + 2, rows + 2, pairs, wide), BF16),
-        stage,
+        pltpu.VMEM((frames // 2, 3, 2 * rows * pairs, LANES), F32),
     ]
     first_out = pl.pallas_call(
         functools.partial(first_block_kernel, bands),

time: 14.2 us -> 15.4 us (1.085)
  Pallas kernels: 8.29 us -> 9.5 us
    pallas_call x1, Pallas kernels: 3.97 us -> 5.17 us  [shards(): pl.pallas_call(functools.partial(last_kernel, bands), out_shape=result, i...]
  transfers between devices with their start and end apart: 3 -> 3, of which waited for: 1 -> 1; matrix products, arithmetic and copies ran while one was open for 0% -> 0% of each run, Pallas kernels for 31% -> 28%
where the time goes in v12:
time: 15.4 us; the launch traced here: 15.2 us
  Pallas kernels  9.5 us (62%)
  starting transfers between devices  4 us (26%)
  waiting for transfers between devices  0.88 us (6%)
  between operations  0.79 us (5%)
    pallas_call x1, Pallas kernels, shards(): pl.pallas_call(functools.partial(last_kernel, bands), out_shape=result, i...  5.17 us
    ppermute x3, starting transfers between devices, shift(): return lax.ppermute(sent, ('tm', 'space'), pairs_of)  4 us
    pallas_call x1, Pallas kernels, shards(): pl.pallas_call(functools.partial(earlier_kernel, bands, deep), out_shape=...  2.11 us
    pallas_call x1, Pallas kernels, shards(): pl.pallas_call(functools.partial(own_kernel, bands, deep), out_shape=jax....  1.82 us
    ppermute x3, waiting for transfers between devices, shift(): return lax.ppermute(sent, ('tm', 'space'), pairs_of)  0.88 us
    pallas_call x1, Pallas kernels, shards(): pl.pallas_call(functools.partial(norm_kernel, swap), out_shape=[jax.Shape...  0.37 us
  transfers between devices with their start and end apart: 3, of which 1 were waited for; matrix products, arithmetic and copies ran while one was open for 0% of the time, Pallas kernels for 28%

profile of v12, /device:TPU:16, one launch (start us, length us, event | category | flops | bytes accessed | tf_op | source)
XLA Modules:
  0.0 15.2 jit_solution(9806830918895673024)
XLA Ops:
  0.0 0.0 copy-start.2
  0.0 0.0 copy-start.3
  0.0 1.6 %collective-permute-start.2 = (bf16[4,4,6144]{2,1,0:T(4,128)(2,1)}, bf16[4,4,6144]{2,1,0:T(4,128)(2,1)S(1)}, u32[]{:S(2)}, u32[]{:S(2)}) collective-permute-start(bf16[4,4,6144]{2,1,0:T(4,128)(2,1)} %bitcast.14), channel_id=1, source_target_pairs={{0,4},{2,6},{4,8},{6,10},{8,12},{10,14},{12,0},{14,2},{1,5},{3,7},... | collective-permute-start | bytes 589832 | tf_op jit(solution)/shard_map/ppermute | solution.py:307
  1.6 0.0 copy-done.2
  1.6 0.0 copy-done.3
  1.6 0.0 copy-start
  1.6 0.4 %norm_and_cut.1 = (bf16[4,4,16,384]{3,2,1,0:T(8,128)(2,1)S(1)}, bf16[4,2,16,384]{3,2,1,0:T(8,128)(2,1)S(1)}) custom-call(f32[8,384]{1,0:T(8,128)S(1)} %lane_mask.1.mask, bf16[4,4,6144]{2,1,0:T(4,128)(2,1)S(1)} %bitcast.15, f32[1,192]{1,0:T(1,128)S(1)} %bitcast.18), custom_call_target="tpu_custom_call" | custom-call | flops 4294967296 | bytes 1048576 | tf_op jit(solution)/shard_map/norm_and_cut/pallas_call | solution.py:323
  2.0 0.0 copy-start.1
  2.0 0.0 copy-start.4
  2.0 0.0 copy-start.5
  2.0 0.0 copy-start.6
  2.0 1.6 %collective-permute-start = (bf16[4,2,16,384]{3,2,1,0:T(8,128)(2,1)S(1)}, bf16[4,2,16,384]{3,2,1,0:T(8,128)(2,1)S(1)}, u32[]{:S(2)}, u32[]{:S(2)}) collective-permute-start(bf16[4,2,16,384]{3,2,1,0:T(8,128)(2,1)S(1)} %get-tuple-element.7), channel_id=1, source_target_pairs={{0,2},{2,0},{4,6},{6,4},{8,10},{10,8},{12,14},{14,12},{1,3},{3,1},... | collective-permute-start | bytes 294920 | tf_op jit(solution)/shard_map/ppermute | solution.py:307
  3.6 0.9 %collective-permute-start.1 = (bf16[4,2,16,384]{3,2,1,0:T(8,128)(2,1)S(1)}, bf16[4,2,16,384]{3,2,1,0:T(8,128)(2,1)S(1)}, u32[]{:S(2)}, u32[]{:S(2)}) collective-permute-start(bf16[4,2,16,384]{3,2,1,0:T(8,128)(2,1)S(1)} %get-tuple-element.7), channel_id=1, source_target_pairs={{0,6},{2,4},{4,10},{6,8},{8,14},{10,12},{12,0},{14,2},{1,7},{3,5},... | collective-permute-start | bytes 294920 | tf_op jit(solution)/shard_map/ppermute | solution.py:307
  5.1 0.0 copy-done
  5.1 1.8 %conv_one_own.1.from_own = f32[2,4,5,16,192]{4,3,2,1,0:T(8,128)S(1)} custom-call(s32[1]{0:T(128)S(6)} %copy.9.count, bf16[4,4,16,384]{3,2,1,0:T(8,128)(2,1)S(1)} %get-tuple-element.8.normed, bf16[3,3,576,192]{3,2,1,0:T(8,128)(2,1)S(1)} %bitcast.8), custom_call_target="tpu_custom_call" | custom-call | flops 1048576 | bytes 65536 | tf_op jit(solution)/shard_map/conv_one_own/pallas_call | solution.py:349
  7.0 0.0 collective-permute-done.above.below
  7.0 0.0 copy-done.1
  7.0 0.0 copy-done.4
  7.0 0.0 copy-done.5
  7.0 0.0 copy-done.6
  7.0 0.9 %collective-permute-done.2.earlier = bf16[4,4,6144]{2,1,0:T(4,128)(2,1)S(1)} collective-permute-done((bf16[4,4,6144]{2,1,0:T(4,128)(2,1)}, bf16[4,4,6144]{2,1,0:T(4,128)(2,1)S(1)}, u32[]{:S(2)}, u32[]{:S(2)}) %collective-permute-start.2) | collective-permute-done | bytes 196640 | tf_op jit(solution)/shard_map/ppermute | solution.py:307
  7.9 2.1 %conv_one_earlier.1.from_earlier = f32[2,4,5,16,192]{4,3,2,1,0:T(8,128)S(1)} custom-call(s32[1]{0:T(128)S(6)} %copy.9.count, f32[8,384]{1,0:T(8,128)S(1)} %lane_mask.1.mask, bf16[4,4,6144]{2,1,0:T(4,128)(2,1)S(1)} %collective-permute-done.2.earlier, f32[1,192]{1,0:T(1,128)S(1)} %bitcast.19, bf16[3,3,576,192]{3,2,1,0:T(8,128)(2,1)S(1)} %bitcast.10, ...), custom_call_target="tpu_custom_call" | custom-call | flops 1048576 | bytes 65536 | tf_op jit(solution)/shard_map/conv_one_earlier/pallas_call | solution.py:379
  10.0 0.0 collective-permute-done.1.far_above.far_below
  10.0 5.2 %last.1 = bf16[4,4,6144]{2,1,0:T(4,128)(2,1)} custom-call(s32[1]{0:T(128)S(6)} %copy.9.count, bf16[4,4,6144]{2,1,0:T(4,128)(2,1)S(1)} %bitcast.17, bf16[4,2,16,384]{3,2,1,0:T(8,128)(2,1)S(1)} %collective-permute-done.above.below, bf16[4,2,16,384]{3,2,1,0:T(8,128)(2,1)S(1)} %collective-permute-done.above.below, ...), custom_call_target="tpu_custom_call" | custom-call | flops 4294967296 | bytes 6291456 | tf_op jit(solution)/shard_map/last/pallas_call | solution.py:389
  (2 shorter events, 0.0 us)
Async XLA Ops:
  0.0 1.6 %copy-start.2 = (bf16[1,4,4,6144]{3,2,1,0:T(4,128)(2,1)S(1)}, bf16[1,4,4,6144]{3,2,1,0:T(4,128)(2,1)}, u32[]{:S(2)}) copy-start(bf16[1,4,4,6144]{3,2,1,0:T(4,128)(2,1)} %param.8) | copy-start | bytes 589828
  0.0 1.6 %copy-start.3 = (f32[192]{0:T(256)S(1)}, f32[192]{0:T(256)}, u32[]{:S(2)}) copy-start(f32[192]{0:T(256)} %param.10) | copy-start | bytes 2308
  0.0 7.9 %collective-permute-start.2 = (bf16[4,4,6144]{2,1,0:T(4,128)(2,1)}, bf16[4,4,6144]{2,1,0:T(4,128)(2,1)S(1)}, u32[]{:S(2)}, u32[]{:S(2)}) collective-permute-start(bf16[4,4,6144]{2,1,0:T(4,128)(2,1)} %bitcast.14), channel_id=1, source_target_pairs={{0,4},{2,6},{4,8},{6,10},{8,12},{10,14},{12,0},{14,2},{1,5},{3,7},... | collective-permute-start | bytes 589832 | tf_op jit(solution)/shard_map/ppermute | solution.py:307
  1.6 3.5 %copy-start = (bf16[3,3,3,192,192]{4,3,2,1,0:T(8,128)(2,1)S(1)}, bf16[3,3,3,192,192]{4,3,2,1,0:T(8,128)(2,1)}, u32[]{:S(2)}) copy-start(bf16[3,3,3,192,192]{4,3,2,1,0:T(8,128)(2,1)} %param.12) | copy-start | bytes 5971972
  2.0 5.0 %copy-start.1 = (bf16[3,3,3,192,192]{4,3,2,1,0:T(8,128)(2,1)S(1)}, bf16[3,3,3,192,192]{4,3,2,1,0:T(8,128)(2,1)}, u32[]{:S(2)}) copy-start(bf16[3,3,3,192,192]{4,3,2,1,0:T(8,128)(2,1)} %param.15) | copy-start | bytes 5971972
  2.0 5.0 %copy-start.4 = (f32[192]{0:T(256)S(1)}, f32[192]{0:T(256)}, u32[]{:S(2)}) copy-start(f32[192]{0:T(256)} %param.11) | copy-start | bytes 2308
  2.0 5.0 %copy-start.5 = (f32[192]{0:T(256)S(1)}, f32[192]{0:T(256)}, u32[]{:S(2)}) copy-start(f32[192]{0:T(256)} %param.13) | copy-start | bytes 2308
  2.0 5.0 %copy-start.6 = (f32[192]{0:T(256)S(1)}, f32[192]{0:T(256)}, u32[]{:S(2)}) copy-start(f32[192]{0:T(256)} %param.14) | copy-start | bytes 2308
  2.0 4.9 %collective-permute-start = (bf16[4,2,16,384]{3,2,1,0:T(8,128)(2,1)S(1)}, bf16[4,2,16,384]{3,2,1,0:T(8,128)(2,1)S(1)}, u32[]{:S(2)}, u32[]{:S(2)}) collective-permute-start(bf16[4,2,16,384]{3,2,1,0:T(8,128)(2,1)S(1)} %get-tuple-element.7), channel_id=1, source_target_pairs={{0,2},{2,0},{4,6},{6,4},{8,10},{10,8},{12,14},{14,12},{1,3},{3,1},... | collective-permute-start | bytes 294920 | tf_op jit(solution)/shard_map/ppermute | solution.py:307
  3.6 6.4 %collective-permute-start.1 = (bf16[4,2,16,384]{3,2,1,0:T(8,128)(2,1)S(1)}, bf16[4,2,16,384]{3,2,1,0:T(8,128)(2,1)S(1)}, u32[]{:S(2)}, u32[]{:S(2)}) collective-permute-start(bf16[4,2,16,384]{3,2,1,0:T(8,128)(2,1)S(1)} %get-tuple-element.7), channel_id=1, source_target_pairs={{0,6},{2,4},{4,10},{6,8},{8,14},{10,12},{12,0},{14,2},{1,7},{3,5},... | collective-permute-start | bytes 294920 | tf_op jit(solution)/shard_map/ppermute | solution.py:307

commit v13 on v9

--- a/solution.py
+++ b/solution.py
@@ -31,32 +31,31 @@
     return jnp.concatenate([ref[...], ref[...]], axis=1)
 
 
-def norm_block(block, gain_wide, first, stage, store, pairs):
-    frames, rows = block.shape[0], block.shape[1]
+def norm_frames(block, f, gain_wide, first, stage, store, pairs):
+    rows = block.shape[1]
     wide = gain_wide.shape[1]
-    for f in range(0, frames, 2):
-        for p in range(pairs):
-            lanes = pl.ds(p * wide, wide)
-            t = jnp.concatenate([block[f + n, :, lanes].astype(F32) for n in range(2)], axis=0)
-            y = norm_silu_pair(t, gain_wide, first, wide // 2)
-            for k in range(3):
-                at = pl.ds(f * rows * pairs + p, 2 * rows, stride=pairs)
-                stage[k, at, :] = y[:, k * LANES : (k + 1) * LANES]
-        for n in range(2):
-            for r in range(rows):
-                at = pl.ds(((f + n) * rows + r) * pairs, pairs)
-                store(f + n, r, [stage[k, at, :].astype(BF16) for k in range(3)])
+    for p in range(pairs):
+        lanes = pl.ds(p * wide, wide)
+        t = jnp.concatenate([block[f + n, :, lanes].astype(F32) for n in range(2)], axis=0)
+        y = norm_silu_pair(t, gain_wide, first, wide // 2)
+        for k in range(3):
+            stage[k, pl.ds(p, 2 * rows, stride=pairs), :] = y[:, k * LANES : (k + 1) * LANES]
+    for n in range(2):
+        for r in range(rows):
+            at = pl.ds((n * rows + r) * pairs, pairs)
+            store(f + n, r, [stage[k, at, :].astype(BF16) for k in range(3)])
 
 
 def norm_kernel(swap, mask, block, gain, normed, *rest):
-    sent, stage = rest[:-1], rest[-1]
-    rows, pairs = normed.shape[1], normed.shape[2]
+    frames, rows, pairs, _ = normed.shape
+    sent, stages = rest[: -(frames // 2)], rest[-(frames // 2) :]
 
     def store(f, r, parts):
         for k in range(3):
             normed[f, r, :, k * LANES : (k + 1) * LANES] = parts[k]
 
-    norm_block(block, twice(gain), mask[...] > 0.5, stage, store, pairs)
+    for f in range(0, frames, 2):
+        norm_frames(block, f, twice(gain), mask[...] > 0.5, stages[f // 2], store, pairs)
     if swap:
         first = (rows - 2) * (1 - lax.axis_index("space"))
         sent[0][...] = normed[:, pl.ds(first, 2)]
@@ -107,66 +106,71 @@
     return mine[0] + left, mine[1] + right
 
 
-def own_kernel(bands, deep, count, normed, weight, total, window):
+def own_kernel(bands, deep, count, normed, weight, total, *window):
     frames, rows, pairs, wide = normed.shape
     tm, space = lax.axis_index("tm"), lax.axis_index("space")
     nothing = jnp.zeros((pairs, wide), BF16)
-    top = clear_rims(window, bands, space, rows, range(1, frames + 1))
-    window[0] = jnp.zeros(window.shape[1:], BF16)
+    top = clear_rims(window[1:], bands, space, rows)
+    window[0][...] = jnp.zeros(window[0].shape, BF16)
     for f in range(frames):
         good = tm * frames + f < count[0]
         for r in range(rows):
-            window[f + 1, top + r] = jnp.where(good, normed[f, r], nothing)
-    late = conv([window.at[f] for f in range(frames + 1)], weight, 1, frames - 2, deep, (0, 1, 2), wide // 2)
-    soon = conv([window.at[f] for f in range(frames + 1)], weight, 0, 2, deep, (1, 2), wide // 2)
+            window[f + 1][top + r] = jnp.where(good, normed[f, r], nothing)
+    late = conv(window, weight, 1, frames - 2, deep, (0, 1, 2), wide // 2)
+    soon = conv(window, weight, 0, 2, deep, (1, 2), wide // 2)
     for q in range(2):
         total[q, 0:2] = soon[q].reshape(2, *total.shape[2:])
         total[q, 2:] = late[q].reshape(frames - 2, *total.shape[2:])
 
 
-def clear_rims(window, bands, space, rows, at):
-    nothing = jnp.zeros(window.shape[2:], BF16)
-    for f in at:
+def clear_rims(window, bands, space, rows):
+    for part in window:
+        nothing = jnp.zeros(part.shape[1:], BF16)
         if bands == 2:
-            window[f, (rows + 2) * space] = nothing
+            part[(rows + 2) * space] = nothing
             for r in range(2):
-                window[f, (rows + 1) * (1 - space) + r] = nothing
+                part[(rows + 1) * (1 - space) + r] = nothing
         else:
             for r in range(2):
-                window[f, r] = nothing
-                window[f, rows + 2 + r] = nothing
+                part[r] = nothing
+                part[rows + 2 + r] = nothing
     return 1 + space if bands == 2 else 2
 
 
-def earlier_kernel(
-    bands, deep, count, mask, earlier, gain, weight, after, total, window, stage
-):
+def earlier_kernel(bands, deep, count, mask, earlier, gain, weight, after, total, *scratch):
     frames, rows = earlier.shape[0], earlier.shape[1]
-    pairs, wide = window.shape[2], window.shape[3]
+    window, stages = scratch[: frames + 1], scratch[frames + 1 :]
+    pairs, wide = window[0].shape[1:]
     tm, space = lax.axis_index("tm"), lax.axis_index("space")
 
     @pl.when(tm > 0)
     def _():
-        top = clear_rims(window, bands, space, rows, range(frames))
-        window[frames] = jnp.zeros(window.shape[1:], BF16)
+        top = clear_rims(window[:frames], bands, space, rows)
+        window[frames][...] = jnp.zeros(window[frames].shape, BF16)
 
         def store(f, r, parts):
             good = (tm - 1) * frames + f < count[0]
             for k in range(3):
                 part = jnp.where(good, parts[k], jnp.zeros_like(parts[k]))
-                window[f, top + r, :, k * LANES : (k + 1) * LANES] = part
-
-        norm_block(earlier, twice(gain), mask[...] > 0.5, stage, store, pairs)
-        soon = conv([window.at[f] for f in range(frames + 1)], weight, 0, frames - 2, deep, (0, 1, 2), wide // 2)
-        late = conv([window.at[f] for f in range(frames + 1)], weight, frames - 2, 2, deep, (0, 1), wide // 2)
+                window[f][top + r, :, k * LANES : (k + 1) * LANES] = part
+
+        def norm(f):
+            norm_frames(earlier, f, twice(gain), mask[...] > 0.5, stages[f // 2], store, pairs)
+
+        norm(frames - 2)
+        late = conv(window, weight, frames - 2, 2, deep, (0, 1), wide // 2)
+        for f in range(0, frames - 2, 2):
+            norm(f)
+        for q in range(2):
+            total[q, frames - 2 :] = late[q].reshape(2, *total.shape[2:])
+        soon = conv(window, weight, 0, frames - 2, deep, (0, 1, 2), wide // 2)
         for q in range(2):
             total[q, 0 : frames - 2] = soon[q].reshape(frames - 2, *total.shape[2:])
-            total[q, frames - 2 :] = late[q].reshape(2, *total.shape[2:])
-
-
-def add_rims(total, near, far, weight, side, keep, channels):
+
+
+def add_rims(total, near, far, weight, side, keep, channels, wanted):
     frames, pairs, wide = near.shape[0], near.shape[2], near.shape[3]
-    deep = total.shape[2]
+    deep = total[0].shape[1]
     low = (deep - 2) * side
     halo = (deep - 1) * side
     nothing = jnp.zeros((pairs, wide), BF16)
@@ -175,25 +179,27 @@
         ref, at = (far, f) if f < frames else (near, f - frames)
         return jnp.where(keep(f), ref[at, r], nothing)
 
-    rows = [[row(f, r) for r in range(2)] for f in range(2 * frames)]
-    inner = [row(f, 1 - side) for f in range(2 * frames)]
-    span = frames + 2
-    parts = [
-        jnp.concatenate([x for f in range(span) for x in rows[f + a]], axis=0) for a in range(3)
-    ]
+    span = len(wanted)
+    rows = {f: [row(f, r) for r in range(2)] for f in range(wanted[0], wanted[-1] + 3)}
+    inner = {f: row(f, 1 - side) for f in rows}
+    parts = [jnp.concatenate([x for h in wanted for x in rows[h + a]], axis=0) for a in range(3)]
     added = add_moved(*products(parts, [weight[a, 2 * side] for a in range(3)], channels), pairs)
     for q in range(2):
-        total[q, :, pl.ds(low, 2)] += added[q].reshape(span, 2, pairs, channels)
-    parts = [jnp.concatenate([inner[f + a] for f in range(span)], axis=0) for a in range(3)]
+        both = added[q].reshape(span, 2, pairs, channels)
+        for n, h in enumerate(wanted):
+            total[h][q, pl.ds(low, 2)] += both[n]
+    parts = [jnp.concatenate([inner[h + a] for h in wanted], axis=0) for a in range(3)]
     added = add_moved(*products(parts, [weight[a, 1] for a in range(3)], channels), pairs)
     for q in range(2):
-        total[q, :, halo] += added[q].reshape(span, pairs, channels)
-
-
-def finish(bands, count, own, near, far, bias, weight, gain_two, bias_two, weight_two, out, total, hidden, final):
+        one = added[q].reshape(span, pairs, channels)
+        for n, h in enumerate(wanted):
+            total[h][q, halo] += one[n]
+
+
+def finish(bands, count, own, near, far, bias, weight, gain_two, bias_two, weight_two, out, total, hidden, final, ready):
     frames, rows, pairs, wide = near[0].shape[0], own.shape[1], near[0].shape[2], near[0].shape[3]
     channels = wide // 2
-    deep = total.shape[2]
+    deep = total[0].shape[1]
     tm, space = lax.axis_index("tm"), lax.axis_index("space")
     fill = deep * pairs
 
@@ -201,13 +207,14 @@
         at = (tm - 1) * frames + f
         return (at >= 0) & (at < count[0])
 
-    if bands == 2:
-        add_rims(total, near[0], far[0], weight, 1 - space, valid, channels)
-    else:
-        above = lambda f: valid(f) & (space > 0)
-        below = lambda f: valid(f) & (space < bands - 1)
-        add_rims(total, near[0], far[0], weight, 0, above, channels)
-        add_rims(total, near[1], far[1], weight, 1, below, channels)
+    def rims(wanted):
+        if bands == 2:
+            add_rims(total, near[0], far[0], weight, 1 - space, valid, channels, wanted)
+        else:
+            above = lambda f: valid(f) & (space > 0)
+            below = lambda f: valid(f) & (space < bands - 1)
+            add_rims(total, near[0], far[0], weight, 0, above, channels, wanted)
+            add_rims(total, near[1], far[1], weight, 1, below, channels, wanted)
 
     start = (1 - space) if bands == 2 else 0
     row = lax.broadcasted_iota(jnp.int32, (fill, 1), 0) // pairs + (space * rows - 1 + start)
@@ -217,7 +224,7 @@
 
     def norm_hidden(h):
         good = row_ok & valid(frames + h - 2)
-        t = jnp.concatenate([total[q, h].reshape(fill, channels) for q in range(2)], axis=1)
+        t = jnp.concatenate([total[h][q].reshape(fill, channels) for q in range(2)], axis=1)
         t = jnp.where(good, t + bias_wide, 0.0).astype(BF16).astype(F32)
         y = norm_silu_pair(t, gain_wide, first_lanes, channels).astype(BF16)
         hidden[h][0] = jnp.zeros((pairs, wide), BF16)
@@ -242,6 +249,9 @@
                     out[f + n, :, lanes] = jnp.where(good[n], value, 0.0).astype(BF16)
 
     bias_two_wide = twice(bias_two)
+    rims(range(4))
+    for f in range(2, frames, 2):
+        rims(range(f + 2, f + 4))
     for h in range(4):
         norm_hidden(h)
     second_conv(0)
@@ -249,49 +259,66 @@
         norm_hidden(f + 2)
         norm_hidden(f + 3)
         emit(f - 2)
+        ready(f - 2)
         second_conv(f)
     emit(frames - 2)
+    ready(frames - 2)
 
 
 def first_block_kernel(
     bands, count, own, above, below, from_own, bias, weight, gain_two, bias_two, weight_two,
-    out, total, *scratch,
+    out, *scratch,
 ):
-    frames = own.shape[0]
-    hidden, final = scratch[: frames + 2], scratch[frames + 2 :]
+    total, hidden, final = split(scratch, own.shape[0])
 
     @pl.when(lax.axis_index("tm") == 0)
     def _():
-        total[:, :2] = jnp.zeros((2, 2, *total.shape[2:]), F32)
-        total[:, 2:] = from_own[...]
+        for h, part in enumerate(total):
+            part[...] = jnp.zeros(part.shape, F32) if h < 2 else from_own[:, h - 2]
         near = (above, below)
         finish(
             bands, count, own, near, near, bias, weight, gain_two, bias_two, weight_two,
-            out, total, hidden, final,
+            out, total, hidden, final, lambda f: None,
         )
+
+
+def split(scratch, frames):
+    return scratch[: frames + 2], scratch[frames + 2 : 2 * frames + 4], scratch[2 * frames + 4 :]
 
 
 def last_kernel(
     bands, count, own, above, below, far_above, far_below, from_own, from_earlier, first_out, bias,
-    weight, gain_two, bias_two, weight_two, out, total, *scratch,
+    weight, gain_two, bias_two, weight_two, out, result, sems, *scratch,
 ):
     frames = own.shape[0]
-    hidden, final = scratch[: frames + 2], scratch[frames + 2 :]
+    total, hidden, final = split(scratch, frames)
     tm = lax.axis_index("tm")
 
     @pl.when(tm == 0)
     def _():
-        out[...] = first_out[...]
+        copy = pltpu.make_async_copy(first_out, out, sems.at[0])
+        copy.start()
+        copy.wait()
 
     @pl.when(tm > 0)
     def _():
-        total[:, :2] = from_earlier[:, :2]
-        total[:, 2:frames] = from_own[:, : frames - 2] + from_earlier[:, 2:]
-        total[:, frames:] = from_own[:, frames - 2 :]
+        for h, part in enumerate(total):
+            if h < 2:
+                part[...] = from_earlier[:, h]
+            elif h < frames:
+                part[...] = from_own[:, h - 2] + from_earlier[:, h]
+            else:
+                part[...] = from_own[:, h - 2]
+        copies = [
+            pltpu.make_async_copy(result.at[pl.ds(f, 2)], out.at[pl.ds(f, 2)], sems.at[f // 2])
+            for f in range(0, frames, 2)
+        ]
         finish(
             bands, count, own, (above, below), (far_above, far_below), bias, weight, gain_two,
-            bias_two, weight_two, out, total, hidden, final,
+            bias_two, weight_two, result, total, hidden, final, lambda f: copies[f // 2].start(),
         )
+        for copy in copies:
+            copy.wait()
 
 
 def shards(latents, counts, gain_first, bias_first, weight_first, gain_second, bias_second, weight_second):
@@ -316,6 +343,7 @@
     swap = bands == 2
     rims = 1 if swap else 2
     rim = jax.ShapeDtypeStruct((frames, 2, pairs, wide), BF16)
+    stages = [pltpu.VMEM((3, 2 * rows * pairs, LANES), F32)] * (frames // 2)
     mask = pl.pallas_call(
         functools.partial(mask_kernel, channels),
         out_shape=jax.ShapeDtypeStruct((2 * rows, wide), F32),
@@ -329,7 +357,7 @@
         out_shape=[jax.ShapeDtypeStruct((frames, rows, pairs, wide), BF16)] + [rim] * rims,
         in_specs=[vmem] * 3,
         out_specs=[vmem] * (1 + rims),
-        scratch_shapes=[pltpu.VMEM((3, frames * rows * pairs, LANES), F32)],
+        scratch_shapes=stages,
         compiler_params=params,
         cost_estimate=pl.CostEstimate(flops=4 << 30, bytes_accessed=1 << 20, transcendentals=0),
         name="norm_and_cut",
@@ -347,15 +375,14 @@
     first_weight = weight_first.reshape(3, 3, 3 * channels, channels)
     second_weight = weight_second.reshape(3, 3, 3 * channels, channels)
     share = (2, frames, deep, pairs, channels)
-    window = pltpu.VMEM((frames + 1, deep + 2, pairs, wide), BF16)
-    stage = pltpu.VMEM((3, frames * rows * pairs, LANES), F32)
+    window = [pltpu.VMEM((deep + 2, pairs, wide), BF16)] * (frames + 1)
     cost = pl.CostEstimate(flops=1 << 20, bytes_accessed=1 << 16, transcendentals=0)
     from_own = pl.pallas_call(
         functools.partial(own_kernel, bands, deep),
         out_shape=jax.ShapeDtypeStruct(share, F32),
         in_specs=[smem] + [vmem] * 2,
         out_specs=vmem,
-        scratch_shapes=[window],
+        scratch_shapes=window,
         compiler_params=params,
         cost_estimate=cost,
         name="conv_one_own",
@@ -365,11 +392,11 @@
         gain_second.reshape(1, channels), bias_second.reshape(1, channels), second_weight,
     )
     result = jax.ShapeDtypeStruct((frames, rows, flat), BF16)
-    scratch = [
-        pltpu.VMEM((2, frames + 2, deep, pairs, channels), F32),
-        *[pltpu.VMEM((rows + 2, pairs, wide), BF16)] * (frames + 2),
-        *[pltpu.VMEM((3, 2 * rows * pairs, LANES), F32)] * (frames // 2),
-    ]
+    scratch = (
+        [pltpu.VMEM((2, deep, pairs, channels), F32)] * (frames + 2)
+        + [pltpu.VMEM((rows + 2, pairs, wide), BF16)] * (frames + 2)
+        + stages
+    )
     first_out = pl.pallas_call(
         functools.partial(first_block_kernel, bands),
         out_shape=result,
@@ -385,7 +412,7 @@
         out_shape=jax.ShapeDtypeStruct(share, F32),
         in_specs=[smem] + [vmem] * 5,
         out_specs=vmem,
-        scratch_shapes=[window, stage],
+        scratch_shapes=window + stages,
         compiler_params=params,
         cost_estimate=cost,
         name="conv_one_earlier",
@@ -394,8 +421,10 @@
         functools.partial(last_kernel, bands),
         out_shape=result,
         in_specs=[smem] + [vmem] * 13,
-        out_specs=vmem,
-        scratch_shapes=scratch,
+        out_specs=pl.BlockSpec(memory_space=pl.ANY),
+        scratch_shapes=[
+            pltpu.VMEM((frames, rows, flat), BF16), pltpu.SemaphoreType.DMA((frames // 2,))
+        ] + scratch,
         compiler_params=params,
         cost_estimate=pl.CostEstimate(flops=4 << 30, bytes_accessed=6 << 20, transcendentals=0),
         name="last",

time: 14.2 us -> 14.1 us (level)
  Pallas kernels: 8.36 us -> 8.18 us
where the time goes in v13:
time: 14.1 us; the launch traced here: 13.9 us
  Pallas kernels  8.18 us (58%)
  starting transfers between devices  4 us (28%)
  waiting for transfers between devices  0.93 us (7%)
  between operations  0.78 us (6%)
    ppermute x3, starting transfers between devices, shift(): return lax.ppermute(sent, ('tm', 'space'), pairs_of)  4 us
    pallas_call x1, Pallas kernels, shards(): pl.pallas_call(functools.partial(last_kernel, bands), out_shape=result, i...  3.94 us
    pallas_call x1, Pallas kernels, shards(): pl.pallas_call(functools.partial(earlier_kernel, bands, deep), out_shape=...  2.07 us
    pallas_call x1, Pallas kernels, shards(): pl.pallas_call(functools.partial(own_kernel, bands, deep), out_shape=jax....  1.8 us
    ppermute x3, waiting for transfers between devices, shift(): return lax.ppermute(sent, ('tm', 'space'), pairs_of)  0.93 us
    pallas_call x1, Pallas kernels, shards(): pl.pallas_call(functools.partial(norm_kernel, swap), out_shape=[jax.Shape...  0.35 us
  transfers between devices with their start and end apart: 3, of which 1 were waited for; matrix products, arithmetic and copies ran while one was open for 0% of the time, Pallas kernels for 31%

profile of v13, /device:TPU:16, one launch (start us, length us, event | category | flops | bytes accessed | tf_op | source)
XLA Modules:
  0.0 13.9 jit_solution(6443587496463858848)
XLA Ops:
  0.0 0.0 copy-start.2
  0.0 0.0 copy-start.3
  0.0 1.6 %collective-permute-start.2 = (bf16[4,4,6144]{2,1,0:T(4,128)(2,1)}, bf16[4,4,6144]{2,1,0:T(4,128)(2,1)S(1)}, u32[]{:S(2)}, u32[]{:S(2)}) collective-permute-start(bf16[4,4,6144]{2,1,0:T(4,128)(2,1)} %bitcast.14), channel_id=1, source_target_pairs={{0,4},{2,6},{4,8},{6,10},{8,12},{10,14},{12,0},{14,2},{1,5},{3,7},... | collective-permute-start | bytes 589832 | tf_op jit(solution)/shard_map/ppermute | solution.py:338
  1.6 0.0 copy-done.2
  1.6 0.0 copy-done.3
  1.6 0.0 copy-start
  1.6 0.4 %norm_and_cut.1 = (bf16[4,4,16,384]{3,2,1,0:T(8,128)(2,1)S(1)}, bf16[4,2,16,384]{3,2,1,0:T(8,128)(2,1)S(1)}) custom-call(f32[8,384]{1,0:T(8,128)S(1)} %lane_mask.1.mask, bf16[4,4,6144]{2,1,0:T(4,128)(2,1)S(1)} %bitcast.15, f32[1,192]{1,0:T(1,128)S(1)} %bitcast.18), custom_call_target="tpu_custom_call" | custom-call | flops 4294967296 | bytes 1048576 | tf_op jit(solution)/shard_map/norm_and_cut/pallas_call | solution.py:355
  2.0 0.0 copy-start.1
  2.0 0.0 copy-start.4
  2.0 0.0 copy-start.5
  2.0 0.0 copy-start.6
  2.0 1.6 %collective-permute-start = (bf16[4,2,16,384]{3,2,1,0:T(8,128)(2,1)S(1)}, bf16[4,2,16,384]{3,2,1,0:T(8,128)(2,1)S(1)}, u32[]{:S(2)}, u32[]{:S(2)}) collective-permute-start(bf16[4,2,16,384]{3,2,1,0:T(8,128)(2,1)S(1)} %get-tuple-element.7), channel_id=1, source_target_pairs={{0,2},{2,0},{4,6},{6,4},{8,10},{10,8},{12,14},{14,12},{1,3},{3,1},... | collective-permute-start | bytes 294920 | tf_op jit(solution)/shard_map/ppermute | solution.py:338
  3.6 0.9 %collective-permute-start.1 = (bf16[4,2,16,384]{3,2,1,0:T(8,128)(2,1)S(1)}, bf16[4,2,16,384]{3,2,1,0:T(8,128)(2,1)S(1)}, u32[]{:S(2)}, u32[]{:S(2)}) collective-permute-start(bf16[4,2,16,384]{3,2,1,0:T(8,128)(2,1)S(1)} %get-tuple-element.7), channel_id=1, source_target_pairs={{0,6},{2,4},{4,10},{6,8},{8,14},{10,12},{12,0},{14,2},{1,7},{3,5},... | collective-permute-start | bytes 294920 | tf_op jit(solution)/shard_map/ppermute | solution.py:338
  5.1 0.0 copy-done
  5.1 1.8 %conv_one_own.1.from_own = f32[2,4,5,16,192]{4,3,2,1,0:T(8,128)S(1)} custom-call(s32[1]{0:T(128)S(6)} %copy.9.count, bf16[4,4,16,384]{3,2,1,0:T(8,128)(2,1)S(1)} %get-tuple-element.8.normed, bf16[3,3,576,192]{3,2,1,0:T(8,128)(2,1)S(1)} %bitcast.8), custom_call_target="tpu_custom_call" | custom-call | flops 1048576 | bytes 65536 | tf_op jit(solution)/shard_map/conv_one_own/pallas_call | solution.py:380
  6.9 0.0 collective-permute-done.above.below
  6.9 0.0 copy-done.1
  6.9 0.0 copy-done.4
  6.9 0.0 copy-done.5
  6.9 0.0 copy-done.6
  7.0 0.9 %collective-permute-done.2.earlier = bf16[4,4,6144]{2,1,0:T(4,128)(2,1)S(1)} collective-permute-done((bf16[4,4,6144]{2,1,0:T(4,128)(2,1)}, bf16[4,4,6144]{2,1,0:T(4,128)(2,1)S(1)}, u32[]{:S(2)}, u32[]{:S(2)}) %collective-permute-start.2) | collective-permute-done | bytes 196640 | tf_op jit(solution)/shard_map/ppermute | solution.py:338
  7.9 2.1 %conv_one_earlier.1.from_earlier = f32[2,4,5,16,192]{4,3,2,1,0:T(8,128)S(1)} custom-call(s32[1]{0:T(128)S(6)} %copy.9.count, f32[8,384]{1,0:T(8,128)S(1)} %lane_mask.1.mask, bf16[4,4,6144]{2,1,0:T(4,128)(2,1)S(1)} %collective-permute-done.2.earlier, f32[1,192]{1,0:T(1,128)S(1)} %bitcast.19, bf16[3,3,576,192]{3,2,1,0:T(8,128)(2,1)S(1)} %bitcast.10, ...), custom_call_target="tpu_custom_call" | custom-call | flops 1048576 | bytes 65536 | tf_op jit(solution)/shard_map/conv_one_earlier/pallas_call | solution.py:410
  10.0 0.0 collective-permute-done.1.far_above.far_below
  10.0 3.9 %last.1 = bf16[4,4,6144]{2,1,0:T(4,128)(2,1)} custom-call(s32[1]{0:T(128)S(6)} %copy.9.count, bf16[4,4,6144]{2,1,0:T(4,128)(2,1)S(1)} %bitcast.17, bf16[4,2,16,384]{3,2,1,0:T(8,128)(2,1)S(1)} %collective-permute-done.above.below, bf16[4,2,16,384]{3,2,1,0:T(8,128)(2,1)S(1)} %collective-permute-done.above.below, ...), custom_call_target="tpu_custom_call" | custom-call | flops 4294967296 | bytes 6291456 | tf_op jit(solution)/shard_map/last/pallas_call | solution.py:420
  (2 shorter events, 0.0 us)
Async XLA Ops:
  0.0 1.6 %copy-start.2 = (bf16[1,4,4,6144]{3,2,1,0:T(4,128)(2,1)S(1)}, bf16[1,4,4,6144]{3,2,1,0:T(4,128)(2,1)}, u32[]{:S(2)}) copy-start(bf16[1,4,4,6144]{3,2,1,0:T(4,128)(2,1)} %param.8) | copy-start | bytes 589828
  0.0 1.6 %copy-start.3 = (f32[192]{0:T(256)S(1)}, f32[192]{0:T(256)}, u32[]{:S(2)}) copy-start(f32[192]{0:T(256)} %param.10) | copy-start | bytes 2308
  0.0 7.9 %collective-permute-start.2 = (bf16[4,4,6144]{2,1,0:T(4,128)(2,1)}, bf16[4,4,6144]{2,1,0:T(4,128)(2,1)S(1)}, u32[]{:S(2)}, u32[]{:S(2)}) collective-permute-start(bf16[4,4,6144]{2,1,0:T(4,128)(2,1)} %bitcast.14), channel_id=1, source_target_pairs={{0,4},{2,6},{4,8},{6,10},{8,12},{10,14},{12,0},{14,2},{1,5},{3,7},... | collective-permute-start | bytes 589832 | tf_op jit(solution)/shard_map/ppermute | solution.py:338
  1.6 3.5 %copy-start = (bf16[3,3,3,192,192]{4,3,2,1,0:T(8,128)(2,1)S(1)}, bf16[3,3,3,192,192]{4,3,2,1,0:T(8,128)(2,1)}, u32[]{:S(2)}) copy-start(bf16[3,3,3,192,192]{4,3,2,1,0:T(8,128)(2,1)} %param.12) | copy-start | bytes 5971972
  2.0 5.0 %copy-start.1 = (bf16[3,3,3,192,192]{4,3,2,1,0:T(8,128)(2,1)S(1)}, bf16[3,3,3,192,192]{4,3,2,1,0:T(8,128)(2,1)}, u32[]{:S(2)}) copy-start(bf16[3,3,3,192,192]{4,3,2,1,0:T(8,128)(2,1)} %param.15) | copy-start | bytes 5971972
  2.0 5.0 %copy-start.4 = (f32[192]{0:T(256)S(1)}, f32[192]{0:T(256)}, u32[]{:S(2)}) copy-start(f32[192]{0:T(256)} %param.11) | copy-start | bytes 2308
  2.0 5.0 %copy-start.5 = (f32[192]{0:T(256)S(1)}, f32[192]{0:T(256)}, u32[]{:S(2)}) copy-start(f32[192]{0:T(256)} %param.13) | copy-start | bytes 2308
  2.0 5.0 %copy-start.6 = (f32[192]{0:T(256)S(1)}, f32[192]{0:T(256)}, u32[]{:S(2)}) copy-start(f32[192]{0:T(256)} %param.14) | copy-start | bytes 2308
  2.0 4.9 %collective-permute-start = (bf16[4,2,16,384]{3,2,1,0:T(8,128)(2,1)S(1)}, bf16[4,2,16,384]{3,2,1,0:T(8,128)(2,1)S(1)}, u32[]{:S(2)}, u32[]{:S(2)}) collective-permute-start(bf16[4,2,16,384]{3,2,1,0:T(8,128)(2,1)S(1)} %get-tuple-element.7), channel_id=1, source_target_pairs={{0,2},{2,0},{4,6},{6,4},{8,10},{10,8},{12,14},{14,12},{1,3},{3,1},... | collective-permute-start | bytes 294920 | tf_op jit(solution)/shard_map/ppermute | solution.py:338
  3.6 6.4 %collective-permute-start.1 = (bf16[4,2,16,384]{3,2,1,0:T(8,128)(2,1)S(1)}, bf16[4,2,16,384]{3,2,1,0:T(8,128)(2,1)S(1)}, u32[]{:S(2)}, u32[]{:S(2)}) collective-permute-start(bf16[4,2,16,384]{3,2,1,0:T(8,128)(2,1)S(1)} %get-tuple-element.7), channel_id=1, source_target_pairs={{0,6},{2,4},{4,10},{6,8},{8,14},{10,12},{12,0},{14,2},{1,7},{3,5},... | collective-permute-start | bytes 294920 | tf_op jit(solution)/shard_map/ppermute | solution.py:338

commit v14 on v13

--- a/solution.py
+++ b/solution.py
@@ -85,17 +85,48 @@
     return mine, moved
 
 
-def conv(window, weight, source, frames, rows, times, channels):
-    pairs, wide = window[0].shape[1:]
-    taps = [(a, b) for a in times for b in range(3)]
-
-    def patch(a, b):
-        at = source + a - times[0]
-        rows_of = [window[f][b : b + rows].reshape(rows * pairs, wide) for f in range(at, at + frames)]
-        return jnp.concatenate(rows_of, axis=0)
-
-    parts = [patch(a, b) for a, b in taps]
-    return add_moved(*products(parts, [weight[a, b] for a, b in taps], channels), pairs)
+def mix(frames, mixed):
+    d = [frame[...] for frame in frames]
+    for ref, value in zip(mixed, (d[0] - d[2], d[1] + d[2], d[2] - d[1], d[1] - d[3])):
+        ref[...] = value
+
+
+def mix_weights(weight, mixed):
+    for b in range(3):
+        g = [weight[a, b].astype(F32) for a in range(3)]
+        both = (g[0] + g[1] + g[2]) * -0.5
+        mixed[0, b] = both.astype(BF16)
+        mixed[1, b] = (both + g[1]).astype(BF16)
+
+
+def conv_pairs(mixed, weight, weight_mixed, rows, channels):
+    pairs, wide = mixed[0][0].shape[1:]
+    mine, moved = [], []
+    for i in range(4):
+        parts = [
+            jnp.concatenate([m[i][b : b + rows].reshape(rows * pairs, wide) for m in mixed], axis=0)
+            for b in range(3)
+        ]
+        rims = [(weight[0, b], weight_mixed[0, b], weight_mixed[1, b], weight[2, b])[i] for b in range(3)]
+        own, other = products(parts, rims, channels)
+        mine.append(own)
+        moved.append(other)
+
+    def outputs(m):
+        soon = [m[0][q] - m[1][q] - m[2][q] for q in range(2)]
+        late = [m[2][q] - m[1][q] - m[3][q] for q in range(2)]
+        return soon, late
+
+    return [add_moved(x, y, pairs) for x, y in zip(outputs(mine), outputs(moved))]
+
+
+def put_pairs(total, results, first):
+    _, _, deep, pairs, channels = total.shape
+    for n, both in enumerate(results):
+        for q in range(2):
+            value = both[q].reshape(-1, deep, pairs, channels)
+            for m in range(value.shape[0]):
+                total[q, first + 2 * m + n] = value[m]
 
 
 def add_moved(mine, moved, pairs):
@@ -106,21 +137,28 @@
     return mine[0] + left, mine[1] + right
 
 
-def own_kernel(bands, deep, count, normed, weight, total, *window):
+def own_window(window, normed, source, count, bands):
     frames, rows, pairs, wide = normed.shape
     tm, space = lax.axis_index("tm"), lax.axis_index("space")
     nothing = jnp.zeros((pairs, wide), BF16)
-    top = clear_rims(window[1:], bands, space, rows)
-    window[0][...] = jnp.zeros(window[0].shape, BF16)
-    for f in range(frames):
-        good = tm * frames + f < count[0]
+    top = clear_rims(window, bands, space, rows)
+    for n, part in enumerate(window):
+        good = tm * frames + source + n < count[0]
         for r in range(rows):
-            window[f + 1][top + r] = jnp.where(good, normed[f, r], nothing)
-    late = conv(window, weight, 1, frames - 2, deep, (0, 1, 2), wide // 2)
-    soon = conv(window, weight, 0, 2, deep, (1, 2), wide // 2)
-    for q in range(2):
-        total[q, 0:2] = soon[q].reshape(2, *total.shape[2:])
-        total[q, 2:] = late[q].reshape(frames - 2, *total.shape[2:])
+            part[top + r] = jnp.where(good, normed[source + n, r], nothing)
+
+
+def own_kernel(
+    bands, deep, count, normed, weight, weight_two, gain_two, bias, bias_two, total, mixed_one,
+    mixed_two, *scratch,
+):
+    channels = normed.shape[3] // 2
+    window, mixed = scratch[:4], scratch[4:]
+    mix_weights(weight, mixed_one)
+    own_window(window, normed, 0, count, bands)
+    mix(window, mixed)
+    put_pairs(total, conv_pairs([mixed], weight, mixed_one, deep, channels), 0)
+    mix_weights(weight_two, mixed_two)
 
 
 def clear_rims(window, bands, space, rows):
@@ -137,16 +175,19 @@
     return 1 + space if bands == 2 else 2
 
 
-def earlier_kernel(bands, deep, count, mask, earlier, gain, weight, after, total, *scratch):
+def earlier_kernel(
+    bands, deep, count, mask, earlier, normed, gain, weight, mixed_one, after, total, *scratch
+):
     frames, rows = earlier.shape[0], earlier.shape[1]
-    window, stages = scratch[: frames + 1], scratch[frames + 1 :]
+    window, scratch = scratch[: frames + 2], scratch[frames + 2 :]
+    mixed, stages = (scratch[:4], scratch[4:8]), scratch[8:]
     pairs, wide = window[0].shape[1:]
     tm, space = lax.axis_index("tm"), lax.axis_index("space")
 
     @pl.when(tm > 0)
     def _():
         top = clear_rims(window[:frames], bands, space, rows)
-        window[frames][...] = jnp.zeros(window[frames].shape, BF16)
+        own_window(window[frames:], normed, 0, count, bands)
 
         def store(f, r, parts):
             good = (tm - 1) * frames + f < count[0]
@@ -154,18 +195,11 @@
                 part = jnp.where(good, parts[k], jnp.zeros_like(parts[k]))
                 window[f][top + r, :, k * LANES : (k + 1) * LANES] = part
 
-        def norm(f):
+        for f in range(0, frames, 2):
             norm_frames(earlier, f, twice(gain), mask[...] > 0.5, stages[f // 2], store, pairs)
-
-        norm(frames - 2)
-        late = conv(window, weight, frames - 2, 2, deep, (0, 1), wide // 2)
-        for f in range(0, frames - 2, 2):
-            norm(f)
-        for q in range(2):
-            total[q, frames - 2 :] = late[q].reshape(2, *total.shape[2:])
-        soon = conv(window, weight, 0, frames - 2, deep, (0, 1, 2), wide // 2)
-        for q in range(2):
-            total[q, 0 : frames - 2] = soon[q].reshape(frames - 2, *total.shape[2:])
+        for n in range(2):
+            mix(window[2 * n : 2 * n + 4], mixed[n])
+        put_pairs(total, conv_pairs(mixed, weight, mixed_one, deep, wide // 2), 0)
 
 
 def add_rims(total, near, far, weight, side, keep, channels, wanted):
@@ -196,7 +230,7 @@
             total[h][q, halo] += one[n]
 
 
-def finish(bands, count, own, near, far, bias, weight, gain_two, bias_two, weight_two, out, total, hidden, final, ready):
+def finish(bands, count, own, near, far, bias, weight, gain_two, bias_two, weight_two, mixed_two, out, total, hidden, mixed, final, ready):
     frames, rows, pairs, wide = near[0].shape[0], own.shape[1], near[0].shape[2], near[0].shape[3]
     channels = wide // 2
     deep = total[0].shape[1]
@@ -232,11 +266,17 @@
         for r in range(deep):
             hidden[h][start + r] = y[r * pairs : (r + 1) * pairs]
 
-    def second_conv(f):
-        both = conv(hidden, weight_two, f, 2, rows, (0, 1, 2), channels)
-        both = jnp.concatenate(both, axis=1) + bias_two_wide
-        for k in range(3):
-            final[f // 2][k] = both[:, k * LANES : (k + 1) * LANES]
+    def second_conv():
+        for n, parts in enumerate(mixed):
+            mix(hidden[2 * n : 2 * n + 4], parts)
+        results = conv_pairs(mixed, weight_two, mixed_two, rows, channels)
+        for n, both in enumerate(results):
+            both = jnp.concatenate(both, axis=1) + bias_two_wide
+            for m in range(frames // 2):
+                at = pl.ds(n * rows * pairs, rows * pairs)
+                part = both[m * rows * pairs : (m + 1) * rows * pairs]
+                for k in range(3):
+                    final[m][k, at, :] = part[:, k * LANES : (k + 1) * LANES]
 
     def emit(f):
         good = [valid(frames + f + n) for n in range(2)]
@@ -252,46 +292,58 @@
     rims(range(4))
     for f in range(2, frames, 2):
         rims(range(f + 2, f + 4))
-    for h in range(4):
+    for h in range(frames + 2):
         norm_hidden(h)
-    second_conv(0)
-    for f in range(2, frames, 2):
-        norm_hidden(f + 2)
-        norm_hidden(f + 3)
-        emit(f - 2)
-        ready(f - 2)
-        second_conv(f)
-    emit(frames - 2)
-    ready(frames - 2)
+    second_conv()
+    for f in range(0, frames, 2):
+        emit(f)
+        ready(f)
+
+
+def split(scratch, frames):
+    total, hidden, rest = scratch[: frames + 2], scratch[frames + 2 : 2 * frames + 4], scratch[2 * frames + 4 :]
+    half = frames // 2
+    return total, hidden, [rest[4 * n : 4 * n + 4] for n in range(half)], rest[4 * half : 5 * half]
 
 
 def first_block_kernel(
-    bands, count, own, above, below, from_own, bias, weight, gain_two, bias_two, weight_two,
-    out, *scratch,
+    bands, count, own, normed, above, below, from_own, mixed_one, mixed_two, bias, weight,
+    gain_two, bias_two, weight_two, out, *scratch,
 ):
-    total, hidden, final = split(scratch, own.shape[0])
+    frames = own.shape[0]
+    window, blend, scratch = scratch[:4], scratch[4:8], scratch[8:]
+    parts = split(scratch, frames)
+    total = parts[0]
 
     @pl.when(lax.axis_index("tm") == 0)
     def _():
+        for part in window[:2]:
+            part[...] = jnp.zeros(part.shape, BF16)
+        own_window(window[2:], normed, 0, count, bands)
+        mix(window, blend)
+        deep, pairs, channels = total[0].shape[1:]
+        results = conv_pairs([blend], weight, mixed_one, deep, channels)
         for h, part in enumerate(total):
-            part[...] = jnp.zeros(part.shape, F32) if h < 2 else from_own[:, h - 2]
+            if h < 2:
+                part[...] = jnp.zeros(part.shape, F32)
+            elif h < 4:
+                for q in range(2):
+                    part[q] = results[h - 2][q].reshape(deep, pairs, channels)
+            else:
+                part[...] = from_own[:, h - 4]
         near = (above, below)
         finish(
-            bands, count, own, near, near, bias, weight, gain_two, bias_two, weight_two,
-            out, total, hidden, final, lambda f: None,
+            bands, count, own, near, near, bias, weight, gain_two, bias_two, weight_two, mixed_two,
+            out, *parts, lambda f: None,
         )
 
 
-def split(scratch, frames):
-    return scratch[: frames + 2], scratch[frames + 2 : 2 * frames + 4], scratch[2 * frames + 4 :]
-
-
 def last_kernel(
-    bands, count, own, above, below, far_above, far_below, from_own, from_earlier, first_out, bias,
-    weight, gain_two, bias_two, weight_two, out, result, sems, *scratch,
+    bands, count, own, above, below, far_above, far_below, from_own, from_earlier, first_out,
+    mixed_two, bias, weight, gain_two, bias_two, weight_two, out, result, sems, *scratch,
 ):
     frames = own.shape[0]
-    total, hidden, final = split(scratch, frames)
+    parts = split(scratch, frames)
     tm = lax.axis_index("tm")
 
     @pl.when(tm == 0)
@@ -302,20 +354,15 @@
 
     @pl.when(tm > 0)
     def _():
-        for h, part in enumerate(total):
-            if h < 2:
-                part[...] = from_earlier[:, h]
-            elif h < frames:
-                part[...] = from_own[:, h - 2] + from_earlier[:, h]
-            else:
-                part[...] = from_own[:, h - 2]
+        for h, part in enumerate(parts[0]):
+            part[...] = from_earlier[:, h] if h < frames else from_own[:, h - frames]
         copies = [
             pltpu.make_async_copy(result.at[pl.ds(f, 2)], out.at[pl.ds(f, 2)], sems.at[f // 2])
             for f in range(0, frames, 2)
         ]
         finish(
             bands, count, own, (above, below), (far_above, far_below), bias, weight, gain_two,
-            bias_two, weight_two, result, total, hidden, final, lambda f: copies[f // 2].start(),
+            bias_two, weight_two, mixed_two, result, *parts, lambda f: copies[f // 2].start(),
         )
         for copy in copies:
             copy.wait()
@@ -374,19 +421,22 @@
 
     first_weight = weight_first.reshape(3, 3, 3 * channels, channels)
     second_weight = weight_second.reshape(3, 3, 3 * channels, channels)
-    share = (2, frames, deep, pairs, channels)
-    window = [pltpu.VMEM((deep + 2, pairs, wide), BF16)] * (frames + 1)
+    row_window = pltpu.VMEM((deep + 2, pairs, wide), BF16)
+    taps = jax.ShapeDtypeStruct((2, *first_weight.shape[1:]), BF16)
     cost = pl.CostEstimate(flops=1 << 20, bytes_accessed=1 << 16, transcendentals=0)
-    from_own = pl.pallas_call(
+    from_own, mixed_one, mixed_two = pl.pallas_call(
         functools.partial(own_kernel, bands, deep),
-        out_shape=jax.ShapeDtypeStruct(share, F32),
-        in_specs=[smem] + [vmem] * 2,
-        out_specs=vmem,
-        scratch_shapes=window,
+        out_shape=[jax.ShapeDtypeStruct((2, 2, deep, pairs, channels), F32), taps, taps],
+        in_specs=[smem] + [vmem] * 6,
+        out_specs=[vmem] * 3,
+        scratch_shapes=[row_window] * 8,
         compiler_params=params,
         cost_estimate=cost,
         name="conv_one_own",
-    )(counts, normed, first_weight)
+    )(
+        counts, normed, first_weight, second_weight, gain_second.reshape(1, channels),
+        bias_first.reshape(1, channels), bias_second.reshape(1, channels),
+    )
     constants = (
         bias_first.reshape(1, channels), first_weight,
         gain_second.reshape(1, channels), bias_second.reshape(1, channels), second_weight,
@@ -394,33 +444,36 @@
     result = jax.ShapeDtypeStruct((frames, rows, flat), BF16)
     scratch = (
         [pltpu.VMEM((2, deep, pairs, channels), F32)] * (frames + 2)
-        + [pltpu.VMEM((rows + 2, pairs, wide), BF16)] * (frames + 2)
+        + [pltpu.VMEM((rows + 2, pairs, wide), BF16)] * (frames + 2 + 2 * frames)
         + stages
     )
     first_out = pl.pallas_call(
         functools.partial(first_block_kernel, bands),
         out_shape=result,
-        in_specs=[smem] + [vmem] * 9,
+        in_specs=[smem] + [vmem] * 12,
         out_specs=vmem,
-        scratch_shapes=scratch,
+        scratch_shapes=[row_window] * 8 + scratch,
         compiler_params=params,
         cost_estimate=cost,
         name="first_block",
-    )(counts, block, *near, from_own, *constants)
+    )(counts, block, normed, *near, from_own, mixed_one, mixed_two, *constants)
     from_earlier = pl.pallas_call(
         functools.partial(earlier_kernel, bands, deep),
-        out_shape=jax.ShapeDtypeStruct(share, F32),
-        in_specs=[smem] + [vmem] * 5,
+        out_shape=jax.ShapeDtypeStruct((2, frames, deep, pairs, channels), F32),
+        in_specs=[smem] + [vmem] * 7,
         out_specs=vmem,
-        scratch_shapes=window + stages,
+        scratch_shapes=[row_window] * (frames + 2 + 8) + stages,
         compiler_params=params,
         cost_estimate=cost,
         name="conv_one_earlier",
-    )(counts, mask, earlier, gain_first.reshape(1, channels), first_weight, first_out)
+    )(
+        counts, mask, earlier, normed, gain_first.reshape(1, channels), first_weight, mixed_one,
+        first_out,
+    )
     out = pl.pallas_call(
         functools.partial(last_kernel, bands),
         out_shape=result,
-        in_specs=[smem] + [vmem] * 13,
+        in_specs=[smem] + [vmem] * 14,
         out_specs=pl.BlockSpec(memory_space=pl.ANY),
         scratch_shapes=[
             pltpu.VMEM((frames, rows, flat), BF16), pltpu.SemaphoreType.DMA((frames // 2,))
@@ -428,7 +481,7 @@
         compiler_params=params,
         cost_estimate=pl.CostEstimate(flops=4 << 30, bytes_accessed=6 << 20, transcendentals=0),
         name="last",
-    )(counts, block, *near, *far, from_own, from_earlier, first_out, *constants)
+    )(counts, block, *near, *far, from_own, from_earlier, first_out, mixed_two, *constants)
     return out.reshape(1, frames, rows, flat)
 
 

time: 14.1 us -> 15.2 us (1.078)
  the two profiles are of different devices: /device:TPU:16 before, /device:TPU:0 now
where the time goes in v14:
time: 15.2 us; the launch traced here: 15.1 us
  Pallas kernels  8.1 us (53%)
  starting transfers between devices  6.13 us (40%)
  between operations  0.79 us (5%)
    ppermute x3, starting transfers between devices, shift(): return lax.ppermute(sent, ('tm', 'space'), pairs_of)  6.13 us
    pallas_call x1, Pallas kernels, shards(): pl.pallas_call(functools.partial(first_block_kernel, bands), out_shape=re...  4.46 us
    pallas_call x1, Pallas kernels, shards(): pl.pallas_call(functools.partial(own_kernel, bands, deep), out_shape=[jax...  2.56 us
    pallas_call x1, Pallas kernels, shards(): pl.pallas_call(functools.partial(last_kernel, bands), out_shape=result, i...  0.71 us
    pallas_call x1, Pallas kernels, shards(): pl.pallas_call(functools.partial(norm_kernel, swap), out_shape=[jax.Shape...  0.35 us
  transfers between devices with their start and end apart: 3, of which 0 were waited for; matrix products, arithmetic and copies ran while one was open for 0% of the time, Pallas kernels for 49%

profile of v14, /device:TPU:0, one launch (start us, length us, event | category | flops | bytes accessed | tf_op | source)
XLA Modules:
  0.0 15.1 jit_solution(13527220037014058612)
XLA Ops:
  0.0 0.0 copy-start.2
  0.0 0.0 copy-start.6
  0.0 3.0 %collective-permute-start.2 = (bf16[4,4,6144]{2,1,0:T(4,128)(2,1)}, bf16[4,4,6144]{2,1,0:T(4,128)(2,1)S(1)}, u32[]{:S(2)}, u32[]{:S(2)}) collective-permute-start(bf16[4,4,6144]{2,1,0:T(4,128)(2,1)} %bitcast.15), channel_id=1, source_target_pairs={{0,4},{2,6},{4,8},{6,10},{8,12},{10,14},{12,0},{14,2},{1,5},{3,7},... | collective-permute-start | bytes 589832 | tf_op jit(solution)/shard_map/ppermute | solution.py:385
  3.0 0.0 copy-done.2
  3.0 0.0 copy-done.6
  3.0 0.0 copy-start
  3.1 0.0 copy-start.1
  3.1 0.0 copy-start.3
  3.1 0.0 copy-start.4
  3.1 0.0 copy-start.5
  3.1 0.4 %norm_and_cut.1 = (bf16[4,4,16,384]{3,2,1,0:T(8,128)(2,1)S(1)}, bf16[4,2,16,384]{3,2,1,0:T(8,128)(2,1)S(1)}) custom-call(f32[8,384]{1,0:T(8,128)S(1)} %lane_mask.1.mask, bf16[4,4,6144]{2,1,0:T(4,128)(2,1)S(1)} %bitcast.16, f32[1,192]{1,0:T(1,128)S(1)} %bitcast.28), custom_call_target="tpu_custom_call" | custom-call | flops 4294967296 | bytes 1048576 | tf_op jit(solution)/shard_map/norm_and_cut/pallas_call | solution.py:402
  3.5 1.6 %collective-permute-start = (bf16[4,2,16,384]{3,2,1,0:T(8,128)(2,1)S(1)}, bf16[4,2,16,384]{3,2,1,0:T(8,128)(2,1)S(1)}, u32[]{:S(2)}, u32[]{:S(2)}) collective-permute-start(bf16[4,2,16,384]{3,2,1,0:T(8,128)(2,1)S(1)} %get-tuple-element.10), channel_id=1, source_target_pairs={{0,2},{2,0},{4,6},{6,4},{8,10},{10,8},{12,14},{14,12},{1,3},{3,1},... | collective-permute-start | bytes 294920 | tf_op jit(solution)/shard_map/ppermute | solution.py:385
  5.0 1.5 %collective-permute-start.1 = (bf16[4,2,16,384]{3,2,1,0:T(8,128)(2,1)S(1)}, bf16[4,2,16,384]{3,2,1,0:T(8,128)(2,1)S(1)}, u32[]{:S(2)}, u32[]{:S(2)}) collective-permute-start(bf16[4,2,16,384]{3,2,1,0:T(8,128)(2,1)S(1)} %get-tuple-element.10), channel_id=1, source_target_pairs={{0,6},{2,4},{4,10},{6,8},{8,14},{10,12},{12,0},{14,2},{1,7},{3,5},... | collective-permute-start | bytes 294920 | tf_op jit(solution)/shard_map/ppermute | solution.py:385
  7.2 0.0 copy-done
  7.2 0.0 copy-done.1
  7.2 0.0 copy-done.3
  7.2 0.0 copy-done.4
  7.3 0.0 copy-done.5
  7.3 2.6 %conv_one_own.1 = (f32[2,2,5,16,192]{4,3,2,1,0:T(8,128)S(1)}, bf16[2,3,576,192]{3,2,1,0:T(8,128)(2,1)S(1)}, bf16[2,3,576,192]{3,2,1,0:T(8,128)(2,1)S(1)}) custom-call(s32[1]{0:T(128)S(6)} %copy.9.count, bf16[4,4,16,384]{3,2,1,0:T(8,128)(2,1)S(1)} %get-tuple-element.11.normed, bf16[3,3,576,192]{3,2,1,0:T(8,128)(2,1)S(1)} %bitcast.8, ...), custom_call_target="tpu_custom_call" | custom-call | flops 1048576 | bytes 65536 | tf_op jit(solution)/shard_map/conv_one_own/pallas_call | solution.py:427
  9.8 0.0 collective-permute-done.above.below
  9.8 4.5 %first_block.1.after.first_out = bf16[4,4,6144]{2,1,0:T(4,128)(2,1)S(1)} custom-call(s32[1]{0:T(128)S(6)} %copy.9.count, bf16[4,4,6144]{2,1,0:T(4,128)(2,1)S(1)} %bitcast.17, bf16[4,4,16,384]{3,2,1,0:T(8,128)(2,1)S(1)} %get-tuple-element.11.normed, bf16[4,2,16,384]{3,2,1,0:T(8,128)(2,1)S(1)} %collective-permute-done.above.below, ...), custom_call_target="tpu_custom_call" | custom-call | flops 1048576 | bytes 65536 | tf_op jit(solution)/shard_map/first_block/pallas_call | solution.py:450
  14.3 0.0 collective-permute-done.2.earlier
  14.3 0.0 collective-permute-done.1.far_above.far_below
  14.4 0.7 %last.1 = bf16[4,4,6144]{2,1,0:T(4,128)(2,1)} custom-call(s32[1]{0:T(128)S(6)} %copy.9.count, bf16[4,4,6144]{2,1,0:T(4,128)(2,1)S(1)} %bitcast.18, bf16[4,2,16,384]{3,2,1,0:T(8,128)(2,1)S(1)} %collective-permute-done.above.below, bf16[4,2,16,384]{3,2,1,0:T(8,128)(2,1)S(1)} %collective-permute-done.above.below, ...), custom_call_target="tpu_custom_call" | custom-call | flops 4294967296 | bytes 6291456 | tf_op jit(solution)/shard_map/last/pallas_call | solution.py:473
  (2 shorter events, 0.0 us)
Async XLA Ops:
  0.0 3.0 %copy-start.2 = (bf16[1,4,4,6144]{3,2,1,0:T(4,128)(2,1)S(1)}, bf16[1,4,4,6144]{3,2,1,0:T(4,128)(2,1)}, u32[]{:S(2)}) copy-start(bf16[1,4,4,6144]{3,2,1,0:T(4,128)(2,1)} %param.8) | copy-start | bytes 589828
  0.0 3.0 %copy-start.6 = (f32[192]{0:T(256)S(1)}, f32[192]{0:T(256)}, u32[]{:S(2)}) copy-start(f32[192]{0:T(256)} %param.10) | copy-start | bytes 2308
  0.0 14.3 %collective-permute-start.2 = (bf16[4,4,6144]{2,1,0:T(4,128)(2,1)}, bf16[4,4,6144]{2,1,0:T(4,128)(2,1)S(1)}, u32[]{:S(2)}, u32[]{:S(2)}) collective-permute-start(bf16[4,4,6144]{2,1,0:T(4,128)(2,1)} %bitcast.15), channel_id=1, source_target_pairs={{0,4},{2,6},{4,8},{6,10},{8,12},{10,14},{12,0},{14,2},{1,5},{3,7},... | collective-permute-start | bytes 589832 | tf_op jit(solution)/shard_map/ppermute | solution.py:385
  3.0 4.2 %copy-start = (bf16[3,3,3,192,192]{4,3,2,1,0:T(8,128)(2,1)S(1)}, bf16[3,3,3,192,192]{4,3,2,1,0:T(8,128)(2,1)}, u32[]{:S(2)}) copy-start(bf16[3,3,3,192,192]{4,3,2,1,0:T(8,128)(2,1)} %param.12) | copy-start | bytes 5971972
  3.1 4.2 %copy-start.1 = (bf16[3,3,3,192,192]{4,3,2,1,0:T(8,128)(2,1)S(1)}, bf16[3,3,3,192,192]{4,3,2,1,0:T(8,128)(2,1)}, u32[]{:S(2)}) copy-start(bf16[3,3,3,192,192]{4,3,2,1,0:T(8,128)(2,1)} %param.15) | copy-start | bytes 5971972
  3.1 4.2 %copy-start.3 = (f32[192]{0:T(256)S(1)}, f32[192]{0:T(256)}, u32[]{:S(2)}) copy-start(f32[192]{0:T(256)} %param.13) | copy-start | bytes 2308
  3.1 4.2 %copy-start.4 = (f32[192]{0:T(256)S(1)}, f32[192]{0:T(256)}, u32[]{:S(2)}) copy-start(f32[192]{0:T(256)} %param.11) | copy-start | bytes 2308
  3.1 4.2 %copy-start.5 = (f32[192]{0:T(256)S(1)}, f32[192]{0:T(256)}, u32[]{:S(2)}) copy-start(f32[192]{0:T(256)} %param.14) | copy-start | bytes 2308
  3.5 6.4 %collective-permute-start = (bf16[4,2,16,384]{3,2,1,0:T(8,128)(2,1)S(1)}, bf16[4,2,16,384]{3,2,1,0:T(8,128)(2,1)S(1)}, u32[]{:S(2)}, u32[]{:S(2)}) collective-permute-start(bf16[4,2,16,384]{3,2,1,0:T(8,128)(2,1)S(1)} %get-tuple-element.10), channel_id=1, source_target_pairs={{0,2},{2,0},{4,6},{6,4},{8,10},{10,8},{12,14},{14,12},{1,3},{3,1},... | collective-permute-start | bytes 294920 | tf_op jit(solution)/shard_map/ppermute | solution.py:385
  5.0 9.3 %collective-permute-start.1 = (bf16[4,2,16,384]{3,2,1,0:T(8,128)(2,1)S(1)}, bf16[4,2,16,384]{3,2,1,0:T(8,128)(2,1)S(1)}, u32[]{:S(2)}, u32[]{:S(2)}) collective-permute-start(bf16[4,2,16,384]{3,2,1,0:T(8,128)(2,1)S(1)} %get-tuple-element.10), channel_id=1, source_target_pairs={{0,6},{2,4},{4,10},{6,8},{8,14},{10,12},{12,0},{14,2},{1,7},{3,5},... | collective-permute-start | bytes 294920 | tf_op jit(solution)/shard_map/ppermute | solution.py:385

commit v15 on v13

--- a/solution.py
+++ b/solution.py
@@ -98,6 +98,31 @@
     return add_moved(*products(parts, [weight[a, b] for a, b in taps], channels), pairs)
 
 
+def mix_weights(weight, mixed):
+    for b in range(3):
+        outer = weight[0, b] + weight[2, b]
+        mixed[0, b] = (outer + weight[1, b]) * -0.5
+        mixed[1, b] = (outer - weight[1, b]) * -0.5
+
+
+def mix(frames, i, out):
+    if i == 1:
+        out[...] = frames[1][...] + frames[2][...]
+    else:
+        one, other = ((0, 2), None, (2, 1), (1, 3))[i]
+        out[...] = frames[one][...] - frames[other][...]
+
+
+def mixed_product(mixed, taps, rows, channels):
+    pairs, wide = mixed[0].shape[1:]
+    parts = [
+        jnp.concatenate([m[b : b + rows].reshape(rows * pairs, wide) for m in mixed], axis=0)
+        for b in range(3)
+    ]
+    mine, moved = products(parts, taps, channels)
+    return [*mine, *moved]
+
+
 def add_moved(mine, moved, pairs):
     place = lax.broadcasted_iota(jnp.int32, mine[0].shape, 0) % pairs
     count = mine[0].shape[0]
@@ -106,7 +131,9 @@
     return mine[0] + left, mine[1] + right
 
 
-def own_kernel(bands, deep, count, normed, weight, total, *window):
+def own_kernel(
+    bands, deep, count, normed, weight, weight_two, gain_two, bias, bias_two, total, mixed_two, *window
+):
     frames, rows, pairs, wide = normed.shape
     tm, space = lax.axis_index("tm"), lax.axis_index("space")
     nothing = jnp.zeros((pairs, wide), BF16)
@@ -118,6 +145,7 @@
             window[f + 1][top + r] = jnp.where(good, normed[f, r], nothing)
     late = conv(window, weight, 1, frames - 2, deep, (0, 1, 2), wide // 2)
     soon = conv(window, weight, 0, 2, deep, (1, 2), wide // 2)
+    mix_weights(weight_two, mixed_two)
     for q in range(2):
         total[q, 0:2] = soon[q].reshape(2, *total.shape[2:])
         total[q, 2:] = late[q].reshape(frames - 2, *total.shape[2:])
@@ -196,7 +224,7 @@
             total[h][q, halo] += one[n]
 
 
-def finish(bands, count, own, near, far, bias, weight, gain_two, bias_two, weight_two, out, total, hidden, final, ready):
+def finish(bands, count, own, near, far, bias, weight, gain_two, bias_two, weight_two, mixed_two, out, total, hidden, mixed, final, ready):
     frames, rows, pairs, wide = near[0].shape[0], own.shape[1], near[0].shape[2], near[0].shape[3]
     channels = wide // 2
     deep = total[0].shape[1]
@@ -232,66 +260,76 @@
         for r in range(deep):
             hidden[h][start + r] = y[r * pairs : (r + 1) * pairs]
 
-    def second_conv(f):
-        both = conv(hidden, weight_two, f, 2, rows, (0, 1, 2), channels)
+    def product(i):
+        for n in range(half):
+            mix(hidden[2 * n : 2 * n + 4], i, mixed[half * i + n])
+        taps = [(weight_two[0, b], mixed_two[0, b], mixed_two[1, b], weight_two[2, b])[i] for b in range(3)]
+        return mixed_product(mixed[half * i : half * (i + 1)], taps, rows, channels)
+
+    def emit(n, result):
+        both = add_moved(result[:2], result[2:], pairs)
         both = jnp.concatenate(both, axis=1) + bias_two_wide
         for k in range(3):
-            final[f // 2][k] = both[:, k * LANES : (k + 1) * LANES]
-
-    def emit(f):
-        good = [valid(frames + f + n) for n in range(2)]
-        for p in range(pairs):
-            for k in range(3):
-                block = final[f // 2][k, pl.ds(p, 2 * rows, stride=pairs), :]
-                lanes = pl.ds(p * wide + k * LANES, LANES)
-                for n in range(2):
-                    value = own[f + n, :, lanes].astype(F32) + block[n * rows : (n + 1) * rows]
-                    out[f + n, :, lanes] = jnp.where(good[n], value, 0.0).astype(BF16)
-
+            final[n][k] = both[:, k * LANES : (k + 1) * LANES]
+        for m in range(0, half, 2):
+            good = [valid(frames + n + 2 * (m + j)) for j in range(2)]
+            for p in range(pairs):
+                for k in range(3):
+                    at = pl.ds(m * rows * pairs + p, 2 * rows, stride=pairs)
+                    block = final[n][k, at, :]
+                    lanes = pl.ds(p * wide + k * LANES, LANES)
+                    for j in range(2):
+                        f = n + 2 * (m + j)
+                        value = own[f, :, lanes].astype(F32) + block[j * rows : (j + 1) * rows]
+                        out[f, :, lanes] = jnp.where(good[j], value, 0.0).astype(BF16)
+        for m in range(half):
+            ready(n + 2 * m)
+
+    half = frames // 2
     bias_two_wide = twice(bias_two)
     rims(range(4))
     for f in range(2, frames, 2):
         rims(range(f + 2, f + 4))
-    for h in range(4):
+    for h in range(1, frames + 1):
         norm_hidden(h)
-    second_conv(0)
-    for f in range(2, frames, 2):
-        norm_hidden(f + 2)
-        norm_hidden(f + 3)
-        emit(f - 2)
-        ready(f - 2)
-        second_conv(f)
-    emit(frames - 2)
-    ready(frames - 2)
+    one = product(1)
+    two = product(2)
+    norm_hidden(0)
+    zero = product(0)
+    norm_hidden(frames + 1)
+    three = product(3)
+    emit(0, [x - y - z for x, y, z in zip(zero, one, two)])
+    emit(1, [z - y - x for x, y, z in zip(three, one, two)])
 
 
 def first_block_kernel(
-    bands, count, own, above, below, from_own, bias, weight, gain_two, bias_two, weight_two,
-    out, *scratch,
+    bands, count, own, above, below, from_own, mixed_two, bias, weight, gain_two, bias_two,
+    weight_two, out, *scratch,
 ):
-    total, hidden, final = split(scratch, own.shape[0])
+    parts = split(scratch, own.shape[0])
 
     @pl.when(lax.axis_index("tm") == 0)
     def _():
-        for h, part in enumerate(total):
+        for h, part in enumerate(parts[0]):
             part[...] = jnp.zeros(part.shape, F32) if h < 2 else from_own[:, h - 2]
         near = (above, below)
         finish(
             bands, count, own, near, near, bias, weight, gain_two, bias_two, weight_two,
-            out, total, hidden, final, lambda f: None,
+            mixed_two, out, *parts, lambda f: None,
         )
 
 
 def split(scratch, frames):
-    return scratch[: frames + 2], scratch[frames + 2 : 2 * frames + 4], scratch[2 * frames + 4 :]
+    rest = scratch[2 * frames + 4 :]
+    return scratch[: frames + 2], scratch[frames + 2 : 2 * frames + 4], rest[: 2 * frames], rest[2 * frames :]
 
 
 def last_kernel(
-    bands, count, own, above, below, far_above, far_below, from_own, from_earlier, first_out, bias,
-    weight, gain_two, bias_two, weight_two, out, result, sems, *scratch,
+    bands, count, own, above, below, far_above, far_below, from_own, from_earlier, first_out,
+    mixed_two, bias, weight, gain_two, bias_two, weight_two, out, result, sems, *scratch,
 ):
     frames = own.shape[0]
-    total, hidden, final = split(scratch, frames)
+    parts = split(scratch, frames)
     tm = lax.axis_index("tm")
 
     @pl.when(tm == 0)
@@ -302,7 +340,7 @@
 
     @pl.when(tm > 0)
     def _():
-        for h, part in enumerate(total):
+        for h, part in enumerate(parts[0]):
             if h < 2:
                 part[...] = from_earlier[:, h]
             elif h < frames:
@@ -310,12 +348,11 @@
             else:
                 part[...] = from_own[:, h - 2]
         copies = [
-            pltpu.make_async_copy(result.at[pl.ds(f, 2)], out.at[pl.ds(f, 2)], sems.at[f // 2])
-            for f in range(0, frames, 2)
+            pltpu.make_async_copy(result.at[f], out.at[f], sems.at[f]) for f in range(frames)
         ]
         finish(
             bands, count, own, (above, below), (far_above, far_below), bias, weight, gain_two,
-            bias_two, weight_two, result, total, hidden, final, lambda f: copies[f // 2].start(),
+            bias_two, weight_two, mixed_two, result, *parts, lambda f: copies[f].start(),
         )
         for copy in copies:
             copy.wait()
@@ -377,16 +414,20 @@
     share = (2, frames, deep, pairs, channels)
     window = [pltpu.VMEM((deep + 2, pairs, wide), BF16)] * (frames + 1)
     cost = pl.CostEstimate(flops=1 << 20, bytes_accessed=1 << 16, transcendentals=0)
-    from_own = pl.pallas_call(
+    taps = jax.ShapeDtypeStruct((2, *first_weight.shape[1:]), BF16)
+    from_own, mixed_two = pl.pallas_call(
         functools.partial(own_kernel, bands, deep),
-        out_shape=jax.ShapeDtypeStruct(share, F32),
-        in_specs=[smem] + [vmem] * 2,
-        out_specs=vmem,
+        out_shape=[jax.ShapeDtypeStruct(share, F32), taps],
+        in_specs=[smem] + [vmem] * 6,
+        out_specs=[vmem] * 2,
         scratch_shapes=window,
         compiler_params=params,
         cost_estimate=cost,
         name="conv_one_own",
-    )(counts, normed, first_weight)
+    )(
+        counts, normed, first_weight, second_weight, gain_second.reshape(1, channels),
+        bias_first.reshape(1, channels), bias_second.reshape(1, channels),
+    )
     constants = (
         bias_first.reshape(1, channels), first_weight,
         gain_second.reshape(1, channels), bias_second.reshape(1, channels), second_weight,
@@ -394,19 +435,19 @@
     result = jax.ShapeDtypeStruct((frames, rows, flat), BF16)
     scratch = (
         [pltpu.VMEM((2, deep, pairs, channels), F32)] * (frames + 2)
-        + [pltpu.VMEM((rows + 2, pairs, wide), BF16)] * (frames + 2)
-        + stages
+        + [pltpu.VMEM((rows + 2, pairs, wide), BF16)] * (frames + 2 + 2 * frames)
+        + [pltpu.VMEM((3, frames // 2 * rows * pairs, LANES), F32)] * 2
     )
     first_out = pl.pallas_call(
         functools.partial(first_block_kernel, bands),
         out_shape=result,
-        in_specs=[smem] + [vmem] * 9,
+        in_specs=[smem] + [vmem] * 10,
         out_specs=vmem,
         scratch_shapes=scratch,
         compiler_params=params,
         cost_estimate=cost,
         name="first_block",
-    )(counts, block, *near, from_own, *constants)
+    )(counts, block, *near, from_own, mixed_two, *constants)
     from_earlier = pl.pallas_call(
         functools.partial(earlier_kernel, bands, deep),
         out_shape=jax.ShapeDtypeStruct(share, F32),
@@ -420,15 +461,15 @@
     out = pl.pallas_call(
         functools.partial(last_kernel, bands),
         out_shape=result,
-        in_specs=[smem] + [vmem] * 13,
+        in_specs=[smem] + [vmem] * 14,
         out_specs=pl.BlockSpec(memory_space=pl.ANY),
         scratch_shapes=[
-            pltpu.VMEM((frames, rows, flat), BF16), pltpu.SemaphoreType.DMA((frames // 2,))
+            pltpu.VMEM((frames, rows, flat), BF16), pltpu.SemaphoreType.DMA((frames,))
         ] + scratch,
         compiler_params=params,
         cost_estimate=pl.CostEstimate(flops=4 << 30, bytes_accessed=6 << 20, transcendentals=0),
         name="last",
-    )(counts, block, *near, *far, from_own, from_earlier, first_out, *constants)
+    )(counts, block, *near, *far, from_own, from_earlier, first_out, mixed_two, *constants)
     return out.reshape(1, frames, rows, flat)
 
 

time: 14.1 us -> 14.1 us (level)
  waiting for transfers between devices: 0.93 us -> 0.67 us
  Pallas kernels: 8.18 us -> 8.38 us
    pallas_call x1, Pallas kernels: 1.8 us -> 2.07 us  [shards(): pl.pallas_call(functools.partial(own_kernel, bands, deep), out_shape=[jax...]
    ppermute x3, waiting for transfers between devices: 0.93 us -> 0.67 us  [shift(): return lax.ppermute(sent, ('tm', 'space'), pairs_of)]
  transfers between devices with their start and end apart: 3 -> 3, of which waited for: 1 -> 1; matrix products, arithmetic and copies ran while one was open for 0% -> 0% of each run, Pallas kernels for 31% -> 32%
where the time goes in v15:
time: 14.1 us; the launch traced here: 13.9 us
  Pallas kernels  8.38 us (59%)
  starting transfers between devices  3.99 us (28%)
  between operations  0.78 us (6%)
  waiting for transfers between devices  0.67 us (5%)
    ppermute x3, starting transfers between devices, shift(): return lax.ppermute(sent, ('tm', 'space'), pairs_of)  3.99 us
    pallas_call x1, Pallas kernels, shards(): pl.pallas_call(functools.partial(last_kernel, bands), out_shape=result, i...  3.86 us
    pallas_call x1, Pallas kernels, shards(): pl.pallas_call(functools.partial(own_kernel, bands, deep), out_shape=[jax...  2.07 us
    pallas_call x1, Pallas kernels, shards(): pl.pallas_call(functools.partial(earlier_kernel, bands, deep), out_shape=...  2.07 us
    ppermute x3, waiting for transfers between devices, shift(): return lax.ppermute(sent, ('tm', 'space'), pairs_of)  0.67 us
    pallas_call x1, Pallas kernels, shards(): pl.pallas_call(functools.partial(norm_kernel, swap), out_shape=[jax.Shape...  0.35 us
  transfers between devices with their start and end apart: 3, of which 1 were waited for; matrix products, arithmetic and copies ran while one was open for 0% of the time, Pallas kernels for 32%

profile of v15, /device:TPU:16, one launch (start us, length us, event | category | flops | bytes accessed | tf_op | source)
XLA Modules:
  0.0 13.9 jit_solution(407106515643831346)
XLA Ops:
  0.0 0.0 copy-start.2
  0.0 0.0 copy-start.6
  0.0 1.6 %collective-permute-start.2 = (bf16[4,4,6144]{2,1,0:T(4,128)(2,1)}, bf16[4,4,6144]{2,1,0:T(4,128)(2,1)S(1)}, u32[]{:S(2)}, u32[]{:S(2)}) collective-permute-start(bf16[4,4,6144]{2,1,0:T(4,128)(2,1)} %bitcast.15), channel_id=1, source_target_pairs={{0,4},{2,6},{4,8},{6,10},{8,12},{10,14},{12,0},{14,2},{1,5},{3,7},... | collective-permute-start | bytes 589832 | tf_op jit(solution)/shard_map/ppermute | solution.py:375
  1.6 0.0 copy-done.2
  1.6 0.0 copy-done.6
  1.6 0.0 copy-start
  1.6 0.0 copy-start.1
  1.6 0.0 copy-start.3
  1.6 0.0 copy-start.4
  1.6 0.0 copy-start.5
  1.7 0.4 %norm_and_cut.1 = (bf16[4,4,16,384]{3,2,1,0:T(8,128)(2,1)S(1)}, bf16[4,2,16,384]{3,2,1,0:T(8,128)(2,1)S(1)}) custom-call(f32[8,384]{1,0:T(8,128)S(1)} %lane_mask.1.mask, bf16[4,4,6144]{2,1,0:T(4,128)(2,1)S(1)} %bitcast.16, f32[1,192]{1,0:T(1,128)S(1)} %bitcast.28), custom_call_target="tpu_custom_call" | custom-call | flops 4294967296 | bytes 1048576 | tf_op jit(solution)/shard_map/norm_and_cut/pallas_call | solution.py:392
  2.0 1.6 %collective-permute-start = (bf16[4,2,16,384]{3,2,1,0:T(8,128)(2,1)S(1)}, bf16[4,2,16,384]{3,2,1,0:T(8,128)(2,1)S(1)}, u32[]{:S(2)}, u32[]{:S(2)}) collective-permute-start(bf16[4,2,16,384]{3,2,1,0:T(8,128)(2,1)S(1)} %get-tuple-element.9), channel_id=1, source_target_pairs={{0,2},{2,0},{4,6},{6,4},{8,10},{10,8},{12,14},{14,12},{1,3},{3,1},... | collective-permute-start | bytes 294920 | tf_op jit(solution)/shard_map/ppermute | solution.py:375
  3.6 0.9 %collective-permute-start.1 = (bf16[4,2,16,384]{3,2,1,0:T(8,128)(2,1)S(1)}, bf16[4,2,16,384]{3,2,1,0:T(8,128)(2,1)S(1)}, u32[]{:S(2)}, u32[]{:S(2)}) collective-permute-start(bf16[4,2,16,384]{3,2,1,0:T(8,128)(2,1)S(1)} %get-tuple-element.9), channel_id=1, source_target_pairs={{0,6},{2,4},{4,10},{6,8},{8,14},{10,12},{12,0},{14,2},{1,7},{3,5},... | collective-permute-start | bytes 294920 | tf_op jit(solution)/shard_map/ppermute | solution.py:375
  5.1 0.0 copy-done
  5.1 0.0 copy-done.1
  5.1 0.0 copy-done.3
  5.1 0.0 copy-done.4
  5.1 0.0 copy-done.5
  5.1 2.1 %conv_one_own.1 = (f32[2,4,5,16,192]{4,3,2,1,0:T(8,128)S(1)}, bf16[2,3,576,192]{3,2,1,0:T(8,128)(2,1)S(1)}) custom-call(s32[1]{0:T(128)S(6)} %copy.9.count, bf16[4,4,16,384]{3,2,1,0:T(8,128)(2,1)S(1)} %get-tuple-element.10.normed, bf16[3,3,576,192]{3,2,1,0:T(8,128)(2,1)S(1)} %bitcast.8, bf16[3,3,576,192]{3,2,1,0:T(8,128)(2,1)S(1)} %bitcast.12, ...), custom_call_target="tpu_custom_call" | custom-call | flops 1048576 | bytes 65536 | tf_op jit(solution)/shard_map/conv_one_own/pallas_call | solution.py:418
  7.2 0.0 collective-permute-done.above.below
  7.2 0.7 %collective-permute-done.2.earlier = bf16[4,4,6144]{2,1,0:T(4,128)(2,1)S(1)} collective-permute-done((bf16[4,4,6144]{2,1,0:T(4,128)(2,1)}, bf16[4,4,6144]{2,1,0:T(4,128)(2,1)S(1)}, u32[]{:S(2)}, u32[]{:S(2)}) %collective-permute-start.2) | collective-permute-done | bytes 196640 | tf_op jit(solution)/shard_map/ppermute | solution.py:375
  7.9 2.1 %conv_one_earlier.1.from_earlier = f32[2,4,5,16,192]{4,3,2,1,0:T(8,128)S(1)} custom-call(s32[1]{0:T(128)S(6)} %copy.9.count, f32[8,384]{1,0:T(8,128)S(1)} %lane_mask.1.mask, bf16[4,4,6144]{2,1,0:T(4,128)(2,1)S(1)} %collective-permute-done.2.earlier, f32[1,192]{1,0:T(1,128)S(1)} %bitcast.29, bf16[3,3,576,192]{3,2,1,0:T(8,128)(2,1)S(1)} %bitcast.10, ...), custom_call_target="tpu_custom_call" | custom-call | flops 1048576 | bytes 65536 | tf_op jit(solution)/shard_map/conv_one_earlier/pallas_call | solution.py:451
  10.0 0.0 collective-permute-done.1.far_above.far_below
  10.0 3.9 %last.1 = bf16[4,4,6144]{2,1,0:T(4,128)(2,1)} custom-call(s32[1]{0:T(128)S(6)} %copy.9.count, bf16[4,4,6144]{2,1,0:T(4,128)(2,1)S(1)} %bitcast.18, bf16[4,2,16,384]{3,2,1,0:T(8,128)(2,1)S(1)} %collective-permute-done.above.below, bf16[4,2,16,384]{3,2,1,0:T(8,128)(2,1)S(1)} %collective-permute-done.above.below, ...), custom_call_target="tpu_custom_call" | custom-call | flops 4294967296 | bytes 6291456 | tf_op jit(solution)/shard_map/last/pallas_call | solution.py:461
  (2 shorter events, 0.0 us)
Async XLA Ops:
  0.0 1.6 %copy-start.2 = (bf16[1,4,4,6144]{3,2,1,0:T(4,128)(2,1)S(1)}, bf16[1,4,4,6144]{3,2,1,0:T(4,128)(2,1)}, u32[]{:S(2)}) copy-start(bf16[1,4,4,6144]{3,2,1,0:T(4,128)(2,1)} %param.8) | copy-start | bytes 589828
  0.0 1.6 %copy-start.6 = (f32[192]{0:T(256)S(1)}, f32[192]{0:T(256)}, u32[]{:S(2)}) copy-start(f32[192]{0:T(256)} %param.10) | copy-start | bytes 2308
  0.0 7.9 %collective-permute-start.2 = (bf16[4,4,6144]{2,1,0:T(4,128)(2,1)}, bf16[4,4,6144]{2,1,0:T(4,128)(2,1)S(1)}, u32[]{:S(2)}, u32[]{:S(2)}) collective-permute-start(bf16[4,4,6144]{2,1,0:T(4,128)(2,1)} %bitcast.15), channel_id=1, source_target_pairs={{0,4},{2,6},{4,8},{6,10},{8,12},{10,14},{12,0},{14,2},{1,5},{3,7},... | collective-permute-start | bytes 589832 | tf_op jit(solution)/shard_map/ppermute | solution.py:375
  1.6 3.5 %copy-start = (bf16[3,3,3,192,192]{4,3,2,1,0:T(8,128)(2,1)S(1)}, bf16[3,3,3,192,192]{4,3,2,1,0:T(8,128)(2,1)}, u32[]{:S(2)}) copy-start(bf16[3,3,3,192,192]{4,3,2,1,0:T(8,128)(2,1)} %param.12) | copy-start | bytes 5971972
  1.6 3.5 %copy-start.1 = (bf16[3,3,3,192,192]{4,3,2,1,0:T(8,128)(2,1)S(1)}, bf16[3,3,3,192,192]{4,3,2,1,0:T(8,128)(2,1)}, u32[]{:S(2)}) copy-start(bf16[3,3,3,192,192]{4,3,2,1,0:T(8,128)(2,1)} %param.15) | copy-start | bytes 5971972
  1.6 3.5 %copy-start.3 = (f32[192]{0:T(256)S(1)}, f32[192]{0:T(256)}, u32[]{:S(2)}) copy-start(f32[192]{0:T(256)} %param.13) | copy-start | bytes 2308
  1.6 3.5 %copy-start.4 = (f32[192]{0:T(256)S(1)}, f32[192]{0:T(256)}, u32[]{:S(2)}) copy-start(f32[192]{0:T(256)} %param.11) | copy-start | bytes 2308
  1.6 3.5 %copy-start.5 = (f32[192]{0:T(256)S(1)}, f32[192]{0:T(256)}, u32[]{:S(2)}) copy-start(f32[192]{0:T(256)} %param.14) | copy-start | bytes 2308
  2.0 5.2 %collective-permute-start = (bf16[4,2,16,384]{3,2,1,0:T(8,128)(2,1)S(1)}, bf16[4,2,16,384]{3,2,1,0:T(8,128)(2,1)S(1)}, u32[]{:S(2)}, u32[]{:S(2)}) collective-permute-start(bf16[4,2,16,384]{3,2,1,0:T(8,128)(2,1)S(1)} %get-tuple-element.9), channel_id=1, source_target_pairs={{0,2},{2,0},{4,6},{6,4},{8,10},{10,8},{12,14},{14,12},{1,3},{3,1},... | collective-permute-start | bytes 294920 | tf_op jit(solution)/shard_map/ppermute | solution.py:375
  3.6 6.4 %collective-permute-start.1 = (bf16[4,2,16,384]{3,2,1,0:T(8,128)(2,1)S(1)}, bf16[4,2,16,384]{3,2,1,0:T(8,128)(2,1)S(1)}, u32[]{:S(2)}, u32[]{:S(2)}) collective-permute-start(bf16[4,2,16,384]{3,2,1,0:T(8,128)(2,1)S(1)} %get-tuple-element.9), channel_id=1, source_target_pairs={{0,6},{2,4},{4,10},{6,8},{8,14},{10,12},{12,0},{14,2},{1,7},{3,5},... | collective-permute-start | bytes 294920 | tf_op jit(solution)/shard_map/ppermute | solution.py:375

commit v16 on v15

--- a/solution.py
+++ b/solution.py
@@ -101,15 +101,17 @@
 def mix_weights(weight, mixed):
     for b in range(3):
         outer = weight[0, b] + weight[2, b]
-        mixed[0, b] = (outer + weight[1, b]) * -0.5
-        mixed[1, b] = (outer - weight[1, b]) * -0.5
+        mixed[0, b] = outer + weight[1, b]
+        mixed[1, b] = outer - weight[1, b]
 
 
 def mix(frames, i, out):
     if i == 1:
-        out[...] = frames[1][...] + frames[2][...]
+        out[...] = (frames[1][...] + frames[2][...]) * -0.5
+    elif i == 2:
+        out[...] = (frames[1][...] - frames[2][...]) * 0.5
     else:
-        one, other = ((0, 2), None, (2, 1), (1, 3))[i]
+        one, other = (0, 2) if i == 0 else (1, 3)
         out[...] = frames[one][...] - frames[other][...]
 
 
@@ -287,9 +289,7 @@
 
     half = frames // 2
     bias_two_wide = twice(bias_two)
-    rims(range(4))
-    for f in range(2, frames, 2):
-        rims(range(f + 2, f + 4))
+    rims(range(frames + 2))
     for h in range(1, frames + 1):
         norm_hidden(h)
     one = product(1)

time: 14.1 us -> 13.6 us (0.965)
  Pallas kernels: 8.38 us -> 7.93 us
    pallas_call x1, Pallas kernels: 3.86 us -> 3.47 us  [shards(): pl.pallas_call(functools.partial(last_kernel, bands), out_shape=result, i...]
  transfers between devices with their start and end apart: 3 -> 3, of which waited for: 1 -> 1; matrix products, arithmetic and copies ran while one was open for 0% -> 0% of each run, Pallas kernels for 32% -> 33%
where the time goes in v16:
time: 13.6 us; the launch traced here: 13.5 us
  Pallas kernels  7.93 us (58%)
  starting transfers between devices  3.99 us (29%)
  between operations  0.78 us (6%)
  waiting for transfers between devices  0.73 us (5%)
    ppermute x3, starting transfers between devices, shift(): return lax.ppermute(sent, ('tm', 'space'), pairs_of)  3.99 us
    pallas_call x1, Pallas kernels, shards(): pl.pallas_call(functools.partial(last_kernel, bands), out_shape=result, i...  3.47 us
    pallas_call x1, Pallas kernels, shards(): pl.pallas_call(functools.partial(earlier_kernel, bands, deep), out_shape=...  2.07 us
    pallas_call x1, Pallas kernels, shards(): pl.pallas_call(functools.partial(own_kernel, bands, deep), out_shape=[jax...  2.02 us
    ppermute x3, waiting for transfers between devices, shift(): return lax.ppermute(sent, ('tm', 'space'), pairs_of)  0.73 us
    pallas_call x1, Pallas kernels, shards(): pl.pallas_call(functools.partial(norm_kernel, swap), out_shape=[jax.Shape...  0.35 us
  transfers between devices with their start and end apart: 3, of which 1 were waited for; matrix products, arithmetic and copies ran while one was open for 0% of the time, Pallas kernels for 33%

profile of v16, /device:TPU:16, one launch (start us, length us, event | category | flops | bytes accessed | tf_op | source)
XLA Modules:
  0.0 13.5 jit_solution(691585133382844597)
XLA Ops:
  0.0 0.0 copy-start.2
  0.0 0.0 copy-start.6
  0.0 1.6 %collective-permute-start.2 = (bf16[4,4,6144]{2,1,0:T(4,128)(2,1)}, bf16[4,4,6144]{2,1,0:T(4,128)(2,1)S(1)}, u32[]{:S(2)}, u32[]{:S(2)}) collective-permute-start(bf16[4,4,6144]{2,1,0:T(4,128)(2,1)} %bitcast.15), channel_id=1, source_target_pairs={{0,4},{2,6},{4,8},{6,10},{8,12},{10,14},{12,0},{14,2},{1,5},{3,7},... | collective-permute-start | bytes 589832 | tf_op jit(solution)/shard_map/ppermute | solution.py:375
  1.6 0.0 copy-done.2
  1.6 0.0 copy-done.6
  1.6 0.0 copy-start
  1.6 0.0 copy-start.1
  1.6 0.0 copy-start.3
  1.6 0.0 copy-start.4
  1.6 0.0 copy-start.5
  1.7 0.4 %norm_and_cut.1 = (bf16[4,4,16,384]{3,2,1,0:T(8,128)(2,1)S(1)}, bf16[4,2,16,384]{3,2,1,0:T(8,128)(2,1)S(1)}) custom-call(f32[8,384]{1,0:T(8,128)S(1)} %lane_mask.1.mask, bf16[4,4,6144]{2,1,0:T(4,128)(2,1)S(1)} %bitcast.16, f32[1,192]{1,0:T(1,128)S(1)} %bitcast.28), custom_call_target="tpu_custom_call" | custom-call | flops 4294967296 | bytes 1048576 | tf_op jit(solution)/shard_map/norm_and_cut/pallas_call | solution.py:392
  2.0 1.6 %collective-permute-start = (bf16[4,2,16,384]{3,2,1,0:T(8,128)(2,1)S(1)}, bf16[4,2,16,384]{3,2,1,0:T(8,128)(2,1)S(1)}, u32[]{:S(2)}, u32[]{:S(2)}) collective-permute-start(bf16[4,2,16,384]{3,2,1,0:T(8,128)(2,1)S(1)} %get-tuple-element.9), channel_id=1, source_target_pairs={{0,2},{2,0},{4,6},{6,4},{8,10},{10,8},{12,14},{14,12},{1,3},{3,1},... | collective-permute-start | bytes 294920 | tf_op jit(solution)/shard_map/ppermute | solution.py:375
  3.6 0.9 %collective-permute-start.1 = (bf16[4,2,16,384]{3,2,1,0:T(8,128)(2,1)S(1)}, bf16[4,2,16,384]{3,2,1,0:T(8,128)(2,1)S(1)}, u32[]{:S(2)}, u32[]{:S(2)}) collective-permute-start(bf16[4,2,16,384]{3,2,1,0:T(8,128)(2,1)S(1)} %get-tuple-element.9), channel_id=1, source_target_pairs={{0,6},{2,4},{4,10},{6,8},{8,14},{10,12},{12,0},{14,2},{1,7},{3,5},... | collective-permute-start | bytes 294920 | tf_op jit(solution)/shard_map/ppermute | solution.py:375
  5.1 0.0 copy-done
  5.1 0.0 copy-done.1
  5.1 0.0 copy-done.3
  5.1 0.0 copy-done.4
  5.1 0.0 copy-done.5
  5.1 2.0 %conv_one_own.1 = (f32[2,4,5,16,192]{4,3,2,1,0:T(8,128)S(1)}, bf16[2,3,576,192]{3,2,1,0:T(8,128)(2,1)S(1)}) custom-call(s32[1]{0:T(128)S(6)} %copy.9.count, bf16[4,4,16,384]{3,2,1,0:T(8,128)(2,1)S(1)} %get-tuple-element.10.normed, bf16[3,3,576,192]{3,2,1,0:T(8,128)(2,1)S(1)} %bitcast.8, bf16[3,3,576,192]{3,2,1,0:T(8,128)(2,1)S(1)} %bitcast.12, ...), custom_call_target="tpu_custom_call" | custom-call | flops 1048576 | bytes 65536 | tf_op jit(solution)/shard_map/conv_one_own/pallas_call | solution.py:418
  7.1 0.0 collective-permute-done.above.below
  7.2 0.7 %collective-permute-done.2.earlier = bf16[4,4,6144]{2,1,0:T(4,128)(2,1)S(1)} collective-permute-done((bf16[4,4,6144]{2,1,0:T(4,128)(2,1)}, bf16[4,4,6144]{2,1,0:T(4,128)(2,1)S(1)}, u32[]{:S(2)}, u32[]{:S(2)}) %collective-permute-start.2) | collective-permute-done | bytes 196640 | tf_op jit(solution)/shard_map/ppermute | solution.py:375
  7.9 2.1 %conv_one_earlier.1.from_earlier = f32[2,4,5,16,192]{4,3,2,1,0:T(8,128)S(1)} custom-call(s32[1]{0:T(128)S(6)} %copy.9.count, f32[8,384]{1,0:T(8,128)S(1)} %lane_mask.1.mask, bf16[4,4,6144]{2,1,0:T(4,128)(2,1)S(1)} %collective-permute-done.2.earlier, f32[1,192]{1,0:T(1,128)S(1)} %bitcast.29, bf16[3,3,576,192]{3,2,1,0:T(8,128)(2,1)S(1)} %bitcast.10, ...), custom_call_target="tpu_custom_call" | custom-call | flops 1048576 | bytes 65536 | tf_op jit(solution)/shard_map/conv_one_earlier/pallas_call | solution.py:451
  10.0 0.0 collective-permute-done.1.far_above.far_below
  10.0 3.5 %last.1 = bf16[4,4,6144]{2,1,0:T(4,128)(2,1)} custom-call(s32[1]{0:T(128)S(6)} %copy.9.count, bf16[4,4,6144]{2,1,0:T(4,128)(2,1)S(1)} %bitcast.18, bf16[4,2,16,384]{3,2,1,0:T(8,128)(2,1)S(1)} %collective-permute-done.above.below, bf16[4,2,16,384]{3,2,1,0:T(8,128)(2,1)S(1)} %collective-permute-done.above.below, ...), custom_call_target="tpu_custom_call" | custom-call | flops 4294967296 | bytes 6291456 | tf_op jit(solution)/shard_map/last/pallas_call | solution.py:461
  (2 shorter events, 0.0 us)
Async XLA Ops:
  0.0 1.6 %copy-start.2 = (bf16[1,4,4,6144]{3,2,1,0:T(4,128)(2,1)S(1)}, bf16[1,4,4,6144]{3,2,1,0:T(4,128)(2,1)}, u32[]{:S(2)}) copy-start(bf16[1,4,4,6144]{3,2,1,0:T(4,128)(2,1)} %param.8) | copy-start | bytes 589828
  0.0 1.6 %copy-start.6 = (f32[192]{0:T(256)S(1)}, f32[192]{0:T(256)}, u32[]{:S(2)}) copy-start(f32[192]{0:T(256)} %param.10) | copy-start | bytes 2308
  0.0 7.9 %collective-permute-start.2 = (bf16[4,4,6144]{2,1,0:T(4,128)(2,1)}, bf16[4,4,6144]{2,1,0:T(4,128)(2,1)S(1)}, u32[]{:S(2)}, u32[]{:S(2)}) collective-permute-start(bf16[4,4,6144]{2,1,0:T(4,128)(2,1)} %bitcast.15), channel_id=1, source_target_pairs={{0,4},{2,6},{4,8},{6,10},{8,12},{10,14},{12,0},{14,2},{1,5},{3,7},... | collective-permute-start | bytes 589832 | tf_op jit(solution)/shard_map/ppermute | solution.py:375
  1.6 3.5 %copy-start = (bf16[3,3,3,192,192]{4,3,2,1,0:T(8,128)(2,1)S(1)}, bf16[3,3,3,192,192]{4,3,2,1,0:T(8,128)(2,1)}, u32[]{:S(2)}) copy-start(bf16[3,3,3,192,192]{4,3,2,1,0:T(8,128)(2,1)} %param.12) | copy-start | bytes 5971972
  1.6 3.5 %copy-start.1 = (bf16[3,3,3,192,192]{4,3,2,1,0:T(8,128)(2,1)S(1)}, bf16[3,3,3,192,192]{4,3,2,1,0:T(8,128)(2,1)}, u32[]{:S(2)}) copy-start(bf16[3,3,3,192,192]{4,3,2,1,0:T(8,128)(2,1)} %param.15) | copy-start | bytes 5971972
  1.6 3.5 %copy-start.3 = (f32[192]{0:T(256)S(1)}, f32[192]{0:T(256)}, u32[]{:S(2)}) copy-start(f32[192]{0:T(256)} %param.13) | copy-start | bytes 2308
  1.6 3.5 %copy-start.4 = (f32[192]{0:T(256)S(1)}, f32[192]{0:T(256)}, u32[]{:S(2)}) copy-start(f32[192]{0:T(256)} %param.11) | copy-start | bytes 2308
  1.6 3.5 %copy-start.5 = (f32[192]{0:T(256)S(1)}, f32[192]{0:T(256)}, u32[]{:S(2)}) copy-start(f32[192]{0:T(256)} %param.14) | copy-start | bytes 2308
  2.0 5.1 %collective-permute-start = (bf16[4,2,16,384]{3,2,1,0:T(8,128)(2,1)S(1)}, bf16[4,2,16,384]{3,2,1,0:T(8,128)(2,1)S(1)}, u32[]{:S(2)}, u32[]{:S(2)}) collective-permute-start(bf16[4,2,16,384]{3,2,1,0:T(8,128)(2,1)S(1)} %get-tuple-element.9), channel_id=1, source_target_pairs={{0,2},{2,0},{4,6},{6,4},{8,10},{10,8},{12,14},{14,12},{1,3},{3,1},... | collective-permute-start | bytes 294920 | tf_op jit(solution)/shard_map/ppermute | solution.py:375
  3.6 6.4 %collective-permute-start.1 = (bf16[4,2,16,384]{3,2,1,0:T(8,128)(2,1)S(1)}, bf16[4,2,16,384]{3,2,1,0:T(8,128)(2,1)S(1)}, u32[]{:S(2)}, u32[]{:S(2)}) collective-permute-start(bf16[4,2,16,384]{3,2,1,0:T(8,128)(2,1)S(1)} %get-tuple-element.9), channel_id=1, source_target_pairs={{0,6},{2,4},{4,10},{6,8},{8,14},{10,12},{12,0},{14,2},{1,7},{3,5},... | collective-permute-start | bytes 294920 | tf_op jit(solution)/shard_map/ppermute | solution.py:375

commit v17 on v16

--- a/solution.py
+++ b/solution.py
@@ -198,32 +198,32 @@
             total[q, 0 : frames - 2] = soon[q].reshape(frames - 2, *total.shape[2:])
 
 
-def add_rims(total, near, far, weight, side, keep, channels, wanted):
-    frames, pairs, wide = near.shape[0], near.shape[2], near.shape[3]
-    deep = total[0].shape[1]
-    low = (deep - 2) * side
-    halo = (deep - 1) * side
+def rim_sums(near, far, weight, side, keep, channels, frames):
+    pairs, wide = near.shape[2], near.shape[3]
     nothing = jnp.zeros((pairs, wide), BF16)
 
     def row(f, r):
         ref, at = (far, f) if f < frames else (near, f - frames)
         return jnp.where(keep(f), ref[at, r], nothing)
 
-    span = len(wanted)
-    rows = {f: [row(f, r) for r in range(2)] for f in range(wanted[0], wanted[-1] + 3)}
-    inner = {f: row(f, 1 - side) for f in rows}
-    parts = [jnp.concatenate([x for h in wanted for x in rows[h + a]], axis=0) for a in range(3)]
-    added = add_moved(*products(parts, [weight[a, 2 * side] for a in range(3)], channels), pairs)
-    for q in range(2):
-        both = added[q].reshape(span, 2, pairs, channels)
-        for n, h in enumerate(wanted):
-            total[h][q, pl.ds(low, 2)] += both[n]
-    parts = [jnp.concatenate([inner[h + a] for h in wanted], axis=0) for a in range(3)]
-    added = add_moved(*products(parts, [weight[a, 1] for a in range(3)], channels), pairs)
-    for q in range(2):
-        one = added[q].reshape(span, pairs, channels)
-        for n, h in enumerate(wanted):
-            total[h][q, halo] += one[n]
+    span = frames + 2
+    rows = [[row(f, r) for r in range(2)] for f in range(2 * frames)]
+    inner = [row(f, 1 - side) for f in range(2 * frames)]
+    parts = [
+        jnp.concatenate([x for f in range(span) for x in rows[f + a]], axis=0) for a in range(3)
+    ]
+    both = add_moved(*products(parts, [weight[a, 2 * side] for a in range(3)], channels), pairs)
+    parts = [jnp.concatenate([inner[f + a] for f in range(span)], axis=0) for a in range(3)]
+    outer = add_moved(*products(parts, [weight[a, 1] for a in range(3)], channels), pairs)
+    tall = 2 * pairs
+    halo = lax.broadcasted_iota(jnp.int32, (tall, channels), 0) // pairs == side
+
+    def at(q, h):
+        one = outer[q][h * pairs : (h + 1) * pairs]
+        one = jnp.where(halo, jnp.concatenate([one, one], axis=0), 0.0)
+        return both[q][h * tall : (h + 1) * tall] + one
+
+    return at
 
 
 def finish(bands, count, own, near, far, bias, weight, gain_two, bias_two, weight_two, mixed_two, out, total, hidden, mixed, final, ready):
@@ -237,30 +237,37 @@
         at = (tm - 1) * frames + f
         return (at >= 0) & (at < count[0])
 
-    def rims(wanted):
-        if bands == 2:
-            add_rims(total, near[0], far[0], weight, 1 - space, valid, channels, wanted)
-        else:
-            above = lambda f: valid(f) & (space > 0)
-            below = lambda f: valid(f) & (space < bands - 1)
-            add_rims(total, near[0], far[0], weight, 0, above, channels, wanted)
-            add_rims(total, near[1], far[1], weight, 1, below, channels, wanted)
-
     start = (1 - space) if bands == 2 else 0
-    row = lax.broadcasted_iota(jnp.int32, (fill, 1), 0) // pairs + (space * rows - 1 + start)
-    row_ok = (row >= 0) & (row < bands * rows)
+    if bands == 2:
+        sides = [(near[0], far[0], 1 - space, valid)]
+        first, deep_inner = 2 * space, deep - 2
+    else:
+        sides = [
+            (near[0], far[0], 0, lambda f: valid(f) & (space > 0)),
+            (near[1], far[1], 1, lambda f: valid(f) & (space < bands - 1)),
+        ]
+        first, deep_inner = 2, deep - 4
     bias_wide, gain_wide = twice(bias), twice(gain_two)
-    first_lanes = lax.broadcasted_iota(jnp.int32, (fill, wide), 1) < channels
-
-    def norm_hidden(h):
-        good = row_ok & valid(frames + h - 2)
-        t = jnp.concatenate([total[h][q].reshape(fill, channels) for q in range(2)], axis=1)
+
+    def norm_rows(h, sums, base):
+        t = jnp.concatenate(sums, axis=1)
+        number = t.shape[0] // pairs
+        row = lax.broadcasted_iota(jnp.int32, (t.shape[0], 1), 0) // pairs
+        row = row + (space * rows - 1 + start + base)
+        good = (row >= 0) & (row < bands * rows) & valid(frames + h - 2)
         t = jnp.where(good, t + bias_wide, 0.0).astype(BF16).astype(F32)
-        y = norm_silu_pair(t, gain_wide, first_lanes, channels).astype(BF16)
-        hidden[h][0] = jnp.zeros((pairs, wide), BF16)
-        hidden[h][rows + 1] = jnp.zeros((pairs, wide), BF16)
-        for r in range(deep):
-            hidden[h][start + r] = y[r * pairs : (r + 1) * pairs]
+        lanes = lax.broadcasted_iota(jnp.int32, t.shape, 1) < channels
+        y = norm_silu_pair(t, gain_wide, lanes, channels).astype(BF16)
+        for r in range(number):
+            hidden[h][start + base + r] = y[r * pairs : (r + 1) * pairs]
+
+    def rows_of(h, q, base, number):
+        return total[h][q, pl.ds(base, number)].reshape(number * pairs, channels)
+
+    def norm_rims(h):
+        for (_, _, side, _), sums in zip(sides, added):
+            low = (deep - 2) * side
+            norm_rows(h, [rows_of(h, q, low, 2) + sums(q, h) for q in range(2)], low)
 
     def product(i):
         for n in range(half):
@@ -289,14 +296,18 @@
 
     half = frames // 2
     bias_two_wide = twice(bias_two)
-    rims(range(frames + 2))
+    added = [rim_sums(n, f, weight, side, keep, channels, frames) for n, f, side, keep in sides]
+    for h in range(frames + 2):
+        hidden[h][0] = jnp.zeros((pairs, wide), BF16)
+        hidden[h][rows + 1] = jnp.zeros((pairs, wide), BF16)
+        norm_rows(h, [rows_of(h, q, first, deep_inner) for q in range(2)], first)
     for h in range(1, frames + 1):
-        norm_hidden(h)
+        norm_rims(h)
     one = product(1)
     two = product(2)
-    norm_hidden(0)
+    norm_rims(0)
     zero = product(0)
-    norm_hidden(frames + 1)
+    norm_rims(frames + 1)
     three = product(3)
     emit(0, [x - y - z for x, y, z in zip(zero, one, two)])
     emit(1, [z - y - x for x, y, z in zip(three, one, two)])

time: 13.6 us -> 13.6 us (level)
  no operation moved by 1% of the time
where the time goes in v17:
time: 13.6 us; the launch traced here: 13.5 us
  Pallas kernels  7.93 us (58%)
  starting transfers between devices  3.99 us (29%)
  between operations  0.78 us (6%)
  waiting for transfers between devices  0.73 us (5%)
    ppermute x3, starting transfers between devices, shift(): return lax.ppermute(sent, ('tm', 'space'), pairs_of)  3.99 us
    pallas_call x1, Pallas kernels, shards(): pl.pallas_call(functools.partial(last_kernel, bands), out_shape=result, i...  3.47 us
    pallas_call x1, Pallas kernels, shards(): pl.pallas_call(functools.partial(earlier_kernel, bands, deep), out_shape=...  2.07 us
    pallas_call x1, Pallas kernels, shards(): pl.pallas_call(functools.partial(own_kernel, bands, deep), out_shape=[jax...  2.02 us
    ppermute x3, waiting for transfers between devices, shift(): return lax.ppermute(sent, ('tm', 'space'), pairs_of)  0.73 us
    pallas_call x1, Pallas kernels, shards(): pl.pallas_call(functools.partial(norm_kernel, swap), out_shape=[jax.Shape...  0.35 us
  transfers between devices with their start and end apart: 3, of which 1 were waited for; matrix products, arithmetic and copies ran while one was open for 0% of the time, Pallas kernels for 33%

profile of v17, /device:TPU:16, one launch (start us, length us, event | category | flops | bytes accessed | tf_op | source)
XLA Modules:
  0.0 13.5 jit_solution(12349516366373224222)
XLA Ops:
  0.0 0.0 copy-start.2
  0.0 0.0 copy-start.6
  0.0 1.6 %collective-permute-start.2 = (bf16[4,4,6144]{2,1,0:T(4,128)(2,1)}, bf16[4,4,6144]{2,1,0:T(4,128)(2,1)S(1)}, u32[]{:S(2)}, u32[]{:S(2)}) collective-permute-start(bf16[4,4,6144]{2,1,0:T(4,128)(2,1)} %bitcast.15), channel_id=1, source_target_pairs={{0,4},{2,6},{4,8},{6,10},{8,12},{10,14},{12,0},{14,2},{1,5},{3,7},... | collective-permute-start | bytes 589832 | tf_op jit(solution)/shard_map/ppermute | solution.py:386
  1.6 0.0 copy-done.2
  1.6 0.0 copy-done.6
  1.6 0.0 copy-start
  1.6 0.0 copy-start.1
  1.6 0.0 copy-start.3
  1.6 0.0 copy-start.4
  1.6 0.0 copy-start.5
  1.7 0.4 %norm_and_cut.1 = (bf16[4,4,16,384]{3,2,1,0:T(8,128)(2,1)S(1)}, bf16[4,2,16,384]{3,2,1,0:T(8,128)(2,1)S(1)}) custom-call(f32[8,384]{1,0:T(8,128)S(1)} %lane_mask.1.mask, bf16[4,4,6144]{2,1,0:T(4,128)(2,1)S(1)} %bitcast.16, f32[1,192]{1,0:T(1,128)S(1)} %bitcast.28), custom_call_target="tpu_custom_call" | custom-call | flops 4294967296 | bytes 1048576 | tf_op jit(solution)/shard_map/norm_and_cut/pallas_call | solution.py:403
  2.0 1.6 %collective-permute-start = (bf16[4,2,16,384]{3,2,1,0:T(8,128)(2,1)S(1)}, bf16[4,2,16,384]{3,2,1,0:T(8,128)(2,1)S(1)}, u32[]{:S(2)}, u32[]{:S(2)}) collective-permute-start(bf16[4,2,16,384]{3,2,1,0:T(8,128)(2,1)S(1)} %get-tuple-element.9), channel_id=1, source_target_pairs={{0,2},{2,0},{4,6},{6,4},{8,10},{10,8},{12,14},{14,12},{1,3},{3,1},... | collective-permute-start | bytes 294920 | tf_op jit(solution)/shard_map/ppermute | solution.py:386
  3.6 0.9 %collective-permute-start.1 = (bf16[4,2,16,384]{3,2,1,0:T(8,128)(2,1)S(1)}, bf16[4,2,16,384]{3,2,1,0:T(8,128)(2,1)S(1)}, u32[]{:S(2)}, u32[]{:S(2)}) collective-permute-start(bf16[4,2,16,384]{3,2,1,0:T(8,128)(2,1)S(1)} %get-tuple-element.9), channel_id=1, source_target_pairs={{0,6},{2,4},{4,10},{6,8},{8,14},{10,12},{12,0},{14,2},{1,7},{3,5},... | collective-permute-start | bytes 294920 | tf_op jit(solution)/shard_map/ppermute | solution.py:386
  5.1 0.0 copy-done
  5.1 0.0 copy-done.1
  5.1 0.0 copy-done.3
  5.1 0.0 copy-done.4
  5.1 0.0 copy-done.5
  5.1 2.0 %conv_one_own.1 = (f32[2,4,5,16,192]{4,3,2,1,0:T(8,128)S(1)}, bf16[2,3,576,192]{3,2,1,0:T(8,128)(2,1)S(1)}) custom-call(s32[1]{0:T(128)S(6)} %copy.9.count, bf16[4,4,16,384]{3,2,1,0:T(8,128)(2,1)S(1)} %get-tuple-element.10.normed, bf16[3,3,576,192]{3,2,1,0:T(8,128)(2,1)S(1)} %bitcast.8, bf16[3,3,576,192]{3,2,1,0:T(8,128)(2,1)S(1)} %bitcast.12, ...), custom_call_target="tpu_custom_call" | custom-call | flops 1048576 | bytes 65536 | tf_op jit(solution)/shard_map/conv_one_own/pallas_call | solution.py:429
  7.2 0.0 collective-permute-done.above.below
  7.2 0.7 %collective-permute-done.2.earlier = bf16[4,4,6144]{2,1,0:T(4,128)(2,1)S(1)} collective-permute-done((bf16[4,4,6144]{2,1,0:T(4,128)(2,1)}, bf16[4,4,6144]{2,1,0:T(4,128)(2,1)S(1)}, u32[]{:S(2)}, u32[]{:S(2)}) %collective-permute-start.2) | collective-permute-done | bytes 196640 | tf_op jit(solution)/shard_map/ppermute | solution.py:386
  7.9 2.1 %conv_one_earlier.1.from_earlier = f32[2,4,5,16,192]{4,3,2,1,0:T(8,128)S(1)} custom-call(s32[1]{0:T(128)S(6)} %copy.9.count, f32[8,384]{1,0:T(8,128)S(1)} %lane_mask.1.mask, bf16[4,4,6144]{2,1,0:T(4,128)(2,1)S(1)} %collective-permute-done.2.earlier, f32[1,192]{1,0:T(1,128)S(1)} %bitcast.29, bf16[3,3,576,192]{3,2,1,0:T(8,128)(2,1)S(1)} %bitcast.10, ...), custom_call_target="tpu_custom_call" | custom-call | flops 1048576 | bytes 65536 | tf_op jit(solution)/shard_map/conv_one_earlier/pallas_call | solution.py:462
  10.0 0.0 collective-permute-done.1.far_above.far_below
  10.0 3.5 %last.1 = bf16[4,4,6144]{2,1,0:T(4,128)(2,1)} custom-call(s32[1]{0:T(128)S(6)} %copy.9.count, bf16[4,4,6144]{2,1,0:T(4,128)(2,1)S(1)} %bitcast.18, bf16[4,2,16,384]{3,2,1,0:T(8,128)(2,1)S(1)} %collective-permute-done.above.below, bf16[4,2,16,384]{3,2,1,0:T(8,128)(2,1)S(1)} %collective-permute-done.above.below, ...), custom_call_target="tpu_custom_call" | custom-call | flops 4294967296 | bytes 6291456 | tf_op jit(solution)/shard_map/last/pallas_call | solution.py:472
  (2 shorter events, 0.0 us)
Async XLA Ops:
  0.0 1.6 %copy-start.2 = (bf16[1,4,4,6144]{3,2,1,0:T(4,128)(2,1)S(1)}, bf16[1,4,4,6144]{3,2,1,0:T(4,128)(2,1)}, u32[]{:S(2)}) copy-start(bf16[1,4,4,6144]{3,2,1,0:T(4,128)(2,1)} %param.8) | copy-start | bytes 589828
  0.0 1.6 %copy-start.6 = (f32[192]{0:T(256)S(1)}, f32[192]{0:T(256)}, u32[]{:S(2)}) copy-start(f32[192]{0:T(256)} %param.10) | copy-start | bytes 2308
  0.0 7.9 %collective-permute-start.2 = (bf16[4,4,6144]{2,1,0:T(4,128)(2,1)}, bf16[4,4,6144]{2,1,0:T(4,128)(2,1)S(1)}, u32[]{:S(2)}, u32[]{:S(2)}) collective-permute-start(bf16[4,4,6144]{2,1,0:T(4,128)(2,1)} %bitcast.15), channel_id=1, source_target_pairs={{0,4},{2,6},{4,8},{6,10},{8,12},{10,14},{12,0},{14,2},{1,5},{3,7},... | collective-permute-start | bytes 589832 | tf_op jit(solution)/shard_map/ppermute | solution.py:386
  1.6 3.5 %copy-start = (bf16[3,3,3,192,192]{4,3,2,1,0:T(8,128)(2,1)S(1)}, bf16[3,3,3,192,192]{4,3,2,1,0:T(8,128)(2,1)}, u32[]{:S(2)}) copy-start(bf16[3,3,3,192,192]{4,3,2,1,0:T(8,128)(2,1)} %param.12) | copy-start | bytes 5971972
  1.6 3.5 %copy-start.1 = (bf16[3,3,3,192,192]{4,3,2,1,0:T(8,128)(2,1)S(1)}, bf16[3,3,3,192,192]{4,3,2,1,0:T(8,128)(2,1)}, u32[]{:S(2)}) copy-start(bf16[3,3,3,192,192]{4,3,2,1,0:T(8,128)(2,1)} %param.15) | copy-start | bytes 5971972
  1.6 3.5 %copy-start.3 = (f32[192]{0:T(256)S(1)}, f32[192]{0:T(256)}, u32[]{:S(2)}) copy-start(f32[192]{0:T(256)} %param.13) | copy-start | bytes 2308
  1.6 3.5 %copy-start.4 = (f32[192]{0:T(256)S(1)}, f32[192]{0:T(256)}, u32[]{:S(2)}) copy-start(f32[192]{0:T(256)} %param.11) | copy-start | bytes 2308
  1.6 3.5 %copy-start.5 = (f32[192]{0:T(256)S(1)}, f32[192]{0:T(256)}, u32[]{:S(2)}) copy-start(f32[192]{0:T(256)} %param.14) | copy-start | bytes 2308
  2.0 5.1 %collective-permute-start = (bf16[4,2,16,384]{3,2,1,0:T(8,128)(2,1)S(1)}, bf16[4,2,16,384]{3,2,1,0:T(8,128)(2,1)S(1)}, u32[]{:S(2)}, u32[]{:S(2)}) collective-permute-start(bf16[4,2,16,384]{3,2,1,0:T(8,128)(2,1)S(1)} %get-tuple-element.9), channel_id=1, source_target_pairs={{0,2},{2,0},{4,6},{6,4},{8,10},{10,8},{12,14},{14,12},{1,3},{3,1},... | collective-permute-start | bytes 294920 | tf_op jit(solution)/shard_map/ppermute | solution.py:386
  3.6 6.4 %collective-permute-start.1 = (bf16[4,2,16,384]{3,2,1,0:T(8,128)(2,1)S(1)}, bf16[4,2,16,384]{3,2,1,0:T(8,128)(2,1)S(1)}, u32[]{:S(2)}, u32[]{:S(2)}) collective-permute-start(bf16[4,2,16,384]{3,2,1,0:T(8,128)(2,1)S(1)} %get-tuple-element.9), channel_id=1, source_target_pairs={{0,6},{2,4},{4,10},{6,8},{8,14},{10,12},{12,0},{14,2},{1,7},{3,5},... | collective-permute-start | bytes 294920 | tf_op jit(solution)/shard_map/ppermute | solution.py:386

commit v18 on v17

--- a/solution.py
+++ b/solution.py
@@ -226,12 +226,10 @@
     return at
 
 
-def finish(bands, count, own, near, far, bias, weight, gain_two, bias_two, weight_two, mixed_two, out, total, hidden, mixed, final, ready):
+def finish(bands, count, own, near, far, bias, weight, gain_two, bias_two, weight_two, mixed_two, out, deep, sums_at, hidden, mixed, final, ready):
     frames, rows, pairs, wide = near[0].shape[0], own.shape[1], near[0].shape[2], near[0].shape[3]
     channels = wide // 2
-    deep = total[0].shape[1]
     tm, space = lax.axis_index("tm"), lax.axis_index("space")
-    fill = deep * pairs
 
     def valid(f):
         at = (tm - 1) * frames + f
@@ -262,7 +260,7 @@
             hidden[h][start + base + r] = y[r * pairs : (r + 1) * pairs]
 
     def rows_of(h, q, base, number):
-        return total[h][q, pl.ds(base, number)].reshape(number * pairs, channels)
+        return sums_at(h, q, pl.ds(base, number)).reshape(number * pairs, channels)
 
     def norm_rims(h):
         for (_, _, side, _), sums in zip(sides, added):
@@ -308,8 +306,8 @@
     norm_rims(0)
     zero = product(0)
     norm_rims(frames + 1)
+    emit(0, [x - y - z for x, y, z in zip(zero, one, two)])
     three = product(3)
-    emit(0, [x - y - z for x, y, z in zip(zero, one, two)])
     emit(1, [z - y - x for x, y, z in zip(three, one, two)])
 
 
@@ -321,18 +319,20 @@
 
     @pl.when(lax.axis_index("tm") == 0)
     def _():
-        for h, part in enumerate(parts[0]):
-            part[...] = jnp.zeros(part.shape, F32) if h < 2 else from_own[:, h - 2]
+        def sums_at(h, q, rows):
+            value = from_own[q, max(h - 2, 0), rows]
+            return value if h >= 2 else jnp.zeros_like(value)
+
         near = (above, below)
         finish(
             bands, count, own, near, near, bias, weight, gain_two, bias_two, weight_two,
-            mixed_two, out, *parts, lambda f: None,
+            mixed_two, out, from_own.shape[2], sums_at, *parts, lambda f: None,
         )
 
 
 def split(scratch, frames):
-    rest = scratch[2 * frames + 4 :]
-    return scratch[: frames + 2], scratch[frames + 2 : 2 * frames + 4], rest[: 2 * frames], rest[2 * frames :]
+    rest = scratch[frames + 2 :]
+    return scratch[: frames + 2], rest[: 2 * frames], rest[2 * frames :]
 
 
 def last_kernel(
@@ -351,19 +351,20 @@
 
     @pl.when(tm > 0)
     def _():
-        for h, part in enumerate(parts[0]):
+        def sums_at(h, q, rows):
             if h < 2:
-                part[...] = from_earlier[:, h]
-            elif h < frames:
-                part[...] = from_own[:, h - 2] + from_earlier[:, h]
-            else:
-                part[...] = from_own[:, h - 2]
+                return from_earlier[q, h, rows]
+            if h < frames:
+                return from_own[q, h - 2, rows] + from_earlier[q, h, rows]
+            return from_own[q, h - 2, rows]
+
         copies = [
             pltpu.make_async_copy(result.at[f], out.at[f], sems.at[f]) for f in range(frames)
         ]
         finish(
             bands, count, own, (above, below), (far_above, far_below), bias, weight, gain_two,
-            bias_two, weight_two, mixed_two, result, *parts, lambda f: copies[f].start(),
+            bias_two, weight_two, mixed_two, result, from_own.shape[2], sums_at, *parts,
+            lambda f: copies[f].start(),
         )
         for copy in copies:
             copy.wait()
@@ -445,8 +446,7 @@
     )
     result = jax.ShapeDtypeStruct((frames, rows, flat), BF16)
     scratch = (
-        [pltpu.VMEM((2, deep, pairs, channels), F32)] * (frames + 2)
-        + [pltpu.VMEM((rows + 2, pairs, wide), BF16)] * (frames + 2 + 2 * frames)
+        [pltpu.VMEM((rows + 2, pairs, wide), BF16)] * (frames + 2 + 2 * frames)
         + [pltpu.VMEM((3, frames // 2 * rows * pairs, LANES), F32)] * 2
     )
     first_out = pl.pallas_call(

time: 13.6 us -> 13.6 us (level)
  no operation moved by 1% of the time
where the time goes in v18:
time: 13.6 us; the launch traced here: 13.4 us
  Pallas kernels  7.88 us (58%)
  starting transfers between devices  3.99 us (29%)
  between operations  0.78 us (6%)
  waiting for transfers between devices  0.73 us (5%)
    ppermute x3, starting transfers between devices, shift(): return lax.ppermute(sent, ('tm', 'space'), pairs_of)  3.99 us
    pallas_call x1, Pallas kernels, shards(): pl.pallas_call(functools.partial(last_kernel, bands), out_shape=result, i...  3.42 us
    pallas_call x1, Pallas kernels, shards(): pl.pallas_call(functools.partial(earlier_kernel, bands, deep), out_shape=...  2.07 us
    pallas_call x1, Pallas kernels, shards(): pl.pallas_call(functools.partial(own_kernel, bands, deep), out_shape=[jax...  2.02 us
    ppermute x3, waiting for transfers between devices, shift(): return lax.ppermute(sent, ('tm', 'space'), pairs_of)  0.73 us
    pallas_call x1, Pallas kernels, shards(): pl.pallas_call(functools.partial(norm_kernel, swap), out_shape=[jax.Shape...  0.35 us
  transfers between devices with their start and end apart: 3, of which 1 were waited for; matrix products, arithmetic and copies ran while one was open for 0% of the time, Pallas kernels for 33%

profile of v18, /device:TPU:16, one launch (start us, length us, event | category | flops | bytes accessed | tf_op | source)
XLA Modules:
  0.0 13.4 jit_solution(9202106674321753751)
XLA Ops:
  0.0 0.0 copy-start.2
  0.0 0.0 copy-start.6
  0.0 1.6 %collective-permute-start.2 = (bf16[4,4,6144]{2,1,0:T(4,128)(2,1)}, bf16[4,4,6144]{2,1,0:T(4,128)(2,1)S(1)}, u32[]{:S(2)}, u32[]{:S(2)}) collective-permute-start(bf16[4,4,6144]{2,1,0:T(4,128)(2,1)} %bitcast.15), channel_id=1, source_target_pairs={{0,4},{2,6},{4,8},{6,10},{8,12},{10,14},{12,0},{14,2},{1,5},{3,7},... | collective-permute-start | bytes 589832 | tf_op jit(solution)/shard_map/ppermute | solution.py:387
  1.6 0.0 copy-done.2
  1.6 0.0 copy-done.6
  1.6 0.0 copy-start
  1.6 0.0 copy-start.1
  1.6 0.0 copy-start.3
  1.6 0.0 copy-start.4
  1.6 0.0 copy-start.5
  1.7 0.4 %norm_and_cut.1 = (bf16[4,4,16,384]{3,2,1,0:T(8,128)(2,1)S(1)}, bf16[4,2,16,384]{3,2,1,0:T(8,128)(2,1)S(1)}) custom-call(f32[8,384]{1,0:T(8,128)S(1)} %lane_mask.1.mask, bf16[4,4,6144]{2,1,0:T(4,128)(2,1)S(1)} %bitcast.16, f32[1,192]{1,0:T(1,128)S(1)} %bitcast.28), custom_call_target="tpu_custom_call" | custom-call | flops 4294967296 | bytes 1048576 | tf_op jit(solution)/shard_map/norm_and_cut/pallas_call | solution.py:404
  2.0 1.6 %collective-permute-start = (bf16[4,2,16,384]{3,2,1,0:T(8,128)(2,1)S(1)}, bf16[4,2,16,384]{3,2,1,0:T(8,128)(2,1)S(1)}, u32[]{:S(2)}, u32[]{:S(2)}) collective-permute-start(bf16[4,2,16,384]{3,2,1,0:T(8,128)(2,1)S(1)} %get-tuple-element.9), channel_id=1, source_target_pairs={{0,2},{2,0},{4,6},{6,4},{8,10},{10,8},{12,14},{14,12},{1,3},{3,1},... | collective-permute-start | bytes 294920 | tf_op jit(solution)/shard_map/ppermute | solution.py:387
  3.6 0.9 %collective-permute-start.1 = (bf16[4,2,16,384]{3,2,1,0:T(8,128)(2,1)S(1)}, bf16[4,2,16,384]{3,2,1,0:T(8,128)(2,1)S(1)}, u32[]{:S(2)}, u32[]{:S(2)}) collective-permute-start(bf16[4,2,16,384]{3,2,1,0:T(8,128)(2,1)S(1)} %get-tuple-element.9), channel_id=1, source_target_pairs={{0,6},{2,4},{4,10},{6,8},{8,14},{10,12},{12,0},{14,2},{1,7},{3,5},... | collective-permute-start | bytes 294920 | tf_op jit(solution)/shard_map/ppermute | solution.py:387
  5.1 0.0 copy-done
  5.1 0.0 copy-done.1
  5.1 0.0 copy-done.3
  5.1 0.0 copy-done.4
  5.1 0.0 copy-done.5
  5.1 2.0 %conv_one_own.1 = (f32[2,4,5,16,192]{4,3,2,1,0:T(8,128)S(1)}, bf16[2,3,576,192]{3,2,1,0:T(8,128)(2,1)S(1)}) custom-call(s32[1]{0:T(128)S(6)} %copy.9.count, bf16[4,4,16,384]{3,2,1,0:T(8,128)(2,1)S(1)} %get-tuple-element.10.normed, bf16[3,3,576,192]{3,2,1,0:T(8,128)(2,1)S(1)} %bitcast.8, bf16[3,3,576,192]{3,2,1,0:T(8,128)(2,1)S(1)} %bitcast.12, ...), custom_call_target="tpu_custom_call" | custom-call | flops 1048576 | bytes 65536 | tf_op jit(solution)/shard_map/conv_one_own/pallas_call | solution.py:430
  7.2 0.0 collective-permute-done.above.below
  7.2 0.7 %collective-permute-done.2.earlier = bf16[4,4,6144]{2,1,0:T(4,128)(2,1)S(1)} collective-permute-done((bf16[4,4,6144]{2,1,0:T(4,128)(2,1)}, bf16[4,4,6144]{2,1,0:T(4,128)(2,1)S(1)}, u32[]{:S(2)}, u32[]{:S(2)}) %collective-permute-start.2) | collective-permute-done | bytes 196640 | tf_op jit(solution)/shard_map/ppermute | solution.py:387
  7.9 2.1 %conv_one_earlier.1.from_earlier = f32[2,4,5,16,192]{4,3,2,1,0:T(8,128)S(1)} custom-call(s32[1]{0:T(128)S(6)} %copy.9.count, f32[8,384]{1,0:T(8,128)S(1)} %lane_mask.1.mask, bf16[4,4,6144]{2,1,0:T(4,128)(2,1)S(1)} %collective-permute-done.2.earlier, f32[1,192]{1,0:T(1,128)S(1)} %bitcast.29, bf16[3,3,576,192]{3,2,1,0:T(8,128)(2,1)S(1)} %bitcast.10, ...), custom_call_target="tpu_custom_call" | custom-call | flops 1048576 | bytes 65536 | tf_op jit(solution)/shard_map/conv_one_earlier/pallas_call | solution.py:462
  10.0 0.0 collective-permute-done.1.far_above.far_below
  10.0 3.4 %last.1 = bf16[4,4,6144]{2,1,0:T(4,128)(2,1)} custom-call(s32[1]{0:T(128)S(6)} %copy.9.count, bf16[4,4,6144]{2,1,0:T(4,128)(2,1)S(1)} %bitcast.18, bf16[4,2,16,384]{3,2,1,0:T(8,128)(2,1)S(1)} %collective-permute-done.above.below, bf16[4,2,16,384]{3,2,1,0:T(8,128)(2,1)S(1)} %collective-permute-done.above.below, ...), custom_call_target="tpu_custom_call" | custom-call | flops 4294967296 | bytes 6291456 | tf_op jit(solution)/shard_map/last/pallas_call | solution.py:472
  (2 shorter events, 0.0 us)
Async XLA Ops:
  0.0 1.6 %copy-start.2 = (bf16[1,4,4,6144]{3,2,1,0:T(4,128)(2,1)S(1)}, bf16[1,4,4,6144]{3,2,1,0:T(4,128)(2,1)}, u32[]{:S(2)}) copy-start(bf16[1,4,4,6144]{3,2,1,0:T(4,128)(2,1)} %param.8) | copy-start | bytes 589828
  0.0 1.6 %copy-start.6 = (f32[192]{0:T(256)S(1)}, f32[192]{0:T(256)}, u32[]{:S(2)}) copy-start(f32[192]{0:T(256)} %param.10) | copy-start | bytes 2308
  0.0 7.9 %collective-permute-start.2 = (bf16[4,4,6144]{2,1,0:T(4,128)(2,1)}, bf16[4,4,6144]{2,1,0:T(4,128)(2,1)S(1)}, u32[]{:S(2)}, u32[]{:S(2)}) collective-permute-start(bf16[4,4,6144]{2,1,0:T(4,128)(2,1)} %bitcast.15), channel_id=1, source_target_pairs={{0,4},{2,6},{4,8},{6,10},{8,12},{10,14},{12,0},{14,2},{1,5},{3,7},... | collective-permute-start | bytes 589832 | tf_op jit(solution)/shard_map/ppermute | solution.py:387
  1.6 3.5 %copy-start = (bf16[3,3,3,192,192]{4,3,2,1,0:T(8,128)(2,1)S(1)}, bf16[3,3,3,192,192]{4,3,2,1,0:T(8,128)(2,1)}, u32[]{:S(2)}) copy-start(bf16[3,3,3,192,192]{4,3,2,1,0:T(8,128)(2,1)} %param.12) | copy-start | bytes 5971972
  1.6 3.5 %copy-start.1 = (bf16[3,3,3,192,192]{4,3,2,1,0:T(8,128)(2,1)S(1)}, bf16[3,3,3,192,192]{4,3,2,1,0:T(8,128)(2,1)}, u32[]{:S(2)}) copy-start(bf16[3,3,3,192,192]{4,3,2,1,0:T(8,128)(2,1)} %param.15) | copy-start | bytes 5971972
  1.6 3.5 %copy-start.3 = (f32[192]{0:T(256)S(1)}, f32[192]{0:T(256)}, u32[]{:S(2)}) copy-start(f32[192]{0:T(256)} %param.13) | copy-start | bytes 2308
  1.6 3.5 %copy-start.4 = (f32[192]{0:T(256)S(1)}, f32[192]{0:T(256)}, u32[]{:S(2)}) copy-start(f32[192]{0:T(256)} %param.11) | copy-start | bytes 2308
  1.6 3.5 %copy-start.5 = (f32[192]{0:T(256)S(1)}, f32[192]{0:T(256)}, u32[]{:S(2)}) copy-start(f32[192]{0:T(256)} %param.14) | copy-start | bytes 2308
  2.0 5.1 %collective-permute-start = (bf16[4,2,16,384]{3,2,1,0:T(8,128)(2,1)S(1)}, bf16[4,2,16,384]{3,2,1,0:T(8,128)(2,1)S(1)}, u32[]{:S(2)}, u32[]{:S(2)}) collective-permute-start(bf16[4,2,16,384]{3,2,1,0:T(8,128)(2,1)S(1)} %get-tuple-element.9), channel_id=1, source_target_pairs={{0,2},{2,0},{4,6},{6,4},{8,10},{10,8},{12,14},{14,12},{1,3},{3,1},... | collective-permute-start | bytes 294920 | tf_op jit(solution)/shard_map/ppermute | solution.py:387
  3.6 6.4 %collective-permute-start.1 = (bf16[4,2,16,384]{3,2,1,0:T(8,128)(2,1)S(1)}, bf16[4,2,16,384]{3,2,1,0:T(8,128)(2,1)S(1)}, u32[]{:S(2)}, u32[]{:S(2)}) collective-permute-start(bf16[4,2,16,384]{3,2,1,0:T(8,128)(2,1)S(1)} %get-tuple-element.9), channel_id=1, source_target_pairs={{0,6},{2,4},{4,10},{6,8},{8,14},{10,12},{12,0},{14,2},{1,7},{3,5},... | collective-permute-start | bytes 294920 | tf_op jit(solution)/shard_map/ppermute | solution.py:387

commit v19 on v18

--- a/solution.py
+++ b/solution.py
@@ -14,17 +14,23 @@
 
 def mask_kernel(channels, mask):
     lane = lax.broadcasted_iota(jnp.int32, mask.shape, 1)
-    mask[...] = jnp.where(lane < channels, 1.0, 0.0)
-
-
-def norm_silu_pair(t, gain, first, channels):
-    square = t * t
-    left = jnp.sum(jnp.where(first, square, 0.0), axis=1, keepdims=True)
-    right = jnp.sum(jnp.where(first, 0.0, square), axis=1, keepdims=True)
-    left = lax.rsqrt(left * (1.0 / channels) + 1e-06)
-    right = lax.rsqrt(right * (1.0 / channels) + 1e-06)
-    y = t * jnp.where(first, left, right) * gain
-    return y * (0.5 + 0.5 * jnp.tanh(0.5 * y))
+    mask[...] = jnp.where(lane < channels - LANES, 1.0, 0.0)
+
+
+def norm_silu_pair(t, half_gain, middle, channels):
+    tiles = [t[:, k * LANES : (k + 1) * LANES] for k in range(3)]
+    square = [tile * tile for tile in tiles]
+    left = square[0] + jnp.where(middle, square[1], 0.0)
+    right = square[2] + jnp.where(middle, 0.0, square[1])
+    left, right = [
+        lax.rsqrt(jnp.sum(x, axis=1, keepdims=True) * (1.0 / channels) + 1e-06)
+        for x in (left, right)
+    ]
+    results = []
+    for k, scale in enumerate((left, jnp.where(middle, left, right), right)):
+        h = tiles[k] * scale * half_gain[:, k * LANES : (k + 1) * LANES]
+        results.append(h + h * jnp.tanh(h))
+    return jnp.concatenate(results, axis=1)
 
 
 def twice(ref):
@@ -55,7 +61,7 @@
             normed[f, r, :, k * LANES : (k + 1) * LANES] = parts[k]
 
     for f in range(0, frames, 2):
-        norm_frames(block, f, twice(gain), mask[...] > 0.5, stages[f // 2], store, pairs)
+        norm_frames(block, f, twice(gain) * 0.5, mask[...] > 0.5, stages[f // 2], store, pairs)
     if swap:
         first = (rows - 2) * (1 - lax.axis_index("space"))
         sent[0][...] = normed[:, pl.ds(first, 2)]
@@ -185,7 +191,7 @@
                 window[f][top + r, :, k * LANES : (k + 1) * LANES] = part
 
         def norm(f):
-            norm_frames(earlier, f, twice(gain), mask[...] > 0.5, stages[f // 2], store, pairs)
+            norm_frames(earlier, f, twice(gain) * 0.5, mask[...] > 0.5, stages[f // 2], store, pairs)
 
         norm(frames - 2)
         late = conv(window, weight, frames - 2, 2, deep, (0, 1), wide // 2)
@@ -245,7 +251,7 @@
             (near[1], far[1], 1, lambda f: valid(f) & (space < bands - 1)),
         ]
         first, deep_inner = 2, deep - 4
-    bias_wide, gain_wide = twice(bias), twice(gain_two)
+    bias_wide, gain_wide = twice(bias), twice(gain_two) * 0.5
 
     def norm_rows(h, sums, base):
         t = jnp.concatenate(sums, axis=1)
@@ -254,8 +260,8 @@
         row = row + (space * rows - 1 + start + base)
         good = (row >= 0) & (row < bands * rows) & valid(frames + h - 2)
         t = jnp.where(good, t + bias_wide, 0.0).astype(BF16).astype(F32)
-        lanes = lax.broadcasted_iota(jnp.int32, t.shape, 1) < channels
-        y = norm_silu_pair(t, gain_wide, lanes, channels).astype(BF16)
+        middle = lax.broadcasted_iota(jnp.int32, (t.shape[0], LANES), 1) < channels - LANES
+        y = norm_silu_pair(t, gain_wide, middle, channels).astype(BF16)
         for r in range(number):
             hidden[h][start + base + r] = y[r * pairs : (r + 1) * pairs]
 
@@ -395,7 +401,7 @@
     stages = [pltpu.VMEM((3, 2 * rows * pairs, LANES), F32)] * (frames // 2)
     mask = pl.pallas_call(
         functools.partial(mask_kernel, channels),
-        out_shape=jax.ShapeDtypeStruct((2 * rows, wide), F32),
+        out_shape=jax.ShapeDtypeStruct((2 * rows, LANES), F32),
         out_specs=vmem,
         compiler_params=params,
         cost_estimate=pl.CostEstimate(flops=4 << 30, bytes_accessed=1 << 16, transcendentals=0),

time: 13.6 us -> 13.6 us (level)
  transfers between devices with their start and end apart: 3 -> 3, of which waited for: 1 -> 1; matrix products, arithmetic and copies ran while one was open for 0% -> 0% of each run, Pallas kernels for 33% -> 32%
where the time goes in v19:
time: 13.6 us; the launch traced here: 13.4 us
  Pallas kernels  7.84 us (58%)
  starting transfers between devices  3.99 us (29%)
  waiting for transfers between devices  0.79 us (6%)
  between operations  0.78 us (6%)
    ppermute x3, starting transfers between devices, shift(): return lax.ppermute(sent, ('tm', 'space'), pairs_of)  3.99 us
    pallas_call x1, Pallas kernels, shards(): pl.pallas_call(functools.partial(last_kernel, bands), out_shape=result, i...  3.49 us
    pallas_call x1, Pallas kernels, shards(): pl.pallas_call(functools.partial(own_kernel, bands, deep), out_shape=[jax...  2.02 us
    pallas_call x1, Pallas kernels, shards(): pl.pallas_call(functools.partial(earlier_kernel, bands, deep), out_shape=...  2.02 us
    ppermute x3, waiting for transfers between devices, shift(): return lax.ppermute(sent, ('tm', 'space'), pairs_of)  0.79 us
    pallas_call x1, Pallas kernels, shards(): pl.pallas_call(functools.partial(norm_kernel, swap), out_shape=[jax.Shape...  0.28 us
  transfers between devices with their start and end apart: 3, of which 1 were waited for; matrix products, arithmetic and copies ran while one was open for 0% of the time, Pallas kernels for 32%

profile of v19, /device:TPU:16, one launch (start us, length us, event | category | flops | bytes accessed | tf_op | source)
XLA Modules:
  0.0 13.4 jit_solution(7553103042579624002)
XLA Ops:
  0.0 0.0 copy-start.2
  0.0 0.0 copy-start.6
  0.0 1.6 %collective-permute-start.2 = (bf16[4,4,6144]{2,1,0:T(4,128)(2,1)}, bf16[4,4,6144]{2,1,0:T(4,128)(2,1)S(1)}, u32[]{:S(2)}, u32[]{:S(2)}) collective-permute-start(bf16[4,4,6144]{2,1,0:T(4,128)(2,1)} %bitcast.15), channel_id=1, source_target_pairs={{0,4},{2,6},{4,8},{6,10},{8,12},{10,14},{12,0},{14,2},{1,5},{3,7},... | collective-permute-start | bytes 589832 | tf_op jit(solution)/shard_map/ppermute | solution.py:393
  1.6 0.0 copy-done.2
  1.6 0.0 copy-done.6
  1.6 0.0 copy-start
  1.6 0.0 copy-start.1
  1.6 0.0 copy-start.3
  1.6 0.0 copy-start.4
  1.6 0.0 copy-start.5
  1.7 0.3 %norm_and_cut.1 = (bf16[4,4,16,384]{3,2,1,0:T(8,128)(2,1)S(1)}, bf16[4,2,16,384]{3,2,1,0:T(8,128)(2,1)S(1)}) custom-call(f32[8,128]{1,0:T(8,128)S(1)} %lane_mask.1.mask, bf16[4,4,6144]{2,1,0:T(4,128)(2,1)S(1)} %bitcast.16, f32[1,192]{1,0:T(1,128)S(1)} %bitcast.28), custom_call_target="tpu_custom_call" | custom-call | flops 4294967296 | bytes 1048576 | tf_op jit(solution)/shard_map/norm_and_cut/pallas_call | solution.py:410
  1.9 1.6 %collective-permute-start = (bf16[4,2,16,384]{3,2,1,0:T(8,128)(2,1)S(1)}, bf16[4,2,16,384]{3,2,1,0:T(8,128)(2,1)S(1)}, u32[]{:S(2)}, u32[]{:S(2)}) collective-permute-start(bf16[4,2,16,384]{3,2,1,0:T(8,128)(2,1)S(1)} %get-tuple-element.9), channel_id=1, source_target_pairs={{0,2},{2,0},{4,6},{6,4},{8,10},{10,8},{12,14},{14,12},{1,3},{3,1},... | collective-permute-start | bytes 294920 | tf_op jit(solution)/shard_map/ppermute | solution.py:393
  3.5 0.9 %collective-permute-start.1 = (bf16[4,2,16,384]{3,2,1,0:T(8,128)(2,1)S(1)}, bf16[4,2,16,384]{3,2,1,0:T(8,128)(2,1)S(1)}, u32[]{:S(2)}, u32[]{:S(2)}) collective-permute-start(bf16[4,2,16,384]{3,2,1,0:T(8,128)(2,1)S(1)} %get-tuple-element.9), channel_id=1, source_target_pairs={{0,6},{2,4},{4,10},{6,8},{8,14},{10,12},{12,0},{14,2},{1,7},{3,5},... | collective-permute-start | bytes 294920 | tf_op jit(solution)/shard_map/ppermute | solution.py:393
  5.0 0.0 copy-done
  5.0 0.0 copy-done.1
  5.0 0.0 copy-done.3
  5.0 0.0 copy-done.4
  5.0 0.0 copy-done.5
  5.1 2.0 %conv_one_own.1 = (f32[2,4,5,16,192]{4,3,2,1,0:T(8,128)S(1)}, bf16[2,3,576,192]{3,2,1,0:T(8,128)(2,1)S(1)}) custom-call(s32[1]{0:T(128)S(6)} %copy.9.count, bf16[4,4,16,384]{3,2,1,0:T(8,128)(2,1)S(1)} %get-tuple-element.10.normed, bf16[3,3,576,192]{3,2,1,0:T(8,128)(2,1)S(1)} %bitcast.8, bf16[3,3,576,192]{3,2,1,0:T(8,128)(2,1)S(1)} %bitcast.12, ...), custom_call_target="tpu_custom_call" | custom-call | flops 1048576 | bytes 65536 | tf_op jit(solution)/shard_map/conv_one_own/pallas_call | solution.py:436
  7.1 0.0 collective-permute-done.above.below
  7.1 0.8 %collective-permute-done.2.earlier = bf16[4,4,6144]{2,1,0:T(4,128)(2,1)S(1)} collective-permute-done((bf16[4,4,6144]{2,1,0:T(4,128)(2,1)}, bf16[4,4,6144]{2,1,0:T(4,128)(2,1)S(1)}, u32[]{:S(2)}, u32[]{:S(2)}) %collective-permute-start.2) | collective-permute-done | bytes 196640 | tf_op jit(solution)/shard_map/ppermute | solution.py:393
  7.9 2.0 %conv_one_earlier.1.from_earlier = f32[2,4,5,16,192]{4,3,2,1,0:T(8,128)S(1)} custom-call(s32[1]{0:T(128)S(6)} %copy.9.count, f32[8,128]{1,0:T(8,128)S(1)} %lane_mask.1.mask, bf16[4,4,6144]{2,1,0:T(4,128)(2,1)S(1)} %collective-permute-done.2.earlier, f32[1,192]{1,0:T(1,128)S(1)} %bitcast.29, bf16[3,3,576,192]{3,2,1,0:T(8,128)(2,1)S(1)} %bitcast.10, ...), custom_call_target="tpu_custom_call" | custom-call | flops 1048576 | bytes 65536 | tf_op jit(solution)/shard_map/conv_one_earlier/pallas_call | solution.py:468
  9.9 0.0 collective-permute-done.1.far_above.far_below
  9.9 3.5 %last.1 = bf16[4,4,6144]{2,1,0:T(4,128)(2,1)} custom-call(s32[1]{0:T(128)S(6)} %copy.9.count, bf16[4,4,6144]{2,1,0:T(4,128)(2,1)S(1)} %bitcast.18, bf16[4,2,16,384]{3,2,1,0:T(8,128)(2,1)S(1)} %collective-permute-done.above.below, bf16[4,2,16,384]{3,2,1,0:T(8,128)(2,1)S(1)} %collective-permute-done.above.below, ...), custom_call_target="tpu_custom_call" | custom-call | flops 4294967296 | bytes 6291456 | tf_op jit(solution)/shard_map/last/pallas_call | solution.py:478
  (2 shorter events, 0.0 us)
Async XLA Ops:
  0.0 1.6 %copy-start.2 = (bf16[1,4,4,6144]{3,2,1,0:T(4,128)(2,1)S(1)}, bf16[1,4,4,6144]{3,2,1,0:T(4,128)(2,1)}, u32[]{:S(2)}) copy-start(bf16[1,4,4,6144]{3,2,1,0:T(4,128)(2,1)} %param.8) | copy-start | bytes 589828
  0.0 1.6 %copy-start.6 = (f32[192]{0:T(256)S(1)}, f32[192]{0:T(256)}, u32[]{:S(2)}) copy-start(f32[192]{0:T(256)} %param.10) | copy-start | bytes 2308
  0.0 7.9 %collective-permute-start.2 = (bf16[4,4,6144]{2,1,0:T(4,128)(2,1)}, bf16[4,4,6144]{2,1,0:T(4,128)(2,1)S(1)}, u32[]{:S(2)}, u32[]{:S(2)}) collective-permute-start(bf16[4,4,6144]{2,1,0:T(4,128)(2,1)} %bitcast.15), channel_id=1, source_target_pairs={{0,4},{2,6},{4,8},{6,10},{8,12},{10,14},{12,0},{14,2},{1,5},{3,7},... | collective-permute-start | bytes 589832 | tf_op jit(solution)/shard_map/ppermute | solution.py:393
  1.6 3.4 %copy-start = (bf16[3,3,3,192,192]{4,3,2,1,0:T(8,128)(2,1)S(1)}, bf16[3,3,3,192,192]{4,3,2,1,0:T(8,128)(2,1)}, u32[]{:S(2)}) copy-start(bf16[3,3,3,192,192]{4,3,2,1,0:T(8,128)(2,1)} %param.12) | copy-start | bytes 5971972
  1.6 3.4 %copy-start.1 = (bf16[3,3,3,192,192]{4,3,2,1,0:T(8,128)(2,1)S(1)}, bf16[3,3,3,192,192]{4,3,2,1,0:T(8,128)(2,1)}, u32[]{:S(2)}) copy-start(bf16[3,3,3,192,192]{4,3,2,1,0:T(8,128)(2,1)} %param.15) | copy-start | bytes 5971972
  1.6 3.4 %copy-start.3 = (f32[192]{0:T(256)S(1)}, f32[192]{0:T(256)}, u32[]{:S(2)}) copy-start(f32[192]{0:T(256)} %param.13) | copy-start | bytes 2308
  1.6 3.4 %copy-start.4 = (f32[192]{0:T(256)S(1)}, f32[192]{0:T(256)}, u32[]{:S(2)}) copy-start(f32[192]{0:T(256)} %param.11) | copy-start | bytes 2308
  1.6 3.4 %copy-start.5 = (f32[192]{0:T(256)S(1)}, f32[192]{0:T(256)}, u32[]{:S(2)}) copy-start(f32[192]{0:T(256)} %param.14) | copy-start | bytes 2308
  1.9 5.1 %collective-permute-start = (bf16[4,2,16,384]{3,2,1,0:T(8,128)(2,1)S(1)}, bf16[4,2,16,384]{3,2,1,0:T(8,128)(2,1)S(1)}, u32[]{:S(2)}, u32[]{:S(2)}) collective-permute-start(bf16[4,2,16,384]{3,2,1,0:T(8,128)(2,1)S(1)} %get-tuple-element.9), channel_id=1, source_target_pairs={{0,2},{2,0},{4,6},{6,4},{8,10},{10,8},{12,14},{14,12},{1,3},{3,1},... | collective-permute-start | bytes 294920 | tf_op jit(solution)/shard_map/ppermute | solution.py:393
  3.5 6.4 %collective-permute-start.1 = (bf16[4,2,16,384]{3,2,1,0:T(8,128)(2,1)S(1)}, bf16[4,2,16,384]{3,2,1,0:T(8,128)(2,1)S(1)}, u32[]{:S(2)}, u32[]{:S(2)}) collective-permute-start(bf16[4,2,16,384]{3,2,1,0:T(8,128)(2,1)S(1)} %get-tuple-element.9), channel_id=1, source_target_pairs={{0,6},{2,4},{4,10},{6,8},{8,14},{10,12},{12,0},{14,2},{1,7},{3,5},... | collective-permute-start | bytes 294920 | tf_op jit(solution)/shard_map/ppermute | solution.py:393

commit v20 on v19

--- a/solution.py
+++ b/solution.py
@@ -31,6 +31,17 @@
         h = tiles[k] * scale * half_gain[:, k * LANES : (k + 1) * LANES]
         results.append(h + h * jnp.tanh(h))
     return jnp.concatenate(results, axis=1)
+
+
+def norm_silu_rows(t, gain, channels):
+    square = t * t
+    first = lax.broadcasted_iota(jnp.int32, t.shape, 1) < channels
+    left = jnp.sum(jnp.where(first, square, 0.0), axis=1, keepdims=True)
+    right = jnp.sum(jnp.where(first, 0.0, square), axis=1, keepdims=True)
+    left = lax.rsqrt(left * (1.0 / channels) + 1e-06)
+    right = lax.rsqrt(right * (1.0 / channels) + 1e-06)
+    y = t * jnp.where(first, left, right) * gain
+    return y * (0.5 + 0.5 * jnp.tanh(0.5 * y))
 
 
 def twice(ref):
@@ -251,7 +262,7 @@
             (near[1], far[1], 1, lambda f: valid(f) & (space < bands - 1)),
         ]
         first, deep_inner = 2, deep - 4
-    bias_wide, gain_wide = twice(bias), twice(gain_two) * 0.5
+    bias_wide, gain_wide = twice(bias), twice(gain_two)
 
     def norm_rows(h, sums, base):
         t = jnp.concatenate(sums, axis=1)
@@ -260,8 +271,7 @@
         row = row + (space * rows - 1 + start + base)
         good = (row >= 0) & (row < bands * rows) & valid(frames + h - 2)
         t = jnp.where(good, t + bias_wide, 0.0).astype(BF16).astype(F32)
-        middle = lax.broadcasted_iota(jnp.int32, (t.shape[0], LANES), 1) < channels - LANES
-        y = norm_silu_pair(t, gain_wide, middle, channels).astype(BF16)
+        y = norm_silu_rows(t, gain_wide, channels).astype(BF16)
         for r in range(number):
             hidden[h][start + base + r] = y[r * pairs : (r + 1) * pairs]
 

time: 13.6 us -> 13.6 us (level)
  no operation moved by 1% of the time
where the time goes in v20:
time: 13.6 us; the launch traced here: 13.5 us
  Pallas kernels  7.85 us (58%)
  starting transfers between devices  3.99 us (29%)
  waiting for transfers between devices  0.79 us (6%)
  between operations  0.78 us (6%)
    ppermute x3, starting transfers between devices, shift(): return lax.ppermute(sent, ('tm', 'space'), pairs_of)  3.99 us
    pallas_call x1, Pallas kernels, shards(): pl.pallas_call(functools.partial(last_kernel, bands), out_shape=result, i...  3.51 us
    pallas_call x1, Pallas kernels, shards(): pl.pallas_call(functools.partial(own_kernel, bands, deep), out_shape=[jax...  2.02 us
    pallas_call x1, Pallas kernels, shards(): pl.pallas_call(functools.partial(earlier_kernel, bands, deep), out_shape=...  2.02 us
    ppermute x3, waiting for transfers between devices, shift(): return lax.ppermute(sent, ('tm', 'space'), pairs_of)  0.79 us
    pallas_call x1, Pallas kernels, shards(): pl.pallas_call(functools.partial(norm_kernel, swap), out_shape=[jax.Shape...  0.28 us
  transfers between devices with their start and end apart: 3, of which 1 were waited for; matrix products, arithmetic and copies ran while one was open for 0% of the time, Pallas kernels for 32%

profile of v20, /device:TPU:16, one launch (start us, length us, event | category | flops | bytes accessed | tf_op | source)
XLA Modules:
  0.0 13.5 jit_solution(4136366261936200249)
XLA Ops:
  0.0 0.0 copy-start.2
  0.0 0.0 copy-start.6
  0.0 1.6 %collective-permute-start.2 = (bf16[4,4,6144]{2,1,0:T(4,128)(2,1)}, bf16[4,4,6144]{2,1,0:T(4,128)(2,1)S(1)}, u32[]{:S(2)}, u32[]{:S(2)}) collective-permute-start(bf16[4,4,6144]{2,1,0:T(4,128)(2,1)} %bitcast.15), channel_id=1, source_target_pairs={{0,4},{2,6},{4,8},{6,10},{8,12},{10,14},{12,0},{14,2},{1,5},{3,7},... | collective-permute-start | bytes 589832 | tf_op jit(solution)/shard_map/ppermute | solution.py:403
  1.6 0.0 copy-done.2
  1.6 0.0 copy-done.6
  1.6 0.0 copy-start
  1.6 0.0 copy-start.1
  1.6 0.0 copy-start.3
  1.6 0.0 copy-start.4
  1.6 0.0 copy-start.5
  1.7 0.3 %norm_and_cut.1 = (bf16[4,4,16,384]{3,2,1,0:T(8,128)(2,1)S(1)}, bf16[4,2,16,384]{3,2,1,0:T(8,128)(2,1)S(1)}) custom-call(f32[8,128]{1,0:T(8,128)S(1)} %lane_mask.1.mask, bf16[4,4,6144]{2,1,0:T(4,128)(2,1)S(1)} %bitcast.16, f32[1,192]{1,0:T(1,128)S(1)} %bitcast.28), custom_call_target="tpu_custom_call" | custom-call | flops 4294967296 | bytes 1048576 | tf_op jit(solution)/shard_map/norm_and_cut/pallas_call | solution.py:420
  1.9 1.6 %collective-permute-start = (bf16[4,2,16,384]{3,2,1,0:T(8,128)(2,1)S(1)}, bf16[4,2,16,384]{3,2,1,0:T(8,128)(2,1)S(1)}, u32[]{:S(2)}, u32[]{:S(2)}) collective-permute-start(bf16[4,2,16,384]{3,2,1,0:T(8,128)(2,1)S(1)} %get-tuple-element.9), channel_id=1, source_target_pairs={{0,2},{2,0},{4,6},{6,4},{8,10},{10,8},{12,14},{14,12},{1,3},{3,1},... | collective-permute-start | bytes 294920 | tf_op jit(solution)/shard_map/ppermute | solution.py:403
  3.5 0.9 %collective-permute-start.1 = (bf16[4,2,16,384]{3,2,1,0:T(8,128)(2,1)S(1)}, bf16[4,2,16,384]{3,2,1,0:T(8,128)(2,1)S(1)}, u32[]{:S(2)}, u32[]{:S(2)}) collective-permute-start(bf16[4,2,16,384]{3,2,1,0:T(8,128)(2,1)S(1)} %get-tuple-element.9), channel_id=1, source_target_pairs={{0,6},{2,4},{4,10},{6,8},{8,14},{10,12},{12,0},{14,2},{1,7},{3,5},... | collective-permute-start | bytes 294920 | tf_op jit(solution)/shard_map/ppermute | solution.py:403
  5.0 0.0 copy-done
  5.0 0.0 copy-done.1
  5.0 0.0 copy-done.3
  5.0 0.0 copy-done.4
  5.0 0.0 copy-done.5
  5.1 2.0 %conv_one_own.1 = (f32[2,4,5,16,192]{4,3,2,1,0:T(8,128)S(1)}, bf16[2,3,576,192]{3,2,1,0:T(8,128)(2,1)S(1)}) custom-call(s32[1]{0:T(128)S(6)} %copy.9.count, bf16[4,4,16,384]{3,2,1,0:T(8,128)(2,1)S(1)} %get-tuple-element.10.normed, bf16[3,3,576,192]{3,2,1,0:T(8,128)(2,1)S(1)} %bitcast.8, bf16[3,3,576,192]{3,2,1,0:T(8,128)(2,1)S(1)} %bitcast.12, ...), custom_call_target="tpu_custom_call" | custom-call | flops 1048576 | bytes 65536 | tf_op jit(solution)/shard_map/conv_one_own/pallas_call | solution.py:446
  7.1 0.0 collective-permute-done.above.below
  7.1 0.8 %collective-permute-done.2.earlier = bf16[4,4,6144]{2,1,0:T(4,128)(2,1)S(1)} collective-permute-done((bf16[4,4,6144]{2,1,0:T(4,128)(2,1)}, bf16[4,4,6144]{2,1,0:T(4,128)(2,1)S(1)}, u32[]{:S(2)}, u32[]{:S(2)}) %collective-permute-start.2) | collective-permute-done | bytes 196640 | tf_op jit(solution)/shard_map/ppermute | solution.py:403
  7.9 2.0 %conv_one_earlier.1.from_earlier = f32[2,4,5,16,192]{4,3,2,1,0:T(8,128)S(1)} custom-call(s32[1]{0:T(128)S(6)} %copy.9.count, f32[8,128]{1,0:T(8,128)S(1)} %lane_mask.1.mask, bf16[4,4,6144]{2,1,0:T(4,128)(2,1)S(1)} %collective-permute-done.2.earlier, f32[1,192]{1,0:T(1,128)S(1)} %bitcast.29, bf16[3,3,576,192]{3,2,1,0:T(8,128)(2,1)S(1)} %bitcast.10, ...), custom_call_target="tpu_custom_call" | custom-call | flops 1048576 | bytes 65536 | tf_op jit(solution)/shard_map/conv_one_earlier/pallas_call | solution.py:478
  9.9 0.0 collective-permute-done.1.far_above.far_below
  9.9 3.5 %last.1 = bf16[4,4,6144]{2,1,0:T(4,128)(2,1)} custom-call(s32[1]{0:T(128)S(6)} %copy.9.count, bf16[4,4,6144]{2,1,0:T(4,128)(2,1)S(1)} %bitcast.18, bf16[4,2,16,384]{3,2,1,0:T(8,128)(2,1)S(1)} %collective-permute-done.above.below, bf16[4,2,16,384]{3,2,1,0:T(8,128)(2,1)S(1)} %collective-permute-done.above.below, ...), custom_call_target="tpu_custom_call" | custom-call | flops 4294967296 | bytes 6291456 | tf_op jit(solution)/shard_map/last/pallas_call | solution.py:488
  (2 shorter events, 0.0 us)
Async XLA Ops:
  0.0 1.6 %copy-start.2 = (bf16[1,4,4,6144]{3,2,1,0:T(4,128)(2,1)S(1)}, bf16[1,4,4,6144]{3,2,1,0:T(4,128)(2,1)}, u32[]{:S(2)}) copy-start(bf16[1,4,4,6144]{3,2,1,0:T(4,128)(2,1)} %param.8) | copy-start | bytes 589828
  0.0 1.6 %copy-start.6 = (f32[192]{0:T(256)S(1)}, f32[192]{0:T(256)}, u32[]{:S(2)}) copy-start(f32[192]{0:T(256)} %param.10) | copy-start | bytes 2308
  0.0 7.9 %collective-permute-start.2 = (bf16[4,4,6144]{2,1,0:T(4,128)(2,1)}, bf16[4,4,6144]{2,1,0:T(4,128)(2,1)S(1)}, u32[]{:S(2)}, u32[]{:S(2)}) collective-permute-start(bf16[4,4,6144]{2,1,0:T(4,128)(2,1)} %bitcast.15), channel_id=1, source_target_pairs={{0,4},{2,6},{4,8},{6,10},{8,12},{10,14},{12,0},{14,2},{1,5},{3,7},... | collective-permute-start | bytes 589832 | tf_op jit(solution)/shard_map/ppermute | solution.py:403
  1.6 3.4 %copy-start = (bf16[3,3,3,192,192]{4,3,2,1,0:T(8,128)(2,1)S(1)}, bf16[3,3,3,192,192]{4,3,2,1,0:T(8,128)(2,1)}, u32[]{:S(2)}) copy-start(bf16[3,3,3,192,192]{4,3,2,1,0:T(8,128)(2,1)} %param.12) | copy-start | bytes 5971972
  1.6 3.4 %copy-start.1 = (bf16[3,3,3,192,192]{4,3,2,1,0:T(8,128)(2,1)S(1)}, bf16[3,3,3,192,192]{4,3,2,1,0:T(8,128)(2,1)}, u32[]{:S(2)}) copy-start(bf16[3,3,3,192,192]{4,3,2,1,0:T(8,128)(2,1)} %param.15) | copy-start | bytes 5971972
  1.6 3.4 %copy-start.3 = (f32[192]{0:T(256)S(1)}, f32[192]{0:T(256)}, u32[]{:S(2)}) copy-start(f32[192]{0:T(256)} %param.13) | copy-start | bytes 2308
  1.6 3.4 %copy-start.4 = (f32[192]{0:T(256)S(1)}, f32[192]{0:T(256)}, u32[]{:S(2)}) copy-start(f32[192]{0:T(256)} %param.11) | copy-start | bytes 2308
  1.6 3.4 %copy-start.5 = (f32[192]{0:T(256)S(1)}, f32[192]{0:T(256)}, u32[]{:S(2)}) copy-start(f32[192]{0:T(256)} %param.14) | copy-start | bytes 2308
  1.9 5.1 %collective-permute-start = (bf16[4,2,16,384]{3,2,1,0:T(8,128)(2,1)S(1)}, bf16[4,2,16,384]{3,2,1,0:T(8,128)(2,1)S(1)}, u32[]{:S(2)}, u32[]{:S(2)}) collective-permute-start(bf16[4,2,16,384]{3,2,1,0:T(8,128)(2,1)S(1)} %get-tuple-element.9), channel_id=1, source_target_pairs={{0,2},{2,0},{4,6},{6,4},{8,10},{10,8},{12,14},{14,12},{1,3},{3,1},... | collective-permute-start | bytes 294920 | tf_op jit(solution)/shard_map/ppermute | solution.py:403
  3.5 6.4 %collective-permute-start.1 = (bf16[4,2,16,384]{3,2,1,0:T(8,128)(2,1)S(1)}, bf16[4,2,16,384]{3,2,1,0:T(8,128)(2,1)S(1)}, u32[]{:S(2)}, u32[]{:S(2)}) collective-permute-start(bf16[4,2,16,384]{3,2,1,0:T(8,128)(2,1)S(1)} %get-tuple-element.9), channel_id=1, source_target_pairs={{0,6},{2,4},{4,10},{6,8},{8,14},{10,12},{12,0},{14,2},{1,7},{3,5},... | collective-permute-start | bytes 294920 | tf_op jit(solution)/shard_map/ppermute | solution.py:403

commit v21 on v20

--- a/solution.py
+++ b/solution.py
@@ -33,15 +33,15 @@
     return jnp.concatenate(results, axis=1)
 
 
-def norm_silu_rows(t, gain, channels):
+def norm_silu_rows(t, half_gain, channels):
     square = t * t
     first = lax.broadcasted_iota(jnp.int32, t.shape, 1) < channels
     left = jnp.sum(jnp.where(first, square, 0.0), axis=1, keepdims=True)
     right = jnp.sum(jnp.where(first, 0.0, square), axis=1, keepdims=True)
     left = lax.rsqrt(left * (1.0 / channels) + 1e-06)
     right = lax.rsqrt(right * (1.0 / channels) + 1e-06)
-    y = t * jnp.where(first, left, right) * gain
-    return y * (0.5 + 0.5 * jnp.tanh(0.5 * y))
+    h = t * jnp.where(first, left, right) * half_gain
+    return h + h * jnp.tanh(h)
 
 
 def twice(ref):
@@ -162,9 +162,9 @@
         good = tm * frames + f < count[0]
         for r in range(rows):
             window[f + 1][top + r] = jnp.where(good, normed[f, r], nothing)
+    mix_weights(weight_two, mixed_two)
     late = conv(window, weight, 1, frames - 2, deep, (0, 1, 2), wide // 2)
     soon = conv(window, weight, 0, 2, deep, (1, 2), wide // 2)
-    mix_weights(weight_two, mixed_two)
     for q in range(2):
         total[q, 0:2] = soon[q].reshape(2, *total.shape[2:])
         total[q, 2:] = late[q].reshape(frames - 2, *total.shape[2:])
@@ -262,14 +262,16 @@
             (near[1], far[1], 1, lambda f: valid(f) & (space < bands - 1)),
         ]
         first, deep_inner = 2, deep - 4
-    bias_wide, gain_wide = twice(bias), twice(gain_two)
+    bias_wide, gain_wide = twice(bias), twice(gain_two) * 0.5
 
     def norm_rows(h, sums, base):
         t = jnp.concatenate(sums, axis=1)
         number = t.shape[0] // pairs
-        row = lax.broadcasted_iota(jnp.int32, (t.shape[0], 1), 0) // pairs
-        row = row + (space * rows - 1 + start + base)
-        good = (row >= 0) & (row < bands * rows) & valid(frames + h - 2)
+        good = valid(frames + h - 2)
+        if bands != 2:
+            row = lax.broadcasted_iota(jnp.int32, (t.shape[0], 1), 0) // pairs
+            row = row + (space * rows - 1 + start + base)
+            good = (row >= 0) & (row < bands * rows) & good
         t = jnp.where(good, t + bias_wide, 0.0).astype(BF16).astype(F32)
         y = norm_silu_rows(t, gain_wide, channels).astype(BF16)
         for r in range(number):

time: 13.6 us -> 13.6 us (level)
  transfers between devices with their start and end apart: 3 -> 3, of which waited for: 1 -> 1; matrix products, arithmetic and copies ran while one was open for 0% -> 0% of each run, Pallas kernels for 32% -> 33%
where the time goes in v21:
time: 13.6 us; the launch traced here: 13.4 us
  Pallas kernels  7.86 us (58%)
  starting transfers between devices  3.99 us (29%)
  between operations  0.78 us (6%)
  waiting for transfers between devices  0.75 us (6%)
    ppermute x3, starting transfers between devices, shift(): return lax.ppermute(sent, ('tm', 'space'), pairs_of)  3.99 us
    pallas_call x1, Pallas kernels, shards(): pl.pallas_call(functools.partial(last_kernel, bands), out_shape=result, i...  3.48 us
    pallas_call x1, Pallas kernels, shards(): pl.pallas_call(functools.partial(own_kernel, bands, deep), out_shape=[jax...  2.06 us
    pallas_call x1, Pallas kernels, shards(): pl.pallas_call(functools.partial(earlier_kernel, bands, deep), out_shape=...  2.02 us
    ppermute x3, waiting for transfers between devices, shift(): return lax.ppermute(sent, ('tm', 'space'), pairs_of)  0.75 us
    pallas_call x1, Pallas kernels, shards(): pl.pallas_call(functools.partial(norm_kernel, swap), out_shape=[jax.Shape...  0.28 us
  transfers between devices with their start and end apart: 3, of which 1 were waited for; matrix products, arithmetic and copies ran while one was open for 0% of the time, Pallas kernels for 33%

profile of v21, /device:TPU:16, one launch (start us, length us, event | category | flops | bytes accessed | tf_op | source)
XLA Modules:
  0.0 13.4 jit_solution(11230763527448876244)
XLA Ops:
  0.0 0.0 copy-start.2
  0.0 0.0 copy-start.6
  0.0 1.6 %collective-permute-start.2 = (bf16[4,4,6144]{2,1,0:T(4,128)(2,1)}, bf16[4,4,6144]{2,1,0:T(4,128)(2,1)S(1)}, u32[]{:S(2)}, u32[]{:S(2)}) collective-permute-start(bf16[4,4,6144]{2,1,0:T(4,128)(2,1)} %bitcast.15), channel_id=1, source_target_pairs={{0,4},{2,6},{4,8},{6,10},{8,12},{10,14},{12,0},{14,2},{1,5},{3,7},... | collective-permute-start | bytes 589832 | tf_op jit(solution)/shard_map/ppermute | solution.py:405
  1.6 0.0 copy-done.2
  1.6 0.0 copy-done.6
  1.6 0.0 copy-start
  1.6 0.0 copy-start.1
  1.6 0.0 copy-start.3
  1.6 0.0 copy-start.4
  1.6 0.0 copy-start.5
  1.7 0.3 %norm_and_cut.1 = (bf16[4,4,16,384]{3,2,1,0:T(8,128)(2,1)S(1)}, bf16[4,2,16,384]{3,2,1,0:T(8,128)(2,1)S(1)}) custom-call(f32[8,128]{1,0:T(8,128)S(1)} %lane_mask.1.mask, bf16[4,4,6144]{2,1,0:T(4,128)(2,1)S(1)} %bitcast.16, f32[1,192]{1,0:T(1,128)S(1)} %bitcast.28), custom_call_target="tpu_custom_call" | custom-call | flops 4294967296 | bytes 1048576 | tf_op jit(solution)/shard_map/norm_and_cut/pallas_call | solution.py:422
  1.9 1.6 %collective-permute-start = (bf16[4,2,16,384]{3,2,1,0:T(8,128)(2,1)S(1)}, bf16[4,2,16,384]{3,2,1,0:T(8,128)(2,1)S(1)}, u32[]{:S(2)}, u32[]{:S(2)}) collective-permute-start(bf16[4,2,16,384]{3,2,1,0:T(8,128)(2,1)S(1)} %get-tuple-element.9), channel_id=1, source_target_pairs={{0,2},{2,0},{4,6},{6,4},{8,10},{10,8},{12,14},{14,12},{1,3},{3,1},... | collective-permute-start | bytes 294920 | tf_op jit(solution)/shard_map/ppermute | solution.py:405
  3.5 0.9 %collective-permute-start.1 = (bf16[4,2,16,384]{3,2,1,0:T(8,128)(2,1)S(1)}, bf16[4,2,16,384]{3,2,1,0:T(8,128)(2,1)S(1)}, u32[]{:S(2)}, u32[]{:S(2)}) collective-permute-start(bf16[4,2,16,384]{3,2,1,0:T(8,128)(2,1)S(1)} %get-tuple-element.9), channel_id=1, source_target_pairs={{0,6},{2,4},{4,10},{6,8},{8,14},{10,12},{12,0},{14,2},{1,7},{3,5},... | collective-permute-start | bytes 294920 | tf_op jit(solution)/shard_map/ppermute | solution.py:405
  5.0 0.0 copy-done
  5.0 0.0 copy-done.1
  5.0 0.0 copy-done.3
  5.0 0.0 copy-done.4
  5.0 0.0 copy-done.5
  5.1 2.1 %conv_one_own.1 = (f32[2,4,5,16,192]{4,3,2,1,0:T(8,128)S(1)}, bf16[2,3,576,192]{3,2,1,0:T(8,128)(2,1)S(1)}) custom-call(s32[1]{0:T(128)S(6)} %copy.9.count, bf16[4,4,16,384]{3,2,1,0:T(8,128)(2,1)S(1)} %get-tuple-element.10.normed, bf16[3,3,576,192]{3,2,1,0:T(8,128)(2,1)S(1)} %bitcast.8, bf16[3,3,576,192]{3,2,1,0:T(8,128)(2,1)S(1)} %bitcast.12, ...), custom_call_target="tpu_custom_call" | custom-call | flops 1048576 | bytes 65536 | tf_op jit(solution)/shard_map/conv_one_own/pallas_call | solution.py:448
  7.1 0.0 collective-permute-done.above.below
  7.2 0.7 %collective-permute-done.2.earlier = bf16[4,4,6144]{2,1,0:T(4,128)(2,1)S(1)} collective-permute-done((bf16[4,4,6144]{2,1,0:T(4,128)(2,1)}, bf16[4,4,6144]{2,1,0:T(4,128)(2,1)S(1)}, u32[]{:S(2)}, u32[]{:S(2)}) %collective-permute-start.2) | collective-permute-done | bytes 196640 | tf_op jit(solution)/shard_map/ppermute | solution.py:405
  7.9 2.0 %conv_one_earlier.1.from_earlier = f32[2,4,5,16,192]{4,3,2,1,0:T(8,128)S(1)} custom-call(s32[1]{0:T(128)S(6)} %copy.9.count, f32[8,128]{1,0:T(8,128)S(1)} %lane_mask.1.mask, bf16[4,4,6144]{2,1,0:T(4,128)(2,1)S(1)} %collective-permute-done.2.earlier, f32[1,192]{1,0:T(1,128)S(1)} %bitcast.29, bf16[3,3,576,192]{3,2,1,0:T(8,128)(2,1)S(1)} %bitcast.10, ...), custom_call_target="tpu_custom_call" | custom-call | flops 1048576 | bytes 65536 | tf_op jit(solution)/shard_map/conv_one_earlier/pallas_call | solution.py:480
  9.9 0.0 collective-permute-done.1.far_above.far_below
  9.9 3.5 %last.1 = bf16[4,4,6144]{2,1,0:T(4,128)(2,1)} custom-call(s32[1]{0:T(128)S(6)} %copy.9.count, bf16[4,4,6144]{2,1,0:T(4,128)(2,1)S(1)} %bitcast.18, bf16[4,2,16,384]{3,2,1,0:T(8,128)(2,1)S(1)} %collective-permute-done.above.below, bf16[4,2,16,384]{3,2,1,0:T(8,128)(2,1)S(1)} %collective-permute-done.above.below, ...), custom_call_target="tpu_custom_call" | custom-call | flops 4294967296 | bytes 6291456 | tf_op jit(solution)/shard_map/last/pallas_call | solution.py:490
  (2 shorter events, 0.0 us)
Async XLA Ops:
  0.0 1.6 %copy-start.2 = (bf16[1,4,4,6144]{3,2,1,0:T(4,128)(2,1)S(1)}, bf16[1,4,4,6144]{3,2,1,0:T(4,128)(2,1)}, u32[]{:S(2)}) copy-start(bf16[1,4,4,6144]{3,2,1,0:T(4,128)(2,1)} %param.8) | copy-start | bytes 589828
  0.0 1.6 %copy-start.6 = (f32[192]{0:T(256)S(1)}, f32[192]{0:T(256)}, u32[]{:S(2)}) copy-start(f32[192]{0:T(256)} %param.10) | copy-start | bytes 2308
  0.0 7.9 %collective-permute-start.2 = (bf16[4,4,6144]{2,1,0:T(4,128)(2,1)}, bf16[4,4,6144]{2,1,0:T(4,128)(2,1)S(1)}, u32[]{:S(2)}, u32[]{:S(2)}) collective-permute-start(bf16[4,4,6144]{2,1,0:T(4,128)(2,1)} %bitcast.15), channel_id=1, source_target_pairs={{0,4},{2,6},{4,8},{6,10},{8,12},{10,14},{12,0},{14,2},{1,5},{3,7},... | collective-permute-start | bytes 589832 | tf_op jit(solution)/shard_map/ppermute | solution.py:405
  1.6 3.4 %copy-start = (bf16[3,3,3,192,192]{4,3,2,1,0:T(8,128)(2,1)S(1)}, bf16[3,3,3,192,192]{4,3,2,1,0:T(8,128)(2,1)}, u32[]{:S(2)}) copy-start(bf16[3,3,3,192,192]{4,3,2,1,0:T(8,128)(2,1)} %param.12) | copy-start | bytes 5971972
  1.6 3.4 %copy-start.1 = (bf16[3,3,3,192,192]{4,3,2,1,0:T(8,128)(2,1)S(1)}, bf16[3,3,3,192,192]{4,3,2,1,0:T(8,128)(2,1)}, u32[]{:S(2)}) copy-start(bf16[3,3,3,192,192]{4,3,2,1,0:T(8,128)(2,1)} %param.15) | copy-start | bytes 5971972
  1.6 3.4 %copy-start.3 = (f32[192]{0:T(256)S(1)}, f32[192]{0:T(256)}, u32[]{:S(2)}) copy-start(f32[192]{0:T(256)} %param.13) | copy-start | bytes 2308
  1.6 3.4 %copy-start.4 = (f32[192]{0:T(256)S(1)}, f32[192]{0:T(256)}, u32[]{:S(2)}) copy-start(f32[192]{0:T(256)} %param.11) | copy-start | bytes 2308
  1.6 3.4 %copy-start.5 = (f32[192]{0:T(256)S(1)}, f32[192]{0:T(256)}, u32[]{:S(2)}) copy-start(f32[192]{0:T(256)} %param.14) | copy-start | bytes 2308
  1.9 5.2 %collective-permute-start = (bf16[4,2,16,384]{3,2,1,0:T(8,128)(2,1)S(1)}, bf16[4,2,16,384]{3,2,1,0:T(8,128)(2,1)S(1)}, u32[]{:S(2)}, u32[]{:S(2)}) collective-permute-start(bf16[4,2,16,384]{3,2,1,0:T(8,128)(2,1)S(1)} %get-tuple-element.9), channel_id=1, source_target_pairs={{0,2},{2,0},{4,6},{6,4},{8,10},{10,8},{12,14},{14,12},{1,3},{3,1},... | collective-permute-start | bytes 294920 | tf_op jit(solution)/shard_map/ppermute | solution.py:405
  3.5 6.4 %collective-permute-start.1 = (bf16[4,2,16,384]{3,2,1,0:T(8,128)(2,1)S(1)}, bf16[4,2,16,384]{3,2,1,0:T(8,128)(2,1)S(1)}, u32[]{:S(2)}, u32[]{:S(2)}) collective-permute-start(bf16[4,2,16,384]{3,2,1,0:T(8,128)(2,1)S(1)} %get-tuple-element.9), channel_id=1, source_target_pairs={{0,6},{2,4},{4,10},{6,8},{8,14},{10,12},{12,0},{14,2},{1,7},{3,5},... | collective-permute-start | bytes 294920 | tf_op jit(solution)/shard_map/ppermute | solution.py:405

commit v22 on v20

--- a/solution.py
+++ b/solution.py
@@ -204,15 +204,22 @@
         def norm(f):
             norm_frames(earlier, f, twice(gain) * 0.5, mask[...] > 0.5, stages[f // 2], store, pairs)
 
+        def add(a):
+            both = conv(window, weight, a, frames - a, deep, (a,), wide // 2)
+            for q in range(2):
+                value = both[q].reshape(frames - a, *total.shape[2:])
+                if a < 2:
+                    total[q, 0 : frames - a - 1] += value[: frames - a - 1]
+                    total[q, frames - a - 1 : frames - a] = value[frames - a - 1 :]
+                else:
+                    total[q, 0 : frames - a] = value
+
         norm(frames - 2)
-        late = conv(window, weight, frames - 2, 2, deep, (0, 1), wide // 2)
+        add(2)
         for f in range(0, frames - 2, 2):
             norm(f)
-        for q in range(2):
-            total[q, frames - 2 :] = late[q].reshape(2, *total.shape[2:])
-        soon = conv(window, weight, 0, frames - 2, deep, (0, 1, 2), wide // 2)
-        for q in range(2):
-            total[q, 0 : frames - 2] = soon[q].reshape(frames - 2, *total.shape[2:])
+        add(1)
+        add(0)
 
 
 def rim_sums(near, far, weight, side, keep, channels, frames):

time: 13.6 us -> 13.6 us (level)
  no operation moved by 1% of the time
where the time goes in v22:
time: 13.6 us; the launch traced here: 13.4 us
  Pallas kernels  7.79 us (57%)
  starting transfers between devices  3.99 us (29%)
  waiting for transfers between devices  0.8 us (6%)
  between operations  0.78 us (6%)
    ppermute x3, starting transfers between devices, shift(): return lax.ppermute(sent, ('tm', 'space'), pairs_of)  3.99 us
    pallas_call x1, Pallas kernels, shards(): pl.pallas_call(functools.partial(last_kernel, bands), out_shape=result, i...  3.49 us
    pallas_call x1, Pallas kernels, shards(): pl.pallas_call(functools.partial(own_kernel, bands, deep), out_shape=[jax...  2.02 us
    pallas_call x1, Pallas kernels, shards(): pl.pallas_call(functools.partial(earlier_kernel, bands, deep), out_shape=...  1.98 us
    ppermute x3, waiting for transfers between devices, shift(): return lax.ppermute(sent, ('tm', 'space'), pairs_of)  0.8 us
    pallas_call x1, Pallas kernels, shards(): pl.pallas_call(functools.partial(norm_kernel, swap), out_shape=[jax.Shape...  0.28 us
  transfers between devices with their start and end apart: 3, of which 1 were waited for; matrix products, arithmetic and copies ran while one was open for 0% of the time, Pallas kernels for 32%

profile of v22, /device:TPU:16, one launch (start us, length us, event | category | flops | bytes accessed | tf_op | source)
XLA Modules:
  0.0 13.4 jit_solution(18124718642189360359)
XLA Ops:
  0.0 0.0 copy-start.2
  0.0 0.0 copy-start.6
  0.0 1.6 %collective-permute-start.2 = (bf16[4,4,6144]{2,1,0:T(4,128)(2,1)}, bf16[4,4,6144]{2,1,0:T(4,128)(2,1)S(1)}, u32[]{:S(2)}, u32[]{:S(2)}) collective-permute-start(bf16[4,4,6144]{2,1,0:T(4,128)(2,1)} %bitcast.15), channel_id=1, source_target_pairs={{0,4},{2,6},{4,8},{6,10},{8,12},{10,14},{12,0},{14,2},{1,5},{3,7},... | collective-permute-start | bytes 589832 | tf_op jit(solution)/shard_map/ppermute | solution.py:410
  1.6 0.0 copy-done.2
  1.6 0.0 copy-done.6
  1.6 0.0 copy-start
  1.6 0.0 copy-start.1
  1.6 0.0 copy-start.3
  1.6 0.0 copy-start.4
  1.6 0.0 copy-start.5
  1.7 0.3 %norm_and_cut.1 = (bf16[4,4,16,384]{3,2,1,0:T(8,128)(2,1)S(1)}, bf16[4,2,16,384]{3,2,1,0:T(8,128)(2,1)S(1)}) custom-call(f32[8,128]{1,0:T(8,128)S(1)} %lane_mask.1.mask, bf16[4,4,6144]{2,1,0:T(4,128)(2,1)S(1)} %bitcast.16, f32[1,192]{1,0:T(1,128)S(1)} %bitcast.28), custom_call_target="tpu_custom_call" | custom-call | flops 4294967296 | bytes 1048576 | tf_op jit(solution)/shard_map/norm_and_cut/pallas_call | solution.py:427
  1.9 1.6 %collective-permute-start = (bf16[4,2,16,384]{3,2,1,0:T(8,128)(2,1)S(1)}, bf16[4,2,16,384]{3,2,1,0:T(8,128)(2,1)S(1)}, u32[]{:S(2)}, u32[]{:S(2)}) collective-permute-start(bf16[4,2,16,384]{3,2,1,0:T(8,128)(2,1)S(1)} %get-tuple-element.9), channel_id=1, source_target_pairs={{0,2},{2,0},{4,6},{6,4},{8,10},{10,8},{12,14},{14,12},{1,3},{3,1},... | collective-permute-start | bytes 294920 | tf_op jit(solution)/shard_map/ppermute | solution.py:410
  3.5 0.9 %collective-permute-start.1 = (bf16[4,2,16,384]{3,2,1,0:T(8,128)(2,1)S(1)}, bf16[4,2,16,384]{3,2,1,0:T(8,128)(2,1)S(1)}, u32[]{:S(2)}, u32[]{:S(2)}) collective-permute-start(bf16[4,2,16,384]{3,2,1,0:T(8,128)(2,1)S(1)} %get-tuple-element.9), channel_id=1, source_target_pairs={{0,6},{2,4},{4,10},{6,8},{8,14},{10,12},{12,0},{14,2},{1,7},{3,5},... | collective-permute-start | bytes 294920 | tf_op jit(solution)/shard_map/ppermute | solution.py:410
  5.0 0.0 copy-done
  5.0 0.0 copy-done.1
  5.0 0.0 copy-done.3
  5.0 0.0 copy-done.4
  5.0 0.0 copy-done.5
  5.1 2.0 %conv_one_own.1 = (f32[2,4,5,16,192]{4,3,2,1,0:T(8,128)S(1)}, bf16[2,3,576,192]{3,2,1,0:T(8,128)(2,1)S(1)}) custom-call(s32[1]{0:T(128)S(6)} %copy.9.count, bf16[4,4,16,384]{3,2,1,0:T(8,128)(2,1)S(1)} %get-tuple-element.10.normed, bf16[3,3,576,192]{3,2,1,0:T(8,128)(2,1)S(1)} %bitcast.8, bf16[3,3,576,192]{3,2,1,0:T(8,128)(2,1)S(1)} %bitcast.12, ...), custom_call_target="tpu_custom_call" | custom-call | flops 1048576 | bytes 65536 | tf_op jit(solution)/shard_map/conv_one_own/pallas_call | solution.py:453
  7.1 0.0 collective-permute-done.above.below
  7.1 0.8 %collective-permute-done.2.earlier = bf16[4,4,6144]{2,1,0:T(4,128)(2,1)S(1)} collective-permute-done((bf16[4,4,6144]{2,1,0:T(4,128)(2,1)}, bf16[4,4,6144]{2,1,0:T(4,128)(2,1)S(1)}, u32[]{:S(2)}, u32[]{:S(2)}) %collective-permute-start.2) | collective-permute-done | bytes 196640 | tf_op jit(solution)/shard_map/ppermute | solution.py:410
  7.9 2.0 %conv_one_earlier.1.from_earlier = f32[2,4,5,16,192]{4,3,2,1,0:T(8,128)S(1)} custom-call(s32[1]{0:T(128)S(6)} %copy.9.count, f32[8,128]{1,0:T(8,128)S(1)} %lane_mask.1.mask, bf16[4,4,6144]{2,1,0:T(4,128)(2,1)S(1)} %collective-permute-done.2.earlier, f32[1,192]{1,0:T(1,128)S(1)} %bitcast.29, bf16[3,3,576,192]{3,2,1,0:T(8,128)(2,1)S(1)} %bitcast.10, ...), custom_call_target="tpu_custom_call" | custom-call | flops 1048576 | bytes 65536 | tf_op jit(solution)/shard_map/conv_one_earlier/pallas_call | solution.py:485
  9.9 0.0 collective-permute-done.1.far_above.far_below
  9.9 3.5 %last.1 = bf16[4,4,6144]{2,1,0:T(4,128)(2,1)} custom-call(s32[1]{0:T(128)S(6)} %copy.9.count, bf16[4,4,6144]{2,1,0:T(4,128)(2,1)S(1)} %bitcast.18, bf16[4,2,16,384]{3,2,1,0:T(8,128)(2,1)S(1)} %collective-permute-done.above.below, bf16[4,2,16,384]{3,2,1,0:T(8,128)(2,1)S(1)} %collective-permute-done.above.below, ...), custom_call_target="tpu_custom_call" | custom-call | flops 4294967296 | bytes 6291456 | tf_op jit(solution)/shard_map/last/pallas_call | solution.py:495
  (2 shorter events, 0.0 us)
Async XLA Ops:
  0.0 1.6 %copy-start.2 = (bf16[1,4,4,6144]{3,2,1,0:T(4,128)(2,1)S(1)}, bf16[1,4,4,6144]{3,2,1,0:T(4,128)(2,1)}, u32[]{:S(2)}) copy-start(bf16[1,4,4,6144]{3,2,1,0:T(4,128)(2,1)} %param.8) | copy-start | bytes 589828
  0.0 1.6 %copy-start.6 = (f32[192]{0:T(256)S(1)}, f32[192]{0:T(256)}, u32[]{:S(2)}) copy-start(f32[192]{0:T(256)} %param.10) | copy-start | bytes 2308
  0.0 7.9 %collective-permute-start.2 = (bf16[4,4,6144]{2,1,0:T(4,128)(2,1)}, bf16[4,4,6144]{2,1,0:T(4,128)(2,1)S(1)}, u32[]{:S(2)}, u32[]{:S(2)}) collective-permute-start(bf16[4,4,6144]{2,1,0:T(4,128)(2,1)} %bitcast.15), channel_id=1, source_target_pairs={{0,4},{2,6},{4,8},{6,10},{8,12},{10,14},{12,0},{14,2},{1,5},{3,7},... | collective-permute-start | bytes 589832 | tf_op jit(solution)/shard_map/ppermute | solution.py:410
  1.6 3.4 %copy-start = (bf16[3,3,3,192,192]{4,3,2,1,0:T(8,128)(2,1)S(1)}, bf16[3,3,3,192,192]{4,3,2,1,0:T(8,128)(2,1)}, u32[]{:S(2)}) copy-start(bf16[3,3,3,192,192]{4,3,2,1,0:T(8,128)(2,1)} %param.12) | copy-start | bytes 5971972
  1.6 3.4 %copy-start.1 = (bf16[3,3,3,192,192]{4,3,2,1,0:T(8,128)(2,1)S(1)}, bf16[3,3,3,192,192]{4,3,2,1,0:T(8,128)(2,1)}, u32[]{:S(2)}) copy-start(bf16[3,3,3,192,192]{4,3,2,1,0:T(8,128)(2,1)} %param.15) | copy-start | bytes 5971972
  1.6 3.4 %copy-start.3 = (f32[192]{0:T(256)S(1)}, f32[192]{0:T(256)}, u32[]{:S(2)}) copy-start(f32[192]{0:T(256)} %param.13) | copy-start | bytes 2308
  1.6 3.4 %copy-start.4 = (f32[192]{0:T(256)S(1)}, f32[192]{0:T(256)}, u32[]{:S(2)}) copy-start(f32[192]{0:T(256)} %param.11) | copy-start | bytes 2308
  1.6 3.4 %copy-start.5 = (f32[192]{0:T(256)S(1)}, f32[192]{0:T(256)}, u32[]{:S(2)}) copy-start(f32[192]{0:T(256)} %param.14) | copy-start | bytes 2308
  1.9 5.1 %collective-permute-start = (bf16[4,2,16,384]{3,2,1,0:T(8,128)(2,1)S(1)}, bf16[4,2,16,384]{3,2,1,0:T(8,128)(2,1)S(1)}, u32[]{:S(2)}, u32[]{:S(2)}) collective-permute-start(bf16[4,2,16,384]{3,2,1,0:T(8,128)(2,1)S(1)} %get-tuple-element.9), channel_id=1, source_target_pairs={{0,2},{2,0},{4,6},{6,4},{8,10},{10,8},{12,14},{14,12},{1,3},{3,1},... | collective-permute-start | bytes 294920 | tf_op jit(solution)/shard_map/ppermute | solution.py:410
  3.5 6.4 %collective-permute-start.1 = (bf16[4,2,16,384]{3,2,1,0:T(8,128)(2,1)S(1)}, bf16[4,2,16,384]{3,2,1,0:T(8,128)(2,1)S(1)}, u32[]{:S(2)}, u32[]{:S(2)}) collective-permute-start(bf16[4,2,16,384]{3,2,1,0:T(8,128)(2,1)S(1)} %get-tuple-element.9), channel_id=1, source_target_pairs={{0,6},{2,4},{4,10},{6,8},{8,14},{10,12},{12,0},{14,2},{1,7},{3,5},... | collective-permute-start | bytes 294920 | tf_op jit(solution)/shard_map/ppermute | solution.py:410
